TPU v7x, 32 devices: a whole 2x2x4 slice. The times are simulated.
32 devices in a mesh: sub: 32 (over z, y, x, core).
Axes of the slice: x: 2, y: 2, z: 4, core: 2. Of those that a mesh axis runs over, the one named last changes fastest.
Arguments:
- stiffness: float32 [32, 1024, 1024], P('sub'), as said below
- neumann_inv: float32 [32, 1024, 1024], P('sub'), as said below
- coarse_basis: float32 [32, 16, 1024], P('sub'), may hold values from -0.375 to 0.375
- coarse_inv: float32 [512, 512], P('sub'), as said below
- loads: float32 [32, 64, 1024], P('sub'), may hold values from -6 to 6
- face_index: int32 [32, 4, 128], P('sub'), may hold values from 0 to 1023, as said below
- face_len: int32 [32, 4], P('sub'), may hold values from 0 to 128, as said below
Outputs:
- solution: float32 [32, 64, 1024], P('sub')
- residual: float32 [32, 64, 1024], P('sub')
Inputs may be any that keep to these rules, and one draw needn't show every extreme that they name: `face_index`: within one subdomain all 512 entries are distinct. `face_len`: A block without a neighbour has length 0; paired blocks of two neighbours have equal length; some block has length 128. `stiffness`: each matrix is exactly symmetric and positive definite. `neumann_inv`: each matrix is exactly symmetric and positive definite. `coarse_inv`: the matrix is exactly symmetric and positive definite.
All inputs are finite; a program needn't handle non-finite values.
Results may differ from a plain program's by a relative error of at most 0.00022.
Values sent between devices are 32-bit elements; how exact they have to be, the bound alone decides.
No kernel may reach another device: no remote copies, remote signals or barrier semaphores. Data moves between devices by JAX's collectives and lax.ppermute only.
A program may use at most 64 MiB of HBM per device.

v0:
```python
import jax
import jax.numpy as jnp
from jax import lax
from jax.sharding import PartitionSpec as P

CYCLE = 16
ITERS = 4


HIGH = lax.Precision.HIGHEST


def from_behind(value, axis, by):
    length = lax.axis_size(axis)
    pairs = [(i, i + by) for i in range(length) if 0 <= i + by < length]
    return lax.ppermute(value, axis, pairs)


def local(stiffness, neumann_inv, coarse_basis, coarse_inv, loads, face_index, face_len):
    stiff = stiffness[0]
    local_inv = neumann_inv[0]
    basis = coarse_basis[0]
    width = face_index.shape[2]
    face_slots = face_index[0].reshape(-1)
    slot_pos = jnp.arange(width, dtype=jnp.int32)
    live_slots = (slot_pos[None, :] < face_len[0][:, None]).astype(jnp.float32).reshape(-1)
    counts = jnp.ones((stiff.shape[0],), jnp.float32).at[face_slots].add(live_slots)
    weight = 1.0 / counts

    def assemble(local_vals):
        cases = local_vals.shape[0]
        face_vals = jnp.take(local_vals, face_slots, axis=1) * live_slots[None, :]
        blocks = face_vals.reshape(cases, 4, width)
        west_in = from_behind(blocks[:, 1], "sub", 1)
        east_in = from_behind(blocks[:, 0], "sub", -1)
        south_in = from_behind(blocks[:, 3], "sub", CYCLE)
        north_in = from_behind(blocks[:, 2], "sub", -CYCLE)
        incoming = jnp.stack([west_in, east_in, south_in, north_in], axis=1).reshape(cases, -1)
        incoming = incoming * live_slots[None, :]
        return local_vals.at[:, face_slots].add(incoming)

    def inner(left, right):
        return jnp.sum(left * right * weight[None, :], axis=1)

    residual = assemble(loads[0])
    solution = jnp.zeros_like(residual)
    direction = residual
    along = residual
    gamma_old = None
    alpha_old = None
    for step in range(ITERS):
        scaled = weight[None, :] * residual
        local_sol = jnp.dot(scaled, local_inv, precision=HIGH)
        precond_coarse_res = jnp.einsum("cn,kn->ck", basis, scaled, precision=HIGH)
        coarse_sol = jnp.dot(
            coarse_inv,
            lax.all_gather(precond_coarse_res, "sub", axis=0, tiled=True),
            precision=HIGH,
        )
        local_sol = local_sol + jnp.einsum("ck,cn->kn", coarse_sol, basis, precision=HIGH)
        precond_res = assemble(weight[None, :] * local_sol)
        image = assemble(jnp.dot(precond_res, stiff, precision=HIGH))
        gamma, delta = lax.psum((inner(residual, precond_res), inner(image, precond_res)), "sub")
        if step == 0:
            alpha = gamma / delta
            direction = precond_res
            along = image
        else:
            beta = gamma / gamma_old
            alpha = gamma / (delta - beta * gamma / alpha_old)
            direction = precond_res + beta[:, None] * direction
            along = image + beta[:, None] * along
        solution = solution + alpha[:, None] * direction
        residual = residual - alpha[:, None] * along
        gamma_old = gamma
        alpha_old = alpha
    return (solution[None], residual[None])


def solution(mesh):
    placed = (
        P("sub", None, None),
        P("sub", None, None),
        P("sub", None, None),
        P("sub", None),
        P("sub", None, None),
        P("sub", None, None),
        P("sub", None),
    )
    return jax.shard_map(
        local,
        mesh=mesh,
        in_specs=placed,
        out_specs=(P("sub", None, None), P("sub", None, None)),
        check_vma=False,
    )
```

profile of v0, /device:TPU:0, one launch (start us, length us, event | category | flops | bytes accessed | tf_op | source)
XLA Modules:
  0.0 563.1 jit_solution(16011008665549368971)
XLA Ops:
  8.9 5.5 collective-permute-start.2
  16.4 4.1 scatter_custom_fusion.1
  24.7 42.3 %all_gather.12 = f32[512,64]{1,0:T(8,128)S(1)} all-gather(f32[16,64]{1,0:T(8,128)S(1)} %convolution_bitcast_fusion.3), channel_id=1, replica_groups=mesh['sub'=32] {'sub'}, dimensions={0}, use_global_device_ids=true | all-gather | bytes 135168 | tf_op jit(solution)/shard_map/all_gather | solution.py:57
  68.0 4.8 fusion.19
  77.8 5.4 collective-permute-start.6
  90.3 8.5 %fusion.6 = f32[64,1024]{0,1:T(8,128)S(1)} fusion(f32[64,1024]{0,1:T(8,128)S(1)} %scatter_custom_fusion.2, f32[1,1024,1024]{2,1,0:T(8,128)} %param.9), kind=kOutput, calls=%fused_computation.25 | convolution fusion | flops 805306368 | bytes 4718592 | tf_op jit(solution)/shard_map/dot_general | solution.py:62
  100.1 3.8 collective-permute-start.8
  105.2 5.4 collective-permute-start.10
  117.9 41.1 %all-reduce.3 = (f32[64]{0:T(128)S(1)}, f32[64]{0:T(128)S(1)}) all-reduce(f32[64]{0:T(128)S(1)} %get-tuple-element.10, f32[64]{0:T(128)S(1)} %get-tuple-element.9), channel_id=1, replica_groups=mesh['sub'=32] {'sub'}, use_global_device_ids=true, to_apply=%region_4.6 | all-reduce | flops 128 | bytes 1024 | tf_op jit(solution)/shard_map/psum | solution.py:63
  159.3 41.7 %all_gather.13 = f32[512,64]{1,0:T(8,128)S(1)} all-gather(f32[16,64]{1,0:T(8,128)S(1)} %convolution_bitcast_fusion.2), channel_id=1, replica_groups=mesh['sub'=32] {'sub'}, dimensions={0}, use_global_device_ids=true | all-gather | bytes 135168 | tf_op jit(solution)/shard_map/all_gather | solution.py:57
  202.0 4.8 fusion.25
  211.9 5.4 collective-permute-start.14
  220.7 3.9 scatter_custom_fusion.4
  224.6 8.5 %fusion.4 = f32[64,1024]{0,1:T(8,128)S(1)} fusion(f32[64,1024]{0,1:T(8,128)S(1)} %scatter_custom_fusion.4, f32[1,1024,1024]{2,1,0:T(8,128)} %param.9), kind=kOutput, calls=%fused_computation.23 | convolution fusion | flops 805306368 | bytes 4718592 | tf_op jit(solution)/shard_map/dot_general | solution.py:62
  234.3 3.8 collective-permute-start.16
  239.5 5.4 collective-permute-start.18
  252.1 41.1 %all-reduce.2 = (f32[64]{0:T(128)S(1)}, f32[64]{0:T(128)S(1)}) all-reduce(f32[64]{0:T(128)S(1)} %get-tuple-element.8, f32[64]{0:T(128)S(1)} %get-tuple-element.7), channel_id=1, replica_groups=mesh['sub'=32] {'sub'}, use_global_device_ids=true, to_apply=%region_10.12 | all-reduce | flops 128 | bytes 1024 | tf_op jit(solution)/shard_map/psum | solution.py:63
  293.6 41.9 %all_gather.14 = f32[512,64]{1,0:T(8,128)S(1)} all-gather(f32[16,64]{1,0:T(8,128)S(1)} %convolution_bitcast_fusion.1), channel_id=1, replica_groups=mesh['sub'=32] {'sub'}, dimensions={0}, use_global_device_ids=true | all-gather | bytes 135168 | tf_op jit(solution)/shard_map/all_gather | solution.py:57
  336.4 4.8 fusion.31
  346.3 5.4 collective-permute-start.22
  358.6 8.5 %fusion.2 = f32[64,1024]{0,1:T(8,128)S(1)} fusion(f32[64,1024]{0,1:T(8,128)S(1)} %scatter_custom_fusion.6, f32[1,1024,1024]{2,1,0:T(8,128)} %param.9), kind=kOutput, calls=%fused_computation.21 | convolution fusion | flops 805306368 | bytes 4718592 | tf_op jit(solution)/shard_map/dot_general | solution.py:62
  368.4 3.8 collective-permute-start.24
  373.5 5.4 collective-permute-start.26
  386.3 41.1 %all-reduce.1 = (f32[64]{0:T(128)S(1)}, f32[64]{0:T(128)S(1)}) all-reduce(f32[64]{0:T(128)S(1)} %get-tuple-element.6, f32[64]{0:T(128)S(1)} %get-tuple-element.5), channel_id=1, replica_groups=mesh['sub'=32] {'sub'}, use_global_device_ids=true, to_apply=%region_16.18 | all-reduce | flops 128 | bytes 1024 | tf_op jit(solution)/shard_map/psum | solution.py:63
  427.9 41.7 %all_gather.15 = f32[512,64]{1,0:T(8,128)S(1)} all-gather(f32[16,64]{1,0:T(8,128)S(1)} %convolution_bitcast_fusion), channel_id=1, replica_groups=mesh['sub'=32] {'sub'}, dimensions={0}, use_global_device_ids=true | all-gather | bytes 135168 | tf_op jit(solution)/shard_map/all_gather | solution.py:57
  470.5 4.8 fusion.37
  480.4 5.4 collective-permute-start.30
  489.2 3.8 scatter_custom_fusion.8
  493.0 8.5 %fusion = f32[64,1024]{0,1:T(8,128)S(1)} fusion(f32[64,1024]{0,1:T(8,128)S(1)} %scatter_custom_fusion.8, f32[1,1024,1024]{2,1,0:T(8,128)} %param.9), kind=kOutput, calls=%fused_computation.19 | convolution fusion | flops 805306368 | bytes 4718592 | tf_op jit(solution)/shard_map/dot_general | solution.py:62
  502.7 3.8 collective-permute-start.32
  507.8 5.4 collective-permute-start.34
  520.5 41.1 %all-reduce = (f32[64]{0:T(128)S(1)}, f32[64]{0:T(128)S(1)}) all-reduce(f32[64]{0:T(128)S(1)} %get-tuple-element.4, f32[64]{0:T(128)S(1)} %get-tuple-element.3), channel_id=1, replica_groups=mesh['sub'=32] {'sub'}, use_global_device_ids=true, to_apply=%region_22.24 | all-reduce | flops 128 | bytes 1024 | tf_op jit(solution)/shard_map/psum | solution.py:63
  (159 shorter events, 99.5 us)
Async XLA Ops:
  5.2 15.3 %collective-permute-start = (f32[64,128]{0,1:T(8,128)S(1)}, f32[64,128]{0,1:T(8,128)S(1)}, u32[]{:S(2)}, u32[]{:S(2)}) collective-permute-start(f32[64,128]{0,1:T(8,128)S(1)} %get-tuple-element.61), channel_id=1, source_target_pairs={{0,1},{1,2},{2,3},{3,4},{4,5},{5,6},{6,7},{7,8},{8,9},{9,10},{10,1... | collective-permute-start | bytes 98312 | tf_op jit(solution)/shard_map/ppermute | solution.py:16
  7.6 12.9 %collective-permute-start.3 = (f32[64,128]{0,1:T(8,128)S(1)}, f32[64,128]{0,1:T(8,128)S(1)}, u32[]{:S(2)}, u32[]{:S(2)}) collective-permute-start(f32[64,128]{0,1:T(8,128)S(1)} %get-tuple-element.62), channel_id=1, source_target_pairs={{16,0},{17,1},{18,2},{19,3},{20,4},{21,5},{22,6},{23,7},{24,8},{25... | collective-permute-start | bytes 98312 | tf_op jit(solution)/shard_map/ppermute | solution.py:16
  8.9 11.6 %collective-permute-start.2 = (f32[64,128]{0,1:T(8,128)S(1)}, f32[64,128]{0,1:T(8,128)S(1)}, u32[]{:S(2)}, u32[]{:S(2)}) collective-permute-start(f32[64,128]{0,1:T(8,128)S(1)} %get-tuple-element.63), channel_id=1, source_target_pairs={{0,16},{1,17},{2,18},{3,19},{4,20},{5,21},{6,22},{7,23},{8,24},{9,... | collective-permute-start | bytes 98312 | tf_op jit(solution)/shard_map/ppermute | solution.py:16
  14.4 6.1 %collective-permute-start.1 = (f32[64,128]{0,1:T(8,128)S(1)}, f32[64,128]{0,1:T(8,128)S(1)}, u32[]{:S(2)}, u32[]{:S(2)}) collective-permute-start(f32[64,128]{0,1:T(8,128)S(1)} %get-tuple-element.64), channel_id=1, source_target_pairs={{1,0},{2,1},{3,2},{4,3},{5,4},{6,5},{7,6},{8,7},{9,8},{10,9},{11,1... | collective-permute-start | bytes 98312 | tf_op jit(solution)/shard_map/ppermute | solution.py:16
  74.3 10.3 %collective-permute-start.4 = (f32[64,128]{0,1:T(8,128)S(1)}, f32[64,128]{0,1:T(8,128)S(1)}, u32[]{:S(2)}, u32[]{:S(2)}) collective-permute-start(f32[64,128]{0,1:T(8,128)S(1)} %get-tuple-element.57), channel_id=1, source_target_pairs={{0,1},{1,2},{2,3},{3,4},{4,5},{5,6},{6,7},{7,8},{8,9},{9,10},{10,1... | collective-permute-start | bytes 98312 | tf_op jit(solution)/shard_map/ppermute | solution.py:16
  76.5 8.1 %collective-permute-start.7 = (f32[64,128]{0,1:T(8,128)S(1)}, f32[64,128]{0,1:T(8,128)S(1)}, u32[]{:S(2)}, u32[]{:S(2)}) collective-permute-start(f32[64,128]{0,1:T(8,128)S(1)} %get-tuple-element.58), channel_id=1, source_target_pairs={{16,0},{17,1},{18,2},{19,3},{20,4},{21,5},{22,6},{23,7},{24,8},{25... | collective-permute-start | bytes 98312 | tf_op jit(solution)/shard_map/ppermute | solution.py:16
  77.8 7.3 %collective-permute-start.6 = (f32[64,128]{0,1:T(8,128)S(1)}, f32[64,128]{0,1:T(8,128)S(1)}, u32[]{:S(2)}, u32[]{:S(2)}) collective-permute-start(f32[64,128]{0,1:T(8,128)S(1)} %get-tuple-element.59), channel_id=1, source_target_pairs={{0,16},{1,17},{2,18},{3,19},{4,20},{5,21},{6,22},{7,23},{8,24},{9,... | collective-permute-start | bytes 98312 | tf_op jit(solution)/shard_map/ppermute | solution.py:16
  83.3 3.1 collective-permute-start.5
  100.1 12.0 %collective-permute-start.8 = (f32[64,128]{0,1:T(8,128)S(1)}, f32[64,128]{0,1:T(8,128)S(1)}, u32[]{:S(2)}, u32[]{:S(2)}) collective-permute-start(f32[64,128]{0,1:T(8,128)S(1)} %get-tuple-element.53), channel_id=1, source_target_pairs={{0,1},{1,2},{2,3},{3,4},{4,5},{5,6},{6,7},{7,8},{8,9},{9,10},{10,1... | collective-permute-start | bytes 98312 | tf_op jit(solution)/shard_map/ppermute | solution.py:16
  103.9 8.3 %collective-permute-start.11 = (f32[64,128]{0,1:T(8,128)S(1)}, f32[64,128]{0,1:T(8,128)S(1)}, u32[]{:S(2)}, u32[]{:S(2)}) collective-permute-start(f32[64,128]{0,1:T(8,128)S(1)} %get-tuple-element.54), channel_id=1, source_target_pairs={{16,0},{17,1},{18,2},{19,3},{20,4},{21,5},{22,6},{23,7},{24,8},{25... | collective-permute-start | bytes 98312 | tf_op jit(solution)/shard_map/ppermute | solution.py:16
  105.2 7.3 %collective-permute-start.10 = (f32[64,128]{0,1:T(8,128)S(1)}, f32[64,128]{0,1:T(8,128)S(1)}, u32[]{:S(2)}, u32[]{:S(2)}) collective-permute-start(f32[64,128]{0,1:T(8,128)S(1)} %get-tuple-element.55), channel_id=1, source_target_pairs={{0,16},{1,17},{2,18},{3,19},{4,20},{5,21},{6,22},{7,23},{8,24},{9,... | collective-permute-start | bytes 98312 | tf_op jit(solution)/shard_map/ppermute | solution.py:16
  110.7 3.1 collective-permute-start.9
  208.3 10.3 %collective-permute-start.12 = (f32[64,128]{0,1:T(8,128)S(1)}, f32[64,128]{0,1:T(8,128)S(1)}, u32[]{:S(2)}, u32[]{:S(2)}) collective-permute-start(f32[64,128]{0,1:T(8,128)S(1)} %get-tuple-element.49), channel_id=1, source_target_pairs={{0,1},{1,2},{2,3},{3,4},{4,5},{5,6},{6,7},{7,8},{8,9},{9,10},{10,1... | collective-permute-start | bytes 98312 | tf_op jit(solution)/shard_map/ppermute | solution.py:16
  210.6 8.1 %collective-permute-start.15 = (f32[64,128]{0,1:T(8,128)S(1)}, f32[64,128]{0,1:T(8,128)S(1)}, u32[]{:S(2)}, u32[]{:S(2)}) collective-permute-start(f32[64,128]{0,1:T(8,128)S(1)} %get-tuple-element.50), channel_id=1, source_target_pairs={{16,0},{17,1},{18,2},{19,3},{20,4},{21,5},{22,6},{23,7},{24,8},{25... | collective-permute-start | bytes 98312 | tf_op jit(solution)/shard_map/ppermute | solution.py:16
  211.9 7.3 %collective-permute-start.14 = (f32[64,128]{0,1:T(8,128)S(1)}, f32[64,128]{0,1:T(8,128)S(1)}, u32[]{:S(2)}, u32[]{:S(2)}) collective-permute-start(f32[64,128]{0,1:T(8,128)S(1)} %get-tuple-element.51), channel_id=1, source_target_pairs={{0,16},{1,17},{2,18},{3,19},{4,20},{5,21},{6,22},{7,23},{8,24},{9,... | collective-permute-start | bytes 98312 | tf_op jit(solution)/shard_map/ppermute | solution.py:16
  217.3 3.1 collective-permute-start.13
  234.3 12.0 %collective-permute-start.16 = (f32[64,128]{0,1:T(8,128)S(1)}, f32[64,128]{0,1:T(8,128)S(1)}, u32[]{:S(2)}, u32[]{:S(2)}) collective-permute-start(f32[64,128]{0,1:T(8,128)S(1)} %get-tuple-element.45), channel_id=1, source_target_pairs={{0,1},{1,2},{2,3},{3,4},{4,5},{5,6},{6,7},{7,8},{8,9},{9,10},{10,1... | collective-permute-start | bytes 98312 | tf_op jit(solution)/shard_map/ppermute | solution.py:16
  238.2 8.3 %collective-permute-start.19 = (f32[64,128]{0,1:T(8,128)S(1)}, f32[64,128]{0,1:T(8,128)S(1)}, u32[]{:S(2)}, u32[]{:S(2)}) collective-permute-start(f32[64,128]{0,1:T(8,128)S(1)} %get-tuple-element.46), channel_id=1, source_target_pairs={{16,0},{17,1},{18,2},{19,3},{20,4},{21,5},{22,6},{23,7},{24,8},{25... | collective-permute-start | bytes 98312 | tf_op jit(solution)/shard_map/ppermute | solution.py:16
  239.5 7.3 %collective-permute-start.18 = (f32[64,128]{0,1:T(8,128)S(1)}, f32[64,128]{0,1:T(8,128)S(1)}, u32[]{:S(2)}, u32[]{:S(2)}) collective-permute-start(f32[64,128]{0,1:T(8,128)S(1)} %get-tuple-element.47), channel_id=1, source_target_pairs={{0,16},{1,17},{2,18},{3,19},{4,20},{5,21},{6,22},{7,23},{8,24},{9,... | collective-permute-start | bytes 98312 | tf_op jit(solution)/shard_map/ppermute | solution.py:16
  244.9 3.1 collective-permute-start.17
  342.8 10.3 %collective-permute-start.20 = (f32[64,128]{0,1:T(8,128)S(1)}, f32[64,128]{0,1:T(8,128)S(1)}, u32[]{:S(2)}, u32[]{:S(2)}) collective-permute-start(f32[64,128]{0,1:T(8,128)S(1)} %get-tuple-element.41), channel_id=1, source_target_pairs={{0,1},{1,2},{2,3},{3,4},{4,5},{5,6},{6,7},{7,8},{8,9},{9,10},{10,1... | collective-permute-start | bytes 98312 | tf_op jit(solution)/shard_map/ppermute | solution.py:16
  345.0 8.1 %collective-permute-start.23 = (f32[64,128]{0,1:T(8,128)S(1)}, f32[64,128]{0,1:T(8,128)S(1)}, u32[]{:S(2)}, u32[]{:S(2)}) collective-permute-start(f32[64,128]{0,1:T(8,128)S(1)} %get-tuple-element.42), channel_id=1, source_target_pairs={{16,0},{17,1},{18,2},{19,3},{20,4},{21,5},{22,6},{23,7},{24,8},{25... | collective-permute-start | bytes 98312 | tf_op jit(solution)/shard_map/ppermute | solution.py:16
  346.3 7.3 %collective-permute-start.22 = (f32[64,128]{0,1:T(8,128)S(1)}, f32[64,128]{0,1:T(8,128)S(1)}, u32[]{:S(2)}, u32[]{:S(2)}) collective-permute-start(f32[64,128]{0,1:T(8,128)S(1)} %get-tuple-element.43), channel_id=1, source_target_pairs={{0,16},{1,17},{2,18},{3,19},{4,20},{5,21},{6,22},{7,23},{8,24},{9,... | collective-permute-start | bytes 98312 | tf_op jit(solution)/shard_map/ppermute | solution.py:16
  368.4 12.0 %collective-permute-start.24 = (f32[64,128]{0,1:T(8,128)S(1)}, f32[64,128]{0,1:T(8,128)S(1)}, u32[]{:S(2)}, u32[]{:S(2)}) collective-permute-start(f32[64,128]{0,1:T(8,128)S(1)} %get-tuple-element.37), channel_id=1, source_target_pairs={{0,1},{1,2},{2,3},{3,4},{4,5},{5,6},{6,7},{7,8},{8,9},{9,10},{10,1... | collective-permute-start | bytes 98312 | tf_op jit(solution)/shard_map/ppermute | solution.py:16
  372.2 8.3 %collective-permute-start.27 = (f32[64,128]{0,1:T(8,128)S(1)}, f32[64,128]{0,1:T(8,128)S(1)}, u32[]{:S(2)}, u32[]{:S(2)}) collective-permute-start(f32[64,128]{0,1:T(8,128)S(1)} %get-tuple-element.38), channel_id=1, source_target_pairs={{16,0},{17,1},{18,2},{19,3},{20,4},{21,5},{22,6},{23,7},{24,8},{25... | collective-permute-start | bytes 98312 | tf_op jit(solution)/shard_map/ppermute | solution.py:16
  373.5 7.3 %collective-permute-start.26 = (f32[64,128]{0,1:T(8,128)S(1)}, f32[64,128]{0,1:T(8,128)S(1)}, u32[]{:S(2)}, u32[]{:S(2)}) collective-permute-start(f32[64,128]{0,1:T(8,128)S(1)} %get-tuple-element.39), channel_id=1, source_target_pairs={{0,16},{1,17},{2,18},{3,19},{4,20},{5,21},{6,22},{7,23},{8,24},{9,... | collective-permute-start | bytes 98312 | tf_op jit(solution)/shard_map/ppermute | solution.py:16
  476.9 10.3 %collective-permute-start.28 = (f32[64,128]{0,1:T(8,128)S(1)}, f32[64,128]{0,1:T(8,128)S(1)}, u32[]{:S(2)}, u32[]{:S(2)}) collective-permute-start(f32[64,128]{0,1:T(8,128)S(1)} %get-tuple-element.33), channel_id=1, source_target_pairs={{0,1},{1,2},{2,3},{3,4},{4,5},{5,6},{6,7},{7,8},{8,9},{9,10},{10,1... | collective-permute-start | bytes 98312 | tf_op jit(solution)/shard_map/ppermute | solution.py:16
  479.1 8.1 %collective-permute-start.31 = (f32[64,128]{0,1:T(8,128)S(1)}, f32[64,128]{0,1:T(8,128)S(1)}, u32[]{:S(2)}, u32[]{:S(2)}) collective-permute-start(f32[64,128]{0,1:T(8,128)S(1)} %get-tuple-element.34), channel_id=1, source_target_pairs={{16,0},{17,1},{18,2},{19,3},{20,4},{21,5},{22,6},{23,7},{24,8},{25... | collective-permute-start | bytes 98312 | tf_op jit(solution)/shard_map/ppermute | solution.py:16
  480.4 7.3 %collective-permute-start.30 = (f32[64,128]{0,1:T(8,128)S(1)}, f32[64,128]{0,1:T(8,128)S(1)}, u32[]{:S(2)}, u32[]{:S(2)}) collective-permute-start(f32[64,128]{0,1:T(8,128)S(1)} %get-tuple-element.35), channel_id=1, source_target_pairs={{0,16},{1,17},{2,18},{3,19},{4,20},{5,21},{6,22},{7,23},{8,24},{9,... | collective-permute-start | bytes 98312 | tf_op jit(solution)/shard_map/ppermute | solution.py:16
  502.7 12.0 %collective-permute-start.32 = (f32[64,128]{0,1:T(8,128)S(1)}, f32[64,128]{0,1:T(8,128)S(1)}, u32[]{:S(2)}, u32[]{:S(2)}) collective-permute-start(f32[64,128]{0,1:T(8,128)S(1)} %get-tuple-element.29), channel_id=1, source_target_pairs={{0,1},{1,2},{2,3},{3,4},{4,5},{5,6},{6,7},{7,8},{8,9},{9,10},{10,1... | collective-permute-start | bytes 98312 | tf_op jit(solution)/shard_map/ppermute | solution.py:16
  506.5 8.3 %collective-permute-start.35 = (f32[64,128]{0,1:T(8,128)S(1)}, f32[64,128]{0,1:T(8,128)S(1)}, u32[]{:S(2)}, u32[]{:S(2)}) collective-permute-start(f32[64,128]{0,1:T(8,128)S(1)} %get-tuple-element.30), channel_id=1, source_target_pairs={{16,0},{17,1},{18,2},{19,3},{20,4},{21,5},{22,6},{23,7},{24,8},{25... | collective-permute-start | bytes 98312 | tf_op jit(solution)/shard_map/ppermute | solution.py:16
  507.8 7.3 %collective-permute-start.34 = (f32[64,128]{0,1:T(8,128)S(1)}, f32[64,128]{0,1:T(8,128)S(1)}, u32[]{:S(2)}, u32[]{:S(2)}) collective-permute-start(f32[64,128]{0,1:T(8,128)S(1)} %get-tuple-element.31), channel_id=1, source_target_pairs={{0,16},{1,17},{2,18},{3,19},{4,20},{5,21},{6,22},{7,23},{8,24},{9,... | collective-permute-start | bytes 98312 | tf_op jit(solution)/shard_map/ppermute | solution.py:16
  (6 other events, 102.8 us)
where the time goes:
time: 572 us; the launch traced here: 563 us
  blocking collectives  332 us (58%)
  starting transfers between devices  98.9 us (17%)
  matrix products  58 us (10%)
  other arithmetic  44.9 us (8%)
  waiting for transfers between devices  13.9 us (2%)
  local copies, waits for them, and re-layouts  13.1 us (2%)
    all_gather x4, blocking collectives, local(): lax.all_gather(precond_coarse_res, 'sub', axis=0, tiled=True)  168 us
    psum x4, blocking collectives, local(): lax.psum((inner(residual, precond_res), inner(image, precond_res)), 'sub')  164 us
    ppermute x36, starting transfers between devices, from_behind(): return lax.ppermute(value, axis, pairs)  98.9 us
    dot_general x4, matrix products, local(): image = assemble(jnp.dot(precond_res, stiff, precision=HIGH))  33.9 us
    scatter-add x9, other arithmetic, assemble(): return local_vals.at[:, face_slots].add(incoming)  32.8 us
    dot_general x4, matrix products, local(): local_sol = jnp.dot(scaled, local_inv, precision=HIGH)  19.4 us
    ppermute x36, waiting for transfers between devices, from_behind(): return lax.ppermute(value, axis, pairs)  13.9 us
  transfers between devices with their start and end apart: 36, of which 16 were waited for; matrix products, arithmetic and copies ran while one was open for 1% of the time, Pallas kernels for 0%

commit v1 on v0

v1 whole, which is shorter than its diff:
```python
import jax
import jax.numpy as jnp
from jax import lax
from jax.sharding import PartitionSpec as P

CYCLE = 16
ITERS = 4

BF = jnp.bfloat16
F32 = jnp.float32


def split(value):
    high = lax.reduce_precision(value, 8, 7)
    return high.astype(BF), (value - high).astype(BF)


def contract(left, right, dims=((1,), (0,))):
    return lax.dot_general(left, right, (dims, ((), ())), preferred_element_type=F32)


def stacked(value):
    high, low = split(value)
    return jnp.concatenate([high, low], axis=0)


def times(value, parts, dims=((1,), (0,))):
    rows = value.shape[0]
    both = stacked(value)
    first = contract(both, parts[0], dims)
    second = contract(both[:rows], parts[1], dims)
    return first[:rows] + first[rows:] + second


def pick(value, onehot, dims=((1,), (0,))):
    rows = value.shape[0]
    both = contract(stacked(value), onehot, dims)
    return both[:rows] + both[rows:]


def swaps(total):
    sets = []
    for by in (1, CYCLE):
        for parity in (0, 1):
            ahead = [i for i in range(total - by) if (i // by) % 2 == parity]
            sets.append((by, parity, [(i, i + by) for i in ahead] + [(i + by, i) for i in ahead]))
    return sets


def local(stiffness, neumann_inv, coarse_basis, coarse_inv, loads, face_index, face_len):
    total = lax.axis_size("sub")
    me = lax.axis_index("sub")
    basis = coarse_basis[0]
    load = loads[0]
    cases, ndof = load.shape
    primal = basis.shape[0]
    width = face_index.shape[2]

    chosen = []
    for at, (by, parity, pairs) in enumerate(swaps(total)):
        if pairs:
            behind, ahead = (0, 1) if by == 1 else (2, 3)
            forward = (me // by) % 2 == parity
            chosen.append((pairs, behind, ahead, forward))
    blocks = len(chosen)
    index = jnp.concatenate([jnp.where(f, face_index[0, a], face_index[0, b]) for _, b, a, f in chosen])
    length = jnp.stack([jnp.where(f, face_len[0, a], face_len[0, b]) for _, b, a, f in chosen])
    slot = jnp.arange(width, dtype=jnp.int32)
    live = (slot[None, :] < length[:, None]).reshape(-1)
    onehot = ((index[:, None] == jnp.arange(ndof, dtype=jnp.int32)[None, :]) & live[:, None]).astype(BF)
    shared = jnp.sum(onehot.astype(F32), axis=0)
    weight = 1.0 / (1.0 + shared)

    def exchange(faces):
        order = [2, 0, 1, 3][:blocks] if blocks > 2 else list(range(blocks))
        got = [None] * blocks
        for at in order:
            piece = faces[:, at * width:(at + 1) * width]
            got[at] = lax.ppermute(piece, "sub", chosen[at][0])
        return jnp.concatenate(got, axis=1)

    def spread(value):
        flat = value.reshape(1, -1)
        got = lax.all_to_all(jnp.broadcast_to(flat, (total, flat.shape[1])), "sub", 0, 0, tiled=True)
        return got.reshape((total,) + value.shape)

    weighted_basis = basis * weight[None, :]
    basis_faces = pick(weighted_basis, onehot, ((1,), (1,)))
    load_faces = pick(load, onehot, ((1,), (1,)))
    coarse_rows = coarse_inv.shape[1]
    reps = -(-coarse_rows // width)
    inv_packed = jnp.concatenate([coarse_inv[:, i * width:(i + 1) * width] for i in range(reps)], axis=0)
    outgoing = jnp.concatenate([load_faces, basis_faces], axis=0)
    packed = []
    for at in range(blocks):
        packed.append(jnp.concatenate([outgoing[:, at * width:(at + 1) * width], inv_packed], axis=0))
    incoming = exchange(jnp.concatenate(packed, axis=1))

    functions = [weighted_basis]
    rows = [coarse_inv]
    for at in range(blocks):
        part = incoming[:, at * width:(at + 1) * width]
        functions.append(pick(part[cases:cases + primal], onehot[at * width:(at + 1) * width]))
        inv_part = part[cases + primal:]
        rows.append(jnp.concatenate([inv_part[i * primal:(i + 1) * primal] for i in range(reps)], axis=1))
    functions = jnp.concatenate(functions, axis=0)
    rows = split(jnp.concatenate(rows, axis=0))

    def widen(matrix, scale):
        high, low = split(matrix)
        if scale is not None:
            factor = (scale[:, None] * scale[None, :]).astype(BF)
            high, low = high * factor, low * factor
        return [
            jnp.concatenate([part, contract(part, onehot, ((1,), (1,))).astype(BF)], axis=1)
            for part in (high, low)
        ]

    inv_wide = widen(neumann_inv[0], weight)
    stiff_wide = widen(stiffness[0], None)
    function_image = times(functions, stiff_wide)
    function_all = jnp.concatenate([functions, function_image], axis=1)
    function_all = split(function_all)

    def dot(left, right):
        return jnp.sum(left * right, axis=1)


    def apply_both(value, coarse, sums):
        lines = coarse if sums is None else jnp.concatenate([coarse, sums], axis=0)
        everyone = spread(lines)
        wide = times(value, inv_wide)
        inside = wide[:, :ndof] + pick(exchange(wide[:, ndof:]), onehot)
        image = times(inside, stiff_wide)
        gathered = everyone[:, :primal].reshape(total * primal, cases)
        factors = times(gathered.T, rows, ((1,), (1,)))
        extra = times(factors, function_all)
        inside = inside + extra[:, :ndof]
        image = image + extra[:, ndof:]
        summed = None if sums is None else jnp.sum(everyone[:, primal:], axis=0)
        return inside, image, summed

    basis_parts = split(weighted_basis)
    basis_face_parts = split(basis_faces)

    def coarse_of(value):
        return times(value, basis_parts, ((1,), (1,))).T

    load_in = incoming[:cases]
    load_in = jnp.concatenate([load_in[:, at * width:(at + 1) * width] for at in range(blocks)], axis=1)
    residual = load + pick(load_in, onehot)
    u, image, _ = apply_both(residual, coarse_of(residual), None)
    gamma = dot(weight[None, :] * residual, u)
    delta = dot(image[:, :ndof], u)
    w = image[:, :ndof] + pick(exchange(image[:, ndof:]), onehot)
    z = q = s = p = None
    solution = None
    alpha_old = gamma_old = None
    for step in range(ITERS):
        sums = jnp.stack([gamma, delta], axis=0)
        last = step + 1 == ITERS
        if last:
            gamma, delta = jnp.sum(spread(sums), axis=0)
        else:
            m, image, summed = apply_both(w, coarse_of(w), sums)
            gamma, delta = summed
        if step == 0:
            alpha = gamma / delta
            p, s = u, w
            solution = alpha[:, None] * p
            if not last:
                q = m
        else:
            beta = gamma / gamma_old
            alpha = gamma / (delta - beta * gamma / alpha_old)
            p = u + beta[:, None] * p
            s = w + beta[:, None] * s
            solution = solution + alpha[:, None] * p
            if not last:
                q = m + beta[:, None] * q
        residual = residual - alpha[:, None] * s
        if not last:
            u = u - alpha[:, None] * q
            gamma_old, alpha_old = gamma, alpha
            gamma = dot(weight[None, :] * residual, u)
            own = image[:, :ndof]
            n = own + pick(exchange(image[:, ndof:]), onehot)
            before = weight[None, :] * w - alpha[:, None] * own
            if step == 0:
                z = n
            else:
                before = before - (alpha * beta)[:, None] * (weight[None, :] * z)
                z = n + beta[:, None] * z
            delta = dot(before, u)
            w = w - alpha[:, None] * z
    return (solution[None], residual[None])


def solution(mesh):
    placed = (
        P("sub", None, None),
        P("sub", None, None),
        P("sub", None, None),
        P("sub", None),
        P("sub", None, None),
        P("sub", None, None),
        P("sub", None),
    )
    return jax.shard_map(
        local,
        mesh=mesh,
        in_specs=placed,
        out_specs=(P("sub", None, None), P("sub", None, None)),
        check_vma=False,
    )
```

time: 572 us -> 185 us (0.32); the launches traced: 563 us -> 183 us
  blocking collectives: 332 us -> 0 us
  other arithmetic: 44.9 us -> 16.8 us
  starting transfers between devices: 98.9 us -> 71.4 us
  matrix products: 58 us -> 42.3 us
  local copies, waits for them, and re-layouts: 13.1 us -> 23.1 us
  waiting for transfers between devices: 13.9 us -> 23.3 us
    all_gather x4 -> x0, blocking collectives: 168 us -> none  [local(): lax.all_gather(precond_coarse_res, 'sub', axis=0, tiled=True)]
    psum x4 -> x0, blocking collectives: 164 us -> none  [local(): lax.psum((inner(residual, precond_res), inner(image, precond_res)), 'sub')]
    ppermute x36 -> x27, starting transfers between devices: 98.9 us -> 56.2 us  [exchange(): got[at] = lax.ppermute(piece, 'sub', chosen[at][0])]
    scatter-add x10 -> x0, other arithmetic: 36.9 us -> none  [the longest x9 32.8 us: assemble(): return local_vals.at[:, face_slots].add(incoming)]
    dot_general x20 -> x60, matrix products: 58 us -> 42.3 us  [contract(): lax.dot_general(left, right, (dims, ((), ())), preferred_element_type=F32)]
    all_to_all x0 -> x5, starting transfers between devices: none -> 15.2 us  [spread(): lax.all_to_all(jnp.broadcast_to(flat, (total, flat.shape[1])), 'sub', 0,...]
    unnamed x5 -> x158, local copies, waits for them, and re-layouts: 1.16 us -> 11.5 us
    gather x9 -> x0, local copies, waits for them, and re-layouts: 9.33 us -> none  [assemble(): face_vals = jnp.take(local_vals, face_slots, axis=1) * live_slots[None, :]]
  transfers between devices with their start and end apart: 36 -> 32, of which waited for: 16 -> 8; matrix products, arithmetic and copies ran while one was open for 1% -> 21% of each run, Pallas kernels for 0% -> 0%
where the time goes in v1:
time: 185 us; the launch traced here: 183 us
  starting transfers between devices  71.4 us (39%)
  matrix products  42.3 us (23%)
  waiting for transfers between devices  23.3 us (13%)
  local copies, waits for them, and re-layouts  23.1 us (12%)
  other arithmetic  16.8 us (9%)
  between operations  6.34 us (3%)
    ppermute x27, starting transfers between devices, exchange(): got[at] = lax.ppermute(piece, 'sub', chosen[at][0])  56.2 us
    dot_general x60, matrix products, contract(): lax.dot_general(left, right, (dims, ((), ())), preferred_element_type=F32)  42.3 us
    all_to_all x5, starting transfers between devices, spread(): lax.all_to_all(jnp.broadcast_to(flat, (total, flat.shape[1])), 'sub', 0,...  15.2 us
    ppermute x27, waiting for transfers between devices, exchange(): got[at] = lax.ppermute(piece, 'sub', chosen[at][0])  14.7 us
    unnamed x158, local copies, waits for them, and re-layouts  11.5 us
    all_to_all x5, waiting for transfers between devices, spread(): lax.all_to_all(jnp.broadcast_to(flat, (total, flat.shape[1])), 'sub', 0,...  8.55 us
    convert_element_type x4, local copies, waits for them, and re-layouts, widen(): contract(part, onehot, ((1,), (1,))).astype(BF)  5.61 us
    convert_element_type x37, other arithmetic, split(): return (high.astype(BF), (value - high).astype(BF))  4.62 us
  transfers between devices with their start and end apart: 32, of which 8 were waited for; matrix products, arithmetic and copies ran while one was open for 21% of the time, Pallas kernels for 0%

profile of v1, /device:TPU:0, one launch (start us, length us, event | category | flops | bytes accessed | tf_op | source)
XLA Modules:
  0.0 183.3 jit_solution(17206416612308964072)
XLA Ops:
  10.4 4.1 %collective-permute-start.2 = (f32[144,128]{1,0:T(8,128)S(1)}, f32[144,128]{1,0:T(8,128)S(1)}, u32[]{:S(2)}, u32[]{:S(2)}) collective-permute-start(f32[144,128]{1,0:T(8,128)S(1)} %constant_dynamic-update-slice_fusion.10), channel_id=1, source_target_pairs={{0,16},{1,17},{2,18},{3,19},{4,20},{5,21},{6,22},{7,23},{8,24},{9,... | collective-permute-start | bytes 221192 | tf_op jit(solution)/shard_map/ppermute | solution.py:79
  15.2 2.9 %collective-permute-start = (f32[144,128]{1,0:T(8,128)S(1)}, f32[144,128]{1,0:T(8,128)S(1)}, u32[]{:S(2)}, u32[]{:S(2)}) collective-permute-start(f32[144,128]{1,0:T(8,128)S(1)} %get-tuple-element.143), channel_id=1, source_target_pairs={{0,1},{2,3},{4,5},{6,7},{8,9},{10,11},{12,13},{14,15},{16,17},{18,... | collective-permute-start | bytes 221192 | tf_op jit(solution)/shard_map/ppermute | solution.py:79
  18.1 3.1 %fusion.2 = (bf16[1024,1024]{1,0:T(8,128)(2,1)S(1)}, bf16[1024,1024]{1,0:T(8,128)(2,1)S(1)}) fusion(f32[1,1024,1024]{2,1,0:T(8,128)} %param.8, f32[1024]{0:T(1024)S(1)} %add_divide_fusion), kind=kLoop, calls=%fused_computation.11 | loop fusion | flops 13631488 | bytes 8392704 | tf_op jit(solution)/shard_map/mul | solution.py:113
  26.8 2.2 %fusion.9 = bf16[1024,384]{0,1:T(8,128)(2,1)} fusion(bf16[1024,1024]{1,0:T(8,128)(2,1)S(1)} %get-tuple-element.49, s32[384]{0:T(512)S(1)} %pad_add_fusion, pred[384]{0:T(512)(128)(4,1)S(1)} %fusion.189), kind=kOutput, calls=%fused_computation.37 | convolution fusion | flops 806486016 | bytes 2885504 | tf_op jit(solution)/shard_map/dot_general | solution.py:19
  29.0 2.0 %convolution_convert_fusion = bf16[1024,384]{0,1:T(8,128)(2,1)} fusion(bf16[1024,1024]{1,0:T(8,128)(2,1)S(1)} %get-tuple-element.48, s32[384]{0:T(512)S(1)} %pad_add_fusion, pred[384]{0:T(512)(128)(4,1)S(1)} %fusion.189), kind=kOutput, calls=%fused_computation.33 | convolution fusion | flops 806486016 | bytes 2885504 | tf_op jit(solution)/shard_map/dot_general | solution.py:19
  43.9 3.5 %all-to-all-start = ((f32[32,1,1024]{2,1,0:T(1,128)}), f32[32,1,1024]{2,1,0:T(1,128)S(1)}, u32[]{:S(2)}, u32[]{:S(2)}) async-start(f32[32,1,1024]{2,1,0:T(1,128)} %broadcast_in_dim.25), calls=%async_computation | async-start | bytes 262144 | tf_op jit(solution)/shard_map/all_to_all | solution.py:84
  48.2 2.3 %fusion.64 = f32[128,1408]{1,0:T(8,128)S(1)} fusion(bf16[64,1024]{1,0:T(8,128)(2,1)S(1)} %get-tuple-element.90, bf16[64,1024]{1,0:T(8,128)(2,1)S(1)} %get-tuple-element.91, bf16[1024,384]{1,0:T(8,128)(2,1)S(1)} %copy.27, bf16[1024,1024]{1,0:T(8,128)(2,1)} %copy-done.17), kind=kOutput, calls=%fused_computation.159 | convolution fusion | flops 375390208 | bytes 3866624 | tf_op jit(solution)/shard_map/dot_general | solution.py:19
  52.2 6.1 %collective-permute-start.5 = (f32[64,128]{1,0:T(8,128)S(1)}, f32[64,128]{1,0:T(8,128)S(1)}, u32[]{:S(2)}, u32[]{:S(2)}) collective-permute-start(f32[64,128]{1,0:T(8,128)S(1)} %get-tuple-element.81), channel_id=1, source_target_pairs={{0,16},{1,17},{2,18},{3,19},{4,20},{5,21},{6,22},{7,23},{8,24},{9,... | collective-permute-start | bytes 98312 | tf_op jit(solution)/shard_map/ppermute | solution.py:79
  58.3 2.5 %collective-permute-done.5 = f32[64,128]{1,0:T(8,128)S(1)} collective-permute-done((f32[64,128]{1,0:T(8,128)S(1)}, f32[64,128]{1,0:T(8,128)S(1)}, u32[]{:S(2)}, u32[]{:S(2)}) %collective-permute-start.5) | collective-permute-done | bytes 32800 | tf_op jit(solution)/shard_map/ppermute | solution.py:79
  64.5 2.5 %fusion.7 = f32[64,1408]{1,0:T(8,128)S(1)} fusion(bf16[64,1024]{1,0:T(8,128)(2,1)S(1)} %reduce-precision_convert_fusion.14, f32[64,2432]{1,0:T(8,128)S(1)} %convolution_add_fusion.3, f32[128,1408]{1,0:T(8,128)S(1)} %copy-done.67, bf16[1024,384]{1,0:T(8,128)(2,1)} %copy-done.27, bf16[1024,1024]{1,0:T(8,128)(2,1)} %copy-done.12), kind=kOutput, calls=%fused_computation.28 | convolution fusion | flops 190586880 | bytes 4456448 | tf_op jit(solution)/shard_map/dot_general | solution.py:19
  67.9 4.3 %collective-permute-start.8 = (f32[64,128]{1,0:T(8,128)S(1)}, f32[64,128]{1,0:T(8,128)S(1)}, u32[]{:S(2)}, u32[]{:S(2)}) collective-permute-start(f32[64,128]{1,0:T(8,128)S(1)} %get-tuple-element.78), channel_id=1, source_target_pairs={{0,16},{1,17},{2,18},{3,19},{4,20},{5,21},{6,22},{7,23},{8,24},{9,... | collective-permute-start | bytes 98312 | tf_op jit(solution)/shard_map/ppermute | solution.py:79
  72.3 2.5 %collective-permute-done.8 = f32[64,128]{1,0:T(8,128)S(1)} collective-permute-done((f32[64,128]{1,0:T(8,128)S(1)}, f32[64,128]{1,0:T(8,128)S(1)}, u32[]{:S(2)}, u32[]{:S(2)}) %collective-permute-start.8) | collective-permute-done | bytes 32800 | tf_op jit(solution)/shard_map/ppermute | solution.py:79
  78.8 5.3 %collective-permute-start.11 = (f32[64,128]{1,0:T(8,128)S(1)}, f32[64,128]{1,0:T(8,128)S(1)}, u32[]{:S(2)}, u32[]{:S(2)}) collective-permute-start(f32[64,128]{1,0:T(8,128)S(1)} %get-tuple-element.73), channel_id=1, source_target_pairs={{0,16},{1,17},{2,18},{3,19},{4,20},{5,21},{6,22},{7,23},{8,24},{9,... | collective-permute-start | bytes 98312 | tf_op jit(solution)/shard_map/ppermute | solution.py:79
  85.1 2.8 %all-to-all-start.1 = ((f32[32,1,1152]{2,1,0:T(1,128)}), f32[32,1,1152]{2,1,0:T(1,128)S(1)}, u32[]{:S(2)}, u32[]{:S(2)}) async-start(f32[32,1,1152]{2,1,0:T(1,128)} %broadcast_in_dim.27), calls=%async_computation.1 | async-start | bytes 294912 | tf_op jit(solution)/shard_map/all_to_all | solution.py:84
  88.7 3.3 %fusion.68 = f32[128,1408]{1,0:T(8,128)} fusion(bf16[64,1024]{1,0:T(8,128)(2,1)S(1)} %get-tuple-element.35, bf16[64,1024]{1,0:T(8,128)(2,1)S(1)} %reduce-precision_convert_fusion.10, bf16[1024,384]{1,0:T(8,128)(2,1)} %copy-done.30, bf16[1024,1024]{1,0:T(8,128)(2,1)} %copy-done.17), kind=kOutput, calls=%fused_computation.164 | convolution fusion | flops 375390208 | bytes 3866624 | tf_op jit(solution)/shard_map/dot_general | solution.py:19
  92.0 4.3 %all-to-all-done.1 = f32[32,1,1152]{2,1,0:T(1,128)S(1)} async-done(((f32[32,1,1152]{2,1,0:T(1,128)}), f32[32,1,1152]{2,1,0:T(1,128)S(1)}, u32[]{:S(2)}, u32[]{:S(2)}) %all-to-all-start.1) | async-done | bytes 147488 | tf_op jit(solution)/shard_map/all_to_all | solution.py:84
  98.6 2.0 %fusion.6 = f32[64,1408]{1,0:T(8,128)S(1)} fusion(bf16[64,1024]{1,0:T(8,128)(2,1)S(1)} %reduce-precision_convert_fusion.10, f32[64,2432]{1,0:T(8,128)S(1)} %convolution_add_fusion.2, f32[128,1408]{1,0:T(8,128)S(1)} %copy-done.65, bf16[1024,384]{1,0:T(8,128)(2,1)} %copy-done.27, bf16[1024,1024]{1,0:T(8,128)(2,1)S(1)} %copy-done.14), kind=kOutput, calls=%fused_computation.24 | convolution fusion | flops 190586880 | bytes 4456448 | tf_op jit(solution)/shard_map/dot_general | solution.py:19
  102.0 3.7 %collective-permute-start.14 = (f32[64,128]{1,0:T(8,128)S(1)}, f32[64,128]{1,0:T(8,128)S(1)}, u32[]{:S(2)}, u32[]{:S(2)}) collective-permute-start(f32[64,128]{1,0:T(8,128)S(1)} %get-tuple-element.70), channel_id=1, source_target_pairs={{0,16},{1,17},{2,18},{3,19},{4,20},{5,21},{6,22},{7,23},{8,24},{9,... | collective-permute-start | bytes 98312 | tf_op jit(solution)/shard_map/ppermute | solution.py:79
  105.7 2.6 %collective-permute-done.14 = f32[64,128]{1,0:T(8,128)S(1)} collective-permute-done((f32[64,128]{1,0:T(8,128)S(1)}, f32[64,128]{1,0:T(8,128)S(1)}, u32[]{:S(2)}, u32[]{:S(2)}) %collective-permute-start.14) | collective-permute-done | bytes 32800 | tf_op jit(solution)/shard_map/ppermute | solution.py:79
  113.6 3.4 %all-to-all-start.2 = ((f32[32,1,1152]{2,1,0:T(1,128)}), f32[32,1,1152]{2,1,0:T(1,128)S(1)}, u32[]{:S(2)}, u32[]{:S(2)}) async-start(f32[32,1,1152]{2,1,0:T(1,128)} %broadcast_in_dim.29), calls=%async_computation.2 | async-start | bytes 294912 | tf_op jit(solution)/shard_map/all_to_all | solution.py:84
  117.8 6.1 %collective-permute-start.17 = (f32[64,128]{1,0:T(8,128)S(1)}, f32[64,128]{1,0:T(8,128)S(1)}, u32[]{:S(2)}, u32[]{:S(2)}) collective-permute-start(f32[64,128]{1,0:T(8,128)S(1)} %get-tuple-element.67), channel_id=1, source_target_pairs={{0,16},{1,17},{2,18},{3,19},{4,20},{5,21},{6,22},{7,23},{8,24},{9,... | collective-permute-start | bytes 98312 | tf_op jit(solution)/shard_map/ppermute | solution.py:79
  124.0 2.5 %collective-permute-done.17 = f32[64,128]{1,0:T(8,128)S(1)} collective-permute-done((f32[64,128]{1,0:T(8,128)S(1)}, f32[64,128]{1,0:T(8,128)S(1)}, u32[]{:S(2)}, u32[]{:S(2)}) %collective-permute-start.17) | collective-permute-done | bytes 32800 | tf_op jit(solution)/shard_map/ppermute | solution.py:79
  128.1 2.6 %fusion.72 = f32[128,1408]{1,0:T(8,128)} fusion(bf16[64,1024]{1,0:T(8,128)(2,1)S(1)} %get-tuple-element.28, bf16[64,1024]{1,0:T(8,128)(2,1)S(1)} %reduce-precision_convert_fusion.7, bf16[1024,384]{1,0:T(8,128)(2,1)} %copy-done.30, bf16[1024,1024]{1,0:T(8,128)(2,1)S(1)} %copy-done.19), kind=kOutput, calls=%fused_computation.169 | convolution fusion | flops 375390208 | bytes 3866624 | tf_op jit(solution)/shard_map/dot_general | solution.py:19
  135.2 4.3 %collective-permute-start.20 = (f32[64,128]{1,0:T(8,128)S(1)}, f32[64,128]{1,0:T(8,128)S(1)}, u32[]{:S(2)}, u32[]{:S(2)}) collective-permute-start(f32[64,128]{1,0:T(8,128)S(1)} %get-tuple-element.64), channel_id=1, source_target_pairs={{0,16},{1,17},{2,18},{3,19},{4,20},{5,21},{6,22},{7,23},{8,24},{9,... | collective-permute-start | bytes 98312 | tf_op jit(solution)/shard_map/ppermute | solution.py:79
  139.6 2.5 %collective-permute-done.20 = f32[64,128]{1,0:T(8,128)S(1)} collective-permute-done((f32[64,128]{1,0:T(8,128)S(1)}, f32[64,128]{1,0:T(8,128)S(1)}, u32[]{:S(2)}, u32[]{:S(2)}) %collective-permute-start.20) | collective-permute-done | bytes 32800 | tf_op jit(solution)/shard_map/ppermute | solution.py:79
  147.6 5.3 %collective-permute-start.23 = (f32[64,128]{1,0:T(8,128)S(1)}, f32[64,128]{1,0:T(8,128)S(1)}, u32[]{:S(2)}, u32[]{:S(2)}) collective-permute-start(f32[64,128]{1,0:T(8,128)S(1)} %get-tuple-element.61), channel_id=1, source_target_pairs={{0,16},{1,17},{2,18},{3,19},{4,20},{5,21},{6,22},{7,23},{8,24},{9,... | collective-permute-start | bytes 98312 | tf_op jit(solution)/shard_map/ppermute | solution.py:79
  153.9 2.9 %all-to-all-start.3 = ((f32[32,1,1152]{2,1,0:T(1,128)}), f32[32,1,1152]{2,1,0:T(1,128)S(1)}, u32[]{:S(2)}, u32[]{:S(2)}) async-start(f32[32,1,1152]{2,1,0:T(1,128)} %broadcast_in_dim.31), calls=%async_computation.3 | async-start | bytes 294912 | tf_op jit(solution)/shard_map/all_to_all | solution.py:84
  158.4 2.6 %fusion.76 = f32[128,1408]{1,0:T(8,128)} fusion(bf16[64,1024]{1,0:T(8,128)(2,1)S(1)} %get-tuple-element.13, bf16[64,1024]{1,0:T(8,128)(2,1)S(1)} %reduce-precision_convert_fusion.3, bf16[1024,384]{1,0:T(8,128)(2,1)} %copy-done.30, bf16[1024,1024]{1,0:T(8,128)(2,1)S(1)} %copy-done.20), kind=kOutput, calls=%fused_computation.174 | convolution fusion | flops 375390208 | bytes 3866624 | tf_op jit(solution)/shard_map/dot_general | solution.py:19
  161.0 4.2 %all-to-all-done.3 = f32[32,1,1152]{2,1,0:T(1,128)S(1)} async-done(((f32[32,1,1152]{2,1,0:T(1,128)}), f32[32,1,1152]{2,1,0:T(1,128)S(1)}, u32[]{:S(2)}, u32[]{:S(2)}) %all-to-all-start.3) | async-done | bytes 147488 | tf_op jit(solution)/shard_map/all_to_all | solution.py:84
  169.5 2.5 %all-to-all-start.4 = ((f32[32,1,128]{2,1,0:T(1,128)}), f32[32,1,128]{2,1,0:T(1,128)S(1)}, u32[]{:S(2)}, u32[]{:S(2)}) async-start(f32[32,1,128]{2,1,0:T(1,128)} %broadcast_in_dim.33), calls=%async_computation.4 | async-start | bytes 32768 | tf_op jit(solution)/shard_map/all_to_all | solution.py:84
  172.9 6.3 %collective-permute-start.26 = (f32[64,128]{1,0:T(8,128)S(1)}, f32[64,128]{1,0:T(8,128)S(1)}, u32[]{:S(2)}, u32[]{:S(2)}) collective-permute-start(f32[64,128]{1,0:T(8,128)S(1)} %get-tuple-element.58), channel_id=1, source_target_pairs={{0,16},{1,17},{2,18},{3,19},{4,20},{5,21},{6,22},{7,23},{8,24},{9,... | collective-permute-start | bytes 98312 | tf_op jit(solution)/shard_map/ppermute | solution.py:79
  179.3 2.2 %collective-permute-done.26 = f32[64,128]{1,0:T(8,128)S(1)} collective-permute-done((f32[64,128]{1,0:T(8,128)S(1)}, f32[64,128]{1,0:T(8,128)S(1)}, u32[]{:S(2)}, u32[]{:S(2)}) %collective-permute-start.26) | collective-permute-done | bytes 32800 | tf_op jit(solution)/shard_map/ppermute | solution.py:79
  (362 shorter events, 67.4 us)
Async XLA Ops:
  10.4 27.3 %collective-permute-start.2 = (f32[144,128]{1,0:T(8,128)S(1)}, f32[144,128]{1,0:T(8,128)S(1)}, u32[]{:S(2)}, u32[]{:S(2)}) collective-permute-start(f32[144,128]{1,0:T(8,128)S(1)} %constant_dynamic-update-slice_fusion.10), channel_id=1, source_target_pairs={{0,16},{1,17},{2,18},{3,19},{4,20},{5,21},{6,22},{7,23},{8,24},{9,... | collective-permute-start | bytes 221192 | tf_op jit(solution)/shard_map/ppermute | solution.py:79
  14.5 23.2 %collective-permute-start.1 = (f32[144,128]{1,0:T(8,128)S(1)}, f32[144,128]{1,0:T(8,128)S(1)}, u32[]{:S(2)}, u32[]{:S(2)}) collective-permute-start(f32[144,128]{1,0:T(8,128)S(1)} %get-tuple-element.146), channel_id=1, source_target_pairs={{1,2},{3,4},{5,6},{7,8},{9,10},{11,12},{13,14},{15,16},{17,18},{19... | collective-permute-start | bytes 221192 | tf_op jit(solution)/shard_map/ppermute | solution.py:79
  15.2 22.6 %collective-permute-start = (f32[144,128]{1,0:T(8,128)S(1)}, f32[144,128]{1,0:T(8,128)S(1)}, u32[]{:S(2)}, u32[]{:S(2)}) collective-permute-start(f32[144,128]{1,0:T(8,128)S(1)} %get-tuple-element.143), channel_id=1, source_target_pairs={{0,1},{2,3},{4,5},{6,7},{8,9},{10,11},{12,13},{14,15},{16,17},{18,... | collective-permute-start | bytes 221192 | tf_op jit(solution)/shard_map/ppermute | solution.py:79
  42.9 15.4 %collective-permute-start.3 = (f32[64,128]{1,0:T(8,128)S(1)}, f32[64,128]{1,0:T(8,128)S(1)}, u32[]{:S(2)}, u32[]{:S(2)}) collective-permute-start(f32[64,128]{1,0:T(8,128)S(1)} %get-tuple-element.83), channel_id=1, source_target_pairs={{0,1},{2,3},{4,5},{6,7},{8,9},{10,11},{12,13},{14,15},{16,17},{18,... | collective-permute-start | bytes 98312 | tf_op jit(solution)/shard_map/ppermute | solution.py:79
  43.9 19.0 %all-to-all-start = ((f32[32,1,1024]{2,1,0:T(1,128)}), f32[32,1,1024]{2,1,0:T(1,128)S(1)}, u32[]{:S(2)}, u32[]{:S(2)}) async-start(f32[32,1,1024]{2,1,0:T(1,128)} %broadcast_in_dim.25), calls=%async_computation | async-start | bytes 262144 | tf_op jit(solution)/shard_map/all_to_all | solution.py:84
  51.4 6.9 %collective-permute-start.4 = (f32[64,128]{1,0:T(8,128)S(1)}, f32[64,128]{1,0:T(8,128)S(1)}, u32[]{:S(2)}, u32[]{:S(2)}) collective-permute-start(f32[64,128]{1,0:T(8,128)S(1)} %get-tuple-element.82), channel_id=1, source_target_pairs={{1,2},{3,4},{5,6},{7,8},{9,10},{11,12},{13,14},{15,16},{17,18},{19... | collective-permute-start | bytes 98312 | tf_op jit(solution)/shard_map/ppermute | solution.py:79
  52.2 8.6 %collective-permute-start.5 = (f32[64,128]{1,0:T(8,128)S(1)}, f32[64,128]{1,0:T(8,128)S(1)}, u32[]{:S(2)}, u32[]{:S(2)}) collective-permute-start(f32[64,128]{1,0:T(8,128)S(1)} %get-tuple-element.81), channel_id=1, source_target_pairs={{0,16},{1,17},{2,18},{3,19},{4,20},{5,21},{6,22},{7,23},{8,24},{9,... | collective-permute-start | bytes 98312 | tf_op jit(solution)/shard_map/ppermute | solution.py:79
  67.1 5.2 %collective-permute-start.6 = (f32[64,128]{1,0:T(8,128)S(1)}, f32[64,128]{1,0:T(8,128)S(1)}, u32[]{:S(2)}, u32[]{:S(2)}) collective-permute-start(f32[64,128]{1,0:T(8,128)S(1)} %get-tuple-element.80), channel_id=1, source_target_pairs={{0,1},{2,3},{4,5},{6,7},{8,9},{10,11},{12,13},{14,15},{16,17},{18,... | collective-permute-start | bytes 98312 | tf_op jit(solution)/shard_map/ppermute | solution.py:79
  67.1 5.1 %collective-permute-start.7 = (f32[64,128]{1,0:T(8,128)S(1)}, f32[64,128]{1,0:T(8,128)S(1)}, u32[]{:S(2)}, u32[]{:S(2)}) collective-permute-start(f32[64,128]{1,0:T(8,128)S(1)} %get-tuple-element.79), channel_id=1, source_target_pairs={{1,2},{3,4},{5,6},{7,8},{9,10},{11,12},{13,14},{15,16},{17,18},{19... | collective-permute-start | bytes 98312 | tf_op jit(solution)/shard_map/ppermute | solution.py:79
  67.9 6.8 %collective-permute-start.8 = (f32[64,128]{1,0:T(8,128)S(1)}, f32[64,128]{1,0:T(8,128)S(1)}, u32[]{:S(2)}, u32[]{:S(2)}) collective-permute-start(f32[64,128]{1,0:T(8,128)S(1)} %get-tuple-element.78), channel_id=1, source_target_pairs={{0,16},{1,17},{2,18},{3,19},{4,20},{5,21},{6,22},{7,23},{8,24},{9,... | collective-permute-start | bytes 98312 | tf_op jit(solution)/shard_map/ppermute | solution.py:79
  78.0 9.9 %collective-permute-start.9 = (f32[64,128]{1,0:T(8,128)S(1)}, f32[64,128]{1,0:T(8,128)S(1)}, u32[]{:S(2)}, u32[]{:S(2)}) collective-permute-start(f32[64,128]{1,0:T(8,128)S(1)} %get-tuple-element.75), channel_id=1, source_target_pairs={{0,1},{2,3},{4,5},{6,7},{8,9},{10,11},{12,13},{14,15},{16,17},{18,... | collective-permute-start | bytes 98312 | tf_op jit(solution)/shard_map/ppermute | solution.py:79
  78.1 9.9 %collective-permute-start.10 = (f32[64,128]{1,0:T(8,128)S(1)}, f32[64,128]{1,0:T(8,128)S(1)}, u32[]{:S(2)}, u32[]{:S(2)}) collective-permute-start(f32[64,128]{1,0:T(8,128)S(1)} %get-tuple-element.74), channel_id=1, source_target_pairs={{1,2},{3,4},{5,6},{7,8},{9,10},{11,12},{13,14},{15,16},{17,18},{19... | collective-permute-start | bytes 98312 | tf_op jit(solution)/shard_map/ppermute | solution.py:79
  78.8 9.2 %collective-permute-start.11 = (f32[64,128]{1,0:T(8,128)S(1)}, f32[64,128]{1,0:T(8,128)S(1)}, u32[]{:S(2)}, u32[]{:S(2)}) collective-permute-start(f32[64,128]{1,0:T(8,128)S(1)} %get-tuple-element.73), channel_id=1, source_target_pairs={{0,16},{1,17},{2,18},{3,19},{4,20},{5,21},{6,22},{7,23},{8,24},{9,... | collective-permute-start | bytes 98312 | tf_op jit(solution)/shard_map/ppermute | solution.py:79
  85.1 11.3 %all-to-all-start.1 = ((f32[32,1,1152]{2,1,0:T(1,128)}), f32[32,1,1152]{2,1,0:T(1,128)S(1)}, u32[]{:S(2)}, u32[]{:S(2)}) async-start(f32[32,1,1152]{2,1,0:T(1,128)} %broadcast_in_dim.27), calls=%async_computation.1 | async-start | bytes 294912 | tf_op jit(solution)/shard_map/all_to_all | solution.py:84
  100.6 5.1 %collective-permute-start.12 = (f32[64,128]{1,0:T(8,128)S(1)}, f32[64,128]{1,0:T(8,128)S(1)}, u32[]{:S(2)}, u32[]{:S(2)}) collective-permute-start(f32[64,128]{1,0:T(8,128)S(1)} %get-tuple-element.72), channel_id=1, source_target_pairs={{0,1},{2,3},{4,5},{6,7},{8,9},{10,11},{12,13},{14,15},{16,17},{18,... | collective-permute-start | bytes 98312 | tf_op jit(solution)/shard_map/ppermute | solution.py:79
  101.0 4.7 %collective-permute-start.13 = (f32[64,128]{1,0:T(8,128)S(1)}, f32[64,128]{1,0:T(8,128)S(1)}, u32[]{:S(2)}, u32[]{:S(2)}) collective-permute-start(f32[64,128]{1,0:T(8,128)S(1)} %get-tuple-element.71), channel_id=1, source_target_pairs={{1,2},{3,4},{5,6},{7,8},{9,10},{11,12},{13,14},{15,16},{17,18},{19... | collective-permute-start | bytes 98312 | tf_op jit(solution)/shard_map/ppermute | solution.py:79
  102.0 6.3 %collective-permute-start.14 = (f32[64,128]{1,0:T(8,128)S(1)}, f32[64,128]{1,0:T(8,128)S(1)}, u32[]{:S(2)}, u32[]{:S(2)}) collective-permute-start(f32[64,128]{1,0:T(8,128)S(1)} %get-tuple-element.70), channel_id=1, source_target_pairs={{0,16},{1,17},{2,18},{3,19},{4,20},{5,21},{6,22},{7,23},{8,24},{9,... | collective-permute-start | bytes 98312 | tf_op jit(solution)/shard_map/ppermute | solution.py:79
  112.6 11.3 %collective-permute-start.15 = (f32[64,128]{1,0:T(8,128)S(1)}, f32[64,128]{1,0:T(8,128)S(1)}, u32[]{:S(2)}, u32[]{:S(2)}) collective-permute-start(f32[64,128]{1,0:T(8,128)S(1)} %get-tuple-element.69), channel_id=1, source_target_pairs={{0,1},{2,3},{4,5},{6,7},{8,9},{10,11},{12,13},{14,15},{16,17},{18,... | collective-permute-start | bytes 98312 | tf_op jit(solution)/shard_map/ppermute | solution.py:79
  113.6 17.1 %all-to-all-start.2 = ((f32[32,1,1152]{2,1,0:T(1,128)}), f32[32,1,1152]{2,1,0:T(1,128)S(1)}, u32[]{:S(2)}, u32[]{:S(2)}) async-start(f32[32,1,1152]{2,1,0:T(1,128)} %broadcast_in_dim.29), calls=%async_computation.2 | async-start | bytes 294912 | tf_op jit(solution)/shard_map/all_to_all | solution.py:84
  117.0 6.9 %collective-permute-start.16 = (f32[64,128]{1,0:T(8,128)S(1)}, f32[64,128]{1,0:T(8,128)S(1)}, u32[]{:S(2)}, u32[]{:S(2)}) collective-permute-start(f32[64,128]{1,0:T(8,128)S(1)} %get-tuple-element.68), channel_id=1, source_target_pairs={{1,2},{3,4},{5,6},{7,8},{9,10},{11,12},{13,14},{15,16},{17,18},{19... | collective-permute-start | bytes 98312 | tf_op jit(solution)/shard_map/ppermute | solution.py:79
  117.8 8.6 %collective-permute-start.17 = (f32[64,128]{1,0:T(8,128)S(1)}, f32[64,128]{1,0:T(8,128)S(1)}, u32[]{:S(2)}, u32[]{:S(2)}) collective-permute-start(f32[64,128]{1,0:T(8,128)S(1)} %get-tuple-element.67), channel_id=1, source_target_pairs={{0,16},{1,17},{2,18},{3,19},{4,20},{5,21},{6,22},{7,23},{8,24},{9,... | collective-permute-start | bytes 98312 | tf_op jit(solution)/shard_map/ppermute | solution.py:79
  133.9 5.6 %collective-permute-start.18 = (f32[64,128]{1,0:T(8,128)S(1)}, f32[64,128]{1,0:T(8,128)S(1)}, u32[]{:S(2)}, u32[]{:S(2)}) collective-permute-start(f32[64,128]{1,0:T(8,128)S(1)} %get-tuple-element.66), channel_id=1, source_target_pairs={{0,1},{2,3},{4,5},{6,7},{8,9},{10,11},{12,13},{14,15},{16,17},{18,... | collective-permute-start | bytes 98312 | tf_op jit(solution)/shard_map/ppermute | solution.py:79
  134.5 5.0 %collective-permute-start.19 = (f32[64,128]{1,0:T(8,128)S(1)}, f32[64,128]{1,0:T(8,128)S(1)}, u32[]{:S(2)}, u32[]{:S(2)}) collective-permute-start(f32[64,128]{1,0:T(8,128)S(1)} %get-tuple-element.65), channel_id=1, source_target_pairs={{1,2},{3,4},{5,6},{7,8},{9,10},{11,12},{13,14},{15,16},{17,18},{19... | collective-permute-start | bytes 98312 | tf_op jit(solution)/shard_map/ppermute | solution.py:79
  135.2 6.8 %collective-permute-start.20 = (f32[64,128]{1,0:T(8,128)S(1)}, f32[64,128]{1,0:T(8,128)S(1)}, u32[]{:S(2)}, u32[]{:S(2)}) collective-permute-start(f32[64,128]{1,0:T(8,128)S(1)} %get-tuple-element.64), channel_id=1, source_target_pairs={{0,16},{1,17},{2,18},{3,19},{4,20},{5,21},{6,22},{7,23},{8,24},{9,... | collective-permute-start | bytes 98312 | tf_op jit(solution)/shard_map/ppermute | solution.py:79
  146.8 10.0 %collective-permute-start.21 = (f32[64,128]{1,0:T(8,128)S(1)}, f32[64,128]{1,0:T(8,128)S(1)}, u32[]{:S(2)}, u32[]{:S(2)}) collective-permute-start(f32[64,128]{1,0:T(8,128)S(1)} %get-tuple-element.63), channel_id=1, source_target_pairs={{0,1},{2,3},{4,5},{6,7},{8,9},{10,11},{12,13},{14,15},{16,17},{18,... | collective-permute-start | bytes 98312 | tf_op jit(solution)/shard_map/ppermute | solution.py:79
  146.9 9.9 %collective-permute-start.22 = (f32[64,128]{1,0:T(8,128)S(1)}, f32[64,128]{1,0:T(8,128)S(1)}, u32[]{:S(2)}, u32[]{:S(2)}) collective-permute-start(f32[64,128]{1,0:T(8,128)S(1)} %get-tuple-element.62), channel_id=1, source_target_pairs={{1,2},{3,4},{5,6},{7,8},{9,10},{11,12},{13,14},{15,16},{17,18},{19... | collective-permute-start | bytes 98312 | tf_op jit(solution)/shard_map/ppermute | solution.py:79
  147.6 9.3 %collective-permute-start.23 = (f32[64,128]{1,0:T(8,128)S(1)}, f32[64,128]{1,0:T(8,128)S(1)}, u32[]{:S(2)}, u32[]{:S(2)}) collective-permute-start(f32[64,128]{1,0:T(8,128)S(1)} %get-tuple-element.61), channel_id=1, source_target_pairs={{0,16},{1,17},{2,18},{3,19},{4,20},{5,21},{6,22},{7,23},{8,24},{9,... | collective-permute-start | bytes 98312 | tf_op jit(solution)/shard_map/ppermute | solution.py:79
  153.9 11.3 %all-to-all-start.3 = ((f32[32,1,1152]{2,1,0:T(1,128)}), f32[32,1,1152]{2,1,0:T(1,128)S(1)}, u32[]{:S(2)}, u32[]{:S(2)}) async-start(f32[32,1,1152]{2,1,0:T(1,128)} %broadcast_in_dim.31), calls=%async_computation.3 | async-start | bytes 294912 | tf_op jit(solution)/shard_map/all_to_all | solution.py:84
  169.5 9.7 %all-to-all-start.4 = ((f32[32,1,128]{2,1,0:T(1,128)}), f32[32,1,128]{2,1,0:T(1,128)S(1)}, u32[]{:S(2)}, u32[]{:S(2)}) async-start(f32[32,1,128]{2,1,0:T(1,128)} %broadcast_in_dim.33), calls=%async_computation.4 | async-start | bytes 32768 | tf_op jit(solution)/shard_map/all_to_all | solution.py:84
  172.0 7.2 %collective-permute-start.24 = (f32[64,128]{1,0:T(8,128)S(1)}, f32[64,128]{1,0:T(8,128)S(1)}, u32[]{:S(2)}, u32[]{:S(2)}) collective-permute-start(f32[64,128]{1,0:T(8,128)S(1)} %get-tuple-element.60), channel_id=1, source_target_pairs={{0,1},{2,3},{4,5},{6,7},{8,9},{10,11},{12,13},{14,15},{16,17},{18,... | collective-permute-start | bytes 98312 | tf_op jit(solution)/shard_map/ppermute | solution.py:79
  172.2 7.1 %collective-permute-start.25 = (f32[64,128]{1,0:T(8,128)S(1)}, f32[64,128]{1,0:T(8,128)S(1)}, u32[]{:S(2)}, u32[]{:S(2)}) collective-permute-start(f32[64,128]{1,0:T(8,128)S(1)} %get-tuple-element.59), channel_id=1, source_target_pairs={{1,2},{3,4},{5,6},{7,8},{9,10},{11,12},{13,14},{15,16},{17,18},{19... | collective-permute-start | bytes 98312 | tf_op jit(solution)/shard_map/ppermute | solution.py:79
  172.9 8.6 %collective-permute-start.26 = (f32[64,128]{1,0:T(8,128)S(1)}, f32[64,128]{1,0:T(8,128)S(1)}, u32[]{:S(2)}, u32[]{:S(2)}) collective-permute-start(f32[64,128]{1,0:T(8,128)S(1)} %get-tuple-element.58), channel_id=1, source_target_pairs={{0,16},{1,17},{2,18},{3,19},{4,20},{5,21},{6,22},{7,23},{8,24},{9,... | collective-permute-start | bytes 98312 | tf_op jit(solution)/shard_map/ppermute | solution.py:79
  (68 other events, 610.5 us)

commit v2 on v0

v2 whole, which is shorter than its diff:
```python
import functools

import jax
import jax.numpy as jnp
from jax import lax
from jax.experimental import pallas as pl
from jax.experimental.pallas import tpu as pltpu
from jax.sharding import PartitionSpec as P

CYCLE = 16
ITERS = 4

BF = jnp.bfloat16
F32 = jnp.float32
NN = ((1,), (0,))
NT = ((1,), (1,))
TN = ((0,), (0,))
VMEM_BYTES = 40 * 1024 * 1024


def contract(left, right, dims=NN):
    return lax.dot_general(left, right, (dims, ((), ())), preferred_element_type=F32)


def split(value):
    high = value.astype(BF)
    return high, (value - high.astype(F32)).astype(BF)


def times(value, high, low, dims=NN):
    rows = value.shape[0]
    top, rest = split(value)
    both = contract(jnp.concatenate([top, rest], axis=0), high, dims)
    return both[:rows] + both[rows:] + contract(top, low, dims)


def pick(value, onehot, dims=NN):
    rows = value.shape[0]
    top, rest = split(value)
    last = (value - top.astype(F32) - rest.astype(F32)).astype(BF)
    all_three = contract(jnp.concatenate([top, rest, last], axis=0), onehot, dims)
    return all_three[:rows] + (all_three[rows:2 * rows] + all_three[2 * rows:])


def diagonal(count):
    first = lax.broadcasted_iota(jnp.int32, (count, count), 0)
    return first == lax.broadcasted_iota(jnp.int32, (count, count), 1)


def to_column(row):
    count = row.shape[1]
    return jnp.sum(jnp.where(diagonal(count), jnp.broadcast_to(row, (count, count)), 0.0), axis=1, keepdims=True)


def to_row(column):
    count = column.shape[0]
    return jnp.sum(jnp.where(diagonal(count), jnp.broadcast_to(column, (count, count)), 0.0), axis=0, keepdims=True)


def dot(left, right):
    return jnp.sum(left * right, axis=1, keepdims=True)


def stage(name, function, outs, *args):
    def kernel(*refs):
        values = function(*[ref[...] for ref in refs[:len(args)]])
        for ref, value in zip(refs[len(args):], values):
            ref[...] = value

    whole = pl.BlockSpec(memory_space=pltpu.VMEM)
    return pl.pallas_call(
        kernel,
        name=name,
        out_shape=[jax.ShapeDtypeStruct(shape, kind) for shape, kind in outs],
        in_specs=[whole] * len(args),
        out_specs=[whole] * len(outs),
        compiler_params=pltpu.CompilerParams(vmem_limit_bytes=VMEM_BYTES),
    )(*args)


def prepare(name, matrix, picker, tiles=4):
    order, slots = picker.shape
    rows = order // tiles

    def kernel(matrix_ref, picker_ref, high_ref, low_ref, fhigh_ref, flow_ref, block_high_ref, block_low_ref, total_high, total_low):
        at = pl.program_id(0)
        high, low = split(matrix_ref[...])
        high_ref[...] = high
        low_ref[...] = low
        onehot = picker_ref[...]
        mine = picker_ref[pl.ds(pl.multiple_of(at * rows, rows), rows), :]
        for part, face_ref, total in ((high, fhigh_ref, total_high), (low, flow_ref, total_low)):
            face = contract(part, onehot).astype(BF)
            face_ref[...] = face
            block = contract(mine, face, TN)

            @pl.when(at == 0)
            def _():
                total[...] = block

            @pl.when(at > 0)
            def _():
                total[...] += block

        @pl.when(at == tiles - 1)
        def _():
            block_high_ref[...] = total_high[...].astype(BF)
            block_low_ref[...] = total_low[...].astype(BF)

    shape = jax.ShapeDtypeStruct
    return pl.pallas_call(
        kernel,
        name=name,
        grid=(tiles,),
        in_specs=[
            pl.BlockSpec((rows, order), lambda i: (i, 0)),
            pl.BlockSpec((order, slots), lambda i: (0, 0)),
        ],
        out_specs=[
            pl.BlockSpec((rows, order), lambda i: (i, 0)),
            pl.BlockSpec((rows, order), lambda i: (i, 0)),
            pl.BlockSpec((rows, slots), lambda i: (i, 0)),
            pl.BlockSpec((rows, slots), lambda i: (i, 0)),
            pl.BlockSpec((slots, slots), lambda i: (0, 0)),
            pl.BlockSpec((slots, slots), lambda i: (0, 0)),
        ],
        out_shape=[shape((order, order), BF)] * 2 + [shape((order, slots), BF)] * 2 + [shape((slots, slots), BF)] * 2,
        scratch_shapes=[pltpu.VMEM((slots, slots), F32)] * 2,
        compiler_params=pltpu.CompilerParams(vmem_limit_bytes=VMEM_BYTES),
        cost_estimate=pl.CostEstimate(flops=8 * order * order * slots, bytes_accessed=10 * order * order, transcendentals=0),
    )(matrix, picker)


def swaps(total):
    sets = []
    for by in (1, CYCLE):
        for parity in (0, 1):
            ahead = [i for i in range(total - by) if (i // by) % 2 == parity]
            sets.append((by, parity, [(i, i + by) for i in ahead] + [(i + by, i) for i in ahead]))
    return sets


def local(stiffness, neumann_inv, coarse_basis, coarse_inv, loads, face_index, face_len):
    total = lax.axis_size("sub")
    me = lax.axis_index("sub")
    basis = coarse_basis[0]
    load = loads[0]
    cases, ndof = load.shape
    primal = basis.shape[0]
    width = face_index.shape[2]

    chosen = []
    for by, parity, pairs in swaps(total):
        if pairs:
            behind, ahead = (0, 1) if by == 1 else (2, 3)
            chosen.append((pairs, behind, ahead, (me // by) % 2 == parity))
    blocks = len(chosen)
    slots = blocks * width
    own_rows = (blocks + 1) * primal
    index = jnp.concatenate([jnp.where(f, face_index[0, a], face_index[0, b]) for _, b, a, f in chosen])
    length = jnp.stack([jnp.where(f, face_len[0, a], face_len[0, b]) for _, b, a, f in chosen])
    place = jnp.arange(width, dtype=jnp.int32)
    index = jnp.where(place[None, :] < length[:, None], index.reshape(blocks, width), -1).reshape(1, slots)

    vec = ((cases, ndof), F32)
    face = [((cases, width), F32)] * blocks
    column = ((cases, 1), F32)
    lines = ((primal, cases), F32)

    def cut(value):
        return [value[:, i * width:(i + 1) * width] for i in range(blocks)]

    def exchange(pieces):
        return [lax.ppermute(piece, "sub", chosen[at][0]) for at, piece in enumerate(pieces)]

    def spread(payload):
        return lax.all_to_all(payload, "sub", 0, 0, tiled=True)

    def payload_of(rows):
        return jnp.broadcast_to(rows[None], (total,) + rows.shape)

    reps = coarse_inv.shape[1] // width

    def first(index, load, basis, inv):
        picker = (lax.broadcasted_iota(jnp.int32, (ndof, slots), 0) == index).astype(F32).astype(BF)
        shared = contract(jnp.ones((8, slots), BF), picker, NT)[:1]
        weight = 1.0 / (1.0 + shared)
        weighted = basis * weight
        at_slots = pick(jnp.concatenate([load, weighted], axis=0), picker)
        inv_packed = jnp.concatenate([inv[:, i * width:(i + 1) * width] for i in range(reps)], axis=0)
        out = [jnp.concatenate([part, inv_packed], axis=0) for part in cut(at_slots)]
        return [picker, weight, weighted, at_slots[cases:]] + out

    packed = ((cases + primal + reps * primal, width), F32)
    picker, weight, weighted, basis_slots, *sent = stage(
        "first", first,
        [((ndof, slots), BF), ((1, ndof), F32), ((primal, ndof), F32), ((primal, slots), F32)] + [packed] * blocks,
        index, load, basis, coarse_inv)
    came = exchange(sent)

    inv_parts = prepare("prepare_inv", neumann_inv[0], picker)
    stiff_parts = prepare("prepare_stiff", stiffness[0], picker)

    def reach(weighted, inv, picker, high, low, fhigh, flow, *came):
        functions = [weighted]
        rows = [inv]
        for at, part in enumerate(came):
            functions.append(pick(part[cases:cases + primal], picker[:, at * width:(at + 1) * width], NT))
            rest = part[cases + primal:]
            rows.append(jnp.concatenate([rest[i * primal:(i + 1) * primal] for i in range(reps)], axis=1))
        functions = jnp.concatenate(functions, axis=0)
        rows = jnp.concatenate(rows, axis=0)
        image = times(functions, high, low)
        everything = jnp.concatenate([functions, image, times(functions, fhigh, flow)], axis=1)
        return [*split(rows), *split(everything)]

    wide = 2 * ndof + slots
    coarse = stage(
        "reach", reach,
        [((own_rows, total * primal), BF)] * 2 + [((own_rows, wide), BF)] * 2,
        weighted, coarse_inv, picker, *stiff_parts[:4], *came)

    def solve_own(part, weight, weighted, high, low, fhigh, flow):
        scaled = part * weight
        top, rest = split(scaled)
        return [times(scaled, high, low), times(scaled, fhigh, flow), times(weighted, *split(part), NT)]

    solve_outs = [vec, ((cases, slots), F32), lines]

    def solve_rest(scale, inner, inner_faces, lines, sums, weight, basis_slots, fhigh, flow, block_high, block_low, *came):
        came = scale * jnp.concatenate(came, axis=1)
        lines = lines + times(basis_slots, *split(came), NT)
        came = 0.5 * came
        inner = weight * (inner + times(came, fhigh, flow, NT))
        inner_faces = 0.5 * (inner_faces + times(came, block_high, block_low))
        return [payload_of(jnp.concatenate([lines, sums], axis=0)), inner] + cut(inner_faces)

    rest_outs = [((total, primal + 2, cases), F32), vec] + face

    def apply_own(inner, high, low, fhigh, flow):
        return [times(inner, high, low), times(inner, fhigh, flow)]

    def apply_rest(inner, image, image_faces, picker, fhigh, flow, block_high, block_low, *came):
        came = jnp.concatenate(came, axis=1)
        inner = inner + pick(came, picker, NT)
        image = image + times(came, fhigh, flow, NT)
        image_faces = image_faces + times(came, block_high, block_low)
        return [inner, image, image_faces]

    def correct(everyone, inner, image, image_faces, rows_high, rows_low, all_high, all_low):
        gathered = everyone[:, :primal].reshape(total * primal, cases)
        top, rest = split(gathered)
        factors = contract(rows_high, top) + contract(rows_high, rest) + contract(rows_low, top)
        extra = times(factors.T, all_high, all_low)
        sums = jnp.sum(everyone[:, primal:], axis=0)
        return [
            inner + extra[:, :ndof],
            image + extra[:, ndof:2 * ndof],
            to_column(sums[:1]), to_column(sums[1:2]),
        ] + cut(image_faces + extra[:, 2 * ndof:])

    def precondition(part, scale, sums, exchanged):
        inner, inner_faces, lines = stage("solve_own", solve_own, solve_outs, part, weight, weighted, *inv_parts[:4])
        payload, inner, *sent = stage(
            "solve_rest", solve_rest, rest_outs,
            scale, inner, inner_faces, lines, sums, weight, basis_slots, *inv_parts[2:], *exchanged)
        everyone = spread(payload)
        came = exchange(sent)
        image, image_faces = stage("apply_own", apply_own, [vec, ((cases, slots), F32)], inner, *stiff_parts[:4])
        inner, image, image_faces = stage(
            "apply_rest", apply_rest, [vec, vec, ((cases, slots), F32)],
            inner, image, image_faces, picker, *stiff_parts[2:], *came)
        inner, image, gamma, delta, *sent = stage(
            "correct", correct, [vec, vec, column, column] + face, everyone, inner, image, image_faces, *coarse)
        return inner, image, gamma, delta, sent

    def scatter(picker, *came):
        return pick(jnp.concatenate(came, axis=1), picker, NT)

    one = jnp.ones((cases, 1), F32)
    load_in = [part[:cases] for part in came]
    none = jnp.zeros((2, cases), F32)
    u, image, _, _, sent = precondition(load, one, none, load_in)
    came = exchange(sent)

    def begin(load, u, image, weight, picker, *load_in):
        residual = load + scatter(picker, *load_in)
        gamma = dot(residual * weight, u)
        delta = dot(image, u)
        return [residual, jnp.concatenate([to_row(gamma), to_row(delta)], axis=0)]

    pair = ((2, cases), F32)
    residual, sums = stage("begin", begin, [vec, pair], load, u, image, weight, picker, *load_in)
    part, scale = image, one
    w_from = (part, scale, came)
    state = None

    def assembled(part, scale, picker, *came):
        return [part + scale * scatter(picker, *came)]

    for step in range(ITERS - 1):
        m, image, gamma, delta, sent = precondition(part, scale, sums, came)
        (w,) = stage("assembled", assembled, [vec], part, scale, picker, *came)
        if step > 0:
            (z,) = stage("assembled", assembled, [vec], z_part, one, picker, *came)
        came_next = exchange(sent)
        if step == 0:
            def update(gamma, delta, u, w, m, image, residual, weight):
                alpha = gamma / delta
                q, s, p = m, w, u
                x = alpha * p
                residual = residual - alpha * s
                u = u - alpha * q
                part = w - alpha * image
                sums = jnp.concatenate([to_row(dot(weight * residual, u)), to_row(dot(weight * w - alpha * image, u))], axis=0)
                return [alpha, -alpha, q, s, p, x, residual, u, image, part, sums]

            alpha, scale, q, s, p, x, residual, u, z_part, part, sums = stage(
                "update", update, [column] * 2 + [vec] * 8 + [pair], gamma, delta, u, w, m, image, residual, weight)
        else:
            def update(gamma, delta, gamma_old, alpha_old, u, w, m, image, residual, x, p, s, q, z, weight):
                beta = gamma / gamma_old
                alpha = gamma / (delta - beta * gamma / alpha_old)
                q = m + beta * q
                s = w + beta * s
                p = u + beta * p
                x = x + alpha * p
                residual = residual - alpha * s
                u = u - alpha * q
                before = w - (alpha * beta) * z
                part = before - alpha * image
                sums = jnp.concatenate([to_row(dot(weight * residual, u)), to_row(dot(weight * before - alpha * image, u))], axis=0)
                return [alpha, -alpha, q, s, p, x, residual, u, image + beta * z, part, sums]

            alpha, scale, q, s, p, x, residual, u, z_part, part, sums = stage(
                "update", update, [column] * 2 + [vec] * 8 + [pair],
                gamma, delta, gamma_old, alpha_old, u, w, m, image, residual, x, p, s, q, z, weight)
        gamma_old, alpha_old = gamma, alpha
        came = came_next

    everyone = spread(payload_of(sums))

    def finish(everyone, gamma_old, alpha_old, part, scale, u, residual, x, p, s, picker, *came):
        w = part + scale * scatter(picker, *came)
        sums = jnp.sum(everyone, axis=0)
        gamma, delta = to_column(sums[:1]), to_column(sums[1:2])
        beta = gamma / gamma_old
        alpha = gamma / (delta - beta * gamma / alpha_old)
        return [x + alpha * (u + beta * p), residual - alpha * (w + beta * s)]

    x, residual = stage(
        "finish", finish, [vec, vec],
        everyone, gamma_old, alpha_old, part, scale, u, residual, x, p, s, picker, *came)
    return (x[None], residual[None])


def solution(mesh):
    placed = (
        P("sub", None, None),
        P("sub", None, None),
        P("sub", None, None),
        P("sub", None),
        P("sub", None, None),
        P("sub", None, None),
        P("sub", None),
    )
    return jax.shard_map(
        local,
        mesh=mesh,
        in_specs=placed,
        out_specs=(P("sub", None, None), P("sub", None, None)),
        check_vma=False,
    )
```

time: 572 us -> 248 us (0.43); the launches traced: 563 us -> 245 us
  blocking collectives: 332 us -> 9.88 us
  local copies, waits for them, and re-layouts: 13.1 us -> 106 us
  matrix products: 58 us -> 0 us
  Pallas kernels: 0 us -> 40.5 us
  other arithmetic: 44.9 us -> 11.5 us
  starting transfers between devices: 98.9 us -> 70.9 us
  waiting for transfers between devices: 13.9 us -> 0.08 us
    all_gather x4 -> x0, blocking collectives: 168 us -> none  [local(): lax.all_gather(precond_coarse_res, 'sub', axis=0, tiled=True)]
    psum x4 -> x0, blocking collectives: 164 us -> none  [local(): lax.psum((inner(residual, precond_res), inner(image, precond_res)), 'sub')]
    unnamed x5 -> x408, local copies, waits for them, and re-layouts: 1.16 us -> 104 us
    dot_general x20 -> x0, matrix products: 58 us -> none  [the longest x4 33.9 us: local(): image = assemble(jnp.dot(precond_res, stiff, precision=HIGH))]
    ppermute x36 -> x27, starting transfers between devices: 98.9 us -> 57.8 us  [exchange(): lax.ppermute(piece, 'sub', chosen[at][0])]
    pallas_call x0 -> x34, Pallas kernels: none -> 40.5 us  [the longest x32 28.9 us: stage(): pl.pallas_call(kernel, name=name, out_shape=[jax.ShapeDtypeStruct(shape,...]
    scatter-add x10 -> x0, other arithmetic: 36.9 us -> none  [the longest x9 32.8 us: assemble(): return local_vals.at[:, face_slots].add(incoming)]
    ppermute x36 -> x27, waiting for transfers between devices: 13.9 us -> 0.07 us  [exchange(): lax.ppermute(piece, 'sub', chosen[at][0])]
  transfers between devices with their start and end apart: 36 -> 31, of which waited for: 16 -> 0; matrix products, arithmetic and copies ran while one was open for 1% -> 0% of each run, Pallas kernels for 0% -> 12%
where the time goes in v2:
time: 248 us; the launch traced here: 245 us
  local copies, waits for them, and re-layouts  106 us (43%)
  starting transfers between devices  70.9 us (29%)
  Pallas kernels  40.5 us (16%)
  other arithmetic  11.5 us (5%)
  blocking collectives  9.88 us (4%)
  between operations  6.46 us (3%)
    unnamed x408, local copies, waits for them, and re-layouts  104 us
    ppermute x27, starting transfers between devices, exchange(): lax.ppermute(piece, 'sub', chosen[at][0])  57.8 us
    pallas_call x32, Pallas kernels, stage(): pl.pallas_call(kernel, name=name, out_shape=[jax.ShapeDtypeStruct(shape,...  28.9 us
    all_to_all x4, starting transfers between devices, spread(): return lax.all_to_all(payload, 'sub', 0, 0, tiled=True)  13.1 us
    pallas_call x2, Pallas kernels, prepare(): pl.pallas_call(kernel, name=name, grid=(tiles,), in_specs=[pl.BlockSpec((...  11.6 us
    all_to_all x5, other arithmetic, spread(): return lax.all_to_all(payload, 'sub', 0, 0, tiled=True)  10.5 us
    all_to_all x1, blocking collectives, spread(): return lax.all_to_all(payload, 'sub', 0, 0, tiled=True)  9.88 us
  transfers between devices with their start and end apart: 31, of which 0 were waited for; matrix products, arithmetic and copies ran while one was open for 0% of the time, Pallas kernels for 12%

profile of v2, /device:TPU:0, one launch (start us, length us, event | category | flops | bytes accessed | tf_op | source)
XLA Modules:
  0.0 244.9 jit_solution(10876489830252647030)
XLA Ops:
  11.5 7.3 %collective-permute-start.2 = (f32[144,128]{1,0:T(8,128)S(1)}, f32[144,128]{1,0:T(8,128)S(1)}, u32[]{:S(2)}, u32[]{:S(2)}) collective-permute-start(f32[144,128]{1,0:T(8,128)S(1)} %get-tuple-element.153), channel_id=1, source_target_pairs={{0,16},{1,17},{2,18},{3,19},{4,20},{5,21},{6,22},{7,23},{8,24},{9,... | collective-permute-start | bytes 221192 | tf_op jit(solution)/shard_map/ppermute | solution.py:174
  18.9 2.2 copy-done.191
  21.1 5.8 %prepare_inv.1 = (bf16[1024,1024]{1,0:T(8,128)(2,1)S(1)}, bf16[1024,1024]{1,0:T(8,128)(2,1)S(1)}, bf16[1024,384]{1,0:T(8,128)(2,1)S(1)}, bf16[1024,384]{1,0:T(8,...) custom-call(f32[1024,1024]{1,0:T(8,128)S(1)} %bitcast.28, ...), custom_call_target="tpu_custom_call" | custom-call | flops 3221225472 | bytes 10485760 | tf_op jit(solution)/shard_map/prepare_inv/pallas_call | solution.py:111
  32.0 3.3 %all-to-all-start = ((f32[32,1,1152]{2,1,0:T(1,128)}), f32[32,1,1152]{2,1,0:T(1,128)}, u32[]{:S(2)}, u32[]{:S(2)}) async-start(f32[32,1,1152]{2,1,0:T(1,128)} %reshape.82), calls=%async_computation | async-start | bytes 294912 | tf_op jit(solution)/shard_map/all_to_all | solution.py:177
  36.1 6.3 %collective-permute-start.5 = (f32[64,128]{1,0:T(8,128)}, f32[64,128]{1,0:T(8,128)S(1)}, u32[]{:S(2)}, u32[]{:S(2)}) collective-permute-start(f32[64,128]{1,0:T(8,128)} %get-tuple-element.166), channel_id=1, source_target_pairs={{0,16},{1,17},{2,18},{3,19},{4,20},{5,21},{6,22},{7,23},{8,24},{9,... | collective-permute-start | bytes 98312 | tf_op jit(solution)/shard_map/ppermute | solution.py:174
  42.4 2.2 copy-done.192
  44.5 5.8 %prepare_stiff.1 = (bf16[1024,1024]{1,0:T(8,128)(2,1)S(1)}, bf16[1024,1024]{1,0:T(8,128)(2,1)S(1)}, bf16[1024,384]{1,0:T(8,128)(2,1)S(1)}, bf16[1024,384]{1,0:T(...) custom-call(f32[1024,1024]{1,0:T(8,128)S(1)} %bitcast.29, ...), custom_call_target="tpu_custom_call" | custom-call | flops 3221225472 | bytes 10485760 | tf_op jit(solution)/shard_map/prepare_stiff/pallas_call | solution.py:111
  59.4 2.6 %reduce = f32[32,1152]{1,0:T(8,128)} reduce(f32[32,1,1152]{2,1,0:T(1,128)} %all-to-all-done, f32[]{:T(128)} %broadcast.35), dimensions={1}, to_apply=%all_to_all.15.reduce_sub_computation | reduce | bytes 294916 | tf_op jit(solution)/shard_map/all_to_all | solution.py:177
  62.0 1.8 reshape.83.refs_0_
  72.4 4.5 %collective-permute-start.8 = (f32[64,128]{1,0:T(8,128)S(1)}, f32[64,128]{1,0:T(8,128)S(1)}, u32[]{:S(2)}, u32[]{:S(2)}) collective-permute-start(f32[64,128]{1,0:T(8,128)S(1)} %get-tuple-element.182), channel_id=1, source_target_pairs={{0,16},{1,17},{2,18},{3,19},{4,20},{5,21},{6,22},{7,23},{8,24},{9,... | collective-permute-start | bytes 98312 | tf_op jit(solution)/shard_map/ppermute | solution.py:174
  76.8 1.6 copy-done.13
  78.4 1.6 copy-done.17
  86.8 1.8 reshape.84
  88.6 3.3 %all-to-all-start.1 = ((f32[32,1,1152]{2,1,0:T(1,128)}), f32[32,1,1152]{2,1,0:T(1,128)}, u32[]{:S(2)}, u32[]{:S(2)}) async-start(f32[32,1,1152]{2,1,0:T(1,128)} %reshape.84), calls=%async_computation.1 | async-start | bytes 294912 | tf_op jit(solution)/shard_map/all_to_all | solution.py:177
  92.7 6.3 %collective-permute-start.11 = (f32[64,128]{1,0:T(8,128)}, f32[64,128]{1,0:T(8,128)S(1)}, u32[]{:S(2)}, u32[]{:S(2)}) collective-permute-start(f32[64,128]{1,0:T(8,128)} %copy-done.193), channel_id=1, source_target_pairs={{0,16},{1,17},{2,18},{3,19},{4,20},{5,21},{6,22},{7,23},{8,24},{9,... | collective-permute-start | bytes 98312 | tf_op jit(solution)/shard_map/ppermute | solution.py:174
  99.0 1.6 copy-done.1
  107.2 2.6 %reduce.1 = f32[32,1152]{1,0:T(8,128)} reduce(f32[32,1,1152]{2,1,0:T(1,128)} %all-to-all-done.1, f32[]{:T(128)} %broadcast.35), dimensions={1}, to_apply=%all_to_all.16.reduce_sub_computation | reduce | bytes 294916 | tf_op jit(solution)/shard_map/all_to_all | solution.py:177
  109.8 1.8 reshape.85.refs_0_
  119.6 4.3 %collective-permute-start.14 = (f32[64,128]{1,0:T(8,128)S(1)}, f32[64,128]{1,0:T(8,128)S(1)}, u32[]{:S(2)}, u32[]{:S(2)}) collective-permute-start(f32[64,128]{1,0:T(8,128)S(1)} %get-tuple-element.206), channel_id=1, source_target_pairs={{0,16},{1,17},{2,18},{3,19},{4,20},{5,21},{6,22},{7,23},{8,24},{9,... | collective-permute-start | bytes 98312 | tf_op jit(solution)/shard_map/ppermute | solution.py:174
  134.0 1.9 copy-done.18
  141.3 1.8 reshape.86
  143.2 3.3 %all-to-all-start.2 = ((f32[32,1,1152]{2,1,0:T(1,128)}), f32[32,1,1152]{2,1,0:T(1,128)}, u32[]{:S(2)}, u32[]{:S(2)}) async-start(f32[32,1,1152]{2,1,0:T(1,128)} %reshape.86), calls=%async_computation.2 | async-start | bytes 294912 | tf_op jit(solution)/shard_map/all_to_all | solution.py:177
  147.3 6.3 %collective-permute-start.17 = (f32[64,128]{1,0:T(8,128)}, f32[64,128]{1,0:T(8,128)S(1)}, u32[]{:S(2)}, u32[]{:S(2)}) collective-permute-start(f32[64,128]{1,0:T(8,128)} %copy-done.194), channel_id=1, source_target_pairs={{0,16},{1,17},{2,18},{3,19},{4,20},{5,21},{6,22},{7,23},{8,24},{9,... | collective-permute-start | bytes 98312 | tf_op jit(solution)/shard_map/ppermute | solution.py:174
  161.8 2.6 %reduce.2 = f32[32,1152]{1,0:T(8,128)} reduce(f32[32,1,1152]{2,1,0:T(1,128)} %all-to-all-done.2, f32[]{:T(128)} %broadcast.35), dimensions={1}, to_apply=%all_to_all.17.reduce_sub_computation | reduce | bytes 294916 | tf_op jit(solution)/shard_map/all_to_all | solution.py:177
  164.4 1.8 reshape.87.refs_0_
  174.4 4.5 %collective-permute-start.20 = (f32[64,128]{1,0:T(8,128)S(1)}, f32[64,128]{1,0:T(8,128)S(1)}, u32[]{:S(2)}, u32[]{:S(2)}) collective-permute-start(f32[64,128]{1,0:T(8,128)S(1)} %get-tuple-element.237), channel_id=1, source_target_pairs={{0,16},{1,17},{2,18},{3,19},{4,20},{5,21},{6,22},{7,23},{8,24},{9,... | collective-permute-start | bytes 98312 | tf_op jit(solution)/shard_map/ppermute | solution.py:174
  190.9 1.8 reshape.88
  192.7 3.3 %all-to-all-start.3 = ((f32[32,1,1152]{2,1,0:T(1,128)}), f32[32,1,1152]{2,1,0:T(1,128)}, u32[]{:S(2)}, u32[]{:S(2)}) async-start(f32[32,1,1152]{2,1,0:T(1,128)} %reshape.88), calls=%async_computation.3 | async-start | bytes 294912 | tf_op jit(solution)/shard_map/all_to_all | solution.py:177
  196.8 6.3 %collective-permute-start.23 = (f32[64,128]{1,0:T(8,128)}, f32[64,128]{1,0:T(8,128)S(1)}, u32[]{:S(2)}, u32[]{:S(2)}) collective-permute-start(f32[64,128]{1,0:T(8,128)} %get-tuple-element.244), channel_id=1, source_target_pairs={{0,16},{1,17},{2,18},{3,19},{4,20},{5,21},{6,22},{7,23},{8,24},{9,... | collective-permute-start | bytes 98312 | tf_op jit(solution)/shard_map/ppermute | solution.py:174
  213.2 2.0 reduce.3
  220.1 4.5 %collective-permute-start.26 = (f32[64,128]{1,0:T(8,128)}, f32[64,128]{1,0:T(8,128)S(1)}, u32[]{:S(2)}, u32[]{:S(2)}) collective-permute-start(f32[64,128]{1,0:T(8,128)} %get-tuple-element.271), channel_id=1, source_target_pairs={{0,16},{1,17},{2,18},{3,19},{4,20},{5,21},{6,22},{7,23},{8,24},{9,... | collective-permute-start | bytes 98312 | tf_op jit(solution)/shard_map/ppermute | solution.py:174
  232.3 9.9 %all_to_all.25 = f32[32,1,128]{2,1,0:T(1,128)S(1)} all-to-all(f32[32,1,128]{2,1,0:T(1,128)S(1)} %reshape.90), channel_id=1, replica_groups=mesh['sub'=32] {'sub'}, dimensions={0} | all-to-all | bytes 32768 | tf_op jit(solution)/shard_map/all_to_all | solution.py:177
  (490 shorter events, 121.9 us)
Async XLA Ops:
  10.3 19.3 %copy-start.78 = (f32[1,1024]{1,0:T(1,128)}, f32[1,1024]{1,0:T(1,128)S(1)}, u32[]{:S(2)}) copy-start(f32[1,1024]{1,0:T(1,128)S(1)} %get-tuple-element.138.refs_1_.refs_5_.refs_3_.refs_7_.refs_14_) | copy-start | bytes 12292
  10.4 18.5 %collective-permute-start = (f32[144,128]{1,0:T(8,128)S(1)}, f32[144,128]{1,0:T(8,128)S(1)}, u32[]{:S(2)}, u32[]{:S(2)}) collective-permute-start(f32[144,128]{1,0:T(8,128)S(1)} %get-tuple-element.151), channel_id=1, source_target_pairs={{0,1},{2,3},{4,5},{6,7},{8,9},{10,11},{12,13},{14,15},{16,17},{18,... | collective-permute-start | bytes 221192 | tf_op jit(solution)/shard_map/ppermute | solution.py:174
  10.9 18.0 %collective-permute-start.1 = (f32[144,128]{1,0:T(8,128)S(1)}, f32[144,128]{1,0:T(8,128)S(1)}, u32[]{:S(2)}, u32[]{:S(2)}) collective-permute-start(f32[144,128]{1,0:T(8,128)S(1)} %get-tuple-element.152), channel_id=1, source_target_pairs={{1,2},{3,4},{5,6},{7,8},{9,10},{11,12},{13,14},{15,16},{17,18},{19... | collective-permute-start | bytes 221192 | tf_op jit(solution)/shard_map/ppermute | solution.py:174
  11.5 17.4 %collective-permute-start.2 = (f32[144,128]{1,0:T(8,128)S(1)}, f32[144,128]{1,0:T(8,128)S(1)}, u32[]{:S(2)}, u32[]{:S(2)}) collective-permute-start(f32[144,128]{1,0:T(8,128)S(1)} %get-tuple-element.153), channel_id=1, source_target_pairs={{0,16},{1,17},{2,18},{3,19},{4,20},{5,21},{6,22},{7,23},{8,24},{9,... | collective-permute-start | bytes 221192 | tf_op jit(solution)/shard_map/ppermute | solution.py:174
  32.0 26.8 %all-to-all-start = ((f32[32,1,1152]{2,1,0:T(1,128)}), f32[32,1,1152]{2,1,0:T(1,128)}, u32[]{:S(2)}, u32[]{:S(2)}) async-start(f32[32,1,1152]{2,1,0:T(1,128)} %reshape.82), calls=%async_computation | async-start | bytes 294912 | tf_op jit(solution)/shard_map/all_to_all | solution.py:177
  35.3 20.4 %collective-permute-start.3 = (f32[64,128]{1,0:T(8,128)}, f32[64,128]{1,0:T(8,128)S(1)}, u32[]{:S(2)}, u32[]{:S(2)}) collective-permute-start(f32[64,128]{1,0:T(8,128)} %get-tuple-element.164), channel_id=1, source_target_pairs={{0,1},{2,3},{4,5},{6,7},{8,9},{10,11},{12,13},{14,15},{16,17},{18,... | collective-permute-start | bytes 98312 | tf_op jit(solution)/shard_map/ppermute | solution.py:174
  35.4 20.3 %collective-permute-start.4 = (f32[64,128]{1,0:T(8,128)}, f32[64,128]{1,0:T(8,128)S(1)}, u32[]{:S(2)}, u32[]{:S(2)}) collective-permute-start(f32[64,128]{1,0:T(8,128)} %get-tuple-element.165), channel_id=1, source_target_pairs={{1,2},{3,4},{5,6},{7,8},{9,10},{11,12},{13,14},{15,16},{17,18},{19... | collective-permute-start | bytes 98312 | tf_op jit(solution)/shard_map/ppermute | solution.py:174
  36.1 19.7 %collective-permute-start.5 = (f32[64,128]{1,0:T(8,128)}, f32[64,128]{1,0:T(8,128)S(1)}, u32[]{:S(2)}, u32[]{:S(2)}) collective-permute-start(f32[64,128]{1,0:T(8,128)} %get-tuple-element.166), channel_id=1, source_target_pairs={{0,16},{1,17},{2,18},{3,19},{4,20},{5,21},{6,22},{7,23},{8,24},{9,... | collective-permute-start | bytes 98312 | tf_op jit(solution)/shard_map/ppermute | solution.py:174
  71.5 11.0 %collective-permute-start.6 = (f32[64,128]{1,0:T(8,128)S(1)}, f32[64,128]{1,0:T(8,128)S(1)}, u32[]{:S(2)}, u32[]{:S(2)}) collective-permute-start(f32[64,128]{1,0:T(8,128)S(1)} %get-tuple-element.180), channel_id=1, source_target_pairs={{0,1},{2,3},{4,5},{6,7},{8,9},{10,11},{12,13},{14,15},{16,17},{18,... | collective-permute-start | bytes 98312 | tf_op jit(solution)/shard_map/ppermute | solution.py:174
  71.5 11.0 %collective-permute-start.7 = (f32[64,128]{1,0:T(8,128)S(1)}, f32[64,128]{1,0:T(8,128)S(1)}, u32[]{:S(2)}, u32[]{:S(2)}) collective-permute-start(f32[64,128]{1,0:T(8,128)S(1)} %get-tuple-element.181), channel_id=1, source_target_pairs={{1,2},{3,4},{5,6},{7,8},{9,10},{11,12},{13,14},{15,16},{17,18},{19... | collective-permute-start | bytes 98312 | tf_op jit(solution)/shard_map/ppermute | solution.py:174
  72.4 10.2 %collective-permute-start.8 = (f32[64,128]{1,0:T(8,128)S(1)}, f32[64,128]{1,0:T(8,128)S(1)}, u32[]{:S(2)}, u32[]{:S(2)}) collective-permute-start(f32[64,128]{1,0:T(8,128)S(1)} %get-tuple-element.182), channel_id=1, source_target_pairs={{0,16},{1,17},{2,18},{3,19},{4,20},{5,21},{6,22},{7,23},{8,24},{9,... | collective-permute-start | bytes 98312 | tf_op jit(solution)/shard_map/ppermute | solution.py:174
  88.6 18.6 %all-to-all-start.1 = ((f32[32,1,1152]{2,1,0:T(1,128)}), f32[32,1,1152]{2,1,0:T(1,128)}, u32[]{:S(2)}, u32[]{:S(2)}) async-start(f32[32,1,1152]{2,1,0:T(1,128)} %reshape.84), calls=%async_computation.1 | async-start | bytes 294912 | tf_op jit(solution)/shard_map/all_to_all | solution.py:177
  91.9 12.3 %collective-permute-start.9 = (f32[64,128]{1,0:T(8,128)}, f32[64,128]{1,0:T(8,128)S(1)}, u32[]{:S(2)}, u32[]{:S(2)}) collective-permute-start(f32[64,128]{1,0:T(8,128)} %copy-done.197), channel_id=1, source_target_pairs={{0,1},{2,3},{4,5},{6,7},{8,9},{10,11},{12,13},{14,15},{16,17},{18,... | collective-permute-start | bytes 98312 | tf_op jit(solution)/shard_map/ppermute | solution.py:174
  92.0 12.2 %collective-permute-start.10 = (f32[64,128]{1,0:T(8,128)}, f32[64,128]{1,0:T(8,128)S(1)}, u32[]{:S(2)}, u32[]{:S(2)}) collective-permute-start(f32[64,128]{1,0:T(8,128)} %copy-done.195), channel_id=1, source_target_pairs={{1,2},{3,4},{5,6},{7,8},{9,10},{11,12},{13,14},{15,16},{17,18},{19... | collective-permute-start | bytes 98312 | tf_op jit(solution)/shard_map/ppermute | solution.py:174
  92.7 11.5 %collective-permute-start.11 = (f32[64,128]{1,0:T(8,128)}, f32[64,128]{1,0:T(8,128)S(1)}, u32[]{:S(2)}, u32[]{:S(2)}) collective-permute-start(f32[64,128]{1,0:T(8,128)} %copy-done.193), channel_id=1, source_target_pairs={{0,16},{1,17},{2,18},{3,19},{4,20},{5,21},{6,22},{7,23},{8,24},{9,... | collective-permute-start | bytes 98312 | tf_op jit(solution)/shard_map/ppermute | solution.py:174
  118.7 18.3 %collective-permute-start.12 = (f32[64,128]{1,0:T(8,128)S(1)}, f32[64,128]{1,0:T(8,128)S(1)}, u32[]{:S(2)}, u32[]{:S(2)}) collective-permute-start(f32[64,128]{1,0:T(8,128)S(1)} %get-tuple-element.204), channel_id=1, source_target_pairs={{0,1},{2,3},{4,5},{6,7},{8,9},{10,11},{12,13},{14,15},{16,17},{18,... | collective-permute-start | bytes 98312 | tf_op jit(solution)/shard_map/ppermute | solution.py:174
  118.8 18.3 %collective-permute-start.13 = (f32[64,128]{1,0:T(8,128)S(1)}, f32[64,128]{1,0:T(8,128)S(1)}, u32[]{:S(2)}, u32[]{:S(2)}) collective-permute-start(f32[64,128]{1,0:T(8,128)S(1)} %get-tuple-element.205), channel_id=1, source_target_pairs={{1,2},{3,4},{5,6},{7,8},{9,10},{11,12},{13,14},{15,16},{17,18},{19... | collective-permute-start | bytes 98312 | tf_op jit(solution)/shard_map/ppermute | solution.py:174
  119.6 17.5 %collective-permute-start.14 = (f32[64,128]{1,0:T(8,128)S(1)}, f32[64,128]{1,0:T(8,128)S(1)}, u32[]{:S(2)}, u32[]{:S(2)}) collective-permute-start(f32[64,128]{1,0:T(8,128)S(1)} %get-tuple-element.206), channel_id=1, source_target_pairs={{0,16},{1,17},{2,18},{3,19},{4,20},{5,21},{6,22},{7,23},{8,24},{9,... | collective-permute-start | bytes 98312 | tf_op jit(solution)/shard_map/ppermute | solution.py:174
  143.2 18.6 %all-to-all-start.2 = ((f32[32,1,1152]{2,1,0:T(1,128)}), f32[32,1,1152]{2,1,0:T(1,128)}, u32[]{:S(2)}, u32[]{:S(2)}) async-start(f32[32,1,1152]{2,1,0:T(1,128)} %reshape.86), calls=%async_computation.2 | async-start | bytes 294912 | tf_op jit(solution)/shard_map/all_to_all | solution.py:177
  146.5 12.3 %collective-permute-start.15 = (f32[64,128]{1,0:T(8,128)}, f32[64,128]{1,0:T(8,128)S(1)}, u32[]{:S(2)}, u32[]{:S(2)}) collective-permute-start(f32[64,128]{1,0:T(8,128)} %copy-done.198), channel_id=1, source_target_pairs={{0,1},{2,3},{4,5},{6,7},{8,9},{10,11},{12,13},{14,15},{16,17},{18,... | collective-permute-start | bytes 98312 | tf_op jit(solution)/shard_map/ppermute | solution.py:174
  146.6 12.1 %collective-permute-start.16 = (f32[64,128]{1,0:T(8,128)}, f32[64,128]{1,0:T(8,128)S(1)}, u32[]{:S(2)}, u32[]{:S(2)}) collective-permute-start(f32[64,128]{1,0:T(8,128)} %copy-done.196), channel_id=1, source_target_pairs={{1,2},{3,4},{5,6},{7,8},{9,10},{11,12},{13,14},{15,16},{17,18},{19... | collective-permute-start | bytes 98312 | tf_op jit(solution)/shard_map/ppermute | solution.py:174
  147.3 11.5 %collective-permute-start.17 = (f32[64,128]{1,0:T(8,128)}, f32[64,128]{1,0:T(8,128)S(1)}, u32[]{:S(2)}, u32[]{:S(2)}) collective-permute-start(f32[64,128]{1,0:T(8,128)} %copy-done.194), channel_id=1, source_target_pairs={{0,16},{1,17},{2,18},{3,19},{4,20},{5,21},{6,22},{7,23},{8,24},{9,... | collective-permute-start | bytes 98312 | tf_op jit(solution)/shard_map/ppermute | solution.py:174
  173.4 14.3 %collective-permute-start.18 = (f32[64,128]{1,0:T(8,128)S(1)}, f32[64,128]{1,0:T(8,128)S(1)}, u32[]{:S(2)}, u32[]{:S(2)}) collective-permute-start(f32[64,128]{1,0:T(8,128)S(1)} %get-tuple-element.235), channel_id=1, source_target_pairs={{0,1},{2,3},{4,5},{6,7},{8,9},{10,11},{12,13},{14,15},{16,17},{18,... | collective-permute-start | bytes 98312 | tf_op jit(solution)/shard_map/ppermute | solution.py:174
  173.5 14.3 %collective-permute-start.19 = (f32[64,128]{1,0:T(8,128)S(1)}, f32[64,128]{1,0:T(8,128)S(1)}, u32[]{:S(2)}, u32[]{:S(2)}) collective-permute-start(f32[64,128]{1,0:T(8,128)S(1)} %get-tuple-element.236), channel_id=1, source_target_pairs={{1,2},{3,4},{5,6},{7,8},{9,10},{11,12},{13,14},{15,16},{17,18},{19... | collective-permute-start | bytes 98312 | tf_op jit(solution)/shard_map/ppermute | solution.py:174
  174.4 13.4 %collective-permute-start.20 = (f32[64,128]{1,0:T(8,128)S(1)}, f32[64,128]{1,0:T(8,128)S(1)}, u32[]{:S(2)}, u32[]{:S(2)}) collective-permute-start(f32[64,128]{1,0:T(8,128)S(1)} %get-tuple-element.237), channel_id=1, source_target_pairs={{0,16},{1,17},{2,18},{3,19},{4,20},{5,21},{6,22},{7,23},{8,24},{9,... | collective-permute-start | bytes 98312 | tf_op jit(solution)/shard_map/ppermute | solution.py:174
  192.7 20.4 %all-to-all-start.3 = ((f32[32,1,1152]{2,1,0:T(1,128)}), f32[32,1,1152]{2,1,0:T(1,128)}, u32[]{:S(2)}, u32[]{:S(2)}) async-start(f32[32,1,1152]{2,1,0:T(1,128)} %reshape.88), calls=%async_computation.3 | async-start | bytes 294912 | tf_op jit(solution)/shard_map/all_to_all | solution.py:177
  196.0 14.0 %collective-permute-start.21 = (f32[64,128]{1,0:T(8,128)}, f32[64,128]{1,0:T(8,128)S(1)}, u32[]{:S(2)}, u32[]{:S(2)}) collective-permute-start(f32[64,128]{1,0:T(8,128)} %get-tuple-element.242), channel_id=1, source_target_pairs={{0,1},{2,3},{4,5},{6,7},{8,9},{10,11},{12,13},{14,15},{16,17},{18,... | collective-permute-start | bytes 98312 | tf_op jit(solution)/shard_map/ppermute | solution.py:174
  196.1 13.9 %collective-permute-start.22 = (f32[64,128]{1,0:T(8,128)}, f32[64,128]{1,0:T(8,128)S(1)}, u32[]{:S(2)}, u32[]{:S(2)}) collective-permute-start(f32[64,128]{1,0:T(8,128)} %get-tuple-element.243), channel_id=1, source_target_pairs={{1,2},{3,4},{5,6},{7,8},{9,10},{11,12},{13,14},{15,16},{17,18},{19... | collective-permute-start | bytes 98312 | tf_op jit(solution)/shard_map/ppermute | solution.py:174
  196.8 13.2 %collective-permute-start.23 = (f32[64,128]{1,0:T(8,128)}, f32[64,128]{1,0:T(8,128)S(1)}, u32[]{:S(2)}, u32[]{:S(2)}) collective-permute-start(f32[64,128]{1,0:T(8,128)} %get-tuple-element.244), channel_id=1, source_target_pairs={{0,16},{1,17},{2,18},{3,19},{4,20},{5,21},{6,22},{7,23},{8,24},{9,... | collective-permute-start | bytes 98312 | tf_op jit(solution)/shard_map/ppermute | solution.py:174
  219.4 23.5 %collective-permute-start.24 = (f32[64,128]{1,0:T(8,128)}, f32[64,128]{1,0:T(8,128)S(1)}, u32[]{:S(2)}, u32[]{:S(2)}) collective-permute-start(f32[64,128]{1,0:T(8,128)} %get-tuple-element.269), channel_id=1, source_target_pairs={{0,1},{2,3},{4,5},{6,7},{8,9},{10,11},{12,13},{14,15},{16,17},{18,... | collective-permute-start | bytes 98312 | tf_op jit(solution)/shard_map/ppermute | solution.py:174
  219.4 23.5 %collective-permute-start.25 = (f32[64,128]{1,0:T(8,128)}, f32[64,128]{1,0:T(8,128)S(1)}, u32[]{:S(2)}, u32[]{:S(2)}) collective-permute-start(f32[64,128]{1,0:T(8,128)} %get-tuple-element.270), channel_id=1, source_target_pairs={{1,2},{3,4},{5,6},{7,8},{9,10},{11,12},{13,14},{15,16},{17,18},{19... | collective-permute-start | bytes 98312 | tf_op jit(solution)/shard_map/ppermute | solution.py:174
  220.1 22.9 %collective-permute-start.26 = (f32[64,128]{1,0:T(8,128)}, f32[64,128]{1,0:T(8,128)S(1)}, u32[]{:S(2)}, u32[]{:S(2)}) collective-permute-start(f32[64,128]{1,0:T(8,128)} %get-tuple-element.271), channel_id=1, source_target_pairs={{0,16},{1,17},{2,18},{3,19},{4,20},{5,21},{6,22},{7,23},{8,24},{9,... | collective-permute-start | bytes 98312 | tf_op jit(solution)/shard_map/ppermute | solution.py:174
  (198 other events, 537.4 us)

commit v3 on v2

v3 whole, which is shorter than its diff:
```python
import functools

import jax
import jax.numpy as jnp
from jax import lax
from jax.experimental import pallas as pl
from jax.experimental.pallas import tpu as pltpu
from jax.sharding import PartitionSpec as P

CYCLE = 16
ITERS = 4

BF = jnp.bfloat16
F32 = jnp.float32
NN = ((1,), (0,))
NT = ((1,), (1,))
TN = ((0,), (0,))
STAGE_BYTES = 8 * 1024 * 1024
PREPARE_BYTES = 16 * 1024 * 1024


def contract(left, right, dims=NN):
    return lax.dot_general(left, right, (dims, ((), ())), preferred_element_type=F32)


def split(value):
    high = value.astype(BF)
    return high, (value - high.astype(F32)).astype(BF)


def times(value, high, low, dims=NN):
    rows = value.shape[0]
    top, rest = split(value)
    both = contract(jnp.concatenate([top, rest], axis=0), high, dims)
    return both[:rows] + both[rows:] + contract(top, low, dims)


def pick(value, onehot, dims=NN):
    rows = value.shape[0]
    top, rest = split(value)
    last = (value - top.astype(F32) - rest.astype(F32)).astype(BF)
    all_three = contract(jnp.concatenate([top, rest, last], axis=0), onehot, dims)
    return all_three[:rows] + (all_three[rows:2 * rows] + all_three[2 * rows:])


def diagonal(count):
    first = lax.broadcasted_iota(jnp.int32, (count, count), 0)
    return first == lax.broadcasted_iota(jnp.int32, (count, count), 1)


def to_column(row):
    count = row.shape[1]
    return jnp.sum(jnp.where(diagonal(count), jnp.broadcast_to(row, (count, count)), 0.0), axis=1, keepdims=True)


def to_row(column):
    count = column.shape[0]
    return jnp.sum(jnp.where(diagonal(count), jnp.broadcast_to(column, (count, count)), 0.0), axis=0, keepdims=True)


def dot(left, right):
    return jnp.sum(left * right, axis=1, keepdims=True)


def stage(name, function, outs, *args, scalars=0):
    def kernel(*refs):
        values = function(*refs[:scalars], *[ref[...] for ref in refs[scalars:len(args)]])
        for ref, value in zip(refs[len(args):], values):
            ref[...] = value

    whole = pl.BlockSpec(memory_space=pltpu.VMEM)
    return pl.pallas_call(
        kernel,
        name=name,
        out_shape=[jax.ShapeDtypeStruct(shape, kind) for shape, kind in outs],
        in_specs=[pl.BlockSpec(memory_space=pltpu.SMEM)] * scalars + [whole] * (len(args) - scalars),
        out_specs=[whole] * len(outs),
        compiler_params=pltpu.CompilerParams(vmem_limit_bytes=STAGE_BYTES),
    )(*args)


def prepare(name, matrix, picker, unpicker, tiles=4):
    slots, order = picker.shape
    columns = order // tiles

    def kernel(matrix_ref, picker_ref, unpicker_ref, high_ref, low_ref, fhigh_ref, flow_ref, block_high_ref, block_low_ref, total_high, total_low):
        at = pl.program_id(0)
        high, low = split(matrix_ref[0])
        high_ref[...] = high
        low_ref[...] = low
        onehot = picker_ref[...]
        mine = unpicker_ref[...]
        for part, face_ref, total in ((high, fhigh_ref, total_high), (low, flow_ref, total_low)):
            face = contract(onehot, part).astype(BF)
            face_ref[...] = face
            block = contract(face, mine)

            @pl.when(at == 0)
            def _():
                total[...] = block

            @pl.when(at > 0)
            def _():
                total[...] += block

        @pl.when(at == tiles - 1)
        def _():
            block_high_ref[...] = total_high[...].astype(BF)
            block_low_ref[...] = total_low[...].astype(BF)

    shape = jax.ShapeDtypeStruct
    return pl.pallas_call(
        kernel,
        name=name,
        grid=(tiles,),
        in_specs=[
            pl.BlockSpec((1, order, columns), lambda i: (0, 0, i)),
            pl.BlockSpec((slots, order), lambda i: (0, 0)),
            pl.BlockSpec((columns, slots), lambda i: (i, 0)),
        ],
        out_specs=[
            pl.BlockSpec((order, columns), lambda i: (0, i)),
            pl.BlockSpec((order, columns), lambda i: (0, i)),
            pl.BlockSpec((slots, columns), lambda i: (0, i)),
            pl.BlockSpec((slots, columns), lambda i: (0, i)),
            pl.BlockSpec((slots, slots), lambda i: (0, 0)),
            pl.BlockSpec((slots, slots), lambda i: (0, 0)),
        ],
        out_shape=[shape((order, order), BF)] * 2 + [shape((slots, order), BF)] * 2 + [shape((slots, slots), BF)] * 2,
        scratch_shapes=[pltpu.VMEM((slots, slots), F32)] * 2,
        compiler_params=pltpu.CompilerParams(vmem_limit_bytes=PREPARE_BYTES),
        cost_estimate=pl.CostEstimate(flops=8 * order * order * slots, bytes_accessed=10 * order * order, transcendentals=0),
    )(matrix, picker, unpicker)


def swaps(total):
    sets = []
    for by in (1, CYCLE):
        for parity in (0, 1):
            ahead = [i for i in range(total - by) if (i // by) % 2 == parity]
            sets.append((by, parity, [(i, i + by) for i in ahead] + [(i + by, i) for i in ahead]))
    return sets


def local(stiffness, neumann_inv, coarse_basis, coarse_inv, loads, face_index, face_len):
    total = lax.axis_size("sub")
    load = loads[0]
    cases, ndof = load.shape
    primal = coarse_basis.shape[1]
    width = face_index.shape[2]

    chosen = []
    for by, parity, pairs in swaps(total):
        if pairs:
            behind, ahead = (0, 1) if by == 1 else (2, 3)
            chosen.append((pairs, behind, ahead, by, parity))
    blocks = len(chosen)
    slots = blocks * width
    own_rows = (blocks + 1) * primal
    vec = ((cases, ndof), F32)
    face = [((cases, width), F32)] * blocks
    column = ((cases, 1), F32)
    lines = ((primal, cases), F32)

    def cut(value):
        return [value[:, i * width:(i + 1) * width] for i in range(blocks)]

    def exchange(pieces):
        return [lax.ppermute(piece, "sub", chosen[at][0]) for at, piece in enumerate(pieces)]

    def spread(payload):
        return lax.all_to_all(payload, "sub", 0, 0, tiled=True)

    half = primal // 2

    def payload_of(lines, sums):
        pieces = []
        if lines is not None:
            pairs = jnp.concatenate([lines[:half], lines[half:]], axis=1)
            pieces = [pairs[i:i + 1] for i in range(half)]
        row = jnp.concatenate(pieces + [sums], axis=1)
        return jnp.broadcast_to(row, (total, row.shape[1]))

    def both_sums(everyone):
        row = jnp.sum(everyone[:, -2 * cases:], axis=0, keepdims=True)
        return to_column(row[:, :cases]), to_column(row[:, cases:])

    reps = coarse_inv.shape[1] // width

    def first(lengths, index, load, basis, inv):
        me = lax.axis_index("sub")
        load, basis = load[0], basis[0]
        rows = []
        lane = lax.broadcasted_iota(jnp.int32, (1, width), 1)
        for _, behind, ahead, by, parity in chosen:
            forward = (me // by) % 2 == parity
            row = jnp.where(forward, index[0, ahead:ahead + 1], index[0, behind:behind + 1])
            length = jnp.where(forward, lengths[0, ahead], lengths[0, behind])
            rows.append(jnp.where(lane < length, row, -1))
        row = jnp.concatenate(rows, axis=1)
        unpicker = (lax.broadcasted_iota(jnp.int32, (ndof, slots), 0) == row).astype(F32).astype(BF)
        spot = jnp.sum(jnp.where(diagonal(slots), jnp.broadcast_to(row, (slots, slots)), 0), axis=1, keepdims=True)
        picker = (lax.broadcasted_iota(jnp.int32, (slots, ndof), 1) == spot).astype(F32)
        weight = 1.0 / (1.0 + jnp.sum(picker, axis=0, keepdims=True))
        weighted = basis * weight
        at_slots = pick(jnp.concatenate([load, weighted], axis=0), unpicker)
        inv_packed = jnp.concatenate([inv[:, i * width:(i + 1) * width] for i in range(reps)], axis=0)
        out = [jnp.concatenate([part, inv_packed], axis=0) for part in cut(at_slots)]
        return [picker.astype(BF), unpicker, weight, weighted, at_slots[cases:]] + out

    packed = ((cases + primal + reps * primal, width), F32)
    picker, unpicker, weight, weighted, basis_slots, *sent = stage(
        "first", first,
        [((slots, ndof), BF), ((ndof, slots), BF), ((1, ndof), F32), ((primal, ndof), F32), ((primal, slots), F32)] + [packed] * blocks,
        face_len, face_index, loads, coarse_basis, coarse_inv, scalars=1)
    came = exchange(sent)

    inv_parts = prepare("prepare_inv", neumann_inv, picker, unpicker)
    stiff_parts = prepare("prepare_stiff", stiffness, picker, unpicker)

    def reach(weighted, inv, picker, high, low, fhigh, flow, *came):
        functions = [weighted]
        rows = [inv]
        for at, part in enumerate(came):
            functions.append(pick(part[cases:cases + primal], picker[at * width:(at + 1) * width]))
            rest = part[cases + primal:]
            rows.append(jnp.concatenate([rest[i * primal:(i + 1) * primal] for i in range(reps)], axis=1))
        functions = jnp.concatenate(functions, axis=0)
        rows = jnp.concatenate(rows, axis=0)
        image = times(functions, high, low)
        everything = jnp.concatenate([functions, image, times(functions, fhigh, flow, NT)], axis=1)
        return [rows, *split(everything)]

    wide = 2 * ndof + slots
    rows, *function_parts = stage(
        "reach", reach,
        [((own_rows, total * primal), F32)] + [((own_rows, wide), BF)] * 2,
        weighted, coarse_inv, picker, *stiff_parts[:4], *came)
    rows = jnp.transpose(rows.reshape(own_rows, total, 2, half), (2, 0, 3, 1)).reshape(2 * own_rows, half * total)

    def solve_own(part, weight, weighted, high, low, fhigh, flow):
        scaled = part * weight
        return [times(scaled, high, low), times(scaled, fhigh, flow, NT), times(weighted, *split(part), NT)]

    solve_outs = [vec, ((cases, slots), F32), lines]

    def solve_rest(scale, inner, inner_faces, lines, sums, weight, basis_slots, fhigh, flow, block_high, block_low, *came):
        came = scale * jnp.concatenate(came, axis=1)
        lines = lines + times(basis_slots, *split(came), NT)
        came = 0.5 * came
        inner = weight * (inner + times(came, fhigh, flow))
        inner_faces = 0.5 * (inner_faces + times(came, block_high, block_low))
        return [payload_of(lines, sums), inner] + cut(inner_faces)

    rest_outs = [((total, (primal + 2) * cases), F32), vec] + face

    def apply_own(inner, high, low, fhigh, flow):
        return [times(inner, high, low), times(inner, fhigh, flow, NT)]

    def apply_rest(inner, image, image_faces, picker, fhigh, flow, block_high, block_low, *came):
        came = jnp.concatenate(came, axis=1)
        inner = inner + pick(came, picker)
        image = image + times(came, fhigh, flow)
        image_faces = image_faces + times(came, block_high, block_low)
        return [inner, image, image_faces]

    def correct(everyone, inner, image, image_faces, rows, high, low):
        gathered = jnp.concatenate([everyone[:, i * 2 * cases:(i + 1) * 2 * cases] for i in range(half)], axis=0)
        product = times(rows, *split(gathered))
        factors = (product[:own_rows, :cases] + product[own_rows:, cases:]).T
        extra = times(factors, high, low)
        return [
            inner + extra[:, :ndof],
            image + extra[:, ndof:2 * ndof],
            *both_sums(everyone),
        ] + cut(image_faces + extra[:, 2 * ndof:])

    def precondition(part, scale, sums, exchanged):
        inner, inner_faces, lines = stage("solve_own", solve_own, solve_outs, part, weight, weighted, *inv_parts[:4])
        payload, inner, *sent = stage(
            "solve_rest", solve_rest, rest_outs,
            scale, inner, inner_faces, lines, sums, weight, basis_slots, *inv_parts[2:], *exchanged)
        everyone = spread(payload)
        came = exchange(sent)
        image, image_faces = stage("apply_own", apply_own, [vec, ((cases, slots), F32)], inner, *stiff_parts[:4])
        inner, image, image_faces = stage(
            "apply_rest", apply_rest, [vec, vec, ((cases, slots), F32)],
            inner, image, image_faces, picker, *stiff_parts[2:], *came)
        inner, image, gamma, delta, *sent = stage(
            "correct", correct, [vec, vec, column, column] + face, everyone, inner, image, image_faces, rows, *function_parts)
        return inner, image, gamma, delta, sent

    def scatter(picker, *came):
        return pick(jnp.concatenate(came, axis=1), picker)

    one = jnp.ones((cases, 1), F32)
    load_in = [part[:cases] for part in came]
    none = jnp.zeros((1, 2 * cases), F32)
    u, image, _, _, sent = precondition(load, one, none, load_in)
    came = exchange(sent)

    def begin(load, u, image, weight, picker, *load_in):
        residual = load + scatter(picker, *load_in)
        gamma = dot(residual * weight, u)
        delta = dot(image, u)
        return [residual, jnp.concatenate([to_row(gamma), to_row(delta)], axis=1)]

    pair = ((1, 2 * cases), F32)
    residual, sums = stage("begin", begin, [vec, pair], load, u, image, weight, picker, *load_in)
    part, scale = image, one

    def assembled(part, scale, picker, *came):
        return [part + scale * scatter(picker, *came)]

    for step in range(ITERS - 1):
        m, image, gamma, delta, sent = precondition(part, scale, sums, came)
        (w,) = stage("assembled", assembled, [vec], part, scale, picker, *came)
        if step > 0:
            (z,) = stage("assembled", assembled, [vec], z_part, one, picker, *came)
        came_next = exchange(sent)
        if step == 0:
            def update(gamma, delta, u, w, m, image, residual, weight):
                alpha = gamma / delta
                q, s, p = m, w, u
                x = alpha * p
                residual = residual - alpha * s
                u = u - alpha * q
                part = w - alpha * image
                sums = jnp.concatenate([to_row(dot(weight * residual, u)), to_row(dot(weight * w - alpha * image, u))], axis=1)
                return [alpha, -alpha, q, s, p, x, residual, u, image, part, sums]

            alpha, scale, q, s, p, x, residual, u, z_part, part, sums = stage(
                "update", update, [column] * 2 + [vec] * 8 + [pair], gamma, delta, u, w, m, image, residual, weight)
        else:
            def update(gamma, delta, gamma_old, alpha_old, u, w, m, image, residual, x, p, s, q, z, weight):
                beta = gamma / gamma_old
                alpha = gamma / (delta - beta * gamma / alpha_old)
                q = m + beta * q
                s = w + beta * s
                p = u + beta * p
                x = x + alpha * p
                residual = residual - alpha * s
                u = u - alpha * q
                before = w - (alpha * beta) * z
                part = before - alpha * image
                sums = jnp.concatenate([to_row(dot(weight * residual, u)), to_row(dot(weight * before - alpha * image, u))], axis=1)
                return [alpha, -alpha, q, s, p, x, residual, u, image + beta * z, part, sums]

            alpha, scale, q, s, p, x, residual, u, z_part, part, sums = stage(
                "update", update, [column] * 2 + [vec] * 8 + [pair],
                gamma, delta, gamma_old, alpha_old, u, w, m, image, residual, x, p, s, q, z, weight)
        gamma_old, alpha_old = gamma, alpha
        came = came_next

    everyone = spread(jnp.broadcast_to(sums, (total, 2 * cases)))

    def finish(everyone, gamma_old, alpha_old, part, scale, u, residual, x, p, s, picker, *came):
        w = part + scale * scatter(picker, *came)
        gamma, delta = both_sums(everyone)
        beta = gamma / gamma_old
        alpha = gamma / (delta - beta * gamma / alpha_old)
        return [x + alpha * (u + beta * p), residual - alpha * (w + beta * s)]

    x, residual = stage(
        "finish", finish, [vec, vec],
        everyone, gamma_old, alpha_old, part, scale, u, residual, x, p, s, picker, *came)
    return (x[None], residual[None])


def solution(mesh):
    placed = (
        P("sub", None, None),
        P("sub", None, None),
        P("sub", None, None),
        P("sub", None),
        P("sub", None, None),
        P("sub", None, None),
        P("sub", None),
    )
    return jax.shard_map(
        local,
        mesh=mesh,
        in_specs=placed,
        out_specs=(P("sub", None, None), P("sub", None, None)),
        check_vma=False,
    )
```

time: 248 us -> 235 us (0.948)
  other arithmetic: 11.5 us -> 0 us
  Pallas kernels: 40.5 us -> 44.7 us
  between operations: 6.46 us -> 2.47 us
    all_to_all x5 -> x0, other arithmetic: 10.5 us -> none  [spread(): return lax.all_to_all(payload, 'sub', 0, 0, tiled=True)]
    unnamed x408 -> x388, local copies, waits for them, and re-layouts: 104 us -> 93.8 us
    pallas_call x2, Pallas kernels: 11.6 us -> 15.6 us  [prepare(): pl.pallas_call(kernel, name=name, grid=(tiles,), in_specs=[pl.BlockSpec((...]
    reshape x0 -> x2, local copies, waits for them, and re-layouts: none -> 3.45 us  [local(): jnp.transpose(rows.reshape(own_rows, total, 2, half), (2, 0, 3, 1))]
    all_to_all x1 -> x4, local copies, waits for them, and re-layouts: 0.58 us -> 3.24 us  [spread(): return lax.all_to_all(payload, 'sub', 0, 0, tiled=True)]
  transfers between devices with their start and end apart: 31 -> 31, of which waited for: 0 -> 0; matrix products, arithmetic and copies ran while one was open for 0% -> 3% of each run, Pallas kernels for 12% -> 15%
where the time goes in v3:
time: 235 us; the launch traced here: 232 us
  local copies, waits for them, and re-layouts  104 us (44%)
  starting transfers between devices  71 us (30%)
  Pallas kernels  44.7 us (19%)
  blocking collectives  9.89 us (4%)
  between operations  2.47 us (1%)
    unnamed x388, local copies, waits for them, and re-layouts  93.8 us
    ppermute x27, starting transfers between devices, exchange(): lax.ppermute(piece, 'sub', chosen[at][0])  57.7 us
    pallas_call x32, Pallas kernels, stage(): pl.pallas_call(kernel, name=name, out_shape=[jax.ShapeDtypeStruct(shape,...  29.1 us
    pallas_call x2, Pallas kernels, prepare(): pl.pallas_call(kernel, name=name, grid=(tiles,), in_specs=[pl.BlockSpec((...  15.6 us
    all_to_all x4, starting transfers between devices, spread(): return lax.all_to_all(payload, 'sub', 0, 0, tiled=True)  13.3 us
    all_to_all x1, blocking collectives, spread(): return lax.all_to_all(payload, 'sub', 0, 0, tiled=True)  9.89 us
  transfers between devices with their start and end apart: 31, of which 0 were waited for; matrix products, arithmetic and copies ran while one was open for 3% of the time, Pallas kernels for 15%

profile of v3, /device:TPU:0, one launch (start us, length us, event | category | flops | bytes accessed | tf_op | source)
XLA Modules:
  0.0 232.2 jit_solution(6291577076653520021)
XLA Ops:
  7.1 7.3 %collective-permute-start.2 = (f32[144,128]{1,0:T(8,128)S(1)}, f32[144,128]{1,0:T(8,128)S(1)}, u32[]{:S(2)}, u32[]{:S(2)}) collective-permute-start(f32[144,128]{1,0:T(8,128)S(1)} %get-tuple-element.154), channel_id=1, source_target_pairs={{0,16},{1,17},{2,18},{3,19},{4,20},{5,21},{6,22},{7,23},{8,24},{9,... | collective-permute-start | bytes 221192 | tf_op jit(solution)/shard_map/ppermute | solution.py:169
  14.4 2.2 copy-done.182
  16.6 7.8 %prepare_inv.1 = (bf16[1024,1024]{1,0:T(8,128)(2,1)S(1)}, bf16[1024,1024]{1,0:T(8,128)(2,1)S(1)}, bf16[384,1024]{1,0:T(8,128)(2,1)S(1)}, bf16[384,1024]{1,0:T(8,...) custom-call(f32[1,1024,1024]{2,1,0:T(8,128)S(1)} %copy-done.182, ...), custom_call_target="tpu_custom_call" | custom-call | flops 3221225472 | bytes 10485760 | tf_op jit(solution)/shard_map/prepare_inv/pallas_call | solution.py:112
  29.9 3.3 %all-to-all-start = ((f32[32,1,1152]{2,1,0:T(1,128)}), f32[32,1,1152]{2,1,0:T(1,128)}, u32[]{:S(2)}, u32[]{:S(2)}) async-start(f32[32,1,1152]{2,1,0:T(1,128)} %copy.16), calls=%async_computation | async-start | bytes 294912 | tf_op jit(solution)/shard_map/all_to_all | solution.py:172
  34.6 5.7 %collective-permute-start.5 = (f32[64,128]{1,0:T(8,128)}, f32[64,128]{1,0:T(8,128)}, u32[]{:S(2)}, u32[]{:S(2)}) collective-permute-start(f32[64,128]{1,0:T(8,128)} %get-tuple-element.167), channel_id=1, source_target_pairs={{0,16},{1,17},{2,18},{3,19},{4,20},{5,21},{6,22},{7,23},{8,24},{9,... | collective-permute-start | bytes 98312 | tf_op jit(solution)/shard_map/ppermute | solution.py:169
  40.3 2.2 copy-done.183
  43.6 7.8 %prepare_stiff.1 = (bf16[1024,1024]{1,0:T(8,128)(2,1)S(1)}, bf16[1024,1024]{1,0:T(8,128)(2,1)S(1)}, bf16[384,1024]{1,0:T(8,128)(2,1)S(1)}, bf16[384,1024]{1,0:T(...) custom-call(f32[1,1024,1024]{2,1,0:T(8,128)S(1)} %copy-done.183, ...), custom_call_target="tpu_custom_call" | custom-call | flops 3221225472 | bytes 10485760 | tf_op jit(solution)/shard_map/prepare_stiff/pallas_call | solution.py:112
  56.4 1.7 copy.17
  58.1 1.8 copy.18
  59.9 1.8 reshape.25
  61.7 1.7 copy.19.refs_4_
  63.4 1.6 copy-done.1
  65.0 1.6 copy-done.6
  80.0 4.5 %collective-permute-start.8 = (f32[64,128]{1,0:T(8,128)S(1)}, f32[64,128]{1,0:T(8,128)S(1)}, u32[]{:S(2)}, u32[]{:S(2)}) collective-permute-start(f32[64,128]{1,0:T(8,128)S(1)} %get-tuple-element.182), channel_id=1, source_target_pairs={{0,16},{1,17},{2,18},{3,19},{4,20},{5,21},{6,22},{7,23},{8,24},{9,... | collective-permute-start | bytes 98312 | tf_op jit(solution)/shard_map/ppermute | solution.py:169
  84.4 1.6 copy-done.15
  86.0 1.6 copy-done.19
  93.7 3.5 %all-to-all-start.1 = ((f32[32,1,1152]{2,1,0:T(1,128)}), f32[32,1,1152]{2,1,0:T(1,128)}, u32[]{:S(2)}, u32[]{:S(2)}) async-start(f32[32,1,1152]{2,1,0:T(1,128)} %copy.20), calls=%async_computation.1 | async-start | bytes 294912 | tf_op jit(solution)/shard_map/all_to_all | solution.py:172
  97.9 6.3 %collective-permute-start.11 = (f32[64,128]{1,0:T(8,128)}, f32[64,128]{1,0:T(8,128)S(1)}, u32[]{:S(2)}, u32[]{:S(2)}) collective-permute-start(f32[64,128]{1,0:T(8,128)} %copy-done.186), channel_id=1, source_target_pairs={{0,16},{1,17},{2,18},{3,19},{4,20},{5,21},{6,22},{7,23},{8,24},{9,... | collective-permute-start | bytes 98312 | tf_op jit(solution)/shard_map/ppermute | solution.py:169
  104.2 1.6 copy-done.2
  105.8 1.6 copy-done.7
  119.7 4.3 %collective-permute-start.14 = (f32[64,128]{1,0:T(8,128)S(1)}, f32[64,128]{1,0:T(8,128)S(1)}, u32[]{:S(2)}, u32[]{:S(2)}) collective-permute-start(f32[64,128]{1,0:T(8,128)S(1)} %get-tuple-element.206), channel_id=1, source_target_pairs={{0,16},{1,17},{2,18},{3,19},{4,20},{5,21},{6,22},{7,23},{8,24},{9,... | collective-permute-start | bytes 98312 | tf_op jit(solution)/shard_map/ppermute | solution.py:169
  133.1 1.9 copy-done.20
  140.4 3.3 %all-to-all-start.2 = ((f32[32,1,1152]{2,1,0:T(1,128)}), f32[32,1,1152]{2,1,0:T(1,128)}, u32[]{:S(2)}, u32[]{:S(2)}) async-start(f32[32,1,1152]{2,1,0:T(1,128)} %copy.22), calls=%async_computation.2 | async-start | bytes 294912 | tf_op jit(solution)/shard_map/all_to_all | solution.py:172
  144.5 6.3 %collective-permute-start.17 = (f32[64,128]{1,0:T(8,128)}, f32[64,128]{1,0:T(8,128)S(1)}, u32[]{:S(2)}, u32[]{:S(2)}) collective-permute-start(f32[64,128]{1,0:T(8,128)} %copy-done.187), channel_id=1, source_target_pairs={{0,16},{1,17},{2,18},{3,19},{4,20},{5,21},{6,22},{7,23},{8,24},{9,... | collective-permute-start | bytes 98312 | tf_op jit(solution)/shard_map/ppermute | solution.py:169
  150.8 1.6 copy-done.3
  152.4 1.6 copy-done.8
  166.2 4.4 %collective-permute-start.20 = (f32[64,128]{1,0:T(8,128)S(1)}, f32[64,128]{1,0:T(8,128)S(1)}, u32[]{:S(2)}, u32[]{:S(2)}) collective-permute-start(f32[64,128]{1,0:T(8,128)S(1)} %get-tuple-element.237), channel_id=1, source_target_pairs={{0,16},{1,17},{2,18},{3,19},{4,20},{5,21},{6,22},{7,23},{8,24},{9,... | collective-permute-start | bytes 98312 | tf_op jit(solution)/shard_map/ppermute | solution.py:169
  182.5 3.3 %all-to-all-start.3 = ((f32[32,1,1152]{2,1,0:T(1,128)}), f32[32,1,1152]{2,1,0:T(1,128)}, u32[]{:S(2)}, u32[]{:S(2)}) async-start(f32[32,1,1152]{2,1,0:T(1,128)} %copy.24), calls=%async_computation.3 | async-start | bytes 294912 | tf_op jit(solution)/shard_map/all_to_all | solution.py:172
  186.8 6.3 %collective-permute-start.23 = (f32[64,128]{1,0:T(8,128)}, f32[64,128]{1,0:T(8,128)S(1)}, u32[]{:S(2)}, u32[]{:S(2)}) collective-permute-start(f32[64,128]{1,0:T(8,128)} %get-tuple-element.244), channel_id=1, source_target_pairs={{0,16},{1,17},{2,18},{3,19},{4,20},{5,21},{6,22},{7,23},{8,24},{9,... | collective-permute-start | bytes 98312 | tf_op jit(solution)/shard_map/ppermute | solution.py:169
  193.1 1.6 copy-done.4
  207.8 4.4 %collective-permute-start.26 = (f32[64,128]{1,0:T(8,128)S(1)}, f32[64,128]{1,0:T(8,128)S(1)}, u32[]{:S(2)}, u32[]{:S(2)}) collective-permute-start(f32[64,128]{1,0:T(8,128)S(1)} %get-tuple-element.271), channel_id=1, source_target_pairs={{0,16},{1,17},{2,18},{3,19},{4,20},{5,21},{6,22},{7,23},{8,24},{9,... | collective-permute-start | bytes 98312 | tf_op jit(solution)/shard_map/ppermute | solution.py:169
  221.1 9.9 %all_to_all.52 = f32[32,1,128]{2,1,0:T(1,128)S(1)} all-to-all(f32[32,1,128]{2,1,0:T(1,128)S(1)} %broadcast_in_dim.19), channel_id=1, replica_groups=mesh['sub'=32] {'sub'}, dimensions={0} | all-to-all | bytes 32768 | tf_op jit(solution)/shard_map/all_to_all | solution.py:172
  (467 shorter events, 113.8 us)
Async XLA Ops:
  5.9 20.5 %collective-permute-start = (f32[144,128]{1,0:T(8,128)S(1)}, f32[144,128]{1,0:T(8,128)S(1)}, u32[]{:S(2)}, u32[]{:S(2)}) collective-permute-start(f32[144,128]{1,0:T(8,128)S(1)} %get-tuple-element.152), channel_id=1, source_target_pairs={{0,1},{2,3},{4,5},{6,7},{8,9},{10,11},{12,13},{14,15},{16,17},{18,... | collective-permute-start | bytes 221192 | tf_op jit(solution)/shard_map/ppermute | solution.py:169
  6.4 20.6 %collective-permute-start.1 = (f32[144,128]{1,0:T(8,128)S(1)}, f32[144,128]{1,0:T(8,128)S(1)}, u32[]{:S(2)}, u32[]{:S(2)}) collective-permute-start(f32[144,128]{1,0:T(8,128)S(1)} %get-tuple-element.153), channel_id=1, source_target_pairs={{1,2},{3,4},{5,6},{7,8},{9,10},{11,12},{13,14},{15,16},{17,18},{19... | collective-permute-start | bytes 221192 | tf_op jit(solution)/shard_map/ppermute | solution.py:169
  7.1 20.0 %collective-permute-start.2 = (f32[144,128]{1,0:T(8,128)S(1)}, f32[144,128]{1,0:T(8,128)S(1)}, u32[]{:S(2)}, u32[]{:S(2)}) collective-permute-start(f32[144,128]{1,0:T(8,128)S(1)} %get-tuple-element.154), channel_id=1, source_target_pairs={{0,16},{1,17},{2,18},{3,19},{4,20},{5,21},{6,22},{7,23},{8,24},{9,... | collective-permute-start | bytes 221192 | tf_op jit(solution)/shard_map/ppermute | solution.py:169
  27.0 24.4 %copy-start.94 = (f32[64,128]{1,0:T(8,128)}, f32[64,128]{1,0:T(8,128)S(1)}, u32[]{:S(2)}) copy-start(f32[64,128]{1,0:T(8,128)S(1)} %slice.13.refs_12_.refs_6_) | copy-start | bytes 98308
  29.9 42.4 %all-to-all-start = ((f32[32,1,1152]{2,1,0:T(1,128)}), f32[32,1,1152]{2,1,0:T(1,128)}, u32[]{:S(2)}, u32[]{:S(2)}) async-start(f32[32,1,1152]{2,1,0:T(1,128)} %copy.16), calls=%async_computation | async-start | bytes 294912 | tf_op jit(solution)/shard_map/all_to_all | solution.py:172
  33.2 35.5 %collective-permute-start.3 = (f32[64,128]{1,0:T(8,128)}, f32[64,128]{1,0:T(8,128)}, u32[]{:S(2)}, u32[]{:S(2)}) collective-permute-start(f32[64,128]{1,0:T(8,128)} %get-tuple-element.165), channel_id=1, source_target_pairs={{0,1},{2,3},{4,5},{6,7},{8,9},{10,11},{12,13},{14,15},{16,17},{18,... | collective-permute-start | bytes 98312 | tf_op jit(solution)/shard_map/ppermute | solution.py:169
  33.3 35.4 %collective-permute-start.4 = (f32[64,128]{1,0:T(8,128)}, f32[64,128]{1,0:T(8,128)}, u32[]{:S(2)}, u32[]{:S(2)}) collective-permute-start(f32[64,128]{1,0:T(8,128)} %get-tuple-element.166), channel_id=1, source_target_pairs={{1,2},{3,4},{5,6},{7,8},{9,10},{11,12},{13,14},{15,16},{17,18},{19... | collective-permute-start | bytes 98312 | tf_op jit(solution)/shard_map/ppermute | solution.py:169
  34.6 34.2 %collective-permute-start.5 = (f32[64,128]{1,0:T(8,128)}, f32[64,128]{1,0:T(8,128)}, u32[]{:S(2)}, u32[]{:S(2)}) collective-permute-start(f32[64,128]{1,0:T(8,128)} %get-tuple-element.167), channel_id=1, source_target_pairs={{0,16},{1,17},{2,18},{3,19},{4,20},{5,21},{6,22},{7,23},{8,24},{9,... | collective-permute-start | bytes 98312 | tf_op jit(solution)/shard_map/ppermute | solution.py:169
  79.3 10.9 %collective-permute-start.6 = (f32[64,128]{1,0:T(8,128)S(1)}, f32[64,128]{1,0:T(8,128)S(1)}, u32[]{:S(2)}, u32[]{:S(2)}) collective-permute-start(f32[64,128]{1,0:T(8,128)S(1)} %get-tuple-element.180), channel_id=1, source_target_pairs={{0,1},{2,3},{4,5},{6,7},{8,9},{10,11},{12,13},{14,15},{16,17},{18,... | collective-permute-start | bytes 98312 | tf_op jit(solution)/shard_map/ppermute | solution.py:169
  79.3 10.9 %collective-permute-start.7 = (f32[64,128]{1,0:T(8,128)S(1)}, f32[64,128]{1,0:T(8,128)S(1)}, u32[]{:S(2)}, u32[]{:S(2)}) collective-permute-start(f32[64,128]{1,0:T(8,128)S(1)} %get-tuple-element.181), channel_id=1, source_target_pairs={{1,2},{3,4},{5,6},{7,8},{9,10},{11,12},{13,14},{15,16},{17,18},{19... | collective-permute-start | bytes 98312 | tf_op jit(solution)/shard_map/ppermute | solution.py:169
  80.0 10.3 %collective-permute-start.8 = (f32[64,128]{1,0:T(8,128)S(1)}, f32[64,128]{1,0:T(8,128)S(1)}, u32[]{:S(2)}, u32[]{:S(2)}) collective-permute-start(f32[64,128]{1,0:T(8,128)S(1)} %get-tuple-element.182), channel_id=1, source_target_pairs={{0,16},{1,17},{2,18},{3,19},{4,20},{5,21},{6,22},{7,23},{8,24},{9,... | collective-permute-start | bytes 98312 | tf_op jit(solution)/shard_map/ppermute | solution.py:169
  93.7 18.7 %all-to-all-start.1 = ((f32[32,1,1152]{2,1,0:T(1,128)}), f32[32,1,1152]{2,1,0:T(1,128)}, u32[]{:S(2)}, u32[]{:S(2)}) async-start(f32[32,1,1152]{2,1,0:T(1,128)} %copy.20), calls=%async_computation.1 | async-start | bytes 294912 | tf_op jit(solution)/shard_map/all_to_all | solution.py:172
  97.1 12.5 %collective-permute-start.9 = (f32[64,128]{1,0:T(8,128)}, f32[64,128]{1,0:T(8,128)S(1)}, u32[]{:S(2)}, u32[]{:S(2)}) collective-permute-start(f32[64,128]{1,0:T(8,128)} %copy-done.190), channel_id=1, source_target_pairs={{0,1},{2,3},{4,5},{6,7},{8,9},{10,11},{12,13},{14,15},{16,17},{18,... | collective-permute-start | bytes 98312 | tf_op jit(solution)/shard_map/ppermute | solution.py:169
  97.2 12.4 %collective-permute-start.10 = (f32[64,128]{1,0:T(8,128)}, f32[64,128]{1,0:T(8,128)S(1)}, u32[]{:S(2)}, u32[]{:S(2)}) collective-permute-start(f32[64,128]{1,0:T(8,128)} %copy-done.188), channel_id=1, source_target_pairs={{1,2},{3,4},{5,6},{7,8},{9,10},{11,12},{13,14},{15,16},{17,18},{19... | collective-permute-start | bytes 98312 | tf_op jit(solution)/shard_map/ppermute | solution.py:169
  97.9 11.7 %collective-permute-start.11 = (f32[64,128]{1,0:T(8,128)}, f32[64,128]{1,0:T(8,128)S(1)}, u32[]{:S(2)}, u32[]{:S(2)}) collective-permute-start(f32[64,128]{1,0:T(8,128)} %copy-done.186), channel_id=1, source_target_pairs={{0,16},{1,17},{2,18},{3,19},{4,20},{5,21},{6,22},{7,23},{8,24},{9,... | collective-permute-start | bytes 98312 | tf_op jit(solution)/shard_map/ppermute | solution.py:169
  118.8 17.6 %collective-permute-start.12 = (f32[64,128]{1,0:T(8,128)S(1)}, f32[64,128]{1,0:T(8,128)S(1)}, u32[]{:S(2)}, u32[]{:S(2)}) collective-permute-start(f32[64,128]{1,0:T(8,128)S(1)} %get-tuple-element.204), channel_id=1, source_target_pairs={{0,1},{2,3},{4,5},{6,7},{8,9},{10,11},{12,13},{14,15},{16,17},{18,... | collective-permute-start | bytes 98312 | tf_op jit(solution)/shard_map/ppermute | solution.py:169
  118.9 17.5 %collective-permute-start.13 = (f32[64,128]{1,0:T(8,128)S(1)}, f32[64,128]{1,0:T(8,128)S(1)}, u32[]{:S(2)}, u32[]{:S(2)}) collective-permute-start(f32[64,128]{1,0:T(8,128)S(1)} %get-tuple-element.205), channel_id=1, source_target_pairs={{1,2},{3,4},{5,6},{7,8},{9,10},{11,12},{13,14},{15,16},{17,18},{19... | collective-permute-start | bytes 98312 | tf_op jit(solution)/shard_map/ppermute | solution.py:169
  119.7 16.7 %collective-permute-start.14 = (f32[64,128]{1,0:T(8,128)S(1)}, f32[64,128]{1,0:T(8,128)S(1)}, u32[]{:S(2)}, u32[]{:S(2)}) collective-permute-start(f32[64,128]{1,0:T(8,128)S(1)} %get-tuple-element.206), channel_id=1, source_target_pairs={{0,16},{1,17},{2,18},{3,19},{4,20},{5,21},{6,22},{7,23},{8,24},{9,... | collective-permute-start | bytes 98312 | tf_op jit(solution)/shard_map/ppermute | solution.py:169
  140.4 18.6 %all-to-all-start.2 = ((f32[32,1,1152]{2,1,0:T(1,128)}), f32[32,1,1152]{2,1,0:T(1,128)}, u32[]{:S(2)}, u32[]{:S(2)}) async-start(f32[32,1,1152]{2,1,0:T(1,128)} %copy.22), calls=%async_computation.2 | async-start | bytes 294912 | tf_op jit(solution)/shard_map/all_to_all | solution.py:172
  143.7 12.5 %collective-permute-start.15 = (f32[64,128]{1,0:T(8,128)}, f32[64,128]{1,0:T(8,128)S(1)}, u32[]{:S(2)}, u32[]{:S(2)}) collective-permute-start(f32[64,128]{1,0:T(8,128)} %copy-done.191), channel_id=1, source_target_pairs={{0,1},{2,3},{4,5},{6,7},{8,9},{10,11},{12,13},{14,15},{16,17},{18,... | collective-permute-start | bytes 98312 | tf_op jit(solution)/shard_map/ppermute | solution.py:169
  143.9 12.3 %collective-permute-start.16 = (f32[64,128]{1,0:T(8,128)}, f32[64,128]{1,0:T(8,128)S(1)}, u32[]{:S(2)}, u32[]{:S(2)}) collective-permute-start(f32[64,128]{1,0:T(8,128)} %copy-done.189), channel_id=1, source_target_pairs={{1,2},{3,4},{5,6},{7,8},{9,10},{11,12},{13,14},{15,16},{17,18},{19... | collective-permute-start | bytes 98312 | tf_op jit(solution)/shard_map/ppermute | solution.py:169
  144.5 11.7 %collective-permute-start.17 = (f32[64,128]{1,0:T(8,128)}, f32[64,128]{1,0:T(8,128)S(1)}, u32[]{:S(2)}, u32[]{:S(2)}) collective-permute-start(f32[64,128]{1,0:T(8,128)} %copy-done.187), channel_id=1, source_target_pairs={{0,16},{1,17},{2,18},{3,19},{4,20},{5,21},{6,22},{7,23},{8,24},{9,... | collective-permute-start | bytes 98312 | tf_op jit(solution)/shard_map/ppermute | solution.py:169
  165.4 14.2 %collective-permute-start.18 = (f32[64,128]{1,0:T(8,128)S(1)}, f32[64,128]{1,0:T(8,128)S(1)}, u32[]{:S(2)}, u32[]{:S(2)}) collective-permute-start(f32[64,128]{1,0:T(8,128)S(1)} %get-tuple-element.235), channel_id=1, source_target_pairs={{0,1},{2,3},{4,5},{6,7},{8,9},{10,11},{12,13},{14,15},{16,17},{18,... | collective-permute-start | bytes 98312 | tf_op jit(solution)/shard_map/ppermute | solution.py:169
  165.5 14.2 %collective-permute-start.19 = (f32[64,128]{1,0:T(8,128)S(1)}, f32[64,128]{1,0:T(8,128)S(1)}, u32[]{:S(2)}, u32[]{:S(2)}) collective-permute-start(f32[64,128]{1,0:T(8,128)S(1)} %get-tuple-element.236), channel_id=1, source_target_pairs={{1,2},{3,4},{5,6},{7,8},{9,10},{11,12},{13,14},{15,16},{17,18},{19... | collective-permute-start | bytes 98312 | tf_op jit(solution)/shard_map/ppermute | solution.py:169
  166.2 13.5 %collective-permute-start.20 = (f32[64,128]{1,0:T(8,128)S(1)}, f32[64,128]{1,0:T(8,128)S(1)}, u32[]{:S(2)}, u32[]{:S(2)}) collective-permute-start(f32[64,128]{1,0:T(8,128)S(1)} %get-tuple-element.237), channel_id=1, source_target_pairs={{0,16},{1,17},{2,18},{3,19},{4,20},{5,21},{6,22},{7,23},{8,24},{9,... | collective-permute-start | bytes 98312 | tf_op jit(solution)/shard_map/ppermute | solution.py:169
  182.5 19.9 %all-to-all-start.3 = ((f32[32,1,1152]{2,1,0:T(1,128)}), f32[32,1,1152]{2,1,0:T(1,128)}, u32[]{:S(2)}, u32[]{:S(2)}) async-start(f32[32,1,1152]{2,1,0:T(1,128)} %copy.24), calls=%async_computation.3 | async-start | bytes 294912 | tf_op jit(solution)/shard_map/all_to_all | solution.py:172
  185.8 13.9 %collective-permute-start.21 = (f32[64,128]{1,0:T(8,128)}, f32[64,128]{1,0:T(8,128)S(1)}, u32[]{:S(2)}, u32[]{:S(2)}) collective-permute-start(f32[64,128]{1,0:T(8,128)} %get-tuple-element.242), channel_id=1, source_target_pairs={{0,1},{2,3},{4,5},{6,7},{8,9},{10,11},{12,13},{14,15},{16,17},{18,... | collective-permute-start | bytes 98312 | tf_op jit(solution)/shard_map/ppermute | solution.py:169
  185.9 13.7 %collective-permute-start.22 = (f32[64,128]{1,0:T(8,128)}, f32[64,128]{1,0:T(8,128)S(1)}, u32[]{:S(2)}, u32[]{:S(2)}) collective-permute-start(f32[64,128]{1,0:T(8,128)} %get-tuple-element.243), channel_id=1, source_target_pairs={{1,2},{3,4},{5,6},{7,8},{9,10},{11,12},{13,14},{15,16},{17,18},{19... | collective-permute-start | bytes 98312 | tf_op jit(solution)/shard_map/ppermute | solution.py:169
  186.8 12.9 %collective-permute-start.23 = (f32[64,128]{1,0:T(8,128)}, f32[64,128]{1,0:T(8,128)S(1)}, u32[]{:S(2)}, u32[]{:S(2)}) collective-permute-start(f32[64,128]{1,0:T(8,128)} %get-tuple-element.244), channel_id=1, source_target_pairs={{0,16},{1,17},{2,18},{3,19},{4,20},{5,21},{6,22},{7,23},{8,24},{9,... | collective-permute-start | bytes 98312 | tf_op jit(solution)/shard_map/ppermute | solution.py:169
  207.0 24.0 %collective-permute-start.24 = (f32[64,128]{1,0:T(8,128)S(1)}, f32[64,128]{1,0:T(8,128)S(1)}, u32[]{:S(2)}, u32[]{:S(2)}) collective-permute-start(f32[64,128]{1,0:T(8,128)S(1)} %get-tuple-element.269), channel_id=1, source_target_pairs={{0,1},{2,3},{4,5},{6,7},{8,9},{10,11},{12,13},{14,15},{16,17},{18,... | collective-permute-start | bytes 98312 | tf_op jit(solution)/shard_map/ppermute | solution.py:169
  207.1 24.0 %collective-permute-start.25 = (f32[64,128]{1,0:T(8,128)S(1)}, f32[64,128]{1,0:T(8,128)S(1)}, u32[]{:S(2)}, u32[]{:S(2)}) collective-permute-start(f32[64,128]{1,0:T(8,128)S(1)} %get-tuple-element.270), channel_id=1, source_target_pairs={{1,2},{3,4},{5,6},{7,8},{9,10},{11,12},{13,14},{15,16},{17,18},{19... | collective-permute-start | bytes 98312 | tf_op jit(solution)/shard_map/ppermute | solution.py:169
  207.8 23.3 %collective-permute-start.26 = (f32[64,128]{1,0:T(8,128)S(1)}, f32[64,128]{1,0:T(8,128)S(1)}, u32[]{:S(2)}, u32[]{:S(2)}) collective-permute-start(f32[64,128]{1,0:T(8,128)S(1)} %get-tuple-element.271), channel_id=1, source_target_pairs={{0,16},{1,17},{2,18},{3,19},{4,20},{5,21},{6,22},{7,23},{8,24},{9,... | collective-permute-start | bytes 98312 | tf_op jit(solution)/shard_map/ppermute | solution.py:169
  (191 other events, 675.2 us)

commit v4 on v0

v4 whole, which is shorter than its diff:
```python
from types import SimpleNamespace

import jax
import jax.numpy as jnp
import numpy as np
from jax import lax
from jax.experimental import pallas as pl
from jax.experimental.pallas import tpu as pltpu
from jax.sharding import PartitionSpec as P

CYCLE = 16
ITERS = 4

BF = jnp.bfloat16
F32 = jnp.float32
NN = ((1,), (0,))
NT = ((1,), (1,))
STAGE_BYTES = 12 * 1024 * 1024
TILES = 8
AXIS = "sub"


def contract(left, right, dims=NN):
    return lax.dot_general(left, right, (dims, ((), ())), preferred_element_type=F32)


def split(value):
    high = value.astype(BF)
    return high, (value - high.astype(F32)).astype(BF)


def times(value, high, low, dims=NN):
    rows = value.shape[0]
    top, rest = split(value)
    both = contract(jnp.concatenate([top, rest], axis=0), high, dims)
    return both[:rows] + both[rows:] + contract(top, low, dims)


def pick(value, onehot, dims=NN):
    rows = value.shape[0]
    top, rest = split(value)
    last = (value - top.astype(F32) - rest.astype(F32)).astype(BF)
    parts = contract(jnp.concatenate([top, rest, last], axis=0), onehot, dims)
    return parts[:rows] + (parts[rows:2 * rows] + parts[2 * rows:])


def diagonal(count):
    first = lax.broadcasted_iota(jnp.int32, (count, count), 0)
    return first == lax.broadcasted_iota(jnp.int32, (count, count), 1)


def to_column(row):
    count = row.shape[1]
    return jnp.sum(jnp.where(diagonal(count), jnp.broadcast_to(row, (count, count)), 0), axis=1, keepdims=True)


def to_row(column):
    count = column.shape[0]
    return jnp.sum(jnp.where(diagonal(count), jnp.broadcast_to(column, (count, count)), 0), axis=0, keepdims=True)


def dot(left, right):
    return jnp.sum(left * right, axis=1, keepdims=True)


def flat(tree):
    names = [(name, len(held) if isinstance(held, list) else 0) for name, held in tree.items()]
    entries = []
    for held in tree.values():
        entries += held if isinstance(held, list) else [held]
    return names, entries


def named(names, entries):
    space, at = SimpleNamespace(), 0
    for name, count in names:
        setattr(space, name, list(entries[at:at + count]) if count else entries[at])
        at += max(count, 1)
    return space


def stage(name, body, ins, outs):
    in_names, arrays = flat(ins)
    out_names, kinds = flat(outs)

    def kernel(*refs):
        body(named(in_names, refs[:len(arrays)]), named(out_names, refs[len(arrays):]))

    whole = pl.BlockSpec(memory_space=pltpu.VMEM)
    made = pl.pallas_call(
        kernel,
        name=name,
        out_shape=[jax.ShapeDtypeStruct(*kind) for kind in kinds],
        in_specs=[whole] * len(arrays),
        out_specs=[whole] * len(kinds),
        compiler_params=pltpu.CompilerParams(vmem_limit_bytes=STAGE_BYTES),
    )(*arrays)
    return named(out_names, made)


def swaps(total):
    sets = []
    for by in (1, CYCLE):
        for parity in (0, 1):
            ahead = [i for i in range(total - by) if (i // by) % 2 == parity]
            sets.append((by, parity, [(i, i + by) for i in ahead] + [(i + by, i) for i in ahead]))
    return sets


def rounds_of(total):
    bits = total.bit_length() - 1
    assert total == 1 << bits
    rounds = []
    while bits:
        take = 1 if bits % 2 else 2
        low = 1 << (bits - take)
        rounds.append([low * i for i in range(1, 1 << take)])
        bits -= take
    places = [0]
    for distances in rounds:
        places = [place ^ far for far in [0] + distances for place in places]
    return rounds, places


def local(stiffness, neumann_inv, coarse_basis, coarse_inv, loads, face_index, face_len):
    total = lax.axis_size(AXIS)
    _, cases, ndof = loads.shape
    primal = coarse_basis.shape[1]
    width = face_index.shape[2]
    known = coarse_inv.shape[1]
    half = primal // 2
    lines_a_block = half + 1
    reps = known // width
    rounds, places = rounds_of(total)

    chosen = []
    for by, parity, pairs in swaps(total):
        if pairs:
            behind, ahead = (0, 1) if by == 1 else (2, 3)
            chosen.append((pairs, behind, ahead, by, parity))
    blocks = len(chosen)
    slots = blocks * width
    own_rows = (blocks + 1) * primal

    vec = ((cases, ndof), F32)
    faces = ((cases, slots), F32)
    pair = ((1, 2 * cases), F32)
    block_kind = ((lines_a_block, 2 * cases), F32)
    face_kinds = [((cases, width), F32)] * blocks
    blocked = [slice(i * width, (i + 1) * width) for i in range(blocks)]
    strips = [slice(i * ndof // TILES, (i + 1) * ndof // TILES) for i in range(TILES)]

    def joined(refs, rows=slice(None)):
        return jnp.concatenate([ref[rows] for ref in refs], axis=1)

    def put_faces(refs, value):
        for i, ref in enumerate(refs):
            ref[...] = value[:, blocked[i]]

    def exchange(arrays):
        return [lax.ppermute(array, AXIS, chosen[i][0]) for i, array in enumerate(arrays)]

    def gather(block):
        for at, distances in enumerate(rounds):
            pieces = [block] + [lax.ppermute(block, AXIS, [(i, i ^ far) for i in range(total)]) for far in distances]
            if at + 1 == len(rounds):
                return pieces

            def join(i, o):
                o.block[...] = jnp.concatenate([ref[...] for ref in i.pieces], axis=0)

            rows, lanes = block.shape
            block = stage("join", join, dict(pieces=pieces), dict(block=((rows * len(pieces), lanes), F32))).block

    def both_sums(pieces, stride):
        rows = []
        for piece in pieces:
            count = piece.shape[0] // stride
            rows += [piece[i * stride + stride - 1:(i + 1) * stride] for i in range(count)]
        while len(rows) > 1:
            rows = [rows[i] + rows[i + 1] for i in range(0, len(rows), 2)]
        return rows[0]

    def as_columns(row):
        return to_column(row[:, :cases]), to_column(row[:, cases:])

    def first(i, o):
        me = lax.axis_index(AXIS)
        index, lengths = i.index[0], i.lengths[...]
        lane = lax.broadcasted_iota(jnp.int32, (1, width), 1)
        rows = []
        for _, behind, ahead, by, parity in chosen:
            forward = (me // by) % 2 == parity
            row = jnp.where(forward, index[ahead:ahead + 1], index[behind:behind + 1])
            length = jnp.where(forward, lengths[:, ahead:ahead + 1], lengths[:, behind:behind + 1])
            rows.append(jnp.where(lane < length, row, -1))
        row = jnp.concatenate(rows, axis=1)
        unpicker = (lax.broadcasted_iota(jnp.int32, (ndof, slots), 0) == row).astype(F32).astype(BF)
        picker = (lax.broadcasted_iota(jnp.int32, (slots, ndof), 1) == to_column(row)).astype(F32)
        weight = 1.0 / (1.0 + jnp.sum(picker, axis=0, keepdims=True))
        weighted = i.basis[0] * weight
        at_slots = pick(jnp.concatenate([i.load[0], weighted], axis=0), unpicker)
        inv = i.inv[...]
        inv_packed = jnp.concatenate([inv[:, j * width:(j + 1) * width] for j in range(reps)], axis=0)
        put_faces(o.face, jnp.concatenate([at_slots, jnp.concatenate([inv_packed] * blocks, axis=1)], axis=0))
        o.picker[...] = picker.astype(BF)
        o.unpicker[...] = unpicker
        o.weight[...] = weight
        o.weighted[...] = weighted
        o.basis_slots[...] = at_slots[cases:]

    packed = ((cases + primal + reps * primal, width), F32)
    start = stage(
        "first", first,
        dict(lengths=face_len, index=face_index, basis=coarse_basis, load=loads, inv=coarse_inv),
        dict(face=[packed] * blocks, picker=((slots, ndof), BF), unpicker=((ndof, slots), BF), weight=((1, ndof), F32),
             weighted=((primal, ndof), F32), basis_slots=((primal, slots), F32)))
    weight, picker, unpicker = start.weight, start.picker, start.unpicker
    came = exchange(start.face)

    part_kinds = [((ndof, ndof), BF)] * 2 + [((slots, ndof), BF)] * 2 + [((slots, slots), BF)] * 2

    def prepare(name, matrix):
        def body(i, o):
            for strip in strips:
                o.parts[0][strip], o.parts[1][strip] = split(i.matrix[0, strip])
            for at in range(2):
                face = contract(i.picker[...], o.parts[at][...]).astype(BF)
                o.parts[2 + at][...] = face
                o.parts[4 + at][...] = contract(face, i.unpicker[...]).astype(BF)

        return stage(name, body, dict(matrix=matrix, picker=picker, unpicker=unpicker), dict(parts=part_kinds)).parts

    inv = prepare("prepare_inv", neumann_inv)
    stiff = prepare("prepare_stiff", stiffness)

    own_kinds = dict(lines=((primal, cases), F32), inner_faces=faces, inner=vec)

    def solve_own(part, i, o):
        scaled = part * i.weight[...]
        o.lines[...] = times(i.weighted[...], *split(part), NT)
        o.inner_faces[...] = times(scaled, i.inv[2][...], i.inv[3][...], NT)
        o.inner[...] = times(scaled, i.inv[0][...], i.inv[1][...])

    def solve_loads(i, o):
        solve_own(i.load[0], i, o)

    own = stage("solve_loads", solve_loads, dict(load=loads, weight=weight, weighted=start.weighted, inv=inv[:4]), own_kinds)

    def reach(i, o):
        functions, rows = [i.weighted[...]], [i.inv[...]]
        for j in range(blocks):
            part = i.came[j][...]
            functions.append(pick(part[cases:cases + primal], i.picker[blocked[j]]))
            rest = part[cases + primal:]
            rows.append(jnp.concatenate([rest[k * primal:(k + 1) * primal] for k in range(reps)], axis=1))
        functions = jnp.concatenate(functions, axis=0)
        rows = jnp.concatenate(rows, axis=0)
        image = times(functions, i.stiff[0][...], i.stiff[1][...])
        image_faces = times(functions, i.stiff[2][...], i.stiff[3][...], NT)
        o.reach[0][...], o.reach[1][...] = split(jnp.concatenate([functions, image, image_faces], axis=1))
        me = lax.axis_index(AXIS)
        count = i.place.shape[1]
        for upper in range(2):
            for at in range(0, count, 256):
                lanes = slice(at, min(at + 256, count))
                device, line = i.place[:, lanes] ^ me, i.line[:, lanes]
                source = jnp.where(line < half, device * primal + upper * half + line, -1)
                move = lax.broadcasted_iota(jnp.int32, (known, lanes.stop - at), 0) == source
                o.rows[upper * own_rows:(upper + 1) * own_rows, lanes] = pick(rows, move.astype(F32).astype(BF))

    place = jnp.asarray(np.repeat(np.array(places, np.int32), lines_a_block)[None])
    line = jnp.asarray(np.tile(np.arange(lines_a_block, dtype=np.int32), total)[None])
    wide = 2 * ndof + slots
    reached = stage(
        "reach", reach,
        dict(weighted=start.weighted, inv=coarse_inv, came=came, picker=picker, stiff=stiff[:4], place=place, line=line),
        dict(reach=[((own_rows, wide), BF)] * 2, rows=((2 * own_rows, total * lines_a_block), F32)))

    def to_solve(came, own, coef=None, sums=None):
        def body(i, o):
            arrived = joined(i.came, slice(0, cases))
            if coef is not None:
                arrived = to_column(i.coef[:, cases:]) * -arrived
            lines = i.lines[...] + times(i.basis_slots[...], *split(arrived), NT)
            o.block[:half] = jnp.concatenate([lines[:half], lines[half:]], axis=1)
            o.block[half:] = i.sums[...] if sums is not None else jnp.zeros((1, 2 * cases), F32)
            put_faces(o.face, 0.5 * (i.inner_faces[...] + times(0.5 * arrived, i.inv[0][...], i.inv[1][...])))

        ins = dict(came=came, basis_slots=start.basis_slots, lines=own.lines, inner_faces=own.inner_faces, inv=inv[4:])
        if coef is not None:
            ins.update(coef=coef)
        if sums is not None:
            ins.update(sums=sums)
        made = stage("solve_rest", body, ins, dict(block=block_kind, face=face_kinds))
        return gather(made.block), exchange(made.face)

    def to_apply(step, came, own, state, coef):
        def body(i, o):
            arrived = joined(i.came, slice(0, cases))
            if step == 0:
                o.residual[...] = i.load[0] + pick(arrived, i.picker[...])
            else:
                if step > 1:
                    o.z[...] = i.z_part[...] + pick(arrived, i.picker[...])
                    arrived = to_column(i.coef[:, cases:]) * -arrived
                o.w[...] = i.w_part[...] + pick(arrived, i.picker[...])
            inner = i.weight[...] * (i.inner[...] + times(0.5 * arrived, i.inv[0][...], i.inv[1][...]))
            o.v[...] = inner
            o.image_faces[...] = times(inner, i.stiff[2][...], i.stiff[3][...], NT)
            o.image[...] = times(inner, i.stiff[0][...], i.stiff[1][...])

        ins = dict(came=came, picker=picker, weight=weight, inner=own.inner, inv=inv[2:4], stiff=stiff[:4])
        outs = dict(v=vec, image_faces=faces, image=vec)
        if step == 0:
            ins.update(load=loads)
            outs.update(residual=vec)
        else:
            ins.update(w_part=state.w_part)
            outs.update(w=vec)
        if step > 1:
            ins.update(z_part=state.z_part, coef=coef)
            outs.update(z=vec)
        return stage("apply_own", body, ins, outs)

    def apply_rest(i, o):
        rows = jnp.concatenate([ref[...] for ref in i.everyone], axis=0)
        product = times(i.rows[...], *split(rows))
        factors = (product[:own_rows, :cases] + product[own_rows:, cases:]).T
        extra = times(factors, i.reach[0][...], i.reach[1][...])
        arrived = joined(i.came)
        put_faces(o.face, i.image_faces[...] + times(arrived, i.stiff[2][...], i.stiff[3][...]) + extra[:, 2 * ndof:])
        o.inner[...] = i.v[...] + extra[:, :ndof]
        o.image[...] = i.image[...] + extra[:, ndof:2 * ndof]
        o.sums[...] = both_sums([ref[...] for ref in i.everyone], lines_a_block)

    state = SimpleNamespace()
    came_image, coef, sums = came, None, None
    for step in range(ITERS):
        final = step + 1 == ITERS
        everyone, came_solve = to_solve(came_image, own, coef, sums)
        applied = to_apply(step, came_image, own, state, coef)
        vars(state).update(vars(applied))
        made = stage(
            "apply_rest", apply_rest,
            dict(everyone=everyone, rows=reached.rows, reach=reached.reach, came=came_solve, stiff=stiff[2:],
                 image_faces=state.image_faces, v=state.v, image=state.image),
            dict(face=face_kinds, inner=vec, image=vec, sums=pair))
        came_image = exchange(made.face)

        def update(i, o, step=step, final=final):
            arrived = joined(i.came)
            inner = i.inner[...] + pick(arrived, i.picker[...])
            image = i.image[...] + times(arrived, i.stiff[0][...], i.stiff[1][...])
            weight = i.weight[...]
            if step == 0:
                part, u, residual = image, inner, i.residual[...]
                delta = dot(image, u)
            else:
                both = i.both[...]
                gamma, delta = as_columns(both)
                w = i.w[...]
                if step == 1:
                    alpha = gamma / delta
                    q, s, p = inner, w, i.u[...]
                    x = alpha * p
                    before = w
                else:
                    gamma_old, alpha_old = as_columns(i.coef[...])
                    beta = gamma / gamma_old
                    alpha = gamma / (delta - beta * gamma / alpha_old)
                    q = inner + beta * i.q[...]
                    s = w + beta * i.s[...]
                    p = i.u[...] + beta * i.p[...]
                    x = i.x[...] + alpha * p
                    before = w - (alpha * beta) * i.z[...]
                residual = i.residual[...] - alpha * s
                u = i.u[...] - alpha * q
                part = before - alpha * image
                delta = dot(weight * before - alpha * image, u)
                o.coef[...] = jnp.concatenate([both[:, :cases], to_row(alpha)], axis=1)
                o.s[...], o.p[...], o.x[...], o.residual[...], o.q[...] = s, p, x, residual, q
                o.z_part[...] = image if step == 1 else image + beta * i.z[...]
            o.u[...] = u
            o.w_part[...] = part
            o.sums[...] = jnp.concatenate([to_row(dot(weight * residual, u)), to_row(delta)], axis=1)
            if not final:
                solve_own(part, i, o)

        ins = dict(came=came_solve, picker=picker, inner=made.inner, image=made.image, stiff=stiff[2:4], weight=weight, residual=state.residual)
        outs = dict(u=vec, w_part=vec, sums=pair)
        if step > 0:
            ins.update(both=made.sums, w=state.w, u=state.u)
            outs.update(coef=pair, s=vec, p=vec, x=vec, residual=vec, q=vec, z_part=vec)
        if step > 1:
            ins.update(coef=coef, q=state.q, s=state.s, p=state.p, x=state.x, z=state.z)
        if not final:
            ins.update(weighted=start.weighted, inv=inv[:4])
            outs.update(own_kinds)
        own = stage("update", update, ins, outs)
        vars(state).update(vars(own))
        sums = own.sums
        if step > 0:
            coef = own.coef

    def finish(i, o):
        gamma_old, alpha_old = as_columns(i.coef[...])
        w = i.w_part[...] - alpha_old * pick(joined(i.came), i.picker[...])
        gamma, delta = as_columns(both_sums([ref[...] for ref in i.everyone], 1))
        beta = gamma / gamma_old
        alpha = gamma / (delta - beta * gamma / alpha_old)
        o.solution[0] = i.x[...] + alpha * (i.u[...] + beta * i.p[...])
        o.remainder[0] = i.residual[...] - alpha * (w + beta * i.s[...])

    whole = ((1, cases, ndof), F32)
    made = stage(
        "finish", finish,
        dict(everyone=gather(sums), came=came_image, picker=picker, coef=coef, w_part=state.w_part, x=state.x, u=state.u, p=state.p,
             residual=state.residual, s=state.s),
        dict(solution=whole, remainder=whole))
    return made.solution, made.remainder


def solution(mesh):
    placed = (
        P(AXIS, None, None),
        P(AXIS, None, None),
        P(AXIS, None, None),
        P(AXIS, None),
        P(AXIS, None, None),
        P(AXIS, None, None),
        P(AXIS, None),
    )
    return jax.shard_map(
        local,
        mesh=mesh,
        in_specs=placed,
        out_specs=(P(AXIS, None, None), P(AXIS, None, None)),
        check_vma=False,
    )
```

time: 572 us -> 164 us (0.29); the launches traced: 563 us -> 164 us
  blocking collectives: 332 us -> 0 us
  matrix products: 58 us -> 0 us
  other arithmetic: 44.9 us -> 0 us
  Pallas kernels: 0 us -> 32.4 us
  waiting for transfers between devices: 13.9 us -> 36.2 us
  starting transfers between devices: 98.9 us -> 87.6 us
  local copies, waits for them, and re-layouts: 13.1 us -> 6.09 us
    all_gather x4 -> x0, blocking collectives: 168 us -> none  [local(): lax.all_gather(precond_coarse_res, 'sub', axis=0, tiled=True)]
    psum x4 -> x0, blocking collectives: 164 us -> none  [local(): lax.psum((inner(residual, precond_res), inner(image, precond_res)), 'sub')]
    dot_general x20 -> x0, matrix products: 58 us -> none  [the longest x4 33.9 us: local(): image = assemble(jnp.dot(precond_res, stiff, precision=HIGH))]
    scatter-add x10 -> x0, other arithmetic: 36.9 us -> none  [the longest x9 32.8 us: assemble(): return local_vals.at[:, face_slots].add(incoming)]
    pallas_call x0 -> x32, Pallas kernels: none -> 32.4 us  [stage(): pl.pallas_call(kernel, name=name, out_shape=[jax.ShapeDtypeStruct(*kind)...]
    ppermute x36 -> x62, waiting for transfers between devices: 13.9 us -> 36.2 us  [the longest x35 35.1 us: gather(): lax.ppermute(block, AXIS, [(i, i ^ far) for i in range(total)])]
    ppermute x36 -> x62, starting transfers between devices: 98.9 us -> 87.6 us  [the longest x27 53.1 us: exchange(): lax.ppermute(array, AXIS, chosen[i][0])]
    gather x9 -> x0, local copies, waits for them, and re-layouts: 9.33 us -> none  [assemble(): face_vals = jnp.take(local_vals, face_slots, axis=1) * live_slots[None, :]]
  transfers between devices with their start and end apart: 36 -> 62, of which waited for: 16 -> 25; matrix products, arithmetic and copies ran while one was open for 1% -> 0% of each run, Pallas kernels for 0% -> 15%
where the time goes in v4:
time: 164 us
  starting transfers between devices  87.6 us (53%)
  waiting for transfers between devices  36.2 us (22%)
  Pallas kernels  32.4 us (20%)
  local copies, waits for them, and re-layouts  6.09 us (4%)
    ppermute x27, starting transfers between devices, exchange(): lax.ppermute(array, AXIS, chosen[i][0])  53.1 us
    ppermute x35, waiting for transfers between devices, gather(): lax.ppermute(block, AXIS, [(i, i ^ far) for i in range(total)])  35.1 us
    ppermute x35, starting transfers between devices, gather(): lax.ppermute(block, AXIS, [(i, i ^ far) for i in range(total)])  34.5 us
    pallas_call x32, Pallas kernels, stage(): pl.pallas_call(kernel, name=name, out_shape=[jax.ShapeDtypeStruct(*kind)...  32.4 us
    unnamed x22, local copies, waits for them, and re-layouts  6.09 us
  transfers between devices with their start and end apart: 62, of which 25 were waited for; matrix products, arithmetic and copies ran while one was open for 0% of the time, Pallas kernels for 15%

profile of v4, /device:TPU:0, one launch (start us, length us, event | category | flops | bytes accessed | tf_op | source)
XLA Modules:
  0.0 163.6 jit_solution(13724194119083508008)
XLA Ops:
  6.7 7.3 %collective-permute-start.2 = (f32[144,128]{1,0:T(8,128)S(1)}, f32[144,128]{1,0:T(8,128)S(1)}, u32[]{:S(2)}, u32[]{:S(2)}) collective-permute-start(f32[144,128]{1,0:T(8,128)S(1)} %get-tuple-element.127), channel_id=1, source_target_pairs={{0,16},{1,17},{2,18},{3,19},{4,20},{5,21},{6,22},{7,23},{8,24},{9,... | collective-permute-start | bytes 221192 | tf_op jit(solution)/shard_map/ppermute | solution.py:161
  14.0 2.2 %copy-done = f32[1,1024,1024]{2,1,0:T(8,128)S(1)} copy-done((f32[1,1024,1024]{2,1,0:T(8,128)S(1)}, f32[1,1024,1024]{2,1,0:T(8,128)}, u32[]{:S(2)}) %copy-start) | copy-done | bytes 4194328
  16.2 2.7 %prepare_inv.1 = (bf16[1024,1024]{1,0:T(8,128)(2,1)S(1)}, bf16[1024,1024]{1,0:T(8,128)(2,1)S(1)}, bf16[384,1024]{1,0:T(8,128)(2,1)S(1)}, bf16[384,1024]{1,0:T(8,...) custom-call(f32[1,1024,1024]{2,1,0:T(8,128)S(1)} %copy-done, ...), custom_call_target="tpu_custom_call" | custom-call | tf_op jit(solution)/shard_map/prepare_inv/pallas_call | solution.py:90
  20.7 4.5 %collective-permute-done.3.refs_1_ = f32[9,128]{1,0:T(8,128)S(1)} collective-permute-done((f32[9,128]{1,0:T(8,128)S(1)}, f32[9,128]{1,0:T(8,128)S(1)}, u32[]{:S(2)}, u32[]{:S(2)}) %collective-permute-start.3) | collective-permute-done | bytes 4640 | tf_op jit(solution)/shard_map/ppermute | solution.py:165
  29.5 2.5 %collective-permute-done.6.refs_3_ = f32[18,128]{1,0:T(8,128)S(1)} collective-permute-done((f32[18,128]{1,0:T(8,128)S(1)}, f32[18,128]{1,0:T(8,128)S(1)}, u32[]{:S(2)}, u32[]{:S(2)}) %collective-permute-start.6) | collective-permute-done | bytes 9248 | tf_op jit(solution)/shard_map/ppermute | solution.py:165
  34.6 3.8 %collective-permute-start.12 = (f32[64,128]{1,0:T(8,128)S(1)}, f32[64,128]{1,0:T(8,128)S(1)}, u32[]{:S(2)}, u32[]{:S(2)}) collective-permute-start(f32[64,128]{1,0:T(8,128)S(1)} %get-tuple-element.151), channel_id=1, source_target_pairs={{0,16},{1,17},{2,18},{3,19},{4,20},{5,21},{6,22},{7,23},{8,24},{9,... | collective-permute-start | bytes 98312 | tf_op jit(solution)/shard_map/ppermute | solution.py:161
  38.3 2.7 %prepare_stiff.1 = (bf16[1024,1024]{1,0:T(8,128)(2,1)S(1)}, bf16[1024,1024]{1,0:T(8,128)(2,1)S(1)}, bf16[384,1024]{1,0:T(8,128)(2,1)S(1)}, bf16[384,1024]{1,0:T(...) custom-call(f32[1,1024,1024]{2,1,0:T(8,128)S(1)} %copy-done.1, ...), custom_call_target="tpu_custom_call" | custom-call | tf_op jit(solution)/shard_map/prepare_stiff/pallas_call | solution.py:90
  41.1 2.0 %apply_own.4 = (f32[64,1024]{1,0:T(8,128)S(1)}, f32[64,384]{1,0:T(8,128)S(1)}, f32[64,1024]{1,0:T(8,128)S(1)}, f32[64,1024]{1,0:T(8,128)S(1)}) custom-call(f32[144,128]{1,0:T(8,128)S(1)} %collective-permute-done.refs_0_.refs_2_, f32[144,128]{1,0:T(8,128)S(1)} %collective-permute-done.1.refs_1_.refs_3_, ...), custom_call_target="tpu_custom_call" | custom-call | tf_op jit(solution)/shard_map/apply_own/pallas_call | solution.py:90
  46.9 3.1 %collective-permute-start.15 = (f32[64,128]{1,0:T(8,128)S(1)}, f32[64,128]{1,0:T(8,128)S(1)}, u32[]{:S(2)}, u32[]{:S(2)}) collective-permute-start(f32[64,128]{1,0:T(8,128)S(1)} %get-tuple-element.160), channel_id=1, source_target_pairs={{0,16},{1,17},{2,18},{3,19},{4,20},{5,21},{6,22},{7,23},{8,24},{9,... | collective-permute-start | bytes 98312 | tf_op jit(solution)/shard_map/ppermute | solution.py:161
  50.1 2.2 %update.4 = (f32[64,1024]{1,0:T(8,128)S(1)}, f32[64,1024]{1,0:T(8,128)S(1)}, f32[1,128]{1,0:T(1,128)S(1)}, f32[16,64]{1,0:T(8,128)S(1)}, f32[64,384]{1,0:T(8,128)S(1)}, /*index=5*/f32[64,1024]{1,0:T(8,128)S(1)}) custom-call(f32[64,128]{1,0:T(8,128)S(1)} %collective-permute-done.10.refs_7_.refs_0_, f32[64,128]{1,0:T(8,128)S(1)} %collective-permute-done.11.refs_8_.refs_1_, ...), custom_call_target="tpu_custom_call" | custom-call | tf_op jit(solution)/shard_map/update/pallas_call | solution.py:90
  53.8 1.7 %collective-permute-start.16 = (f32[9,128]{1,0:T(8,128)S(1)}, f32[9,128]{1,0:T(8,128)S(1)}, u32[]{:S(2)}, u32[]{:S(2)}) collective-permute-start(f32[9,128]{1,0:T(8,128)S(1)} %get-tuple-element.167.refs_0_), channel_id=1, source_target_pairs={{0,16},{1,17},{2,18},{3,19},{4,20},{5,21},{6,22},{7,23},{8,24},{9,... | collective-permute-start | bytes 13832 | tf_op jit(solution)/shard_map/ppermute | solution.py:165
  55.5 2.9 %collective-permute-done.16.refs_1_ = f32[9,128]{1,0:T(8,128)S(1)} collective-permute-done((f32[9,128]{1,0:T(8,128)S(1)}, f32[9,128]{1,0:T(8,128)S(1)}, u32[]{:S(2)}, u32[]{:S(2)}) %collective-permute-start.16) | collective-permute-done | bytes 4640 | tf_op jit(solution)/shard_map/ppermute | solution.py:165
  67.5 5.4 %collective-permute-start.25 = (f32[64,128]{1,0:T(8,128)S(1)}, f32[64,128]{1,0:T(8,128)S(1)}, u32[]{:S(2)}, u32[]{:S(2)}) collective-permute-start(f32[64,128]{1,0:T(8,128)S(1)} %get-tuple-element.170), channel_id=1, source_target_pairs={{0,16},{1,17},{2,18},{3,19},{4,20},{5,21},{6,22},{7,23},{8,24},{9,... | collective-permute-start | bytes 98312 | tf_op jit(solution)/shard_map/ppermute | solution.py:161
  73.0 2.0 %apply_own.5 = (f32[64,1024]{1,0:T(8,128)S(1)}, f32[64,384]{1,0:T(8,128)S(1)}, f32[64,1024]{1,0:T(8,128)S(1)}, f32[64,1024]{1,0:T(8,128)S(1)}) custom-call(f32[64,128]{1,0:T(8,128)S(1)} %collective-permute-done.13.refs_0_, f32[64,128]{1,0:T(8,128)S(1)} %collective-permute-done.14.refs_1_, f32[64,128]{1,0:T(8,128)S(1)} %collective-permute-done.15.refs_2_, ...), custom_call_target="tpu_custom_call" | custom-call | tf_op jit(solution)/shard_map/apply_own/pallas_call | solution.py:90
  76.7 4.8 %collective-permute-start.28 = (f32[64,128]{1,0:T(8,128)S(1)}, f32[64,128]{1,0:T(8,128)S(1)}, u32[]{:S(2)}, u32[]{:S(2)}) collective-permute-start(f32[64,128]{1,0:T(8,128)S(1)} %get-tuple-element.178), channel_id=1, source_target_pairs={{0,16},{1,17},{2,18},{3,19},{4,20},{5,21},{6,22},{7,23},{8,24},{9,... | collective-permute-start | bytes 98312 | tf_op jit(solution)/shard_map/ppermute | solution.py:161
  81.5 2.3 %update.5 = (f32[64,1024]{1,0:T(8,128)S(1)}, f32[64,1024]{1,0:T(8,128)S(1)}, f32[1,128]{1,0:T(1,128)S(1)}, f32[1,128]{1,0:T(1,128)S(1)}, f32[64,1024]{1,0:T(8,12...) custom-call(f32[64,128]{1,0:T(8,128)S(1)} %collective-permute-done.2, ...), custom_call_target="tpu_custom_call" | custom-call | tf_op jit(solution)/shard_map/update/pallas_call | solution.py:90
  84.9 2.0 %collective-permute-start.29 = (f32[9,128]{1,0:T(8,128)S(1)}, f32[9,128]{1,0:T(8,128)S(1)}, u32[]{:S(2)}, u32[]{:S(2)}) collective-permute-start(f32[9,128]{1,0:T(8,128)S(1)} %get-tuple-element.188.refs_0_), channel_id=1, source_target_pairs={{0,16},{1,17},{2,18},{3,19},{4,20},{5,21},{6,22},{7,23},{8,24},{9,... | collective-permute-start | bytes 13832 | tf_op jit(solution)/shard_map/ppermute | solution.py:165
  86.9 2.6 %collective-permute-done.29.refs_1_ = f32[9,128]{1,0:T(8,128)S(1)} collective-permute-done((f32[9,128]{1,0:T(8,128)S(1)}, f32[9,128]{1,0:T(8,128)S(1)}, u32[]{:S(2)}, u32[]{:S(2)}) %collective-permute-start.29) | collective-permute-done | bytes 4640 | tf_op jit(solution)/shard_map/ppermute | solution.py:165
  94.3 2.1 %collective-permute-done.32.refs_3_ = f32[18,128]{1,0:T(8,128)S(1)} collective-permute-done((f32[18,128]{1,0:T(8,128)S(1)}, f32[18,128]{1,0:T(8,128)S(1)}, u32[]{:S(2)}, u32[]{:S(2)}) %collective-permute-start.32) | collective-permute-done | bytes 9248 | tf_op jit(solution)/shard_map/ppermute | solution.py:165
  96.4 1.9 %collective-permute-start.34 = (f32[72,128]{1,0:T(8,128)S(1)}, f32[72,128]{1,0:T(8,128)S(1)}, u32[]{:S(2)}, u32[]{:S(2)}) collective-permute-start(f32[72,128]{1,0:T(8,128)S(1)} %join.15.refs_0_), channel_id=1, source_target_pairs={{0,2},{1,3},{2,0},{3,1},{4,6},{5,7},{6,4},{7,5},{8,10},{9,11},{10,... | collective-permute-start | bytes 110600 | tf_op jit(solution)/shard_map/ppermute | solution.py:165
  99.1 4.4 %collective-permute-start.38 = (f32[64,128]{1,0:T(8,128)S(1)}, f32[64,128]{1,0:T(8,128)S(1)}, u32[]{:S(2)}, u32[]{:S(2)}) collective-permute-start(f32[64,128]{1,0:T(8,128)S(1)} %get-tuple-element.191), channel_id=1, source_target_pairs={{0,16},{1,17},{2,18},{3,19},{4,20},{5,21},{6,22},{7,23},{8,24},{9,... | collective-permute-start | bytes 98312 | tf_op jit(solution)/shard_map/ppermute | solution.py:161
  103.5 2.2 %apply_own.6 = (f32[64,1024]{1,0:T(8,128)S(1)}, f32[64,384]{1,0:T(8,128)S(1)}, f32[64,1024]{1,0:T(8,128)S(1)}, f32[64,1024]{1,0:T(8,128)S(1)}, f32[64,1024]{1,0:T(8,128)S(1)}) custom-call(f32[64,128]{1,0:T(8,128)S(1)} %collective-permute-done.26.refs_0_, f32[64,128]{1,0:T(8,128)S(1)} %collective-permute-done.27.refs_1_, ...), custom_call_target="tpu_custom_call" | custom-call | tf_op jit(solution)/shard_map/apply_own/pallas_call | solution.py:90
  107.7 5.6 %collective-permute-start.41 = (f32[64,128]{1,0:T(8,128)S(1)}, f32[64,128]{1,0:T(8,128)S(1)}, u32[]{:S(2)}, u32[]{:S(2)}) collective-permute-start(f32[64,128]{1,0:T(8,128)S(1)} %get-tuple-element.200), channel_id=1, source_target_pairs={{0,16},{1,17},{2,18},{3,19},{4,20},{5,21},{6,22},{7,23},{8,24},{9,... | collective-permute-start | bytes 98312 | tf_op jit(solution)/shard_map/ppermute | solution.py:161
  113.4 2.3 %update.6 = (f32[64,1024]{1,0:T(8,128)S(1)}, f32[64,1024]{1,0:T(8,128)S(1)}, f32[1,128]{1,0:T(1,128)S(1)}, f32[1,128]{1,0:T(1,128)S(1)}, f32[64,1024]{1,0:T(8,12...) custom-call(f32[64,128]{1,0:T(8,128)S(1)} %collective-permute-done.3, ...), custom_call_target="tpu_custom_call" | custom-call | tf_op jit(solution)/shard_map/update/pallas_call | solution.py:90
  116.5 2.2 %collective-permute-start.45 = (f32[9,128]{1,0:T(8,128)S(1)}, f32[9,128]{1,0:T(8,128)S(1)}, u32[]{:S(2)}, u32[]{:S(2)}) collective-permute-start(f32[9,128]{1,0:T(8,128)S(1)} %get-tuple-element.219.refs_0_), channel_id=1, source_target_pairs={{0,16},{1,17},{2,18},{3,19},{4,20},{5,21},{6,22},{7,23},{8,24},{9,... | collective-permute-start | bytes 13832 | tf_op jit(solution)/shard_map/ppermute | solution.py:165
  118.7 2.4 %collective-permute-done.45.refs_1_ = f32[9,128]{1,0:T(8,128)S(1)} collective-permute-done((f32[9,128]{1,0:T(8,128)S(1)}, f32[9,128]{1,0:T(8,128)S(1)}, u32[]{:S(2)}, u32[]{:S(2)}) %collective-permute-start.45) | collective-permute-done | bytes 4640 | tf_op jit(solution)/shard_map/ppermute | solution.py:165
  130.3 5.1 %collective-permute-start.44 = (f32[64,128]{1,0:T(8,128)S(1)}, f32[64,128]{1,0:T(8,128)S(1)}, u32[]{:S(2)}, u32[]{:S(2)}) collective-permute-start(f32[64,128]{1,0:T(8,128)S(1)} %get-tuple-element.218), channel_id=1, source_target_pairs={{0,16},{1,17},{2,18},{3,19},{4,20},{5,21},{6,22},{7,23},{8,24},{9,... | collective-permute-start | bytes 98312 | tf_op jit(solution)/shard_map/ppermute | solution.py:161
  135.4 2.2 %apply_own.7 = (f32[64,1024]{1,0:T(8,128)S(1)}, f32[64,384]{1,0:T(8,128)S(1)}, f32[64,1024]{1,0:T(8,128)S(1)}, f32[64,1024]{1,0:T(8,128)S(1)}, f32[64,1024]{1,0:T(8,128)S(1)}) custom-call(f32[64,128]{1,0:T(8,128)S(1)} %collective-permute-done.39.refs_0_, f32[64,128]{1,0:T(8,128)S(1)} %collective-permute-done.40.refs_1_, ...), custom_call_target="tpu_custom_call" | custom-call | tf_op jit(solution)/shard_map/apply_own/pallas_call | solution.py:90
  139.3 4.8 %collective-permute-start.61 = (f32[64,128]{1,0:T(8,128)S(1)}, f32[64,128]{1,0:T(8,128)S(1)}, u32[]{:S(2)}, u32[]{:S(2)}) collective-permute-start(f32[64,128]{1,0:T(8,128)S(1)} %get-tuple-element.240), channel_id=1, source_target_pairs={{0,16},{1,17},{2,18},{3,19},{4,20},{5,21},{6,22},{7,23},{8,24},{9,... | collective-permute-start | bytes 98312 | tf_op jit(solution)/shard_map/ppermute | solution.py:161
  145.7 4.4 %collective-permute-done.52.refs_1_ = f32[1,128]{1,0:T(1,128)S(1)} collective-permute-done((f32[1,128]{1,0:T(1,128)S(1)}, f32[1,128]{1,0:T(1,128)S(1)}, u32[]{:S(2)}, u32[]{:S(2)}) %collective-permute-start.52) | collective-permute-done | bytes 544 | tf_op jit(solution)/shard_map/ppermute | solution.py:165
  153.7 2.1 %collective-permute-start.55 = (f32[2,128]{1,0:T(2,128)S(1)}, f32[2,128]{1,0:T(2,128)S(1)}, u32[]{:S(2)}, u32[]{:S(2)}) collective-permute-start(f32[2,128]{1,0:T(2,128)S(1)} %join.18.refs_0_), channel_id=1, source_target_pairs={{0,12},{1,13},{2,14},{3,15},{4,8},{5,9},{6,10},{7,11},{8,4},{9,5},... | collective-permute-start | bytes 3080 | tf_op jit(solution)/shard_map/ppermute | solution.py:165
  155.8 2.4 %collective-permute-done.55.refs_3_ = f32[2,128]{1,0:T(2,128)S(1)} collective-permute-done((f32[2,128]{1,0:T(2,128)S(1)}, f32[2,128]{1,0:T(2,128)S(1)}, u32[]{:S(2)}, u32[]{:S(2)}) %collective-permute-start.55) | collective-permute-done | bytes 1056 | tf_op jit(solution)/shard_map/ppermute | solution.py:165
  (146 shorter events, 61.5 us)
Async XLA Ops:
  5.5 14.7 %collective-permute-start = (f32[144,128]{1,0:T(8,128)S(1)}, f32[144,128]{1,0:T(8,128)S(1)}, u32[]{:S(2)}, u32[]{:S(2)}) collective-permute-start(f32[144,128]{1,0:T(8,128)S(1)} %get-tuple-element.125), channel_id=1, source_target_pairs={{0,1},{2,3},{4,5},{6,7},{8,9},{10,11},{12,13},{14,15},{16,17},{18,... | collective-permute-start | bytes 221192 | tf_op jit(solution)/shard_map/ppermute | solution.py:161
  6.0 14.2 %collective-permute-start.1 = (f32[144,128]{1,0:T(8,128)S(1)}, f32[144,128]{1,0:T(8,128)S(1)}, u32[]{:S(2)}, u32[]{:S(2)}) collective-permute-start(f32[144,128]{1,0:T(8,128)S(1)} %get-tuple-element.126), channel_id=1, source_target_pairs={{1,2},{3,4},{5,6},{7,8},{9,10},{11,12},{13,14},{15,16},{17,18},{19... | collective-permute-start | bytes 221192 | tf_op jit(solution)/shard_map/ppermute | solution.py:161
  6.7 13.6 %collective-permute-start.2 = (f32[144,128]{1,0:T(8,128)S(1)}, f32[144,128]{1,0:T(8,128)S(1)}, u32[]{:S(2)}, u32[]{:S(2)}) collective-permute-start(f32[144,128]{1,0:T(8,128)S(1)} %get-tuple-element.127), channel_id=1, source_target_pairs={{0,16},{1,17},{2,18},{3,19},{4,20},{5,21},{6,22},{7,23},{8,24},{9,... | collective-permute-start | bytes 221192 | tf_op jit(solution)/shard_map/ppermute | solution.py:161
  20.5 14.0 %collective-permute-start.10 = (f32[64,128]{1,0:T(8,128)S(1)}, f32[64,128]{1,0:T(8,128)S(1)}, u32[]{:S(2)}, u32[]{:S(2)}) collective-permute-start(f32[64,128]{1,0:T(8,128)S(1)} %get-tuple-element.149), channel_id=1, source_target_pairs={{0,1},{2,3},{4,5},{6,7},{8,9},{10,11},{12,13},{14,15},{16,17},{18,... | collective-permute-start | bytes 98312 | tf_op jit(solution)/shard_map/ppermute | solution.py:161
  32.0 12.7 %collective-permute-start.7 = (f32[72,128]{1,0:T(8,128)S(1)}, f32[72,128]{1,0:T(8,128)S(1)}, u32[]{:S(2)}, u32[]{:S(2)}) collective-permute-start(f32[72,128]{1,0:T(8,128)S(1)} %join.11.refs_0_), channel_id=1, source_target_pairs={{0,1},{1,0},{2,3},{3,2},{4,5},{5,4},{6,7},{7,6},{8,9},{9,8},{10,11... | collective-permute-start | bytes 110600 | tf_op jit(solution)/shard_map/ppermute | solution.py:165
  32.0 12.7 %collective-permute-start.8 = (f32[72,128]{1,0:T(8,128)S(1)}, f32[72,128]{1,0:T(8,128)S(1)}, u32[]{:S(2)}, u32[]{:S(2)}) collective-permute-start(f32[72,128]{1,0:T(8,128)S(1)} %join.11.refs_0_), channel_id=1, source_target_pairs={{0,2},{1,3},{2,0},{3,1},{4,6},{5,7},{6,4},{7,5},{8,10},{9,11},{10,... | collective-permute-start | bytes 110600 | tf_op jit(solution)/shard_map/ppermute | solution.py:165
  32.7 12.1 %collective-permute-start.9 = (f32[72,128]{1,0:T(8,128)S(1)}, f32[72,128]{1,0:T(8,128)S(1)}, u32[]{:S(2)}, u32[]{:S(2)}) collective-permute-start(f32[72,128]{1,0:T(8,128)S(1)} %join.11.refs_0_), channel_id=1, source_target_pairs={{0,3},{1,2},{2,1},{3,0},{4,7},{5,6},{6,5},{7,4},{8,11},{9,10},{10,... | collective-permute-start | bytes 110600 | tf_op jit(solution)/shard_map/ppermute | solution.py:165
  33.9 10.8 %collective-permute-start.11 = (f32[64,128]{1,0:T(8,128)S(1)}, f32[64,128]{1,0:T(8,128)S(1)}, u32[]{:S(2)}, u32[]{:S(2)}) collective-permute-start(f32[64,128]{1,0:T(8,128)S(1)} %get-tuple-element.150), channel_id=1, source_target_pairs={{1,2},{3,4},{5,6},{7,8},{9,10},{11,12},{13,14},{15,16},{17,18},{19... | collective-permute-start | bytes 98312 | tf_op jit(solution)/shard_map/ppermute | solution.py:161
  34.6 10.2 %collective-permute-start.12 = (f32[64,128]{1,0:T(8,128)S(1)}, f32[64,128]{1,0:T(8,128)S(1)}, u32[]{:S(2)}, u32[]{:S(2)}) collective-permute-start(f32[64,128]{1,0:T(8,128)S(1)} %get-tuple-element.151), channel_id=1, source_target_pairs={{0,16},{1,17},{2,18},{3,19},{4,20},{5,21},{6,22},{7,23},{8,24},{9,... | collective-permute-start | bytes 98312 | tf_op jit(solution)/shard_map/ppermute | solution.py:161
  52.6 14.9 %collective-permute-start.23 = (f32[64,128]{1,0:T(8,128)S(1)}, f32[64,128]{1,0:T(8,128)S(1)}, u32[]{:S(2)}, u32[]{:S(2)}) collective-permute-start(f32[64,128]{1,0:T(8,128)S(1)} %get-tuple-element.168), channel_id=1, source_target_pairs={{0,1},{2,3},{4,5},{6,7},{8,9},{10,11},{12,13},{14,15},{16,17},{18,... | collective-permute-start | bytes 98312 | tf_op jit(solution)/shard_map/ppermute | solution.py:161
  65.0 10.1 %collective-permute-start.20 = (f32[72,128]{1,0:T(8,128)S(1)}, f32[72,128]{1,0:T(8,128)S(1)}, u32[]{:S(2)}, u32[]{:S(2)}) collective-permute-start(f32[72,128]{1,0:T(8,128)S(1)} %join.13.refs_0_), channel_id=1, source_target_pairs={{0,1},{1,0},{2,3},{3,2},{4,5},{5,4},{6,7},{7,6},{8,9},{9,8},{10,11... | collective-permute-start | bytes 110600 | tf_op jit(solution)/shard_map/ppermute | solution.py:165
  65.0 10.1 %collective-permute-start.21 = (f32[72,128]{1,0:T(8,128)S(1)}, f32[72,128]{1,0:T(8,128)S(1)}, u32[]{:S(2)}, u32[]{:S(2)}) collective-permute-start(f32[72,128]{1,0:T(8,128)S(1)} %join.13.refs_0_), channel_id=1, source_target_pairs={{0,2},{1,3},{2,0},{3,1},{4,6},{5,7},{6,4},{7,5},{8,10},{9,11},{10,... | collective-permute-start | bytes 110600 | tf_op jit(solution)/shard_map/ppermute | solution.py:165
  66.3 8.8 %collective-permute-start.22 = (f32[72,128]{1,0:T(8,128)S(1)}, f32[72,128]{1,0:T(8,128)S(1)}, u32[]{:S(2)}, u32[]{:S(2)}) collective-permute-start(f32[72,128]{1,0:T(8,128)S(1)} %join.13.refs_0_), channel_id=1, source_target_pairs={{0,3},{1,2},{2,1},{3,0},{4,7},{5,6},{6,5},{7,4},{8,11},{9,10},{10,... | collective-permute-start | bytes 110600 | tf_op jit(solution)/shard_map/ppermute | solution.py:165
  66.8 8.1 %collective-permute-start.24 = (f32[64,128]{1,0:T(8,128)S(1)}, f32[64,128]{1,0:T(8,128)S(1)}, u32[]{:S(2)}, u32[]{:S(2)}) collective-permute-start(f32[64,128]{1,0:T(8,128)S(1)} %get-tuple-element.169), channel_id=1, source_target_pairs={{1,2},{3,4},{5,6},{7,8},{9,10},{11,12},{13,14},{15,16},{17,18},{19... | collective-permute-start | bytes 98312 | tf_op jit(solution)/shard_map/ppermute | solution.py:161
  67.5 7.6 %collective-permute-start.25 = (f32[64,128]{1,0:T(8,128)S(1)}, f32[64,128]{1,0:T(8,128)S(1)}, u32[]{:S(2)}, u32[]{:S(2)}) collective-permute-start(f32[64,128]{1,0:T(8,128)S(1)} %get-tuple-element.170), channel_id=1, source_target_pairs={{0,16},{1,17},{2,18},{3,19},{4,20},{5,21},{6,22},{7,23},{8,24},{9,... | collective-permute-start | bytes 98312 | tf_op jit(solution)/shard_map/ppermute | solution.py:161
  76.0 7.9 %collective-permute-start.26 = (f32[64,128]{1,0:T(8,128)S(1)}, f32[64,128]{1,0:T(8,128)S(1)}, u32[]{:S(2)}, u32[]{:S(2)}) collective-permute-start(f32[64,128]{1,0:T(8,128)S(1)} %get-tuple-element.176), channel_id=1, source_target_pairs={{0,1},{2,3},{4,5},{6,7},{8,9},{10,11},{12,13},{14,15},{16,17},{18,... | collective-permute-start | bytes 98312 | tf_op jit(solution)/shard_map/ppermute | solution.py:161
  76.1 7.8 %collective-permute-start.27 = (f32[64,128]{1,0:T(8,128)S(1)}, f32[64,128]{1,0:T(8,128)S(1)}, u32[]{:S(2)}, u32[]{:S(2)}) collective-permute-start(f32[64,128]{1,0:T(8,128)S(1)} %get-tuple-element.177), channel_id=1, source_target_pairs={{1,2},{3,4},{5,6},{7,8},{9,10},{11,12},{13,14},{15,16},{17,18},{19... | collective-permute-start | bytes 98312 | tf_op jit(solution)/shard_map/ppermute | solution.py:161
  76.7 7.7 %collective-permute-start.28 = (f32[64,128]{1,0:T(8,128)S(1)}, f32[64,128]{1,0:T(8,128)S(1)}, u32[]{:S(2)}, u32[]{:S(2)}) collective-permute-start(f32[64,128]{1,0:T(8,128)S(1)} %get-tuple-element.178), channel_id=1, source_target_pairs={{0,16},{1,17},{2,18},{3,19},{4,20},{5,21},{6,22},{7,23},{8,24},{9,... | collective-permute-start | bytes 98312 | tf_op jit(solution)/shard_map/ppermute | solution.py:161
  84.8 14.3 %collective-permute-start.36 = (f32[64,128]{1,0:T(8,128)S(1)}, f32[64,128]{1,0:T(8,128)S(1)}, u32[]{:S(2)}, u32[]{:S(2)}) collective-permute-start(f32[64,128]{1,0:T(8,128)S(1)} %get-tuple-element.189), channel_id=1, source_target_pairs={{0,1},{2,3},{4,5},{6,7},{8,9},{10,11},{12,13},{14,15},{16,17},{18,... | collective-permute-start | bytes 98312 | tf_op jit(solution)/shard_map/ppermute | solution.py:161
  96.4 9.3 %collective-permute-start.33 = (f32[72,128]{1,0:T(8,128)S(1)}, f32[72,128]{1,0:T(8,128)S(1)}, u32[]{:S(2)}, u32[]{:S(2)}) collective-permute-start(f32[72,128]{1,0:T(8,128)S(1)} %join.15.refs_0_), channel_id=1, source_target_pairs={{0,1},{1,0},{2,3},{3,2},{4,5},{5,4},{6,7},{7,6},{8,9},{9,8},{10,11... | collective-permute-start | bytes 110600 | tf_op jit(solution)/shard_map/ppermute | solution.py:165
  96.4 9.3 %collective-permute-start.34 = (f32[72,128]{1,0:T(8,128)S(1)}, f32[72,128]{1,0:T(8,128)S(1)}, u32[]{:S(2)}, u32[]{:S(2)}) collective-permute-start(f32[72,128]{1,0:T(8,128)S(1)} %join.15.refs_0_), channel_id=1, source_target_pairs={{0,2},{1,3},{2,0},{3,1},{4,6},{5,7},{6,4},{7,5},{8,10},{9,11},{10,... | collective-permute-start | bytes 110600 | tf_op jit(solution)/shard_map/ppermute | solution.py:165
  106.6 9.1 %collective-permute-start.39 = (f32[64,128]{1,0:T(8,128)S(1)}, f32[64,128]{1,0:T(8,128)S(1)}, u32[]{:S(2)}, u32[]{:S(2)}) collective-permute-start(f32[64,128]{1,0:T(8,128)S(1)} %get-tuple-element.198), channel_id=1, source_target_pairs={{0,1},{2,3},{4,5},{6,7},{8,9},{10,11},{12,13},{14,15},{16,17},{18,... | collective-permute-start | bytes 98312 | tf_op jit(solution)/shard_map/ppermute | solution.py:161
  106.8 8.9 %collective-permute-start.40 = (f32[64,128]{1,0:T(8,128)S(1)}, f32[64,128]{1,0:T(8,128)S(1)}, u32[]{:S(2)}, u32[]{:S(2)}) collective-permute-start(f32[64,128]{1,0:T(8,128)S(1)} %get-tuple-element.199), channel_id=1, source_target_pairs={{1,2},{3,4},{5,6},{7,8},{9,10},{11,12},{13,14},{15,16},{17,18},{19... | collective-permute-start | bytes 98312 | tf_op jit(solution)/shard_map/ppermute | solution.py:161
  107.7 8.3 %collective-permute-start.41 = (f32[64,128]{1,0:T(8,128)S(1)}, f32[64,128]{1,0:T(8,128)S(1)}, u32[]{:S(2)}, u32[]{:S(2)}) collective-permute-start(f32[64,128]{1,0:T(8,128)S(1)} %get-tuple-element.200), channel_id=1, source_target_pairs={{0,16},{1,17},{2,18},{3,19},{4,20},{5,21},{6,22},{7,23},{8,24},{9,... | collective-permute-start | bytes 98312 | tf_op jit(solution)/shard_map/ppermute | solution.py:161
  116.4 13.9 %collective-permute-start.42 = (f32[64,128]{1,0:T(8,128)S(1)}, f32[64,128]{1,0:T(8,128)S(1)}, u32[]{:S(2)}, u32[]{:S(2)}) collective-permute-start(f32[64,128]{1,0:T(8,128)S(1)} %get-tuple-element.216), channel_id=1, source_target_pairs={{0,1},{2,3},{4,5},{6,7},{8,9},{10,11},{12,13},{14,15},{16,17},{18,... | collective-permute-start | bytes 98312 | tf_op jit(solution)/shard_map/ppermute | solution.py:161
  127.8 9.9 %collective-permute-start.49 = (f32[72,128]{1,0:T(8,128)S(1)}, f32[72,128]{1,0:T(8,128)S(1)}, u32[]{:S(2)}, u32[]{:S(2)}) collective-permute-start(f32[72,128]{1,0:T(8,128)S(1)} %join.17.refs_0_), channel_id=1, source_target_pairs={{0,1},{1,0},{2,3},{3,2},{4,5},{5,4},{6,7},{7,6},{8,9},{9,8},{10,11... | collective-permute-start | bytes 110600 | tf_op jit(solution)/shard_map/ppermute | solution.py:165
  127.8 9.9 %collective-permute-start.50 = (f32[72,128]{1,0:T(8,128)S(1)}, f32[72,128]{1,0:T(8,128)S(1)}, u32[]{:S(2)}, u32[]{:S(2)}) collective-permute-start(f32[72,128]{1,0:T(8,128)S(1)} %join.17.refs_0_), channel_id=1, source_target_pairs={{0,2},{1,3},{2,0},{3,1},{4,6},{5,7},{6,4},{7,5},{8,10},{9,11},{10,... | collective-permute-start | bytes 110600 | tf_op jit(solution)/shard_map/ppermute | solution.py:165
  129.3 8.4 %collective-permute-start.51 = (f32[72,128]{1,0:T(8,128)S(1)}, f32[72,128]{1,0:T(8,128)S(1)}, u32[]{:S(2)}, u32[]{:S(2)}) collective-permute-start(f32[72,128]{1,0:T(8,128)S(1)} %join.17.refs_0_), channel_id=1, source_target_pairs={{0,3},{1,2},{2,1},{3,0},{4,7},{5,6},{6,5},{7,4},{8,11},{9,10},{10,... | collective-permute-start | bytes 110600 | tf_op jit(solution)/shard_map/ppermute | solution.py:165
  129.6 8.0 %collective-permute-start.43 = (f32[64,128]{1,0:T(8,128)S(1)}, f32[64,128]{1,0:T(8,128)S(1)}, u32[]{:S(2)}, u32[]{:S(2)}) collective-permute-start(f32[64,128]{1,0:T(8,128)S(1)} %get-tuple-element.217), channel_id=1, source_target_pairs={{1,2},{3,4},{5,6},{7,8},{9,10},{11,12},{13,14},{15,16},{17,18},{19... | collective-permute-start | bytes 98312 | tf_op jit(solution)/shard_map/ppermute | solution.py:161
  138.6 23.8 %collective-permute-start.59 = (f32[64,128]{1,0:T(8,128)S(1)}, f32[64,128]{1,0:T(8,128)S(1)}, u32[]{:S(2)}, u32[]{:S(2)}) collective-permute-start(f32[64,128]{1,0:T(8,128)S(1)} %get-tuple-element.238), channel_id=1, source_target_pairs={{0,1},{2,3},{4,5},{6,7},{8,9},{10,11},{12,13},{14,15},{16,17},{18,... | collective-permute-start | bytes 98312 | tf_op jit(solution)/shard_map/ppermute | solution.py:161
  138.7 23.8 %collective-permute-start.60 = (f32[64,128]{1,0:T(8,128)S(1)}, f32[64,128]{1,0:T(8,128)S(1)}, u32[]{:S(2)}, u32[]{:S(2)}) collective-permute-start(f32[64,128]{1,0:T(8,128)S(1)} %get-tuple-element.239), channel_id=1, source_target_pairs={{1,2},{3,4},{5,6},{7,8},{9,10},{11,12},{13,14},{15,16},{17,18},{19... | collective-permute-start | bytes 98312 | tf_op jit(solution)/shard_map/ppermute | solution.py:161
  139.3 23.1 %collective-permute-start.61 = (f32[64,128]{1,0:T(8,128)S(1)}, f32[64,128]{1,0:T(8,128)S(1)}, u32[]{:S(2)}, u32[]{:S(2)}) collective-permute-start(f32[64,128]{1,0:T(8,128)S(1)} %get-tuple-element.240), channel_id=1, source_target_pairs={{0,16},{1,17},{2,18},{3,19},{4,20},{5,21},{6,22},{7,23},{8,24},{9,... | collective-permute-start | bytes 98312 | tf_op jit(solution)/shard_map/ppermute | solution.py:161
  (41 other events, 172.0 us)

commit v5 on v4

--- a/solution.py
+++ b/solution.py
@@ -18,6 +18,7 @@
 STAGE_BYTES = 12 * 1024 * 1024
 TILES = 8
 AXIS = "sub"
+LONGER = 64
 
 
 def contract(left, right, dims=NN):
@@ -64,6 +65,7 @@
 
 
 def flat(tree):
+    tree = {name: held for name, held in tree.items() if not isinstance(held, list) or held}
     names = [(name, len(held) if isinstance(held, list) else 0) for name, held in tree.items()]
     entries = []
     for held in tree.values():
@@ -108,14 +110,14 @@
 
 
 def rounds_of(total):
-    bits = total.bit_length() - 1
-    assert total == 1 << bits
-    rounds = []
+    bits = [1 << i for i in reversed(range(total.bit_length() - 1)) if 1 << i != CYCLE]
+    assert total == 1 << (len(bits) + 1)
+    rounds = [[CYCLE]]
+    if len(bits) % 2:
+        rounds.append([bits.pop(0)])
     while bits:
-        take = 1 if bits % 2 else 2
-        low = 1 << (bits - take)
-        rounds.append([low * i for i in range(1, 1 << take)])
-        bits -= take
+        far, near = bits.pop(0), bits.pop(0)
+        rounds.append([near, far, near + far])
     places = [0]
     for distances in rounds:
         places = [place ^ far for far in [0] + distances for place in places]
@@ -139,38 +141,40 @@
             behind, ahead = (0, 1) if by == 1 else (2, 3)
             chosen.append((pairs, behind, ahead, by, parity))
     blocks = len(chosen)
+    paired = [at for at, block in enumerate(chosen) if block[3:] == (CYCLE, 0)][0]
     slots = blocks * width
     own_rows = (blocks + 1) * primal
 
     vec = ((cases, ndof), F32)
     faces = ((cases, slots), F32)
     pair = ((1, 2 * cases), F32)
-    block_kind = ((lines_a_block, 2 * cases), F32)
     face_kinds = [((cases, width), F32)] * blocks
+    extra_rows = [lines_a_block if at == paired else LONGER if block[3:] == (1, 1) else 0 for at, block in enumerate(chosen)]
+    solve_kinds = [((cases + extra, width), F32) for extra in extra_rows]
+    last_kinds = [((cases + (8 if at == paired else 0), width), F32) for at in range(blocks)]
     blocked = [slice(i * width, (i + 1) * width) for i in range(blocks)]
     strips = [slice(i * ndof // TILES, (i + 1) * ndof // TILES) for i in range(TILES)]
 
-    def joined(refs, rows=slice(None)):
-        return jnp.concatenate([ref[rows] for ref in refs], axis=1)
+    def joined(refs):
+        return jnp.concatenate([ref[:cases] for ref in refs], axis=1)
 
     def put_faces(refs, value):
         for i, ref in enumerate(refs):
-            ref[...] = value[:, blocked[i]]
+            ref[:value.shape[0]] = value[:, blocked[i]]
 
     def exchange(arrays):
         return [lax.ppermute(array, AXIS, chosen[i][0]) for i, array in enumerate(arrays)]
 
-    def gather(block):
-        for at, distances in enumerate(rounds):
+    def gather(own, got, lines, after):
+        pieces, start = [own, got], cases
+        for distances in rounds[1:]:
+            def join(i, o):
+                o.block[...] = jnp.concatenate([ref[start:start + lines] for ref in i.pieces], axis=0)
+
+            block = stage("join", join, dict(pieces=pieces, after=after), dict(block=((lines * len(pieces), 2 * cases), F32))).block
             pieces = [block] + [lax.ppermute(block, AXIS, [(i, i ^ far) for i in range(total)]) for far in distances]
-            if at + 1 == len(rounds):
-                return pieces
-
-            def join(i, o):
-                o.block[...] = jnp.concatenate([ref[...] for ref in i.pieces], axis=0)
-
-            rows, lanes = block.shape
-            block = stage("join", join, dict(pieces=pieces), dict(block=((rows * len(pieces), lanes), F32))).block
+            start, lines, after = 0, block.shape[0], []
+        return pieces
 
     def both_sums(pieces, stride):
         rows = []
@@ -279,25 +283,28 @@
 
     def to_solve(came, own, coef=None, sums=None):
         def body(i, o):
-            arrived = joined(i.came, slice(0, cases))
+            arrived = joined(i.came)
             if coef is not None:
                 arrived = to_column(i.coef[:, cases:]) * -arrived
             lines = i.lines[...] + times(i.basis_slots[...], *split(arrived), NT)
-            o.block[:half] = jnp.concatenate([lines[:half], lines[half:]], axis=1)
-            o.block[half:] = i.sums[...] if sums is not None else jnp.zeros((1, 2 * cases), F32)
             put_faces(o.face, 0.5 * (i.inner_faces[...] + times(0.5 * arrived, i.inv[0][...], i.inv[1][...])))
+            o.face[paired][cases:cases + half] = jnp.concatenate([lines[:half], lines[half:]], axis=1)
+            o.face[paired][cases + half:] = i.sums[...] if sums is not None else jnp.zeros((1, 2 * cases), F32)
+            for at, extra in enumerate(extra_rows):
+                if extra and at != paired:
+                    o.face[at][cases:] = jnp.zeros((extra, width), F32)
 
         ins = dict(came=came, basis_slots=start.basis_slots, lines=own.lines, inner_faces=own.inner_faces, inv=inv[4:])
         if coef is not None:
             ins.update(coef=coef)
         if sums is not None:
             ins.update(sums=sums)
-        made = stage("solve_rest", body, ins, dict(block=block_kind, face=face_kinds))
-        return gather(made.block), exchange(made.face)
+        made = stage("solve_rest", body, ins, dict(face=solve_kinds))
+        return made.face[paired], exchange(made.face)
 
     def to_apply(step, came, own, state, coef):
         def body(i, o):
-            arrived = joined(i.came, slice(0, cases))
+            arrived = joined(i.came)
             if step == 0:
                 o.residual[...] = i.load[0] + pick(arrived, i.picker[...])
             else:
@@ -323,80 +330,98 @@
             outs.update(z=vec)
         return stage("apply_own", body, ins, outs)
 
-    def apply_rest(i, o):
+    def corrected(i):
         rows = jnp.concatenate([ref[...] for ref in i.everyone], axis=0)
         product = times(i.rows[...], *split(rows))
         factors = (product[:own_rows, :cases] + product[own_rows:, cases:]).T
         extra = times(factors, i.reach[0][...], i.reach[1][...])
+        at_slots = i.image_faces[...] + times(joined(i.came), i.stiff_block[0][...], i.stiff_block[1][...]) + extra[:, 2 * ndof:]
+        both = both_sums([ref[...] for ref in i.everyone], lines_a_block)
+        return at_slots, i.v[...] + extra[:, :ndof], i.image[...] + extra[:, ndof:2 * ndof], both
+
+    def recur(i, o, step, inner, image, both):
         arrived = joined(i.came)
-        put_faces(o.face, i.image_faces[...] + times(arrived, i.stiff[2][...], i.stiff[3][...]) + extra[:, 2 * ndof:])
-        o.inner[...] = i.v[...] + extra[:, :ndof]
-        o.image[...] = i.image[...] + extra[:, ndof:2 * ndof]
-        o.sums[...] = both_sums([ref[...] for ref in i.everyone], lines_a_block)
+        inner = inner + pick(arrived, i.picker[...])
+        image = image + times(arrived, i.stiff[0][...], i.stiff[1][...])
+        weight = i.weight[...]
+        if step == 0:
+            part, u, residual = image, inner, i.residual[...]
+            delta = dot(image, u)
+        else:
+            gamma, delta = as_columns(both)
+            w = i.w[...]
+            if step == 1:
+                alpha = gamma / delta
+                q, s, p = inner, w, i.u[...]
+                x = alpha * p
+                before = w
+            else:
+                gamma_old, alpha_old = as_columns(i.coef[...])
+                beta = gamma / gamma_old
+                alpha = gamma / (delta - beta * gamma / alpha_old)
+                q = inner + beta * i.q[...]
+                s = w + beta * i.s[...]
+                p = i.u[...] + beta * i.p[...]
+                x = i.x[...] + alpha * p
+                before = w - (alpha * beta) * i.z[...]
+            residual = i.residual[...] - alpha * s
+            u = i.u[...] - alpha * q
+            part = before - alpha * image
+            delta = dot(weight * before - alpha * image, u)
+            o.coef[...] = jnp.concatenate([both[:, :cases], to_row(alpha)], axis=1)
+            o.s[...], o.p[...], o.x[...], o.residual[...] = s, p, x, residual
+            if step + 1 < ITERS:
+                o.q[...] = q
+                o.z_part[...] = image if step == 1 else image + beta * i.z[...]
+        o.u[...] = u
+        o.w_part[...] = part
+        return part, jnp.concatenate([to_row(dot(weight * residual, u)), to_row(delta)], axis=1)
 
     state = SimpleNamespace()
     came_image, coef, sums = came, None, None
     for step in range(ITERS):
         final = step + 1 == ITERS
-        everyone, came_solve = to_solve(came_image, own, coef, sums)
+        sent, came_solve = to_solve(came_image, own, coef, sums)
         applied = to_apply(step, came_image, own, state, coef)
         vars(state).update(vars(applied))
-        made = stage(
-            "apply_rest", apply_rest,
-            dict(everyone=everyone, rows=reached.rows, reach=reached.reach, came=came_solve, stiff=stiff[2:],
-                 image_faces=state.image_faces, v=state.v, image=state.image),
-            dict(face=face_kinds, inner=vec, image=vec, sums=pair))
-        came_image = exchange(made.face)
-
-        def update(i, o, step=step, final=final):
-            arrived = joined(i.came)
-            inner = i.inner[...] + pick(arrived, i.picker[...])
-            image = i.image[...] + times(arrived, i.stiff[0][...], i.stiff[1][...])
-            weight = i.weight[...]
-            if step == 0:
-                part, u, residual = image, inner, i.residual[...]
-                delta = dot(image, u)
-            else:
-                both = i.both[...]
-                gamma, delta = as_columns(both)
-                w = i.w[...]
-                if step == 1:
-                    alpha = gamma / delta
-                    q, s, p = inner, w, i.u[...]
-                    x = alpha * p
-                    before = w
-                else:
-                    gamma_old, alpha_old = as_columns(i.coef[...])
-                    beta = gamma / gamma_old
-                    alpha = gamma / (delta - beta * gamma / alpha_old)
-                    q = inner + beta * i.q[...]
-                    s = w + beta * i.s[...]
-                    p = i.u[...] + beta * i.p[...]
-                    x = i.x[...] + alpha * p
-                    before = w - (alpha * beta) * i.z[...]
-                residual = i.residual[...] - alpha * s
-                u = i.u[...] - alpha * q
-                part = before - alpha * image
-                delta = dot(weight * before - alpha * image, u)
-                o.coef[...] = jnp.concatenate([both[:, :cases], to_row(alpha)], axis=1)
-                o.s[...], o.p[...], o.x[...], o.residual[...], o.q[...] = s, p, x, residual, q
-                o.z_part[...] = image if step == 1 else image + beta * i.z[...]
-            o.u[...] = u
-            o.w_part[...] = part
-            o.sums[...] = jnp.concatenate([to_row(dot(weight * residual, u)), to_row(delta)], axis=1)
+        everyone = gather(sent, came_solve[paired], lines_a_block, [applied.v])
+        rest_ins = dict(everyone=everyone, rows=reached.rows, reach=reached.reach, came=came_solve, stiff_block=stiff[4:],
+                        image_faces=state.image_faces, v=state.v, image=state.image)
+        ins = dict(came=came_solve, picker=picker, stiff=stiff[2:4], weight=weight, residual=state.residual)
+        outs = dict(u=vec, w_part=vec)
+        if step > 0:
+            ins.update(w=state.w, u=state.u)
+            outs.update(coef=pair, s=vec, p=vec, x=vec, residual=vec)
             if not final:
-                solve_own(part, i, o)
-
-        ins = dict(came=came_solve, picker=picker, inner=made.inner, image=made.image, stiff=stiff[2:4], weight=weight, residual=state.residual)
-        outs = dict(u=vec, w_part=vec, sums=pair)
-        if step > 0:
-            ins.update(both=made.sums, w=state.w, u=state.u)
-            outs.update(coef=pair, s=vec, p=vec, x=vec, residual=vec, q=vec, z_part=vec)
+                outs.update(q=vec, z_part=vec)
         if step > 1:
             ins.update(coef=coef, q=state.q, s=state.s, p=state.p, x=state.x, z=state.z)
-        if not final:
-            ins.update(weighted=start.weighted, inv=inv[:4])
-            outs.update(own_kinds)
+        if final:
+            def last(i, o):
+                at_slots, inner, image, both = corrected(i)
+                put_faces(o.face, at_slots)
+                o.face[paired][cases:] = jnp.broadcast_to(recur(i, o, step, inner, image, both)[1], (8, 2 * cases))
+
+            ins.update(rest_ins)
+            outs.update(face=last_kinds)
+            made = stage("last", last, ins, outs)
+            vars(state).update(vars(made))
+            came_image = exchange(made.face)
+            break
+
+        def apply_rest(i, o):
+            at_slots, o.inner[...], o.image[...], o.sums[...] = corrected(i)
+            put_faces(o.face, at_slots)
+
+        made = stage("apply_rest", apply_rest, rest_ins, dict(face=face_kinds, inner=vec, image=vec, sums=pair))
+        came_image = exchange(made.face)
+
+        def update(i, o, step=step):
+            part, o.sums[...] = recur(i, o, step, i.inner[...], i.image[...], i.both[...])
+            solve_own(part, i, o)
+
+        ins.update(inner=made.inner, image=made.image, both=made.sums, weighted=start.weighted, inv=inv[:4])
+        outs.update(own_kinds, sums=pair)
         own = stage("update", update, ins, outs)
         vars(state).update(vars(own))
         sums = own.sums
@@ -413,12 +438,13 @@
         o.remainder[0] = i.residual[...] - alpha * (w + beta * i.s[...])
 
     whole = ((1, cases, ndof), F32)
-    made = stage(
+    everyone = gather(state.face[paired], came_image[paired], 1, [])
+    done = stage(
         "finish", finish,
-        dict(everyone=gather(sums), came=came_image, picker=picker, coef=coef, w_part=state.w_part, x=state.x, u=state.u, p=state.p,
+        dict(everyone=everyone, came=came_image, picker=picker, coef=state.coef, w_part=state.w_part, x=state.x, u=state.u, p=state.p,
              residual=state.residual, s=state.s),
         dict(solution=whole, remainder=whole))
-    return made.solution, made.remainder
+    return done.solution, done.remainder
 
 
 def solution(mesh):

time: 164 us -> 142 us (0.87)
  starting transfers between devices: 87.6 us -> 70.9 us
  waiting for transfers between devices: 36.2 us -> 31.9 us
    ppermute x27, starting transfers between devices: 53.1 us -> 36.9 us  [exchange(): lax.ppermute(array, AXIS, chosen[i][0])]
    ppermute x35 -> x30, waiting for transfers between devices: 35.1 us -> 25.5 us  [gather(): lax.ppermute(block, AXIS, [(i, i ^ far) for i in range(total)])]
    ppermute x27, waiting for transfers between devices: 1.14 us -> 6.41 us  [exchange(): lax.ppermute(array, AXIS, chosen[i][0])]
    pallas_call x32 -> x31, Pallas kernels: 32.4 us -> 31.2 us  [stage(): pl.pallas_call(kernel, name=name, out_shape=[jax.ShapeDtypeStruct(*kind)...]
    ppermute x35 -> x30, starting transfers between devices: 34.5 us -> 34 us  [gather(): lax.ppermute(block, AXIS, [(i, i ^ far) for i in range(total)])]
  transfers between devices with their start and end apart: 62 -> 57, of which waited for: 25 -> 25; matrix products, arithmetic and copies ran while one was open for 0% -> 0% of each run, Pallas kernels for 15% -> 17%
where the time goes in v5:
time: 142 us; the launch traced here: 141 us
  starting transfers between devices  70.9 us (50%)
  waiting for transfers between devices  31.9 us (22%)
  Pallas kernels  31.2 us (22%)
  local copies, waits for them, and re-layouts  6.09 us (4%)
    ppermute x27, starting transfers between devices, exchange(): lax.ppermute(array, AXIS, chosen[i][0])  36.9 us
    ppermute x30, starting transfers between devices, gather(): lax.ppermute(block, AXIS, [(i, i ^ far) for i in range(total)])  34 us
    pallas_call x31, Pallas kernels, stage(): pl.pallas_call(kernel, name=name, out_shape=[jax.ShapeDtypeStruct(*kind)...  31.2 us
    ppermute x30, waiting for transfers between devices, gather(): lax.ppermute(block, AXIS, [(i, i ^ far) for i in range(total)])  25.5 us
    ppermute x27, waiting for transfers between devices, exchange(): lax.ppermute(array, AXIS, chosen[i][0])  6.41 us
    unnamed x22, local copies, waits for them, and re-layouts  6.09 us
  transfers between devices with their start and end apart: 57, of which 25 were waited for; matrix products, arithmetic and copies ran while one was open for 0% of the time, Pallas kernels for 17%

profile of v5, /device:TPU:0, one launch (start us, length us, event | category | flops | bytes accessed | tf_op | source)
XLA Modules:
  0.0 141.2 jit_solution(966870539877742254)
XLA Ops:
  6.7 7.3 %collective-permute-start.2 = (f32[144,128]{1,0:T(8,128)S(1)}, f32[144,128]{1,0:T(8,128)S(1)}, u32[]{:S(2)}, u32[]{:S(2)}) collective-permute-start(f32[144,128]{1,0:T(8,128)S(1)} %get-tuple-element.120), channel_id=1, source_target_pairs={{0,16},{1,17},{2,18},{3,19},{4,20},{5,21},{6,22},{7,23},{8,24},{9,... | collective-permute-start | bytes 221192 | tf_op jit(solution)/shard_map/ppermute | solution.py:166
  14.0 2.2 %copy-done = f32[1,1024,1024]{2,1,0:T(8,128)S(1)} copy-done((f32[1,1024,1024]{2,1,0:T(8,128)S(1)}, f32[1,1024,1024]{2,1,0:T(8,128)}, u32[]{:S(2)}) %copy-start) | copy-done | bytes 4194328
  16.2 2.7 %prepare_inv.1 = (bf16[1024,1024]{1,0:T(8,128)(2,1)S(1)}, bf16[1024,1024]{1,0:T(8,128)(2,1)S(1)}, bf16[384,1024]{1,0:T(8,128)(2,1)S(1)}, bf16[384,1024]{1,0:T(8,...) custom-call(f32[1,1024,1024]{2,1,0:T(8,128)S(1)} %copy-done, ...), custom_call_target="tpu_custom_call" | custom-call | tf_op jit(solution)/shard_map/prepare_inv/pallas_call | solution.py:92
  21.3 2.7 %prepare_stiff.1 = (bf16[1024,1024]{1,0:T(8,128)(2,1)S(1)}, bf16[1024,1024]{1,0:T(8,128)(2,1)S(1)}, bf16[384,1024]{1,0:T(8,128)(2,1)S(1)}, bf16[384,1024]{1,0:T(...) custom-call(f32[1,1024,1024]{2,1,0:T(8,128)S(1)} %copy-done.1, ...), custom_call_target="tpu_custom_call" | custom-call | tf_op jit(solution)/shard_map/prepare_stiff/pallas_call | solution.py:92
  24.0 2.0 %apply_own.4 = (f32[64,1024]{1,0:T(8,128)S(1)}, f32[64,384]{1,0:T(8,128)S(1)}, f32[64,1024]{1,0:T(8,128)S(1)}, f32[64,1024]{1,0:T(8,128)S(1)}) custom-call(f32[144,128]{1,0:T(8,128)S(1)} %collective-permute-done.refs_0_.refs_2_, f32[144,128]{1,0:T(8,128)S(1)} %collective-permute-done.1.refs_1_.refs_3_, ...), custom_call_target="tpu_custom_call" | custom-call | tf_op jit(solution)/shard_map/apply_own/pallas_call | solution.py:92
  26.0 2.8 %collective-permute-start.4 = (f32[18,128]{1,0:T(8,128)S(1)}, f32[18,128]{1,0:T(8,128)S(1)}, u32[]{:S(2)}, u32[]{:S(2)}) collective-permute-start(f32[18,128]{1,0:T(8,128)S(1)} %join.10.refs_0_), channel_id=1, source_target_pairs={{0,4},{1,5},{2,6},{3,7},{4,0},{5,1},{6,2},{7,3},{8,12},{9,13},{10,... | collective-permute-start | bytes 27656 | tf_op jit(solution)/shard_map/ppermute | solution.py:175
  28.8 1.9 %collective-permute-start.5 = (f32[18,128]{1,0:T(8,128)S(1)}, f32[18,128]{1,0:T(8,128)S(1)}, u32[]{:S(2)}, u32[]{:S(2)}) collective-permute-start(f32[18,128]{1,0:T(8,128)S(1)} %join.10.refs_0_), channel_id=1, source_target_pairs={{0,8},{1,9},{2,10},{3,11},{4,12},{5,13},{6,14},{7,15},{8,0},{9,1},... | collective-permute-start | bytes 27656 | tf_op jit(solution)/shard_map/ppermute | solution.py:175
  32.5 2.8 %collective-permute-done.6.refs_3_ = f32[18,128]{1,0:T(8,128)S(1)} collective-permute-done((f32[18,128]{1,0:T(8,128)S(1)}, f32[18,128]{1,0:T(8,128)S(1)}, u32[]{:S(2)}, u32[]{:S(2)}) %collective-permute-start.6) | collective-permute-done | bytes 9248 | tf_op jit(solution)/shard_map/ppermute | solution.py:175
  37.6 1.7 %reach.1 = (bf16[64,2432]{1,0:T(8,128)(2,1)S(1)}, bf16[64,2432]{1,0:T(8,128)(2,1)S(1)}, f32[128,288]{1,0:T(8,128)S(1)}) custom-call(f32[16,1024]{1,0:T(8,128)S(1)} %get-tuple-element.123.refs_2_.refs_0_.refs_11_.refs_13_.refs_19_, f32[16,512]{1,0:T(8,128)S(1)} %copy-done.5, f32[144,128]{1,0:T(8,128)S(1)} %collective-permute-done.refs_0_.refs_2_, ...), custom_call_target="tpu_custom_call" | custom-call | tf_op jit(solution)/shard_map/reach/pallas_call | solution.py:92
  42.3 3.5 %collective-permute-start.14 = (f32[64,128]{1,0:T(8,128)S(1)}, f32[64,128]{1,0:T(8,128)S(1)}, u32[]{:S(2)}, u32[]{:S(2)}) collective-permute-start(f32[64,128]{1,0:T(8,128)S(1)} %get-tuple-element.152), channel_id=1, source_target_pairs={{0,16},{1,17},{2,18},{3,19},{4,20},{5,21},{6,22},{7,23},{8,24},{9,... | collective-permute-start | bytes 98312 | tf_op jit(solution)/shard_map/ppermute | solution.py:166
  45.8 2.2 %update.3 = (f32[64,1024]{1,0:T(8,128)S(1)}, f32[64,1024]{1,0:T(8,128)S(1)}, f32[16,64]{1,0:T(8,128)S(1)}, f32[64,384]{1,0:T(8,128)S(1)}, f32[64,1024]{1,0:T(8,128)S(1)}, /*index=5*/f32[1,128]{1,0:T(1,128)S(1)}) custom-call(f32[64,128]{1,0:T(8,128)S(1)} %collective-permute-done.10.refs_7_.refs_0_, f32[128,128]{1,0:T(8,128)S(1)} %collective-permute-done.11.refs_8_.refs_1_, ...), custom_call_target="tpu_custom_call" | custom-call | tf_op jit(solution)/shard_map/update/pallas_call | solution.py:92
  48.3 2.7 %collective-permute-start.15 = (f32[73,128]{1,0:T(8,128)S(1)}, f32[73,128]{1,0:T(8,128)S(1)}, u32[]{:S(2)}, u32[]{:S(2)}) collective-permute-start(f32[73,128]{1,0:T(8,128)S(1)} %get-tuple-element.160.refs_0_), channel_id=1, source_target_pairs={{0,16},{1,17},{2,18},{3,19},{4,20},{5,21},{6,22},{7,23},{8,24},{9,... | collective-permute-start | bytes 112136 | tf_op jit(solution)/shard_map/ppermute | solution.py:166
  51.7 2.0 %apply_own.5 = (f32[64,1024]{1,0:T(8,128)S(1)}, f32[64,384]{1,0:T(8,128)S(1)}, f32[64,1024]{1,0:T(8,128)S(1)}, f32[64,1024]{1,0:T(8,128)S(1)}) custom-call(f32[64,128]{1,0:T(8,128)S(1)} %collective-permute-done.12.refs_0_, f32[64,128]{1,0:T(8,128)S(1)} %collective-permute-done.13.refs_1_, f32[64,128]{1,0:T(8,128)S(1)} %collective-permute-done.14.refs_2_, ...), custom_call_target="tpu_custom_call" | custom-call | tf_op jit(solution)/shard_map/apply_own/pallas_call | solution.py:92
  53.7 3.6 %collective-permute-start.16 = (f32[18,128]{1,0:T(8,128)S(1)}, f32[18,128]{1,0:T(8,128)S(1)}, u32[]{:S(2)}, u32[]{:S(2)}) collective-permute-start(f32[18,128]{1,0:T(8,128)S(1)} %join.12.refs_0_), channel_id=1, source_target_pairs={{0,4},{1,5},{2,6},{3,7},{4,0},{5,1},{6,2},{7,3},{8,12},{9,13},{10,... | collective-permute-start | bytes 27656 | tf_op jit(solution)/shard_map/ppermute | solution.py:175
  61.0 1.7 %collective-permute-done.18.refs_3_ = f32[18,128]{1,0:T(8,128)S(1)} collective-permute-done((f32[18,128]{1,0:T(8,128)S(1)}, f32[18,128]{1,0:T(8,128)S(1)}, u32[]{:S(2)}, u32[]{:S(2)}) %collective-permute-start.18) | collective-permute-done | bytes 9248 | tf_op jit(solution)/shard_map/ppermute | solution.py:175
  69.4 4.5 %collective-permute-start.26 = (f32[64,128]{1,0:T(8,128)S(1)}, f32[64,128]{1,0:T(8,128)S(1)}, u32[]{:S(2)}, u32[]{:S(2)}) collective-permute-start(f32[64,128]{1,0:T(8,128)S(1)} %get-tuple-element.170), channel_id=1, source_target_pairs={{0,16},{1,17},{2,18},{3,19},{4,20},{5,21},{6,22},{7,23},{8,24},{9,... | collective-permute-start | bytes 98312 | tf_op jit(solution)/shard_map/ppermute | solution.py:166
  73.9 2.3 %update.4 = (f32[64,1024]{1,0:T(8,128)S(1)}, f32[64,1024]{1,0:T(8,128)S(1)}, f32[1,128]{1,0:T(1,128)S(1)}, f32[64,1024]{1,0:T(8,128)S(1)}, f32[64,1024]{1,0:T(8,...) custom-call(f32[64,128]{1,0:T(8,128)S(1)} %collective-permute-done.2, ...), custom_call_target="tpu_custom_call" | custom-call | tf_op jit(solution)/shard_map/update/pallas_call | solution.py:92
  76.8 2.5 %collective-permute-start.27 = (f32[73,128]{1,0:T(8,128)S(1)}, f32[73,128]{1,0:T(8,128)S(1)}, u32[]{:S(2)}, u32[]{:S(2)}) collective-permute-start(f32[73,128]{1,0:T(8,128)S(1)} %get-tuple-element.180.refs_0_), channel_id=1, source_target_pairs={{0,16},{1,17},{2,18},{3,19},{4,20},{5,21},{6,22},{7,23},{8,24},{9,... | collective-permute-start | bytes 112136 | tf_op jit(solution)/shard_map/ppermute | solution.py:166
  80.0 2.2 %apply_own.6 = (f32[64,1024]{1,0:T(8,128)S(1)}, f32[64,384]{1,0:T(8,128)S(1)}, f32[64,1024]{1,0:T(8,128)S(1)}, f32[64,1024]{1,0:T(8,128)S(1)}, f32[64,1024]{1,0:T(8,128)S(1)}) custom-call(f32[64,128]{1,0:T(8,128)S(1)} %collective-permute-done.24.refs_0_, f32[64,128]{1,0:T(8,128)S(1)} %collective-permute-done.25.refs_1_, ...), custom_call_target="tpu_custom_call" | custom-call | tf_op jit(solution)/shard_map/apply_own/pallas_call | solution.py:92
  82.2 1.9 %collective-permute-start.28 = (f32[18,128]{1,0:T(8,128)S(1)}, f32[18,128]{1,0:T(8,128)S(1)}, u32[]{:S(2)}, u32[]{:S(2)}) collective-permute-start(f32[18,128]{1,0:T(8,128)S(1)} %join.14.refs_0_), channel_id=1, source_target_pairs={{0,4},{1,5},{2,6},{3,7},{4,0},{5,1},{6,2},{7,3},{8,12},{9,13},{10,... | collective-permute-start | bytes 27656 | tf_op jit(solution)/shard_map/ppermute | solution.py:175
  84.1 1.7 %collective-permute-start.29 = (f32[18,128]{1,0:T(8,128)S(1)}, f32[18,128]{1,0:T(8,128)S(1)}, u32[]{:S(2)}, u32[]{:S(2)}) collective-permute-start(f32[18,128]{1,0:T(8,128)S(1)} %join.14.refs_0_), channel_id=1, source_target_pairs={{0,8},{1,9},{2,10},{3,11},{4,12},{5,13},{6,14},{7,15},{8,0},{9,1},... | collective-permute-start | bytes 27656 | tf_op jit(solution)/shard_map/ppermute | solution.py:175
  87.8 2.6 %collective-permute-done.30.refs_3_ = f32[18,128]{1,0:T(8,128)S(1)} collective-permute-done((f32[18,128]{1,0:T(8,128)S(1)}, f32[18,128]{1,0:T(8,128)S(1)}, u32[]{:S(2)}, u32[]{:S(2)}) %collective-permute-start.30) | collective-permute-done | bytes 9248 | tf_op jit(solution)/shard_map/ppermute | solution.py:175
  96.8 4.4 %collective-permute-start.38 = (f32[64,128]{1,0:T(8,128)S(1)}, f32[64,128]{1,0:T(8,128)S(1)}, u32[]{:S(2)}, u32[]{:S(2)}) collective-permute-start(f32[64,128]{1,0:T(8,128)S(1)} %get-tuple-element.191), channel_id=1, source_target_pairs={{0,16},{1,17},{2,18},{3,19},{4,20},{5,21},{6,22},{7,23},{8,24},{9,... | collective-permute-start | bytes 98312 | tf_op jit(solution)/shard_map/ppermute | solution.py:166
  101.2 2.3 %update.5 = (f32[64,1024]{1,0:T(8,128)S(1)}, f32[64,1024]{1,0:T(8,128)S(1)}, f32[1,128]{1,0:T(1,128)S(1)}, f32[64,1024]{1,0:T(8,128)S(1)}, f32[64,1024]{1,0:T(8,...) custom-call(f32[64,128]{1,0:T(8,128)S(1)} %collective-permute-done.3, ...), custom_call_target="tpu_custom_call" | custom-call | tf_op jit(solution)/shard_map/update/pallas_call | solution.py:92
  104.4 2.1 %collective-permute-start.41 = (f32[73,128]{1,0:T(8,128)S(1)}, f32[73,128]{1,0:T(8,128)S(1)}, u32[]{:S(2)}, u32[]{:S(2)}) collective-permute-start(f32[73,128]{1,0:T(8,128)S(1)} %get-tuple-element.209.refs_0_), channel_id=1, source_target_pairs={{0,16},{1,17},{2,18},{3,19},{4,20},{5,21},{6,22},{7,23},{8,24},{9,... | collective-permute-start | bytes 112136 | tf_op jit(solution)/shard_map/ppermute | solution.py:166
  107.4 2.2 %apply_own.7 = (f32[64,1024]{1,0:T(8,128)S(1)}, f32[64,384]{1,0:T(8,128)S(1)}, f32[64,1024]{1,0:T(8,128)S(1)}, f32[64,1024]{1,0:T(8,128)S(1)}, f32[64,1024]{1,0:T(8,128)S(1)}) custom-call(f32[64,128]{1,0:T(8,128)S(1)} %collective-permute-done.36.refs_0_, f32[64,128]{1,0:T(8,128)S(1)} %collective-permute-done.37.refs_1_, ...), custom_call_target="tpu_custom_call" | custom-call | tf_op jit(solution)/shard_map/apply_own/pallas_call | solution.py:92
  109.6 2.7 %collective-permute-start.42 = (f32[18,128]{1,0:T(8,128)S(1)}, f32[18,128]{1,0:T(8,128)S(1)}, u32[]{:S(2)}, u32[]{:S(2)}) collective-permute-start(f32[18,128]{1,0:T(8,128)S(1)} %join.16.refs_0_), channel_id=1, source_target_pairs={{0,4},{1,5},{2,6},{3,7},{4,0},{5,1},{6,2},{7,3},{8,12},{9,13},{10,... | collective-permute-start | bytes 27656 | tf_op jit(solution)/shard_map/ppermute | solution.py:175
  116.0 2.0 %collective-permute-done.44.refs_3_ = f32[18,128]{1,0:T(8,128)S(1)} collective-permute-done((f32[18,128]{1,0:T(8,128)S(1)}, f32[18,128]{1,0:T(8,128)S(1)}, u32[]{:S(2)}, u32[]{:S(2)}) %collective-permute-start.44) | collective-permute-done | bytes 9248 | tf_op jit(solution)/shard_map/ppermute | solution.py:175
  123.0 1.7 %last.1 = (f32[64,1024]{1,0:T(8,128)S(1)}, f32[64,1024]{1,0:T(8,128)S(1)}, f32[1,128]{1,0:T(1,128)S(1)}, f32[64,1024]{1,0:T(8,128)S(1)}, f32[64,1024]{1,0:T(8,12...) custom-call(f32[64,128]{1,0:T(8,128)S(1)} %collective-permute-done.3, ...), custom_call_target="tpu_custom_call" | custom-call | tf_op jit(solution)/shard_map/last/pallas_call | solution.py:92
  126.4 3.1 %collective-permute-done.48.refs_1_.refs_6_ = f32[72,128]{1,0:T(8,128)S(1)} collective-permute-done((f32[72,128]{1,0:T(8,128)S(1)}, f32[72,128]{1,0:T(8,128)S(1)}, u32[]{:S(2)}, u32[]{:S(2)}) %collective-permute-start.48) | collective-permute-done | bytes 36896 | tf_op jit(solution)/shard_map/ppermute | solution.py:166
  129.5 1.7 %collective-permute-start.49 = (f32[2,128]{1,0:T(2,128)S(1)}, f32[2,128]{1,0:T(2,128)S(1)}, u32[]{:S(2)}, u32[]{:S(2)}) collective-permute-start(f32[2,128]{1,0:T(2,128)S(1)} %join.18.refs_0_), channel_id=1, source_target_pairs={{0,4},{1,5},{2,6},{3,7},{4,0},{5,1},{6,2},{7,3},{8,12},{9,13},{10,... | collective-permute-start | bytes 3080 | tf_op jit(solution)/shard_map/ppermute | solution.py:175
  138.3 1.8 %collective-permute-done.53.refs_2_ = f32[8,128]{1,0:T(8,128)S(1)} collective-permute-done((f32[8,128]{1,0:T(8,128)S(1)}, f32[8,128]{1,0:T(8,128)S(1)}, u32[]{:S(2)}, u32[]{:S(2)}) %collective-permute-start.53) | collective-permute-done | bytes 4128 | tf_op jit(solution)/shard_map/ppermute | solution.py:175
  (135 shorter events, 56.6 us)
Async XLA Ops:
  5.5 14.7 %collective-permute-start = (f32[144,128]{1,0:T(8,128)S(1)}, f32[144,128]{1,0:T(8,128)S(1)}, u32[]{:S(2)}, u32[]{:S(2)}) collective-permute-start(f32[144,128]{1,0:T(8,128)S(1)} %get-tuple-element.118), channel_id=1, source_target_pairs={{0,1},{2,3},{4,5},{6,7},{8,9},{10,11},{12,13},{14,15},{16,17},{18,... | collective-permute-start | bytes 221192 | tf_op jit(solution)/shard_map/ppermute | solution.py:166
  6.0 14.2 %collective-permute-start.1 = (f32[144,128]{1,0:T(8,128)S(1)}, f32[144,128]{1,0:T(8,128)S(1)}, u32[]{:S(2)}, u32[]{:S(2)}) collective-permute-start(f32[144,128]{1,0:T(8,128)S(1)} %get-tuple-element.119), channel_id=1, source_target_pairs={{1,2},{3,4},{5,6},{7,8},{9,10},{11,12},{13,14},{15,16},{17,18},{19... | collective-permute-start | bytes 221192 | tf_op jit(solution)/shard_map/ppermute | solution.py:166
  6.7 13.6 %collective-permute-start.2 = (f32[144,128]{1,0:T(8,128)S(1)}, f32[144,128]{1,0:T(8,128)S(1)}, u32[]{:S(2)}, u32[]{:S(2)}) collective-permute-start(f32[144,128]{1,0:T(8,128)S(1)} %get-tuple-element.120), channel_id=1, source_target_pairs={{0,16},{1,17},{2,18},{3,19},{4,20},{5,21},{6,22},{7,23},{8,24},{9,... | collective-permute-start | bytes 221192 | tf_op jit(solution)/shard_map/ppermute | solution.py:166
  20.5 5.5 %collective-permute-start.3 = (f32[73,128]{1,0:T(8,128)S(1)}, f32[73,128]{1,0:T(8,128)S(1)}, u32[]{:S(2)}, u32[]{:S(2)}) collective-permute-start(f32[73,128]{1,0:T(8,128)S(1)} %get-tuple-element.134.refs_0_), channel_id=1, source_target_pairs={{0,16},{1,17},{2,18},{3,19},{4,20},{5,21},{6,22},{7,23},{8,24},{9,... | collective-permute-start | bytes 112136 | tf_op jit(solution)/shard_map/ppermute | solution.py:166
  20.6 18.6 %collective-permute-start.11 = (f32[128,128]{1,0:T(8,128)S(1)}, f32[128,128]{1,0:T(8,128)S(1)}, u32[]{:S(2)}, u32[]{:S(2)}) collective-permute-start(f32[128,128]{1,0:T(8,128)S(1)} %get-tuple-element.145), channel_id=1, source_target_pairs={{1,2},{3,4},{5,6},{7,8},{9,10},{11,12},{13,14},{15,16},{17,18},{19... | collective-permute-start | bytes 196616 | tf_op jit(solution)/shard_map/ppermute | solution.py:166
  26.0 5.2 %collective-permute-start.4 = (f32[18,128]{1,0:T(8,128)S(1)}, f32[18,128]{1,0:T(8,128)S(1)}, u32[]{:S(2)}, u32[]{:S(2)}) collective-permute-start(f32[18,128]{1,0:T(8,128)S(1)} %join.10.refs_0_), channel_id=1, source_target_pairs={{0,4},{1,5},{2,6},{3,7},{4,0},{5,1},{6,2},{7,3},{8,12},{9,13},{10,... | collective-permute-start | bytes 27656 | tf_op jit(solution)/shard_map/ppermute | solution.py:175
  30.7 4.6 %collective-permute-start.6 = (f32[18,128]{1,0:T(8,128)S(1)}, f32[18,128]{1,0:T(8,128)S(1)}, u32[]{:S(2)}, u32[]{:S(2)}) collective-permute-start(f32[18,128]{1,0:T(8,128)S(1)} %join.10.refs_0_), channel_id=1, source_target_pairs={{0,12},{1,13},{2,14},{3,15},{4,8},{5,9},{6,10},{7,11},{8,4},{9,5},... | collective-permute-start | bytes 27656 | tf_op jit(solution)/shard_map/ppermute | solution.py:175
  41.3 6.7 %collective-permute-start.12 = (f32[64,128]{1,0:T(8,128)S(1)}, f32[64,128]{1,0:T(8,128)S(1)}, u32[]{:S(2)}, u32[]{:S(2)}) collective-permute-start(f32[64,128]{1,0:T(8,128)S(1)} %get-tuple-element.150), channel_id=1, source_target_pairs={{0,1},{2,3},{4,5},{6,7},{8,9},{10,11},{12,13},{14,15},{16,17},{18,... | collective-permute-start | bytes 98312 | tf_op jit(solution)/shard_map/ppermute | solution.py:166
  41.5 6.5 %collective-permute-start.13 = (f32[64,128]{1,0:T(8,128)S(1)}, f32[64,128]{1,0:T(8,128)S(1)}, u32[]{:S(2)}, u32[]{:S(2)}) collective-permute-start(f32[64,128]{1,0:T(8,128)S(1)} %get-tuple-element.151), channel_id=1, source_target_pairs={{1,2},{3,4},{5,6},{7,8},{9,10},{11,12},{13,14},{15,16},{17,18},{19... | collective-permute-start | bytes 98312 | tf_op jit(solution)/shard_map/ppermute | solution.py:166
  42.3 5.7 %collective-permute-start.14 = (f32[64,128]{1,0:T(8,128)S(1)}, f32[64,128]{1,0:T(8,128)S(1)}, u32[]{:S(2)}, u32[]{:S(2)}) collective-permute-start(f32[64,128]{1,0:T(8,128)S(1)} %get-tuple-element.152), channel_id=1, source_target_pairs={{0,16},{1,17},{2,18},{3,19},{4,20},{5,21},{6,22},{7,23},{8,24},{9,... | collective-permute-start | bytes 98312 | tf_op jit(solution)/shard_map/ppermute | solution.py:166
  48.3 5.3 %collective-permute-start.15 = (f32[73,128]{1,0:T(8,128)S(1)}, f32[73,128]{1,0:T(8,128)S(1)}, u32[]{:S(2)}, u32[]{:S(2)}) collective-permute-start(f32[73,128]{1,0:T(8,128)S(1)} %get-tuple-element.160.refs_0_), channel_id=1, source_target_pairs={{0,16},{1,17},{2,18},{3,19},{4,20},{5,21},{6,22},{7,23},{8,24},{9,... | collective-permute-start | bytes 112136 | tf_op jit(solution)/shard_map/ppermute | solution.py:166
  51.0 14.8 %collective-permute-start.23 = (f32[128,128]{1,0:T(8,128)S(1)}, f32[128,128]{1,0:T(8,128)S(1)}, u32[]{:S(2)}, u32[]{:S(2)}) collective-permute-start(f32[128,128]{1,0:T(8,128)S(1)} %get-tuple-element.165), channel_id=1, source_target_pairs={{1,2},{3,4},{5,6},{7,8},{9,10},{11,12},{13,14},{15,16},{17,18},{19... | collective-permute-start | bytes 196616 | tf_op jit(solution)/shard_map/ppermute | solution.py:166
  53.7 5.9 %collective-permute-start.16 = (f32[18,128]{1,0:T(8,128)S(1)}, f32[18,128]{1,0:T(8,128)S(1)}, u32[]{:S(2)}, u32[]{:S(2)}) collective-permute-start(f32[18,128]{1,0:T(8,128)S(1)} %join.12.refs_0_), channel_id=1, source_target_pairs={{0,4},{1,5},{2,6},{3,7},{4,0},{5,1},{6,2},{7,3},{8,12},{9,13},{10,... | collective-permute-start | bytes 27656 | tf_op jit(solution)/shard_map/ppermute | solution.py:175
  58.1 4.6 %collective-permute-start.18 = (f32[18,128]{1,0:T(8,128)S(1)}, f32[18,128]{1,0:T(8,128)S(1)}, u32[]{:S(2)}, u32[]{:S(2)}) collective-permute-start(f32[18,128]{1,0:T(8,128)S(1)} %join.12.refs_0_), channel_id=1, source_target_pairs={{0,12},{1,13},{2,14},{3,15},{4,8},{5,9},{6,10},{7,11},{8,4},{9,5},... | collective-permute-start | bytes 27656 | tf_op jit(solution)/shard_map/ppermute | solution.py:175
  68.6 7.6 %collective-permute-start.24 = (f32[64,128]{1,0:T(8,128)S(1)}, f32[64,128]{1,0:T(8,128)S(1)}, u32[]{:S(2)}, u32[]{:S(2)}) collective-permute-start(f32[64,128]{1,0:T(8,128)S(1)} %get-tuple-element.168), channel_id=1, source_target_pairs={{0,1},{2,3},{4,5},{6,7},{8,9},{10,11},{12,13},{14,15},{16,17},{18,... | collective-permute-start | bytes 98312 | tf_op jit(solution)/shard_map/ppermute | solution.py:166
  68.7 7.5 %collective-permute-start.25 = (f32[64,128]{1,0:T(8,128)S(1)}, f32[64,128]{1,0:T(8,128)S(1)}, u32[]{:S(2)}, u32[]{:S(2)}) collective-permute-start(f32[64,128]{1,0:T(8,128)S(1)} %get-tuple-element.169), channel_id=1, source_target_pairs={{1,2},{3,4},{5,6},{7,8},{9,10},{11,12},{13,14},{15,16},{17,18},{19... | collective-permute-start | bytes 98312 | tf_op jit(solution)/shard_map/ppermute | solution.py:166
  69.4 7.0 %collective-permute-start.26 = (f32[64,128]{1,0:T(8,128)S(1)}, f32[64,128]{1,0:T(8,128)S(1)}, u32[]{:S(2)}, u32[]{:S(2)}) collective-permute-start(f32[64,128]{1,0:T(8,128)S(1)} %get-tuple-element.170), channel_id=1, source_target_pairs={{0,16},{1,17},{2,18},{3,19},{4,20},{5,21},{6,22},{7,23},{8,24},{9,... | collective-permute-start | bytes 98312 | tf_op jit(solution)/shard_map/ppermute | solution.py:166
  76.8 5.4 %collective-permute-start.27 = (f32[73,128]{1,0:T(8,128)S(1)}, f32[73,128]{1,0:T(8,128)S(1)}, u32[]{:S(2)}, u32[]{:S(2)}) collective-permute-start(f32[73,128]{1,0:T(8,128)S(1)} %get-tuple-element.180.refs_0_), channel_id=1, source_target_pairs={{0,16},{1,17},{2,18},{3,19},{4,20},{5,21},{6,22},{7,23},{8,24},{9,... | collective-permute-start | bytes 112136 | tf_op jit(solution)/shard_map/ppermute | solution.py:166
  79.3 14.1 %collective-permute-start.35 = (f32[128,128]{1,0:T(8,128)S(1)}, f32[128,128]{1,0:T(8,128)S(1)}, u32[]{:S(2)}, u32[]{:S(2)}) collective-permute-start(f32[128,128]{1,0:T(8,128)S(1)} %get-tuple-element.186), channel_id=1, source_target_pairs={{1,2},{3,4},{5,6},{7,8},{9,10},{11,12},{13,14},{15,16},{17,18},{19... | collective-permute-start | bytes 196616 | tf_op jit(solution)/shard_map/ppermute | solution.py:166
  82.2 4.6 %collective-permute-start.28 = (f32[18,128]{1,0:T(8,128)S(1)}, f32[18,128]{1,0:T(8,128)S(1)}, u32[]{:S(2)}, u32[]{:S(2)}) collective-permute-start(f32[18,128]{1,0:T(8,128)S(1)} %join.14.refs_0_), channel_id=1, source_target_pairs={{0,4},{1,5},{2,6},{3,7},{4,0},{5,1},{6,2},{7,3},{8,12},{9,13},{10,... | collective-permute-start | bytes 27656 | tf_op jit(solution)/shard_map/ppermute | solution.py:175
  85.8 4.6 %collective-permute-start.30 = (f32[18,128]{1,0:T(8,128)S(1)}, f32[18,128]{1,0:T(8,128)S(1)}, u32[]{:S(2)}, u32[]{:S(2)}) collective-permute-start(f32[18,128]{1,0:T(8,128)S(1)} %join.14.refs_0_), channel_id=1, source_target_pairs={{0,12},{1,13},{2,14},{3,15},{4,8},{5,9},{6,10},{7,11},{8,4},{9,5},... | collective-permute-start | bytes 27656 | tf_op jit(solution)/shard_map/ppermute | solution.py:175
  95.9 7.6 %collective-permute-start.36 = (f32[64,128]{1,0:T(8,128)S(1)}, f32[64,128]{1,0:T(8,128)S(1)}, u32[]{:S(2)}, u32[]{:S(2)}) collective-permute-start(f32[64,128]{1,0:T(8,128)S(1)} %get-tuple-element.189), channel_id=1, source_target_pairs={{0,1},{2,3},{4,5},{6,7},{8,9},{10,11},{12,13},{14,15},{16,17},{18,... | collective-permute-start | bytes 98312 | tf_op jit(solution)/shard_map/ppermute | solution.py:166
  96.1 7.4 %collective-permute-start.37 = (f32[64,128]{1,0:T(8,128)S(1)}, f32[64,128]{1,0:T(8,128)S(1)}, u32[]{:S(2)}, u32[]{:S(2)}) collective-permute-start(f32[64,128]{1,0:T(8,128)S(1)} %get-tuple-element.190), channel_id=1, source_target_pairs={{1,2},{3,4},{5,6},{7,8},{9,10},{11,12},{13,14},{15,16},{17,18},{19... | collective-permute-start | bytes 98312 | tf_op jit(solution)/shard_map/ppermute | solution.py:166
  96.8 7.2 %collective-permute-start.38 = (f32[64,128]{1,0:T(8,128)S(1)}, f32[64,128]{1,0:T(8,128)S(1)}, u32[]{:S(2)}, u32[]{:S(2)}) collective-permute-start(f32[64,128]{1,0:T(8,128)S(1)} %get-tuple-element.191), channel_id=1, source_target_pairs={{0,16},{1,17},{2,18},{3,19},{4,20},{5,21},{6,22},{7,23},{8,24},{9,... | collective-permute-start | bytes 98312 | tf_op jit(solution)/shard_map/ppermute | solution.py:166
  104.4 5.2 %collective-permute-start.41 = (f32[73,128]{1,0:T(8,128)S(1)}, f32[73,128]{1,0:T(8,128)S(1)}, u32[]{:S(2)}, u32[]{:S(2)}) collective-permute-start(f32[73,128]{1,0:T(8,128)S(1)} %get-tuple-element.209.refs_0_), channel_id=1, source_target_pairs={{0,16},{1,17},{2,18},{3,19},{4,20},{5,21},{6,22},{7,23},{8,24},{9,... | collective-permute-start | bytes 112136 | tf_op jit(solution)/shard_map/ppermute | solution.py:166
  106.5 14.7 %collective-permute-start.40 = (f32[128,128]{1,0:T(8,128)S(1)}, f32[128,128]{1,0:T(8,128)S(1)}, u32[]{:S(2)}, u32[]{:S(2)}) collective-permute-start(f32[128,128]{1,0:T(8,128)S(1)} %get-tuple-element.208), channel_id=1, source_target_pairs={{1,2},{3,4},{5,6},{7,8},{9,10},{11,12},{13,14},{15,16},{17,18},{19... | collective-permute-start | bytes 196616 | tf_op jit(solution)/shard_map/ppermute | solution.py:166
  109.6 5.3 %collective-permute-start.42 = (f32[18,128]{1,0:T(8,128)S(1)}, f32[18,128]{1,0:T(8,128)S(1)}, u32[]{:S(2)}, u32[]{:S(2)}) collective-permute-start(f32[18,128]{1,0:T(8,128)S(1)} %join.16.refs_0_), channel_id=1, source_target_pairs={{0,4},{1,5},{2,6},{3,7},{4,0},{5,1},{6,2},{7,3},{8,12},{9,13},{10,... | collective-permute-start | bytes 27656 | tf_op jit(solution)/shard_map/ppermute | solution.py:175
  113.5 4.6 %collective-permute-start.44 = (f32[18,128]{1,0:T(8,128)S(1)}, f32[18,128]{1,0:T(8,128)S(1)}, u32[]{:S(2)}, u32[]{:S(2)}) collective-permute-start(f32[18,128]{1,0:T(8,128)S(1)} %join.16.refs_0_), channel_id=1, source_target_pairs={{0,12},{1,13},{2,14},{3,15},{4,8},{5,9},{6,10},{7,11},{8,4},{9,5},... | collective-permute-start | bytes 27656 | tf_op jit(solution)/shard_map/ppermute | solution.py:175
  124.6 4.9 %collective-permute-start.48 = (f32[72,128]{1,0:T(8,128)S(1)}, f32[72,128]{1,0:T(8,128)S(1)}, u32[]{:S(2)}, u32[]{:S(2)}) collective-permute-start(f32[72,128]{1,0:T(8,128)S(1)} %get-tuple-element.224.refs_0_), channel_id=1, source_target_pairs={{0,16},{1,17},{2,18},{3,19},{4,20},{5,21},{6,22},{7,23},{8,24},{9,... | collective-permute-start | bytes 110600 | tf_op jit(solution)/shard_map/ppermute | solution.py:166
  125.7 12.6 %collective-permute-start.55 = (f32[64,128]{1,0:T(8,128)S(1)}, f32[64,128]{1,0:T(8,128)S(1)}, u32[]{:S(2)}, u32[]{:S(2)}) collective-permute-start(f32[64,128]{1,0:T(8,128)S(1)} %get-tuple-element.225), channel_id=1, source_target_pairs={{0,1},{2,3},{4,5},{6,7},{8,9},{10,11},{12,13},{14,15},{16,17},{18,... | collective-permute-start | bytes 98312 | tf_op jit(solution)/shard_map/ppermute | solution.py:166
  125.7 12.6 %collective-permute-start.56 = (f32[64,128]{1,0:T(8,128)S(1)}, f32[64,128]{1,0:T(8,128)S(1)}, u32[]{:S(2)}, u32[]{:S(2)}) collective-permute-start(f32[64,128]{1,0:T(8,128)S(1)} %get-tuple-element.226), channel_id=1, source_target_pairs={{1,2},{3,4},{5,6},{7,8},{9,10},{11,12},{13,14},{15,16},{17,18},{19... | collective-permute-start | bytes 98312 | tf_op jit(solution)/shard_map/ppermute | solution.py:166
  131.9 4.5 %collective-permute-start.51 = (f32[2,128]{1,0:T(2,128)S(1)}, f32[2,128]{1,0:T(2,128)S(1)}, u32[]{:S(2)}, u32[]{:S(2)}) collective-permute-start(f32[2,128]{1,0:T(2,128)S(1)} %join.18.refs_0_), channel_id=1, source_target_pairs={{0,12},{1,13},{2,14},{3,15},{4,8},{5,9},{6,10},{7,11},{8,4},{9,5},... | collective-permute-start | bytes 3080 | tf_op jit(solution)/shard_map/ppermute | solution.py:175
  (36 other events, 132.8 us)

commit v6 on v5

--- a/solution.py
+++ b/solution.py
@@ -165,15 +165,15 @@
     def exchange(arrays):
         return [lax.ppermute(array, AXIS, chosen[i][0]) for i, array in enumerate(arrays)]
 
-    def gather(own, got, lines, after):
+    def gather(own, got, lines, after=()):
         pieces, start = [own, got], cases
         for distances in rounds[1:]:
             def join(i, o):
                 o.block[...] = jnp.concatenate([ref[start:start + lines] for ref in i.pieces], axis=0)
 
-            block = stage("join", join, dict(pieces=pieces, after=after), dict(block=((lines * len(pieces), 2 * cases), F32))).block
+            block = stage("join", join, dict(pieces=pieces, after=list(after)), dict(block=((lines * len(pieces), 2 * cases), F32))).block
             pieces = [block] + [lax.ppermute(block, AXIS, [(i, i ^ far) for i in range(total)]) for far in distances]
-            start, lines, after = 0, block.shape[0], []
+            start, lines, after = 0, block.shape[0], ()
         return pieces
 
     def both_sums(pieces, stride):
@@ -262,7 +262,8 @@
         rows = jnp.concatenate(rows, axis=0)
         image = times(functions, i.stiff[0][...], i.stiff[1][...])
         image_faces = times(functions, i.stiff[2][...], i.stiff[3][...], NT)
-        o.reach[0][...], o.reach[1][...] = split(jnp.concatenate([functions, image, image_faces], axis=1))
+        o.reach[0][...], o.reach[1][...] = split(jnp.concatenate([functions, image], axis=1))
+        o.reach_faces[0][...], o.reach_faces[1][...] = split(image_faces)
         me = lax.axis_index(AXIS)
         count = i.place.shape[1]
         for upper in range(2):
@@ -275,11 +276,10 @@
 
     place = jnp.asarray(np.repeat(np.array(places, np.int32), lines_a_block)[None])
     line = jnp.asarray(np.tile(np.arange(lines_a_block, dtype=np.int32), total)[None])
-    wide = 2 * ndof + slots
     reached = stage(
         "reach", reach,
         dict(weighted=start.weighted, inv=coarse_inv, came=came, picker=picker, stiff=stiff[:4], place=place, line=line),
-        dict(reach=[((own_rows, wide), BF)] * 2, rows=((2 * own_rows, total * lines_a_block), F32)))
+        dict(reach=[((own_rows, 2 * ndof), BF)] * 2, reach_faces=[((own_rows, slots), BF)] * 2, rows=((2 * own_rows, total * lines_a_block), F32)))
 
     def to_solve(came, own, coef=None, sums=None):
         def body(i, o):
@@ -334,15 +334,15 @@
         rows = jnp.concatenate([ref[...] for ref in i.everyone], axis=0)
         product = times(i.rows[...], *split(rows))
         factors = (product[:own_rows, :cases] + product[own_rows:, cases:]).T
+        at_slots = i.image_faces[...] + times(joined(i.came), i.stiff_block[0][...], i.stiff_block[1][...])
+        both = both_sums([ref[...] for ref in i.everyone], lines_a_block)
+        return at_slots + times(factors, i.reach_faces[0][...], i.reach_faces[1][...]), factors, both
+
+    def recur(i, o, step, factors, both):
+        arrived = joined(i.came)
         extra = times(factors, i.reach[0][...], i.reach[1][...])
-        at_slots = i.image_faces[...] + times(joined(i.came), i.stiff_block[0][...], i.stiff_block[1][...]) + extra[:, 2 * ndof:]
-        both = both_sums([ref[...] for ref in i.everyone], lines_a_block)
-        return at_slots, i.v[...] + extra[:, :ndof], i.image[...] + extra[:, ndof:2 * ndof], both
-
-    def recur(i, o, step, inner, image, both):
-        arrived = joined(i.came)
-        inner = inner + pick(arrived, i.picker[...])
-        image = image + times(arrived, i.stiff[0][...], i.stiff[1][...])
+        inner = i.v[...] + pick(arrived, i.picker[...]) + extra[:, :ndof]
+        image = i.image[...] + times(arrived, i.stiff[0][...], i.stiff[1][...]) + extra[:, ndof:]
         weight = i.weight[...]
         if step == 0:
             part, u, residual = image, inner, i.residual[...]
@@ -384,10 +384,11 @@
         sent, came_solve = to_solve(came_image, own, coef, sums)
         applied = to_apply(step, came_image, own, state, coef)
         vars(state).update(vars(applied))
-        everyone = gather(sent, came_solve[paired], lines_a_block, [applied.v])
-        rest_ins = dict(everyone=everyone, rows=reached.rows, reach=reached.reach, came=came_solve, stiff_block=stiff[4:],
-                        image_faces=state.image_faces, v=state.v, image=state.image)
-        ins = dict(came=came_solve, picker=picker, stiff=stiff[2:4], weight=weight, residual=state.residual)
+        everyone = gather(sent, came_solve[paired], lines_a_block)
+        rest_ins = dict(everyone=everyone, rows=reached.rows, reach_faces=reached.reach_faces, came=came_solve, stiff_block=stiff[4:],
+                        image_faces=state.image_faces)
+        ins = dict(came=came_solve, picker=picker, stiff=stiff[2:4], weight=weight, residual=state.residual, reach=reached.reach,
+                   v=state.v, image=state.image)
         outs = dict(u=vec, w_part=vec)
         if step > 0:
             ins.update(w=state.w, u=state.u)
@@ -398,9 +399,9 @@
             ins.update(coef=coef, q=state.q, s=state.s, p=state.p, x=state.x, z=state.z)
         if final:
             def last(i, o):
-                at_slots, inner, image, both = corrected(i)
+                at_slots, factors, both = corrected(i)
                 put_faces(o.face, at_slots)
-                o.face[paired][cases:] = jnp.broadcast_to(recur(i, o, step, inner, image, both)[1], (8, 2 * cases))
+                o.face[paired][cases:] = jnp.broadcast_to(recur(i, o, step, factors, both)[1], (8, 2 * cases))
 
             ins.update(rest_ins)
             outs.update(face=last_kinds)
@@ -410,17 +411,17 @@
             break
 
         def apply_rest(i, o):
-            at_slots, o.inner[...], o.image[...], o.sums[...] = corrected(i)
+            at_slots, o.factors[...], o.sums[...] = corrected(i)
             put_faces(o.face, at_slots)
 
-        made = stage("apply_rest", apply_rest, rest_ins, dict(face=face_kinds, inner=vec, image=vec, sums=pair))
+        made = stage("apply_rest", apply_rest, rest_ins, dict(face=face_kinds, factors=((cases, own_rows), F32), sums=pair))
         came_image = exchange(made.face)
 
         def update(i, o, step=step):
-            part, o.sums[...] = recur(i, o, step, i.inner[...], i.image[...], i.both[...])
+            part, o.sums[...] = recur(i, o, step, i.factors[...], i.both[...])
             solve_own(part, i, o)
 
-        ins.update(inner=made.inner, image=made.image, both=made.sums, weighted=start.weighted, inv=inv[:4])
+        ins.update(factors=made.factors, both=made.sums, weighted=start.weighted, inv=inv[:4])
         outs.update(own_kinds, sums=pair)
         own = stage("update", update, ins, outs)
         vars(state).update(vars(own))
@@ -438,7 +439,7 @@
         o.remainder[0] = i.residual[...] - alpha * (w + beta * i.s[...])
 
     whole = ((1, cases, ndof), F32)
-    everyone = gather(state.face[paired], came_image[paired], 1, [])
+    everyone = gather(state.face[paired], came_image[paired], 1)
     done = stage(
         "finish", finish,
         dict(everyone=everyone, came=came_image, picker=picker, coef=state.coef, w_part=state.w_part, x=state.x, u=state.u, p=state.p,

time: 142 us -> 137 us (0.965)
  starting transfers between devices: 70.9 us -> 67.3 us
    ppermute x30, waiting for transfers between devices: 25.5 us -> 18.9 us  [gather(): lax.ppermute(block, AXIS, [(i, i ^ far) for i in range(total)])]
    ppermute x27, waiting for transfers between devices: 6.41 us -> 12.3 us  [exchange(): lax.ppermute(array, AXIS, chosen[i][0])]
    ppermute x30, starting transfers between devices: 34 us -> 28.2 us  [gather(): lax.ppermute(block, AXIS, [(i, i ^ far) for i in range(total)])]
    ppermute x27, starting transfers between devices: 36.9 us -> 39.1 us  [exchange(): lax.ppermute(array, AXIS, chosen[i][0])]
  transfers between devices with their start and end apart: 57 -> 57, of which waited for: 25 -> 23; matrix products, arithmetic and copies ran while one was open for 0% -> 0% of each run, Pallas kernels for 17% -> 18%
where the time goes in v6:
time: 137 us; the launch traced here: 136 us
  starting transfers between devices  67.3 us (49%)
  waiting for transfers between devices  31.2 us (23%)
  Pallas kernels  30.7 us (22%)
  local copies, waits for them, and re-layouts  6.09 us (4%)
    ppermute x27, starting transfers between devices, exchange(): lax.ppermute(array, AXIS, chosen[i][0])  39.1 us
    pallas_call x31, Pallas kernels, stage(): pl.pallas_call(kernel, name=name, out_shape=[jax.ShapeDtypeStruct(*kind)...  30.7 us
    ppermute x30, starting transfers between devices, gather(): lax.ppermute(block, AXIS, [(i, i ^ far) for i in range(total)])  28.2 us
    ppermute x30, waiting for transfers between devices, gather(): lax.ppermute(block, AXIS, [(i, i ^ far) for i in range(total)])  18.9 us
    ppermute x27, waiting for transfers between devices, exchange(): lax.ppermute(array, AXIS, chosen[i][0])  12.3 us
    unnamed x22, local copies, waits for them, and re-layouts  6.09 us
  transfers between devices with their start and end apart: 57, of which 23 were waited for; matrix products, arithmetic and copies ran while one was open for 0% of the time, Pallas kernels for 18%

profile of v6, /device:TPU:0, one launch (start us, length us, event | category | flops | bytes accessed | tf_op | source)
XLA Modules:
  0.0 136.5 jit_solution(548682632468493704)
XLA Ops:
  6.7 7.3 %collective-permute-start.2 = (f32[144,128]{1,0:T(8,128)S(1)}, f32[144,128]{1,0:T(8,128)S(1)}, u32[]{:S(2)}, u32[]{:S(2)}) collective-permute-start(f32[144,128]{1,0:T(8,128)S(1)} %get-tuple-element.119), channel_id=1, source_target_pairs={{0,16},{1,17},{2,18},{3,19},{4,20},{5,21},{6,22},{7,23},{8,24},{9,... | collective-permute-start | bytes 221192 | tf_op jit(solution)/shard_map/ppermute | solution.py:166
  14.0 2.2 %copy-done = f32[1,1024,1024]{2,1,0:T(8,128)S(1)} copy-done((f32[1,1024,1024]{2,1,0:T(8,128)S(1)}, f32[1,1024,1024]{2,1,0:T(8,128)}, u32[]{:S(2)}) %copy-start) | copy-done | bytes 4194328
  16.2 2.7 %prepare_inv.1 = (bf16[1024,1024]{1,0:T(8,128)(2,1)S(1)}, bf16[1024,1024]{1,0:T(8,128)(2,1)S(1)}, bf16[384,1024]{1,0:T(8,128)(2,1)S(1)}, bf16[384,1024]{1,0:T(8,...) custom-call(f32[1,1024,1024]{2,1,0:T(8,128)S(1)} %copy-done, ...), custom_call_target="tpu_custom_call" | custom-call | tf_op jit(solution)/shard_map/prepare_inv/pallas_call | solution.py:92
  21.3 4.2 %collective-permute-done.3.refs_1_.refs_9_.refs_2_ = f32[73,128]{1,0:T(8,128)S(1)} collective-permute-done((f32[73,128]{1,0:T(8,128)S(1)}, f32[73,128]{1,0:T(8,128)S(1)}, u32[]{:S(2)}, u32[]{:S(2)}) %collective-permute-start.3) | collective-permute-done | bytes 37408 | tf_op jit(solution)/shard_map/ppermute | solution.py:166
  30.1 2.2 %collective-permute-done.6.refs_3_ = f32[18,128]{1,0:T(8,128)S(1)} collective-permute-done((f32[18,128]{1,0:T(8,128)S(1)}, f32[18,128]{1,0:T(8,128)S(1)}, u32[]{:S(2)}, u32[]{:S(2)}) %collective-permute-start.6) | collective-permute-done | bytes 9248 | tf_op jit(solution)/shard_map/ppermute | solution.py:175
  34.5 2.7 %prepare_stiff.1 = (bf16[1024,1024]{1,0:T(8,128)(2,1)S(1)}, bf16[1024,1024]{1,0:T(8,128)(2,1)S(1)}, bf16[384,1024]{1,0:T(8,128)(2,1)S(1)}, bf16[384,1024]{1,0:T(...) custom-call(f32[1,1024,1024]{2,1,0:T(8,128)S(1)} %copy-done.1, ...), custom_call_target="tpu_custom_call" | custom-call | tf_op jit(solution)/shard_map/prepare_stiff/pallas_call | solution.py:92
  37.2 2.0 %apply_own.4 = (f32[64,1024]{1,0:T(8,128)S(1)}, f32[64,384]{1,0:T(8,128)S(1)}, f32[64,1024]{1,0:T(8,128)S(1)}, f32[64,1024]{1,0:T(8,128)S(1)}) custom-call(f32[144,128]{1,0:T(8,128)S(1)} %collective-permute-done.refs_0_.refs_2_, f32[144,128]{1,0:T(8,128)S(1)} %collective-permute-done.1.refs_1_.refs_3_, ...), custom_call_target="tpu_custom_call" | custom-call | tf_op jit(solution)/shard_map/apply_own/pallas_call | solution.py:92
  42.6 3.6 %collective-permute-start.14 = (f32[64,128]{1,0:T(8,128)S(1)}, f32[64,128]{1,0:T(8,128)S(1)}, u32[]{:S(2)}, u32[]{:S(2)}) collective-permute-start(f32[64,128]{1,0:T(8,128)S(1)} %get-tuple-element.149), channel_id=1, source_target_pairs={{0,16},{1,17},{2,18},{3,19},{4,20},{5,21},{6,22},{7,23},{8,24},{9,... | collective-permute-start | bytes 98312 | tf_op jit(solution)/shard_map/ppermute | solution.py:166
  46.1 2.4 %update.3 = (f32[64,1024]{1,0:T(8,128)S(1)}, f32[64,1024]{1,0:T(8,128)S(1)}, f32[16,64]{1,0:T(8,128)S(1)}, f32[64,384]{1,0:T(8,128)S(1)}, f32[64,1024]{1,0:T(8,128)S(1)}, /*index=5*/f32[1,128]{1,0:T(1,128)S(1)}) custom-call(f32[64,128]{1,0:T(8,128)S(1)} %collective-permute-done.10.refs_7_.refs_0_, f32[128,128]{1,0:T(8,128)S(1)} %collective-permute-done.11.refs_8_.refs_1_, ...), custom_call_target="tpu_custom_call" | custom-call | tf_op jit(solution)/shard_map/update/pallas_call | solution.py:92
  48.8 2.4 %collective-permute-start.15 = (f32[73,128]{1,0:T(8,128)S(1)}, f32[73,128]{1,0:T(8,128)S(1)}, u32[]{:S(2)}, u32[]{:S(2)}) collective-permute-start(f32[73,128]{1,0:T(8,128)S(1)} %get-tuple-element.160.refs_0_), channel_id=1, source_target_pairs={{0,16},{1,17},{2,18},{3,19},{4,20},{5,21},{6,22},{7,23},{8,24},{9,... | collective-permute-start | bytes 112136 | tf_op jit(solution)/shard_map/ppermute | solution.py:166
  51.9 1.9 %collective-permute-done.15.refs_1_.refs_9_.refs_2_ = f32[73,128]{1,0:T(8,128)S(1)} collective-permute-done((f32[73,128]{1,0:T(8,128)S(1)}, f32[73,128]{1,0:T(8,128)S(1)}, u32[]{:S(2)}, u32[]{:S(2)}) %collective-permute-start.15) | collective-permute-done | bytes 37408 | tf_op jit(solution)/shard_map/ppermute | solution.py:166
  53.8 2.8 %collective-permute-start.16 = (f32[18,128]{1,0:T(8,128)S(1)}, f32[18,128]{1,0:T(8,128)S(1)}, u32[]{:S(2)}, u32[]{:S(2)}) collective-permute-start(f32[18,128]{1,0:T(8,128)S(1)} %join.12.refs_0_), channel_id=1, source_target_pairs={{0,4},{1,5},{2,6},{3,7},{4,0},{5,1},{6,2},{7,3},{8,12},{9,13},{10,... | collective-permute-start | bytes 27656 | tf_op jit(solution)/shard_map/ppermute | solution.py:175
  58.2 2.0 %collective-permute-done.17.refs_2_ = f32[18,128]{1,0:T(8,128)S(1)} collective-permute-done((f32[18,128]{1,0:T(8,128)S(1)}, f32[18,128]{1,0:T(8,128)S(1)}, u32[]{:S(2)}, u32[]{:S(2)}) %collective-permute-start.17) | collective-permute-done | bytes 9248 | tf_op jit(solution)/shard_map/ppermute | solution.py:175
  63.5 2.0 %apply_own.5 = (f32[64,1024]{1,0:T(8,128)S(1)}, f32[64,384]{1,0:T(8,128)S(1)}, f32[64,1024]{1,0:T(8,128)S(1)}, f32[64,1024]{1,0:T(8,128)S(1)}) custom-call(f32[64,128]{1,0:T(8,128)S(1)} %collective-permute-done.12.refs_0_, f32[64,128]{1,0:T(8,128)S(1)} %collective-permute-done.13.refs_1_, f32[64,128]{1,0:T(8,128)S(1)} %collective-permute-done.14.refs_2_, ...), custom_call_target="tpu_custom_call" | custom-call | tf_op jit(solution)/shard_map/apply_own/pallas_call | solution.py:92
  67.3 5.6 %collective-permute-start.26 = (f32[64,128]{1,0:T(8,128)S(1)}, f32[64,128]{1,0:T(8,128)S(1)}, u32[]{:S(2)}, u32[]{:S(2)}) collective-permute-start(f32[64,128]{1,0:T(8,128)S(1)} %get-tuple-element.168), channel_id=1, source_target_pairs={{0,16},{1,17},{2,18},{3,19},{4,20},{5,21},{6,22},{7,23},{8,24},{9,... | collective-permute-start | bytes 98312 | tf_op jit(solution)/shard_map/ppermute | solution.py:166
  72.9 2.5 %update.4 = (f32[64,1024]{1,0:T(8,128)S(1)}, f32[64,1024]{1,0:T(8,128)S(1)}, f32[1,128]{1,0:T(1,128)S(1)}, f32[64,1024]{1,0:T(8,128)S(1)}, f32[64,1024]{1,0:T(8,...) custom-call(f32[64,128]{1,0:T(8,128)S(1)} %collective-permute-done.2, ...), custom_call_target="tpu_custom_call" | custom-call | tf_op jit(solution)/shard_map/update/pallas_call | solution.py:92
  75.8 2.4 %collective-permute-start.27 = (f32[73,128]{1,0:T(8,128)S(1)}, f32[73,128]{1,0:T(8,128)S(1)}, u32[]{:S(2)}, u32[]{:S(2)}) collective-permute-start(f32[73,128]{1,0:T(8,128)S(1)} %get-tuple-element.179.refs_0_), channel_id=1, source_target_pairs={{0,16},{1,17},{2,18},{3,19},{4,20},{5,21},{6,22},{7,23},{8,24},{9,... | collective-permute-start | bytes 112136 | tf_op jit(solution)/shard_map/ppermute | solution.py:166
  78.9 1.9 %collective-permute-done.27.refs_1_.refs_9_.refs_2_ = f32[73,128]{1,0:T(8,128)S(1)} collective-permute-done((f32[73,128]{1,0:T(8,128)S(1)}, f32[73,128]{1,0:T(8,128)S(1)}, u32[]{:S(2)}, u32[]{:S(2)}) %collective-permute-start.27) | collective-permute-done | bytes 37408 | tf_op jit(solution)/shard_map/ppermute | solution.py:166
  81.6 1.7 %collective-permute-start.29 = (f32[18,128]{1,0:T(8,128)S(1)}, f32[18,128]{1,0:T(8,128)S(1)}, u32[]{:S(2)}, u32[]{:S(2)}) collective-permute-start(f32[18,128]{1,0:T(8,128)S(1)} %join.14.refs_0_), channel_id=1, source_target_pairs={{0,8},{1,9},{2,10},{3,11},{4,12},{5,13},{6,14},{7,15},{8,0},{9,1},... | collective-permute-start | bytes 27656 | tf_op jit(solution)/shard_map/ppermute | solution.py:175
  85.3 2.6 %collective-permute-done.30.refs_3_ = f32[18,128]{1,0:T(8,128)S(1)} collective-permute-done((f32[18,128]{1,0:T(8,128)S(1)}, f32[18,128]{1,0:T(8,128)S(1)}, u32[]{:S(2)}, u32[]{:S(2)}) %collective-permute-start.30) | collective-permute-done | bytes 9248 | tf_op jit(solution)/shard_map/ppermute | solution.py:175
  90.2 2.2 %apply_own.6 = (f32[64,1024]{1,0:T(8,128)S(1)}, f32[64,384]{1,0:T(8,128)S(1)}, f32[64,1024]{1,0:T(8,128)S(1)}, f32[64,1024]{1,0:T(8,128)S(1)}, f32[64,1024]{1,0:T(8,128)S(1)}) custom-call(f32[64,128]{1,0:T(8,128)S(1)} %collective-permute-done.24.refs_0_, f32[64,128]{1,0:T(8,128)S(1)} %collective-permute-done.25.refs_1_, ...), custom_call_target="tpu_custom_call" | custom-call | tf_op jit(solution)/shard_map/apply_own/pallas_call | solution.py:92
  94.1 4.1 %collective-permute-start.38 = (f32[64,128]{1,0:T(8,128)S(1)}, f32[64,128]{1,0:T(8,128)S(1)}, u32[]{:S(2)}, u32[]{:S(2)}) collective-permute-start(f32[64,128]{1,0:T(8,128)S(1)} %get-tuple-element.188), channel_id=1, source_target_pairs={{0,16},{1,17},{2,18},{3,19},{4,20},{5,21},{6,22},{7,23},{8,24},{9,... | collective-permute-start | bytes 98312 | tf_op jit(solution)/shard_map/ppermute | solution.py:166
  98.2 2.5 %update.5 = (f32[64,1024]{1,0:T(8,128)S(1)}, f32[64,1024]{1,0:T(8,128)S(1)}, f32[1,128]{1,0:T(1,128)S(1)}, f32[64,1024]{1,0:T(8,128)S(1)}, f32[64,1024]{1,0:T(8,...) custom-call(f32[64,128]{1,0:T(8,128)S(1)} %collective-permute-done.3, ...), custom_call_target="tpu_custom_call" | custom-call | tf_op jit(solution)/shard_map/update/pallas_call | solution.py:92
  101.3 2.3 %collective-permute-start.41 = (f32[73,128]{1,0:T(8,128)S(1)}, f32[73,128]{1,0:T(8,128)S(1)}, u32[]{:S(2)}, u32[]{:S(2)}) collective-permute-start(f32[73,128]{1,0:T(8,128)S(1)} %get-tuple-element.207.refs_0_), channel_id=1, source_target_pairs={{0,16},{1,17},{2,18},{3,19},{4,20},{5,21},{6,22},{7,23},{8,24},{9,... | collective-permute-start | bytes 112136 | tf_op jit(solution)/shard_map/ppermute | solution.py:166
  104.2 2.0 %collective-permute-done.41.refs_1_.refs_2_ = f32[73,128]{1,0:T(8,128)S(1)} collective-permute-done((f32[73,128]{1,0:T(8,128)S(1)}, f32[73,128]{1,0:T(8,128)S(1)}, u32[]{:S(2)}, u32[]{:S(2)}) %collective-permute-start.41) | collective-permute-done | bytes 37408 | tf_op jit(solution)/shard_map/ppermute | solution.py:166
  106.3 2.0 %collective-permute-start.42 = (f32[18,128]{1,0:T(8,128)S(1)}, f32[18,128]{1,0:T(8,128)S(1)}, u32[]{:S(2)}, u32[]{:S(2)}) collective-permute-start(f32[18,128]{1,0:T(8,128)S(1)} %join.16.refs_0_), channel_id=1, source_target_pairs={{0,4},{1,5},{2,6},{3,7},{4,0},{5,1},{6,2},{7,3},{8,12},{9,13},{10,... | collective-permute-start | bytes 27656 | tf_op jit(solution)/shard_map/ppermute | solution.py:175
  110.0 2.0 %collective-permute-done.43.refs_2_ = f32[18,128]{1,0:T(8,128)S(1)} collective-permute-done((f32[18,128]{1,0:T(8,128)S(1)}, f32[18,128]{1,0:T(8,128)S(1)}, u32[]{:S(2)}, u32[]{:S(2)}) %collective-permute-start.43) | collective-permute-done | bytes 9248 | tf_op jit(solution)/shard_map/ppermute | solution.py:175
  115.3 2.2 %apply_own.7 = (f32[64,1024]{1,0:T(8,128)S(1)}, f32[64,384]{1,0:T(8,128)S(1)}, f32[64,1024]{1,0:T(8,128)S(1)}, f32[64,1024]{1,0:T(8,128)S(1)}, f32[64,1024]{1,0:T(8,128)S(1)}) custom-call(f32[64,128]{1,0:T(8,128)S(1)} %collective-permute-done.36.refs_0_, f32[64,128]{1,0:T(8,128)S(1)} %collective-permute-done.37.refs_1_, ...), custom_call_target="tpu_custom_call" | custom-call | tf_op jit(solution)/shard_map/apply_own/pallas_call | solution.py:92
  119.3 2.5 %collective-permute-start.48 = (f32[72,128]{1,0:T(8,128)S(1)}, f32[72,128]{1,0:T(8,128)S(1)}, u32[]{:S(2)}, u32[]{:S(2)}) collective-permute-start(f32[72,128]{1,0:T(8,128)S(1)} %get-tuple-element.222.refs_0_), channel_id=1, source_target_pairs={{0,16},{1,17},{2,18},{3,19},{4,20},{5,21},{6,22},{7,23},{8,24},{9,... | collective-permute-start | bytes 110600 | tf_op jit(solution)/shard_map/ppermute | solution.py:166
  122.5 2.1 %collective-permute-done.48.refs_1_.refs_6_ = f32[72,128]{1,0:T(8,128)S(1)} collective-permute-done((f32[72,128]{1,0:T(8,128)S(1)}, f32[72,128]{1,0:T(8,128)S(1)}, u32[]{:S(2)}, u32[]{:S(2)}) %collective-permute-start.48) | collective-permute-done | bytes 36896 | tf_op jit(solution)/shard_map/ppermute | solution.py:166
  124.5 1.8 %collective-permute-start.49 = (f32[2,128]{1,0:T(2,128)S(1)}, f32[2,128]{1,0:T(2,128)S(1)}, u32[]{:S(2)}, u32[]{:S(2)}) collective-permute-start(f32[2,128]{1,0:T(2,128)S(1)} %join.18.refs_0_), channel_id=1, source_target_pairs={{0,4},{1,5},{2,6},{3,7},{4,0},{5,1},{6,2},{7,3},{8,12},{9,13},{10,... | collective-permute-start | bytes 3080 | tf_op jit(solution)/shard_map/ppermute | solution.py:175
  133.5 1.8 %collective-permute-done.53.refs_2_ = f32[8,128]{1,0:T(8,128)S(1)} collective-permute-done((f32[8,128]{1,0:T(8,128)S(1)}, f32[8,128]{1,0:T(8,128)S(1)}, u32[]{:S(2)}, u32[]{:S(2)}) %collective-permute-start.53) | collective-permute-done | bytes 4128 | tf_op jit(solution)/shard_map/ppermute | solution.py:175
  (135 shorter events, 50.8 us)
Async XLA Ops:
  5.5 14.7 %collective-permute-start = (f32[144,128]{1,0:T(8,128)S(1)}, f32[144,128]{1,0:T(8,128)S(1)}, u32[]{:S(2)}, u32[]{:S(2)}) collective-permute-start(f32[144,128]{1,0:T(8,128)S(1)} %get-tuple-element.117), channel_id=1, source_target_pairs={{0,1},{2,3},{4,5},{6,7},{8,9},{10,11},{12,13},{14,15},{16,17},{18,... | collective-permute-start | bytes 221192 | tf_op jit(solution)/shard_map/ppermute | solution.py:166
  6.0 14.2 %collective-permute-start.1 = (f32[144,128]{1,0:T(8,128)S(1)}, f32[144,128]{1,0:T(8,128)S(1)}, u32[]{:S(2)}, u32[]{:S(2)}) collective-permute-start(f32[144,128]{1,0:T(8,128)S(1)} %get-tuple-element.118), channel_id=1, source_target_pairs={{1,2},{3,4},{5,6},{7,8},{9,10},{11,12},{13,14},{15,16},{17,18},{19... | collective-permute-start | bytes 221192 | tf_op jit(solution)/shard_map/ppermute | solution.py:166
  6.7 13.6 %collective-permute-start.2 = (f32[144,128]{1,0:T(8,128)S(1)}, f32[144,128]{1,0:T(8,128)S(1)}, u32[]{:S(2)}, u32[]{:S(2)}) collective-permute-start(f32[144,128]{1,0:T(8,128)S(1)} %get-tuple-element.119), channel_id=1, source_target_pairs={{0,16},{1,17},{2,18},{3,19},{4,20},{5,21},{6,22},{7,23},{8,24},{9,... | collective-permute-start | bytes 221192 | tf_op jit(solution)/shard_map/ppermute | solution.py:166
  20.5 5.0 %collective-permute-start.3 = (f32[73,128]{1,0:T(8,128)S(1)}, f32[73,128]{1,0:T(8,128)S(1)}, u32[]{:S(2)}, u32[]{:S(2)}) collective-permute-start(f32[73,128]{1,0:T(8,128)S(1)} %get-tuple-element.133.refs_0_), channel_id=1, source_target_pairs={{0,16},{1,17},{2,18},{3,19},{4,20},{5,21},{6,22},{7,23},{8,24},{9,... | collective-permute-start | bytes 112136 | tf_op jit(solution)/shard_map/ppermute | solution.py:166
  20.6 20.3 %collective-permute-start.11 = (f32[128,128]{1,0:T(8,128)S(1)}, f32[128,128]{1,0:T(8,128)S(1)}, u32[]{:S(2)}, u32[]{:S(2)}) collective-permute-start(f32[128,128]{1,0:T(8,128)S(1)} %get-tuple-element.142), channel_id=1, source_target_pairs={{1,2},{3,4},{5,6},{7,8},{9,10},{11,12},{13,14},{15,16},{17,18},{19... | collective-permute-start | bytes 196616 | tf_op jit(solution)/shard_map/ppermute | solution.py:166
  27.7 4.6 %collective-permute-start.6 = (f32[18,128]{1,0:T(8,128)S(1)}, f32[18,128]{1,0:T(8,128)S(1)}, u32[]{:S(2)}, u32[]{:S(2)}) collective-permute-start(f32[18,128]{1,0:T(8,128)S(1)} %join.10.refs_0_), channel_id=1, source_target_pairs={{0,12},{1,13},{2,14},{3,15},{4,8},{5,9},{6,10},{7,11},{8,4},{9,5},... | collective-permute-start | bytes 27656 | tf_op jit(solution)/shard_map/ppermute | solution.py:175
  32.3 8.6 %collective-permute-start.7 = (f32[72,128]{1,0:T(8,128)S(1)}, f32[72,128]{1,0:T(8,128)S(1)}, u32[]{:S(2)}, u32[]{:S(2)}) collective-permute-start(f32[72,128]{1,0:T(8,128)S(1)} %join.11.refs_0_), channel_id=1, source_target_pairs={{0,1},{1,0},{2,3},{3,2},{4,5},{5,4},{6,7},{7,6},{8,9},{9,8},{10,11... | collective-permute-start | bytes 110600 | tf_op jit(solution)/shard_map/ppermute | solution.py:175
  32.3 8.6 %collective-permute-start.8 = (f32[72,128]{1,0:T(8,128)S(1)}, f32[72,128]{1,0:T(8,128)S(1)}, u32[]{:S(2)}, u32[]{:S(2)}) collective-permute-start(f32[72,128]{1,0:T(8,128)S(1)} %join.11.refs_0_), channel_id=1, source_target_pairs={{0,2},{1,3},{2,0},{3,1},{4,6},{5,7},{6,4},{7,5},{8,10},{9,11},{10,... | collective-permute-start | bytes 110600 | tf_op jit(solution)/shard_map/ppermute | solution.py:175
  33.0 8.0 %collective-permute-start.9 = (f32[72,128]{1,0:T(8,128)S(1)}, f32[72,128]{1,0:T(8,128)S(1)}, u32[]{:S(2)}, u32[]{:S(2)}) collective-permute-start(f32[72,128]{1,0:T(8,128)S(1)} %join.11.refs_0_), channel_id=1, source_target_pairs={{0,3},{1,2},{2,1},{3,0},{4,7},{5,6},{6,5},{7,4},{8,11},{9,10},{10,... | collective-permute-start | bytes 110600 | tf_op jit(solution)/shard_map/ppermute | solution.py:175
  34.2 6.8 %collective-permute-start.10 = (f32[64,128]{1,0:T(8,128)S(1)}, f32[64,128]{1,0:T(8,128)S(1)}, u32[]{:S(2)}, u32[]{:S(2)}) collective-permute-start(f32[64,128]{1,0:T(8,128)S(1)} %get-tuple-element.141), channel_id=1, source_target_pairs={{0,1},{2,3},{4,5},{6,7},{8,9},{10,11},{12,13},{14,15},{16,17},{18,... | collective-permute-start | bytes 98312 | tf_op jit(solution)/shard_map/ppermute | solution.py:166
  41.5 7.0 %collective-permute-start.12 = (f32[64,128]{1,0:T(8,128)S(1)}, f32[64,128]{1,0:T(8,128)S(1)}, u32[]{:S(2)}, u32[]{:S(2)}) collective-permute-start(f32[64,128]{1,0:T(8,128)S(1)} %get-tuple-element.147), channel_id=1, source_target_pairs={{0,1},{2,3},{4,5},{6,7},{8,9},{10,11},{12,13},{14,15},{16,17},{18,... | collective-permute-start | bytes 98312 | tf_op jit(solution)/shard_map/ppermute | solution.py:166
  41.7 6.8 %collective-permute-start.13 = (f32[64,128]{1,0:T(8,128)S(1)}, f32[64,128]{1,0:T(8,128)S(1)}, u32[]{:S(2)}, u32[]{:S(2)}) collective-permute-start(f32[64,128]{1,0:T(8,128)S(1)} %get-tuple-element.148), channel_id=1, source_target_pairs={{1,2},{3,4},{5,6},{7,8},{9,10},{11,12},{13,14},{15,16},{17,18},{19... | collective-permute-start | bytes 98312 | tf_op jit(solution)/shard_map/ppermute | solution.py:166
  42.6 6.0 %collective-permute-start.14 = (f32[64,128]{1,0:T(8,128)S(1)}, f32[64,128]{1,0:T(8,128)S(1)}, u32[]{:S(2)}, u32[]{:S(2)}) collective-permute-start(f32[64,128]{1,0:T(8,128)S(1)} %get-tuple-element.149), channel_id=1, source_target_pairs={{0,16},{1,17},{2,18},{3,19},{4,20},{5,21},{6,22},{7,23},{8,24},{9,... | collective-permute-start | bytes 98312 | tf_op jit(solution)/shard_map/ppermute | solution.py:166
  48.8 5.0 %collective-permute-start.15 = (f32[73,128]{1,0:T(8,128)S(1)}, f32[73,128]{1,0:T(8,128)S(1)}, u32[]{:S(2)}, u32[]{:S(2)}) collective-permute-start(f32[73,128]{1,0:T(8,128)S(1)} %get-tuple-element.160.refs_0_), channel_id=1, source_target_pairs={{0,16},{1,17},{2,18},{3,19},{4,20},{5,21},{6,22},{7,23},{8,24},{9,... | collective-permute-start | bytes 112136 | tf_op jit(solution)/shard_map/ppermute | solution.py:166
  51.3 14.2 %collective-permute-start.23 = (f32[128,128]{1,0:T(8,128)S(1)}, f32[128,128]{1,0:T(8,128)S(1)}, u32[]{:S(2)}, u32[]{:S(2)}) collective-permute-start(f32[128,128]{1,0:T(8,128)S(1)} %get-tuple-element.162), channel_id=1, source_target_pairs={{1,2},{3,4},{5,6},{7,8},{9,10},{11,12},{13,14},{15,16},{17,18},{19... | collective-permute-start | bytes 196616 | tf_op jit(solution)/shard_map/ppermute | solution.py:166
  56.7 4.6 %collective-permute-start.18 = (f32[18,128]{1,0:T(8,128)S(1)}, f32[18,128]{1,0:T(8,128)S(1)}, u32[]{:S(2)}, u32[]{:S(2)}) collective-permute-start(f32[18,128]{1,0:T(8,128)S(1)} %join.12.refs_0_), channel_id=1, source_target_pairs={{0,12},{1,13},{2,14},{3,15},{4,8},{5,9},{6,10},{7,11},{8,4},{9,5},... | collective-permute-start | bytes 27656 | tf_op jit(solution)/shard_map/ppermute | solution.py:175
  66.5 8.9 %collective-permute-start.24 = (f32[64,128]{1,0:T(8,128)S(1)}, f32[64,128]{1,0:T(8,128)S(1)}, u32[]{:S(2)}, u32[]{:S(2)}) collective-permute-start(f32[64,128]{1,0:T(8,128)S(1)} %get-tuple-element.166), channel_id=1, source_target_pairs={{0,1},{2,3},{4,5},{6,7},{8,9},{10,11},{12,13},{14,15},{16,17},{18,... | collective-permute-start | bytes 98312 | tf_op jit(solution)/shard_map/ppermute | solution.py:166
  66.7 8.7 %collective-permute-start.25 = (f32[64,128]{1,0:T(8,128)S(1)}, f32[64,128]{1,0:T(8,128)S(1)}, u32[]{:S(2)}, u32[]{:S(2)}) collective-permute-start(f32[64,128]{1,0:T(8,128)S(1)} %get-tuple-element.167), channel_id=1, source_target_pairs={{1,2},{3,4},{5,6},{7,8},{9,10},{11,12},{13,14},{15,16},{17,18},{19... | collective-permute-start | bytes 98312 | tf_op jit(solution)/shard_map/ppermute | solution.py:166
  67.3 8.1 %collective-permute-start.26 = (f32[64,128]{1,0:T(8,128)S(1)}, f32[64,128]{1,0:T(8,128)S(1)}, u32[]{:S(2)}, u32[]{:S(2)}) collective-permute-start(f32[64,128]{1,0:T(8,128)S(1)} %get-tuple-element.168), channel_id=1, source_target_pairs={{0,16},{1,17},{2,18},{3,19},{4,20},{5,21},{6,22},{7,23},{8,24},{9,... | collective-permute-start | bytes 98312 | tf_op jit(solution)/shard_map/ppermute | solution.py:166
  75.8 5.0 %collective-permute-start.27 = (f32[73,128]{1,0:T(8,128)S(1)}, f32[73,128]{1,0:T(8,128)S(1)}, u32[]{:S(2)}, u32[]{:S(2)}) collective-permute-start(f32[73,128]{1,0:T(8,128)S(1)} %get-tuple-element.179.refs_0_), channel_id=1, source_target_pairs={{0,16},{1,17},{2,18},{3,19},{4,20},{5,21},{6,22},{7,23},{8,24},{9,... | collective-permute-start | bytes 112136 | tf_op jit(solution)/shard_map/ppermute | solution.py:166
  78.2 14.2 %collective-permute-start.35 = (f32[128,128]{1,0:T(8,128)S(1)}, f32[128,128]{1,0:T(8,128)S(1)}, u32[]{:S(2)}, u32[]{:S(2)}) collective-permute-start(f32[128,128]{1,0:T(8,128)S(1)} %get-tuple-element.181), channel_id=1, source_target_pairs={{1,2},{3,4},{5,6},{7,8},{9,10},{11,12},{13,14},{15,16},{17,18},{19... | collective-permute-start | bytes 196616 | tf_op jit(solution)/shard_map/ppermute | solution.py:166
  83.3 4.6 %collective-permute-start.30 = (f32[18,128]{1,0:T(8,128)S(1)}, f32[18,128]{1,0:T(8,128)S(1)}, u32[]{:S(2)}, u32[]{:S(2)}) collective-permute-start(f32[18,128]{1,0:T(8,128)S(1)} %join.14.refs_0_), channel_id=1, source_target_pairs={{0,12},{1,13},{2,14},{3,15},{4,8},{5,9},{6,10},{7,11},{8,4},{9,5},... | collective-permute-start | bytes 27656 | tf_op jit(solution)/shard_map/ppermute | solution.py:175
  93.1 7.7 %collective-permute-start.36 = (f32[64,128]{1,0:T(8,128)S(1)}, f32[64,128]{1,0:T(8,128)S(1)}, u32[]{:S(2)}, u32[]{:S(2)}) collective-permute-start(f32[64,128]{1,0:T(8,128)S(1)} %get-tuple-element.186), channel_id=1, source_target_pairs={{0,1},{2,3},{4,5},{6,7},{8,9},{10,11},{12,13},{14,15},{16,17},{18,... | collective-permute-start | bytes 98312 | tf_op jit(solution)/shard_map/ppermute | solution.py:166
  93.2 7.5 %collective-permute-start.37 = (f32[64,128]{1,0:T(8,128)S(1)}, f32[64,128]{1,0:T(8,128)S(1)}, u32[]{:S(2)}, u32[]{:S(2)}) collective-permute-start(f32[64,128]{1,0:T(8,128)S(1)} %get-tuple-element.187), channel_id=1, source_target_pairs={{1,2},{3,4},{5,6},{7,8},{9,10},{11,12},{13,14},{15,16},{17,18},{19... | collective-permute-start | bytes 98312 | tf_op jit(solution)/shard_map/ppermute | solution.py:166
  94.1 6.8 %collective-permute-start.38 = (f32[64,128]{1,0:T(8,128)S(1)}, f32[64,128]{1,0:T(8,128)S(1)}, u32[]{:S(2)}, u32[]{:S(2)}) collective-permute-start(f32[64,128]{1,0:T(8,128)S(1)} %get-tuple-element.188), channel_id=1, source_target_pairs={{0,16},{1,17},{2,18},{3,19},{4,20},{5,21},{6,22},{7,23},{8,24},{9,... | collective-permute-start | bytes 98312 | tf_op jit(solution)/shard_map/ppermute | solution.py:166
  101.3 5.0 %collective-permute-start.41 = (f32[73,128]{1,0:T(8,128)S(1)}, f32[73,128]{1,0:T(8,128)S(1)}, u32[]{:S(2)}, u32[]{:S(2)}) collective-permute-start(f32[73,128]{1,0:T(8,128)S(1)} %get-tuple-element.207.refs_0_), channel_id=1, source_target_pairs={{0,16},{1,17},{2,18},{3,19},{4,20},{5,21},{6,22},{7,23},{8,24},{9,... | collective-permute-start | bytes 112136 | tf_op jit(solution)/shard_map/ppermute | solution.py:166
  103.6 14.0 %collective-permute-start.40 = (f32[128,128]{1,0:T(8,128)S(1)}, f32[128,128]{1,0:T(8,128)S(1)}, u32[]{:S(2)}, u32[]{:S(2)}) collective-permute-start(f32[128,128]{1,0:T(8,128)S(1)} %get-tuple-element.206), channel_id=1, source_target_pairs={{1,2},{3,4},{5,6},{7,8},{9,10},{11,12},{13,14},{15,16},{17,18},{19... | collective-permute-start | bytes 196616 | tf_op jit(solution)/shard_map/ppermute | solution.py:166
  108.5 4.6 %collective-permute-start.44 = (f32[18,128]{1,0:T(8,128)S(1)}, f32[18,128]{1,0:T(8,128)S(1)}, u32[]{:S(2)}, u32[]{:S(2)}) collective-permute-start(f32[18,128]{1,0:T(8,128)S(1)} %join.16.refs_0_), channel_id=1, source_target_pairs={{0,12},{1,13},{2,14},{3,15},{4,8},{5,9},{6,10},{7,11},{8,4},{9,5},... | collective-permute-start | bytes 27656 | tf_op jit(solution)/shard_map/ppermute | solution.py:175
  119.3 5.3 %collective-permute-start.48 = (f32[72,128]{1,0:T(8,128)S(1)}, f32[72,128]{1,0:T(8,128)S(1)}, u32[]{:S(2)}, u32[]{:S(2)}) collective-permute-start(f32[72,128]{1,0:T(8,128)S(1)} %get-tuple-element.222.refs_0_), channel_id=1, source_target_pairs={{0,16},{1,17},{2,18},{3,19},{4,20},{5,21},{6,22},{7,23},{8,24},{9,... | collective-permute-start | bytes 110600 | tf_op jit(solution)/shard_map/ppermute | solution.py:166
  121.8 11.7 %collective-permute-start.55 = (f32[64,128]{1,0:T(8,128)S(1)}, f32[64,128]{1,0:T(8,128)S(1)}, u32[]{:S(2)}, u32[]{:S(2)}) collective-permute-start(f32[64,128]{1,0:T(8,128)S(1)} %get-tuple-element.223), channel_id=1, source_target_pairs={{0,1},{2,3},{4,5},{6,7},{8,9},{10,11},{12,13},{14,15},{16,17},{18,... | collective-permute-start | bytes 98312 | tf_op jit(solution)/shard_map/ppermute | solution.py:166
  121.8 11.7 %collective-permute-start.56 = (f32[64,128]{1,0:T(8,128)S(1)}, f32[64,128]{1,0:T(8,128)S(1)}, u32[]{:S(2)}, u32[]{:S(2)}) collective-permute-start(f32[64,128]{1,0:T(8,128)S(1)} %get-tuple-element.224), channel_id=1, source_target_pairs={{1,2},{3,4},{5,6},{7,8},{9,10},{11,12},{13,14},{15,16},{17,18},{19... | collective-permute-start | bytes 98312 | tf_op jit(solution)/shard_map/ppermute | solution.py:166
  127.2 4.5 %collective-permute-start.51 = (f32[2,128]{1,0:T(2,128)S(1)}, f32[2,128]{1,0:T(2,128)S(1)}, u32[]{:S(2)}, u32[]{:S(2)}) collective-permute-start(f32[2,128]{1,0:T(2,128)S(1)} %join.18.refs_0_), channel_id=1, source_target_pairs={{0,12},{1,13},{2,14},{3,15},{4,8},{5,9},{6,10},{7,11},{8,4},{9,5},... | collective-permute-start | bytes 3080 | tf_op jit(solution)/shard_map/ppermute | solution.py:175
  (36 other events, 121.5 us)

commit v7 on v6

--- a/solution.py
+++ b/solution.py
@@ -117,7 +117,7 @@
         rounds.append([bits.pop(0)])
     while bits:
         far, near = bits.pop(0), bits.pop(0)
-        rounds.append([near, far, near + far])
+        rounds.append([near + far, far, near])
     places = [0]
     for distances in rounds:
         places = [place ^ far for far in [0] + distances for place in places]
@@ -165,15 +165,15 @@
     def exchange(arrays):
         return [lax.ppermute(array, AXIS, chosen[i][0]) for i, array in enumerate(arrays)]
 
-    def gather(own, got, lines, after=()):
+    def gather(own, got, lines, beside=()):
         pieces, start = [own, got], cases
-        for distances in rounds[1:]:
+        for at, distances in enumerate(rounds[1:]):
             def join(i, o):
                 o.block[...] = jnp.concatenate([ref[start:start + lines] for ref in i.pieces], axis=0)
 
-            block = stage("join", join, dict(pieces=pieces, after=list(after)), dict(block=((lines * len(pieces), 2 * cases), F32))).block
+            block = stage("join", join, dict(pieces=pieces, beside=list(beside[at:at + 1])), dict(block=((lines * len(pieces), 2 * cases), F32))).block
             pieces = [block] + [lax.ppermute(block, AXIS, [(i, i ^ far) for i in range(total)]) for far in distances]
-            start, lines, after = 0, block.shape[0], ()
+            start, lines = 0, block.shape[0]
         return pieces
 
     def both_sums(pieces, stride):
@@ -246,10 +246,16 @@
         o.inner_faces[...] = times(scaled, i.inv[2][...], i.inv[3][...], NT)
         o.inner[...] = times(scaled, i.inv[0][...], i.inv[1][...])
 
-    def solve_loads(i, o):
-        solve_own(i.load[0], i, o)
-
-    own = stage("solve_loads", solve_loads, dict(load=loads, weight=weight, weighted=start.weighted, inv=inv[:4]), own_kinds)
+    def loads_faces(i, o):
+        o.lines[...] = times(i.weighted[...], *split(i.load[0]), NT)
+        o.inner_faces[...] = times(i.load[0] * i.weight[...], i.inv[0][...], i.inv[1][...], NT)
+
+    def loads_inner(i, o):
+        o.inner[...] = times(i.load[0] * i.weight[...], i.inv[0][...], i.inv[1][...])
+
+    own = stage("loads_faces", loads_faces, dict(load=loads, weight=weight, weighted=start.weighted, inv=inv[2:4]),
+                dict(lines=own_kinds["lines"], inner_faces=faces))
+    own.inner = stage("loads_inner", loads_inner, dict(load=loads, weight=weight, inv=inv[:2]), dict(inner=vec)).inner
 
     def reach(i, o):
         functions, rows = [i.weighted[...]], [i.inv[...]]
@@ -384,7 +390,7 @@
         sent, came_solve = to_solve(came_image, own, coef, sums)
         applied = to_apply(step, came_image, own, state, coef)
         vars(state).update(vars(applied))
-        everyone = gather(sent, came_solve[paired], lines_a_block)
+        everyone = gather(sent, came_solve[paired], lines_a_block, (stiff[4], reached.rows) if step == 0 else ())
         rest_ins = dict(everyone=everyone, rows=reached.rows, reach_faces=reached.reach_faces, came=came_solve, stiff_block=stiff[4:],
                         image_faces=state.image_faces)
         ins = dict(came=came_solve, picker=picker, stiff=stiff[2:4], weight=weight, residual=state.residual, reach=reached.reach,

time: 137 us -> 131 us (0.956)
  starting transfers between devices: 67.3 us -> 63.8 us
  waiting for transfers between devices: 31.2 us -> 28.4 us
    ppermute x27, starting transfers between devices: 39.1 us -> 35.5 us  [exchange(): lax.ppermute(array, AXIS, chosen[i][0])]
    ppermute x30, waiting for transfers between devices: 18.9 us -> 16.4 us  [gather(): lax.ppermute(block, AXIS, [(i, i ^ far) for i in range(total)])]
    pallas_call x31 -> x32, Pallas kernels: 30.7 us -> 31 us  [stage(): pl.pallas_call(kernel, name=name, out_shape=[jax.ShapeDtypeStruct(*kind)...]
  transfers between devices with their start and end apart: 57 -> 57, of which waited for: 23 -> 25; matrix products, arithmetic and copies ran while one was open for 0% -> 0% of each run, Pallas kernels for 18% -> 19%
where the time goes in v7:
time: 131 us; the launch traced here: 130 us
  starting transfers between devices  63.8 us (49%)
  Pallas kernels  31 us (24%)
  waiting for transfers between devices  28.4 us (22%)
  local copies, waits for them, and re-layouts  6.09 us (5%)
    ppermute x27, starting transfers between devices, exchange(): lax.ppermute(array, AXIS, chosen[i][0])  35.5 us
    pallas_call x32, Pallas kernels, stage(): pl.pallas_call(kernel, name=name, out_shape=[jax.ShapeDtypeStruct(*kind)...  31 us
    ppermute x30, starting transfers between devices, gather(): lax.ppermute(block, AXIS, [(i, i ^ far) for i in range(total)])  28.3 us
    ppermute x30, waiting for transfers between devices, gather(): lax.ppermute(block, AXIS, [(i, i ^ far) for i in range(total)])  16.4 us
    ppermute x27, waiting for transfers between devices, exchange(): lax.ppermute(array, AXIS, chosen[i][0])  12 us
    unnamed x22, local copies, waits for them, and re-layouts  6.09 us
  transfers between devices with their start and end apart: 57, of which 25 were waited for; matrix products, arithmetic and copies ran while one was open for 0% of the time, Pallas kernels for 19%

profile of v7, /device:TPU:0, one launch (start us, length us, event | category | flops | bytes accessed | tf_op | source)
XLA Modules:
  0.0 130.4 jit_solution(11173902215662961846)
XLA Ops:
  6.7 7.3 %collective-permute-start.2 = (f32[144,128]{1,0:T(8,128)S(1)}, f32[144,128]{1,0:T(8,128)S(1)}, u32[]{:S(2)}, u32[]{:S(2)}) collective-permute-start(f32[144,128]{1,0:T(8,128)S(1)} %get-tuple-element.118), channel_id=1, source_target_pairs={{0,16},{1,17},{2,18},{3,19},{4,20},{5,21},{6,22},{7,23},{8,24},{9,... | collective-permute-start | bytes 221192 | tf_op jit(solution)/shard_map/ppermute | solution.py:166
  14.0 2.2 %copy-done = f32[1,1024,1024]{2,1,0:T(8,128)S(1)} copy-done((f32[1,1024,1024]{2,1,0:T(8,128)S(1)}, f32[1,1024,1024]{2,1,0:T(8,128)}, u32[]{:S(2)}) %copy-start) | copy-done | bytes 4194328
  16.2 2.7 %prepare_inv.1 = (bf16[1024,1024]{1,0:T(8,128)(2,1)S(1)}, bf16[1024,1024]{1,0:T(8,128)(2,1)S(1)}, bf16[384,1024]{1,0:T(8,128)(2,1)S(1)}, bf16[384,1024]{1,0:T(8,...) custom-call(f32[1,1024,1024]{2,1,0:T(8,128)S(1)} %copy-done, ...), custom_call_target="tpu_custom_call" | custom-call | tf_op jit(solution)/shard_map/prepare_inv/pallas_call | solution.py:92
  20.9 2.8 %prepare_stiff.1 = (bf16[1024,1024]{1,0:T(8,128)(2,1)S(1)}, bf16[1024,1024]{1,0:T(8,128)(2,1)S(1)}, bf16[384,1024]{1,0:T(8,128)(2,1)S(1)}, bf16[384,1024]{1,0:T(...) custom-call(f32[1,1024,1024]{2,1,0:T(8,128)S(1)} %copy-done.1, ...), custom_call_target="tpu_custom_call" | custom-call | tf_op jit(solution)/shard_map/prepare_stiff/pallas_call | solution.py:92
  24.9 3.5 %collective-permute-start.4 = (f32[18,128]{1,0:T(8,128)S(1)}, f32[18,128]{1,0:T(8,128)S(1)}, u32[]{:S(2)}, u32[]{:S(2)}) collective-permute-start(f32[18,128]{1,0:T(8,128)S(1)} %join.10.refs_0_), channel_id=1, source_target_pairs={{0,12},{1,13},{2,14},{3,15},{4,8},{5,9},{6,10},{7,11},{8,4},{9,5},... | collective-permute-start | bytes 27656 | tf_op jit(solution)/shard_map/ppermute | solution.py:175
  34.8 2.0 %apply_own.4 = (f32[64,1024]{1,0:T(8,128)S(1)}, f32[64,384]{1,0:T(8,128)S(1)}, f32[64,1024]{1,0:T(8,128)S(1)}, f32[64,1024]{1,0:T(8,128)S(1)}) custom-call(f32[144,128]{1,0:T(8,128)S(1)} %collective-permute-done.refs_0_.refs_2_, f32[144,128]{1,0:T(8,128)S(1)} %collective-permute-done.1.refs_1_.refs_3_, ...), custom_call_target="tpu_custom_call" | custom-call | tf_op jit(solution)/shard_map/apply_own/pallas_call | solution.py:92
  38.8 5.2 %collective-permute-start.14 = (f32[64,128]{1,0:T(8,128)S(1)}, f32[64,128]{1,0:T(8,128)S(1)}, u32[]{:S(2)}, u32[]{:S(2)}) collective-permute-start(f32[64,128]{1,0:T(8,128)S(1)} %get-tuple-element.147), channel_id=1, source_target_pairs={{0,16},{1,17},{2,18},{3,19},{4,20},{5,21},{6,22},{7,23},{8,24},{9,... | collective-permute-start | bytes 98312 | tf_op jit(solution)/shard_map/ppermute | solution.py:166
  44.0 2.4 %update.3 = (f32[64,1024]{1,0:T(8,128)S(1)}, f32[64,1024]{1,0:T(8,128)S(1)}, f32[16,64]{1,0:T(8,128)S(1)}, f32[64,384]{1,0:T(8,128)S(1)}, f32[64,1024]{1,0:T(8,128)S(1)}, /*index=5*/f32[1,128]{1,0:T(1,128)S(1)}) custom-call(f32[64,128]{1,0:T(8,128)S(1)} %collective-permute-done.10.refs_7_.refs_0_, f32[128,128]{1,0:T(8,128)S(1)} %collective-permute-done.11.refs_8_.refs_1_, ...), custom_call_target="tpu_custom_call" | custom-call | tf_op jit(solution)/shard_map/update/pallas_call | solution.py:92
  46.7 2.5 %collective-permute-start.15 = (f32[73,128]{1,0:T(8,128)S(1)}, f32[73,128]{1,0:T(8,128)S(1)}, u32[]{:S(2)}, u32[]{:S(2)}) collective-permute-start(f32[73,128]{1,0:T(8,128)S(1)} %get-tuple-element.158.refs_0_), channel_id=1, source_target_pairs={{0,16},{1,17},{2,18},{3,19},{4,20},{5,21},{6,22},{7,23},{8,24},{9,... | collective-permute-start | bytes 112136 | tf_op jit(solution)/shard_map/ppermute | solution.py:166
  49.9 1.8 %collective-permute-done.15.refs_1_.refs_9_.refs_2_ = f32[73,128]{1,0:T(8,128)S(1)} collective-permute-done((f32[73,128]{1,0:T(8,128)S(1)}, f32[73,128]{1,0:T(8,128)S(1)}, u32[]{:S(2)}, u32[]{:S(2)}) %collective-permute-start.15) | collective-permute-done | bytes 37408 | tf_op jit(solution)/shard_map/ppermute | solution.py:166
  51.7 1.9 %collective-permute-start.16 = (f32[18,128]{1,0:T(8,128)S(1)}, f32[18,128]{1,0:T(8,128)S(1)}, u32[]{:S(2)}, u32[]{:S(2)}) collective-permute-start(f32[18,128]{1,0:T(8,128)S(1)} %join.12.refs_0_), channel_id=1, source_target_pairs={{0,12},{1,13},{2,14},{3,15},{4,8},{5,9},{6,10},{7,11},{8,4},{9,5},... | collective-permute-start | bytes 27656 | tf_op jit(solution)/shard_map/ppermute | solution.py:175
  59.9 2.0 %apply_own.5 = (f32[64,1024]{1,0:T(8,128)S(1)}, f32[64,384]{1,0:T(8,128)S(1)}, f32[64,1024]{1,0:T(8,128)S(1)}, f32[64,1024]{1,0:T(8,128)S(1)}) custom-call(f32[64,128]{1,0:T(8,128)S(1)} %collective-permute-done.12.refs_0_, f32[64,128]{1,0:T(8,128)S(1)} %collective-permute-done.13.refs_1_, f32[64,128]{1,0:T(8,128)S(1)} %collective-permute-done.14.refs_2_, ...), custom_call_target="tpu_custom_call" | custom-call | tf_op jit(solution)/shard_map/apply_own/pallas_call | solution.py:92
  64.3 3.8 %collective-permute-start.26 = (f32[64,128]{1,0:T(8,128)S(1)}, f32[64,128]{1,0:T(8,128)S(1)}, u32[]{:S(2)}, u32[]{:S(2)}) collective-permute-start(f32[64,128]{1,0:T(8,128)S(1)} %get-tuple-element.166), channel_id=1, source_target_pairs={{0,16},{1,17},{2,18},{3,19},{4,20},{5,21},{6,22},{7,23},{8,24},{9,... | collective-permute-start | bytes 98312 | tf_op jit(solution)/shard_map/ppermute | solution.py:166
  68.2 2.5 %update.4 = (f32[64,1024]{1,0:T(8,128)S(1)}, f32[64,1024]{1,0:T(8,128)S(1)}, f32[1,128]{1,0:T(1,128)S(1)}, f32[64,1024]{1,0:T(8,128)S(1)}, f32[64,1024]{1,0:T(8,...) custom-call(f32[64,128]{1,0:T(8,128)S(1)} %collective-permute-done.2, ...), custom_call_target="tpu_custom_call" | custom-call | tf_op jit(solution)/shard_map/update/pallas_call | solution.py:92
  71.5 2.1 %collective-permute-start.27 = (f32[73,128]{1,0:T(8,128)S(1)}, f32[73,128]{1,0:T(8,128)S(1)}, u32[]{:S(2)}, u32[]{:S(2)}) collective-permute-start(f32[73,128]{1,0:T(8,128)S(1)} %get-tuple-element.177.refs_0_), channel_id=1, source_target_pairs={{0,16},{1,17},{2,18},{3,19},{4,20},{5,21},{6,22},{7,23},{8,24},{9,... | collective-permute-start | bytes 112136 | tf_op jit(solution)/shard_map/ppermute | solution.py:166
  74.2 2.2 %collective-permute-done.27.refs_1_.refs_9_.refs_2_ = f32[73,128]{1,0:T(8,128)S(1)} collective-permute-done((f32[73,128]{1,0:T(8,128)S(1)}, f32[73,128]{1,0:T(8,128)S(1)}, u32[]{:S(2)}, u32[]{:S(2)}) %collective-permute-start.27) | collective-permute-done | bytes 37408 | tf_op jit(solution)/shard_map/ppermute | solution.py:166
  76.4 2.1 %collective-permute-start.28 = (f32[18,128]{1,0:T(8,128)S(1)}, f32[18,128]{1,0:T(8,128)S(1)}, u32[]{:S(2)}, u32[]{:S(2)}) collective-permute-start(f32[18,128]{1,0:T(8,128)S(1)} %join.14.refs_0_), channel_id=1, source_target_pairs={{0,12},{1,13},{2,14},{3,15},{4,8},{5,9},{6,10},{7,11},{8,4},{9,5},... | collective-permute-start | bytes 27656 | tf_op jit(solution)/shard_map/ppermute | solution.py:175
  78.5 1.9 %collective-permute-start.29 = (f32[18,128]{1,0:T(8,128)S(1)}, f32[18,128]{1,0:T(8,128)S(1)}, u32[]{:S(2)}, u32[]{:S(2)}) collective-permute-start(f32[18,128]{1,0:T(8,128)S(1)} %join.14.refs_0_), channel_id=1, source_target_pairs={{0,8},{1,9},{2,10},{3,11},{4,12},{5,13},{6,14},{7,15},{8,0},{9,1},... | collective-permute-start | bytes 27656 | tf_op jit(solution)/shard_map/ppermute | solution.py:175
  82.2 1.9 %collective-permute-done.30.refs_3_ = f32[18,128]{1,0:T(8,128)S(1)} collective-permute-done((f32[18,128]{1,0:T(8,128)S(1)}, f32[18,128]{1,0:T(8,128)S(1)}, u32[]{:S(2)}, u32[]{:S(2)}) %collective-permute-start.30) | collective-permute-done | bytes 9248 | tf_op jit(solution)/shard_map/ppermute | solution.py:175
  84.1 1.8 %collective-permute-start.33 = (f32[72,128]{1,0:T(8,128)S(1)}, f32[72,128]{1,0:T(8,128)S(1)}, u32[]{:S(2)}, u32[]{:S(2)}) collective-permute-start(f32[72,128]{1,0:T(8,128)S(1)} %join.15.refs_0_), channel_id=1, source_target_pairs={{0,1},{1,0},{2,3},{3,2},{4,5},{5,4},{6,7},{7,6},{8,9},{9,8},{10,11... | collective-permute-start | bytes 110600 | tf_op jit(solution)/shard_map/ppermute | solution.py:175
  85.9 2.2 %apply_own.6 = (f32[64,1024]{1,0:T(8,128)S(1)}, f32[64,384]{1,0:T(8,128)S(1)}, f32[64,1024]{1,0:T(8,128)S(1)}, f32[64,1024]{1,0:T(8,128)S(1)}, f32[64,1024]{1,0:T(8,128)S(1)}) custom-call(f32[64,128]{1,0:T(8,128)S(1)} %collective-permute-done.24.refs_0_, f32[64,128]{1,0:T(8,128)S(1)} %collective-permute-done.25.refs_1_, ...), custom_call_target="tpu_custom_call" | custom-call | tf_op jit(solution)/shard_map/apply_own/pallas_call | solution.py:92
  90.2 3.3 %collective-permute-start.38 = (f32[64,128]{1,0:T(8,128)S(1)}, f32[64,128]{1,0:T(8,128)S(1)}, u32[]{:S(2)}, u32[]{:S(2)}) collective-permute-start(f32[64,128]{1,0:T(8,128)S(1)} %get-tuple-element.186), channel_id=1, source_target_pairs={{0,16},{1,17},{2,18},{3,19},{4,20},{5,21},{6,22},{7,23},{8,24},{9,... | collective-permute-start | bytes 98312 | tf_op jit(solution)/shard_map/ppermute | solution.py:166
  93.5 2.5 %update.5 = (f32[64,1024]{1,0:T(8,128)S(1)}, f32[64,1024]{1,0:T(8,128)S(1)}, f32[1,128]{1,0:T(1,128)S(1)}, f32[64,1024]{1,0:T(8,128)S(1)}, f32[64,1024]{1,0:T(8,...) custom-call(f32[64,128]{1,0:T(8,128)S(1)} %collective-permute-done.3, ...), custom_call_target="tpu_custom_call" | custom-call | tf_op jit(solution)/shard_map/update/pallas_call | solution.py:92
  96.5 2.3 %collective-permute-start.41 = (f32[73,128]{1,0:T(8,128)S(1)}, f32[73,128]{1,0:T(8,128)S(1)}, u32[]{:S(2)}, u32[]{:S(2)}) collective-permute-start(f32[73,128]{1,0:T(8,128)S(1)} %get-tuple-element.205.refs_0_), channel_id=1, source_target_pairs={{0,16},{1,17},{2,18},{3,19},{4,20},{5,21},{6,22},{7,23},{8,24},{9,... | collective-permute-start | bytes 112136 | tf_op jit(solution)/shard_map/ppermute | solution.py:166
  99.5 2.4 %collective-permute-done.41.refs_1_.refs_2_ = f32[73,128]{1,0:T(8,128)S(1)} collective-permute-done((f32[73,128]{1,0:T(8,128)S(1)}, f32[73,128]{1,0:T(8,128)S(1)}, u32[]{:S(2)}, u32[]{:S(2)}) %collective-permute-start.41) | collective-permute-done | bytes 37408 | tf_op jit(solution)/shard_map/ppermute | solution.py:166
  101.9 2.0 %collective-permute-start.42 = (f32[18,128]{1,0:T(8,128)S(1)}, f32[18,128]{1,0:T(8,128)S(1)}, u32[]{:S(2)}, u32[]{:S(2)}) collective-permute-start(f32[18,128]{1,0:T(8,128)S(1)} %join.16.refs_0_), channel_id=1, source_target_pairs={{0,12},{1,13},{2,14},{3,15},{4,8},{5,9},{6,10},{7,11},{8,4},{9,5},... | collective-permute-start | bytes 27656 | tf_op jit(solution)/shard_map/ppermute | solution.py:175
  103.9 1.8 %collective-permute-start.43 = (f32[18,128]{1,0:T(8,128)S(1)}, f32[18,128]{1,0:T(8,128)S(1)}, u32[]{:S(2)}, u32[]{:S(2)}) collective-permute-start(f32[18,128]{1,0:T(8,128)S(1)} %join.16.refs_0_), channel_id=1, source_target_pairs={{0,8},{1,9},{2,10},{3,11},{4,12},{5,13},{6,14},{7,15},{8,0},{9,1},... | collective-permute-start | bytes 27656 | tf_op jit(solution)/shard_map/ppermute | solution.py:175
  107.6 1.8 %collective-permute-done.44.refs_3_ = f32[18,128]{1,0:T(8,128)S(1)} collective-permute-done((f32[18,128]{1,0:T(8,128)S(1)}, f32[18,128]{1,0:T(8,128)S(1)}, u32[]{:S(2)}, u32[]{:S(2)}) %collective-permute-start.44) | collective-permute-done | bytes 9248 | tf_op jit(solution)/shard_map/ppermute | solution.py:175
  111.2 2.2 %apply_own.7 = (f32[64,1024]{1,0:T(8,128)S(1)}, f32[64,384]{1,0:T(8,128)S(1)}, f32[64,1024]{1,0:T(8,128)S(1)}, f32[64,1024]{1,0:T(8,128)S(1)}, f32[64,1024]{1,0:T(8,128)S(1)}) custom-call(f32[64,128]{1,0:T(8,128)S(1)} %collective-permute-done.36.refs_0_, f32[64,128]{1,0:T(8,128)S(1)} %collective-permute-done.37.refs_1_, ...), custom_call_target="tpu_custom_call" | custom-call | tf_op jit(solution)/shard_map/apply_own/pallas_call | solution.py:92
  116.6 3.8 %collective-permute-done.48.refs_1_.refs_6_ = f32[72,128]{1,0:T(8,128)S(1)} collective-permute-done((f32[72,128]{1,0:T(8,128)S(1)}, f32[72,128]{1,0:T(8,128)S(1)}, u32[]{:S(2)}, u32[]{:S(2)}) %collective-permute-start.48) | collective-permute-done | bytes 36896 | tf_op jit(solution)/shard_map/ppermute | solution.py:166
  121.8 2.0 %collective-permute-start.51 = (f32[2,128]{1,0:T(2,128)S(1)}, f32[2,128]{1,0:T(2,128)S(1)}, u32[]{:S(2)}, u32[]{:S(2)}) collective-permute-start(f32[2,128]{1,0:T(2,128)S(1)} %join.18.refs_0_), channel_id=1, source_target_pairs={{0,4},{1,5},{2,6},{3,7},{4,0},{5,1},{6,2},{7,3},{8,12},{9,13},{10,... | collective-permute-start | bytes 3080 | tf_op jit(solution)/shard_map/ppermute | solution.py:175
  125.7 1.7 %collective-permute-start.53 = (f32[8,128]{1,0:T(8,128)S(1)}, f32[8,128]{1,0:T(8,128)S(1)}, u32[]{:S(2)}, u32[]{:S(2)}) collective-permute-start(f32[8,128]{1,0:T(8,128)S(1)} %join.19.refs_0_), channel_id=1, source_target_pairs={{0,2},{1,3},{2,0},{3,1},{4,6},{5,7},{6,4},{7,5},{8,10},{9,11},{10,... | collective-permute-start | bytes 12296 | tf_op jit(solution)/shard_map/ppermute | solution.py:175
  (136 shorter events, 46.8 us)
Async XLA Ops:
  5.5 14.1 %collective-permute-start = (f32[144,128]{1,0:T(8,128)S(1)}, f32[144,128]{1,0:T(8,128)S(1)}, u32[]{:S(2)}, u32[]{:S(2)}) collective-permute-start(f32[144,128]{1,0:T(8,128)S(1)} %get-tuple-element.116), channel_id=1, source_target_pairs={{0,1},{2,3},{4,5},{6,7},{8,9},{10,11},{12,13},{14,15},{16,17},{18,... | collective-permute-start | bytes 221192 | tf_op jit(solution)/shard_map/ppermute | solution.py:166
  6.0 13.6 %collective-permute-start.1 = (f32[144,128]{1,0:T(8,128)S(1)}, f32[144,128]{1,0:T(8,128)S(1)}, u32[]{:S(2)}, u32[]{:S(2)}) collective-permute-start(f32[144,128]{1,0:T(8,128)S(1)} %get-tuple-element.117), channel_id=1, source_target_pairs={{1,2},{3,4},{5,6},{7,8},{9,10},{11,12},{13,14},{15,16},{17,18},{19... | collective-permute-start | bytes 221192 | tf_op jit(solution)/shard_map/ppermute | solution.py:166
  6.7 13.0 %collective-permute-start.2 = (f32[144,128]{1,0:T(8,128)S(1)}, f32[144,128]{1,0:T(8,128)S(1)}, u32[]{:S(2)}, u32[]{:S(2)}) collective-permute-start(f32[144,128]{1,0:T(8,128)S(1)} %get-tuple-element.118), channel_id=1, source_target_pairs={{0,16},{1,17},{2,18},{3,19},{4,20},{5,21},{6,22},{7,23},{8,24},{9,... | collective-permute-start | bytes 221192 | tf_op jit(solution)/shard_map/ppermute | solution.py:166
  19.9 5.0 %collective-permute-start.3 = (f32[73,128]{1,0:T(8,128)S(1)}, f32[73,128]{1,0:T(8,128)S(1)}, u32[]{:S(2)}, u32[]{:S(2)}) collective-permute-start(f32[73,128]{1,0:T(8,128)S(1)} %get-tuple-element.130.refs_0_), channel_id=1, source_target_pairs={{0,16},{1,17},{2,18},{3,19},{4,20},{5,21},{6,22},{7,23},{8,24},{9,... | collective-permute-start | bytes 112136 | tf_op jit(solution)/shard_map/ppermute | solution.py:166
  20.0 16.7 %collective-permute-start.11 = (f32[128,128]{1,0:T(8,128)S(1)}, f32[128,128]{1,0:T(8,128)S(1)}, u32[]{:S(2)}, u32[]{:S(2)}) collective-permute-start(f32[128,128]{1,0:T(8,128)S(1)} %get-tuple-element.140), channel_id=1, source_target_pairs={{1,2},{3,4},{5,6},{7,8},{9,10},{11,12},{13,14},{15,16},{17,18},{19... | collective-permute-start | bytes 196616 | tf_op jit(solution)/shard_map/ppermute | solution.py:166
  24.9 5.8 %collective-permute-start.4 = (f32[18,128]{1,0:T(8,128)S(1)}, f32[18,128]{1,0:T(8,128)S(1)}, u32[]{:S(2)}, u32[]{:S(2)}) collective-permute-start(f32[18,128]{1,0:T(8,128)S(1)} %join.10.refs_0_), channel_id=1, source_target_pairs={{0,12},{1,13},{2,14},{3,15},{4,8},{5,9},{6,10},{7,11},{8,4},{9,5},... | collective-permute-start | bytes 27656 | tf_op jit(solution)/shard_map/ppermute | solution.py:175
  32.1 4.7 %collective-permute-start.7 = (f32[72,128]{1,0:T(8,128)S(1)}, f32[72,128]{1,0:T(8,128)S(1)}, u32[]{:S(2)}, u32[]{:S(2)}) collective-permute-start(f32[72,128]{1,0:T(8,128)S(1)} %join.11.refs_0_), channel_id=1, source_target_pairs={{0,3},{1,2},{2,1},{3,0},{4,7},{5,6},{6,5},{7,4},{8,11},{9,10},{10,... | collective-permute-start | bytes 110600 | tf_op jit(solution)/shard_map/ppermute | solution.py:175
  37.4 9.0 %collective-permute-start.12 = (f32[64,128]{1,0:T(8,128)S(1)}, f32[64,128]{1,0:T(8,128)S(1)}, u32[]{:S(2)}, u32[]{:S(2)}) collective-permute-start(f32[64,128]{1,0:T(8,128)S(1)} %get-tuple-element.145), channel_id=1, source_target_pairs={{0,1},{2,3},{4,5},{6,7},{8,9},{10,11},{12,13},{14,15},{16,17},{18,... | collective-permute-start | bytes 98312 | tf_op jit(solution)/shard_map/ppermute | solution.py:166
  37.9 8.5 %collective-permute-start.13 = (f32[64,128]{1,0:T(8,128)S(1)}, f32[64,128]{1,0:T(8,128)S(1)}, u32[]{:S(2)}, u32[]{:S(2)}) collective-permute-start(f32[64,128]{1,0:T(8,128)S(1)} %get-tuple-element.146), channel_id=1, source_target_pairs={{1,2},{3,4},{5,6},{7,8},{9,10},{11,12},{13,14},{15,16},{17,18},{19... | collective-permute-start | bytes 98312 | tf_op jit(solution)/shard_map/ppermute | solution.py:166
  38.8 7.7 %collective-permute-start.14 = (f32[64,128]{1,0:T(8,128)S(1)}, f32[64,128]{1,0:T(8,128)S(1)}, u32[]{:S(2)}, u32[]{:S(2)}) collective-permute-start(f32[64,128]{1,0:T(8,128)S(1)} %get-tuple-element.147), channel_id=1, source_target_pairs={{0,16},{1,17},{2,18},{3,19},{4,20},{5,21},{6,22},{7,23},{8,24},{9,... | collective-permute-start | bytes 98312 | tf_op jit(solution)/shard_map/ppermute | solution.py:166
  46.7 5.0 %collective-permute-start.15 = (f32[73,128]{1,0:T(8,128)S(1)}, f32[73,128]{1,0:T(8,128)S(1)}, u32[]{:S(2)}, u32[]{:S(2)}) collective-permute-start(f32[73,128]{1,0:T(8,128)S(1)} %get-tuple-element.158.refs_0_), channel_id=1, source_target_pairs={{0,16},{1,17},{2,18},{3,19},{4,20},{5,21},{6,22},{7,23},{8,24},{9,... | collective-permute-start | bytes 112136 | tf_op jit(solution)/shard_map/ppermute | solution.py:166
  49.2 12.7 %collective-permute-start.23 = (f32[128,128]{1,0:T(8,128)S(1)}, f32[128,128]{1,0:T(8,128)S(1)}, u32[]{:S(2)}, u32[]{:S(2)}) collective-permute-start(f32[128,128]{1,0:T(8,128)S(1)} %get-tuple-element.160), channel_id=1, source_target_pairs={{1,2},{3,4},{5,6},{7,8},{9,10},{11,12},{13,14},{15,16},{17,18},{19... | collective-permute-start | bytes 196616 | tf_op jit(solution)/shard_map/ppermute | solution.py:166
  51.7 4.6 %collective-permute-start.16 = (f32[18,128]{1,0:T(8,128)S(1)}, f32[18,128]{1,0:T(8,128)S(1)}, u32[]{:S(2)}, u32[]{:S(2)}) collective-permute-start(f32[18,128]{1,0:T(8,128)S(1)} %join.12.refs_0_), channel_id=1, source_target_pairs={{0,12},{1,13},{2,14},{3,15},{4,8},{5,9},{6,10},{7,11},{8,4},{9,5},... | collective-permute-start | bytes 27656 | tf_op jit(solution)/shard_map/ppermute | solution.py:175
  63.6 7.1 %collective-permute-start.24 = (f32[64,128]{1,0:T(8,128)S(1)}, f32[64,128]{1,0:T(8,128)S(1)}, u32[]{:S(2)}, u32[]{:S(2)}) collective-permute-start(f32[64,128]{1,0:T(8,128)S(1)} %get-tuple-element.164), channel_id=1, source_target_pairs={{0,1},{2,3},{4,5},{6,7},{8,9},{10,11},{12,13},{14,15},{16,17},{18,... | collective-permute-start | bytes 98312 | tf_op jit(solution)/shard_map/ppermute | solution.py:166
  63.7 7.0 %collective-permute-start.25 = (f32[64,128]{1,0:T(8,128)S(1)}, f32[64,128]{1,0:T(8,128)S(1)}, u32[]{:S(2)}, u32[]{:S(2)}) collective-permute-start(f32[64,128]{1,0:T(8,128)S(1)} %get-tuple-element.165), channel_id=1, source_target_pairs={{1,2},{3,4},{5,6},{7,8},{9,10},{11,12},{13,14},{15,16},{17,18},{19... | collective-permute-start | bytes 98312 | tf_op jit(solution)/shard_map/ppermute | solution.py:166
  64.3 6.7 %collective-permute-start.26 = (f32[64,128]{1,0:T(8,128)S(1)}, f32[64,128]{1,0:T(8,128)S(1)}, u32[]{:S(2)}, u32[]{:S(2)}) collective-permute-start(f32[64,128]{1,0:T(8,128)S(1)} %get-tuple-element.166), channel_id=1, source_target_pairs={{0,16},{1,17},{2,18},{3,19},{4,20},{5,21},{6,22},{7,23},{8,24},{9,... | collective-permute-start | bytes 98312 | tf_op jit(solution)/shard_map/ppermute | solution.py:166
  71.5 5.0 %collective-permute-start.27 = (f32[73,128]{1,0:T(8,128)S(1)}, f32[73,128]{1,0:T(8,128)S(1)}, u32[]{:S(2)}, u32[]{:S(2)}) collective-permute-start(f32[73,128]{1,0:T(8,128)S(1)} %get-tuple-element.177.refs_0_), channel_id=1, source_target_pairs={{0,16},{1,17},{2,18},{3,19},{4,20},{5,21},{6,22},{7,23},{8,24},{9,... | collective-permute-start | bytes 112136 | tf_op jit(solution)/shard_map/ppermute | solution.py:166
  73.5 14.6 %collective-permute-start.35 = (f32[128,128]{1,0:T(8,128)S(1)}, f32[128,128]{1,0:T(8,128)S(1)}, u32[]{:S(2)}, u32[]{:S(2)}) collective-permute-start(f32[128,128]{1,0:T(8,128)S(1)} %get-tuple-element.179), channel_id=1, source_target_pairs={{1,2},{3,4},{5,6},{7,8},{9,10},{11,12},{13,14},{15,16},{17,18},{19... | collective-permute-start | bytes 196616 | tf_op jit(solution)/shard_map/ppermute | solution.py:166
  76.4 4.6 %collective-permute-start.28 = (f32[18,128]{1,0:T(8,128)S(1)}, f32[18,128]{1,0:T(8,128)S(1)}, u32[]{:S(2)}, u32[]{:S(2)}) collective-permute-start(f32[18,128]{1,0:T(8,128)S(1)} %join.14.refs_0_), channel_id=1, source_target_pairs={{0,12},{1,13},{2,14},{3,15},{4,8},{5,9},{6,10},{7,11},{8,4},{9,5},... | collective-permute-start | bytes 27656 | tf_op jit(solution)/shard_map/ppermute | solution.py:175
  84.1 4.1 %collective-permute-start.31 = (f32[72,128]{1,0:T(8,128)S(1)}, f32[72,128]{1,0:T(8,128)S(1)}, u32[]{:S(2)}, u32[]{:S(2)}) collective-permute-start(f32[72,128]{1,0:T(8,128)S(1)} %join.15.refs_0_), channel_id=1, source_target_pairs={{0,3},{1,2},{2,1},{3,0},{4,7},{5,6},{6,5},{7,4},{8,11},{9,10},{10,... | collective-permute-start | bytes 110600 | tf_op jit(solution)/shard_map/ppermute | solution.py:175
  84.1 4.2 %collective-permute-start.32 = (f32[72,128]{1,0:T(8,128)S(1)}, f32[72,128]{1,0:T(8,128)S(1)}, u32[]{:S(2)}, u32[]{:S(2)}) collective-permute-start(f32[72,128]{1,0:T(8,128)S(1)} %join.15.refs_0_), channel_id=1, source_target_pairs={{0,2},{1,3},{2,0},{3,1},{4,6},{5,7},{6,4},{7,5},{8,10},{9,11},{10,... | collective-permute-start | bytes 110600 | tf_op jit(solution)/shard_map/ppermute | solution.py:175
  88.8 7.2 %collective-permute-start.36 = (f32[64,128]{1,0:T(8,128)S(1)}, f32[64,128]{1,0:T(8,128)S(1)}, u32[]{:S(2)}, u32[]{:S(2)}) collective-permute-start(f32[64,128]{1,0:T(8,128)S(1)} %get-tuple-element.184), channel_id=1, source_target_pairs={{0,1},{2,3},{4,5},{6,7},{8,9},{10,11},{12,13},{14,15},{16,17},{18,... | collective-permute-start | bytes 98312 | tf_op jit(solution)/shard_map/ppermute | solution.py:166
  89.3 6.7 %collective-permute-start.37 = (f32[64,128]{1,0:T(8,128)S(1)}, f32[64,128]{1,0:T(8,128)S(1)}, u32[]{:S(2)}, u32[]{:S(2)}) collective-permute-start(f32[64,128]{1,0:T(8,128)S(1)} %get-tuple-element.185), channel_id=1, source_target_pairs={{1,2},{3,4},{5,6},{7,8},{9,10},{11,12},{13,14},{15,16},{17,18},{19... | collective-permute-start | bytes 98312 | tf_op jit(solution)/shard_map/ppermute | solution.py:166
  90.2 5.9 %collective-permute-start.38 = (f32[64,128]{1,0:T(8,128)S(1)}, f32[64,128]{1,0:T(8,128)S(1)}, u32[]{:S(2)}, u32[]{:S(2)}) collective-permute-start(f32[64,128]{1,0:T(8,128)S(1)} %get-tuple-element.186), channel_id=1, source_target_pairs={{0,16},{1,17},{2,18},{3,19},{4,20},{5,21},{6,22},{7,23},{8,24},{9,... | collective-permute-start | bytes 98312 | tf_op jit(solution)/shard_map/ppermute | solution.py:166
  96.5 5.4 %collective-permute-start.41 = (f32[73,128]{1,0:T(8,128)S(1)}, f32[73,128]{1,0:T(8,128)S(1)}, u32[]{:S(2)}, u32[]{:S(2)}) collective-permute-start(f32[73,128]{1,0:T(8,128)S(1)} %get-tuple-element.205.refs_0_), channel_id=1, source_target_pairs={{0,16},{1,17},{2,18},{3,19},{4,20},{5,21},{6,22},{7,23},{8,24},{9,... | collective-permute-start | bytes 112136 | tf_op jit(solution)/shard_map/ppermute | solution.py:166
  98.8 14.6 %collective-permute-start.40 = (f32[128,128]{1,0:T(8,128)S(1)}, f32[128,128]{1,0:T(8,128)S(1)}, u32[]{:S(2)}, u32[]{:S(2)}) collective-permute-start(f32[128,128]{1,0:T(8,128)S(1)} %get-tuple-element.204), channel_id=1, source_target_pairs={{1,2},{3,4},{5,6},{7,8},{9,10},{11,12},{13,14},{15,16},{17,18},{19... | collective-permute-start | bytes 196616 | tf_op jit(solution)/shard_map/ppermute | solution.py:166
  101.9 4.6 %collective-permute-start.42 = (f32[18,128]{1,0:T(8,128)S(1)}, f32[18,128]{1,0:T(8,128)S(1)}, u32[]{:S(2)}, u32[]{:S(2)}) collective-permute-start(f32[18,128]{1,0:T(8,128)S(1)} %join.16.refs_0_), channel_id=1, source_target_pairs={{0,12},{1,13},{2,14},{3,15},{4,8},{5,9},{6,10},{7,11},{8,4},{9,5},... | collective-permute-start | bytes 27656 | tf_op jit(solution)/shard_map/ppermute | solution.py:175
  109.4 4.2 %collective-permute-start.46 = (f32[72,128]{1,0:T(8,128)S(1)}, f32[72,128]{1,0:T(8,128)S(1)}, u32[]{:S(2)}, u32[]{:S(2)}) collective-permute-start(f32[72,128]{1,0:T(8,128)S(1)} %join.17.refs_20_), channel_id=1, source_target_pairs={{0,2},{1,3},{2,0},{3,1},{4,6},{5,7},{6,4},{7,5},{8,10},{9,11},{10,... | collective-permute-start | bytes 110600 | tf_op jit(solution)/shard_map/ppermute | solution.py:175
  115.1 5.2 %collective-permute-start.48 = (f32[72,128]{1,0:T(8,128)S(1)}, f32[72,128]{1,0:T(8,128)S(1)}, u32[]{:S(2)}, u32[]{:S(2)}) collective-permute-start(f32[72,128]{1,0:T(8,128)S(1)} %get-tuple-element.220.refs_0_), channel_id=1, source_target_pairs={{0,16},{1,17},{2,18},{3,19},{4,20},{5,21},{6,22},{7,23},{8,24},{9,... | collective-permute-start | bytes 110600 | tf_op jit(solution)/shard_map/ppermute | solution.py:166
  115.9 11.5 %collective-permute-start.55 = (f32[64,128]{1,0:T(8,128)S(1)}, f32[64,128]{1,0:T(8,128)S(1)}, u32[]{:S(2)}, u32[]{:S(2)}) collective-permute-start(f32[64,128]{1,0:T(8,128)S(1)} %get-tuple-element.221), channel_id=1, source_target_pairs={{0,1},{2,3},{4,5},{6,7},{8,9},{10,11},{12,13},{14,15},{16,17},{18,... | collective-permute-start | bytes 98312 | tf_op jit(solution)/shard_map/ppermute | solution.py:166
  115.9 11.5 %collective-permute-start.56 = (f32[64,128]{1,0:T(8,128)S(1)}, f32[64,128]{1,0:T(8,128)S(1)}, u32[]{:S(2)}, u32[]{:S(2)}) collective-permute-start(f32[64,128]{1,0:T(8,128)S(1)} %get-tuple-element.222), channel_id=1, source_target_pairs={{1,2},{3,4},{5,6},{7,8},{9,10},{11,12},{13,14},{15,16},{17,18},{19... | collective-permute-start | bytes 98312 | tf_op jit(solution)/shard_map/ppermute | solution.py:166
  120.3 4.5 %collective-permute-start.49 = (f32[2,128]{1,0:T(2,128)S(1)}, f32[2,128]{1,0:T(2,128)S(1)}, u32[]{:S(2)}, u32[]{:S(2)}) collective-permute-start(f32[2,128]{1,0:T(2,128)S(1)} %join.18.refs_0_), channel_id=1, source_target_pairs={{0,12},{1,13},{2,14},{3,15},{4,8},{5,9},{6,10},{7,11},{8,4},{9,5},... | collective-permute-start | bytes 3080 | tf_op jit(solution)/shard_map/ppermute | solution.py:175
  (36 other events, 125.9 us)

commit v8 on v7

--- a/solution.py
+++ b/solution.py
@@ -19,6 +19,7 @@
 TILES = 8
 AXIS = "sub"
 LONGER = 64
+ROOM_FOR_COPIES = pl.CostEstimate(flops=4 * 10**9, bytes_accessed=16 * 10**6, transcendentals=0)
 
 
 def contract(left, right, dims=NN):
@@ -81,7 +82,7 @@
     return space
 
 
-def stage(name, body, ins, outs):
+def stage(name, body, ins, outs, cost=None):
     in_names, arrays = flat(ins)
     out_names, kinds = flat(outs)
 
@@ -96,6 +97,7 @@
         in_specs=[whole] * len(arrays),
         out_specs=[whole] * len(kinds),
         compiler_params=pltpu.CompilerParams(vmem_limit_bytes=STAGE_BYTES),
+        cost_estimate=cost,
     )(*arrays)
     return named(out_names, made)
 
@@ -148,10 +150,14 @@
     vec = ((cases, ndof), F32)
     faces = ((cases, slots), F32)
     pair = ((1, 2 * cases), F32)
-    face_kinds = [((cases, width), F32)] * blocks
+    faces_kind = ((cases, width), F32)
     extra_rows = [lines_a_block if at == paired else LONGER if block[3:] == (1, 1) else 0 for at, block in enumerate(chosen)]
     solve_kinds = [((cases + extra, width), F32) for extra in extra_rows]
-    last_kinds = [((cases + (8 if at == paired else 0), width), F32) for at in range(blocks)]
+
+    def longer(kind):
+        rows, lanes = kind[0]
+        return [((rows + (8 if at == paired else 0), lanes), F32) for at in range(blocks)]
+
     blocked = [slice(i * width, (i + 1) * width) for i in range(blocks)]
     strips = [slice(i * ndof // TILES, (i + 1) * ndof // TILES) for i in range(TILES)]
 
@@ -159,8 +165,11 @@
         return jnp.concatenate([ref[:cases] for ref in refs], axis=1)
 
     def put_faces(refs, value):
+        rows = value.shape[0]
         for i, ref in enumerate(refs):
-            ref[:value.shape[0]] = value[:, blocked[i]]
+            ref[:rows] = value[:, blocked[i]]
+            if ref.shape[0] > rows:
+                ref[rows:] = jnp.zeros((ref.shape[0] - rows, width), F32)
 
     def exchange(arrays):
         return [lax.ppermute(array, AXIS, chosen[i][0]) for i, array in enumerate(arrays)]
@@ -213,12 +222,17 @@
         o.weighted[...] = weighted
         o.basis_slots[...] = at_slots[cases:]
 
+    def lead(i, o):
+        o.ready[...] = jnp.zeros((8, width), F32)
+
     packed = ((cases + primal + reps * primal, width), F32)
+    ready = stage("lead", lead, dict(), dict(ready=((8, width), F32)), cost=ROOM_FOR_COPIES).ready
     start = stage(
         "first", first,
-        dict(lengths=face_len, index=face_index, basis=coarse_basis, load=loads, inv=coarse_inv),
-        dict(face=[packed] * blocks, picker=((slots, ndof), BF), unpicker=((ndof, slots), BF), weight=((1, ndof), F32),
-             weighted=((primal, ndof), F32), basis_slots=((primal, slots), F32)))
+        dict(ready=ready, lengths=face_len, index=face_index, basis=coarse_basis, load=loads, inv=coarse_inv),
+        dict(face=longer(packed), picker=((slots, ndof), BF), unpicker=((ndof, slots), BF), weight=((1, ndof), F32),
+             weighted=((primal, ndof), F32), basis_slots=((primal, slots), F32)),
+        cost=ROOM_FOR_COPIES)
     weight, picker, unpicker = start.weight, start.picker, start.unpicker
     came = exchange(start.face)
 
@@ -296,9 +310,6 @@
             put_faces(o.face, 0.5 * (i.inner_faces[...] + times(0.5 * arrived, i.inv[0][...], i.inv[1][...])))
             o.face[paired][cases:cases + half] = jnp.concatenate([lines[:half], lines[half:]], axis=1)
             o.face[paired][cases + half:] = i.sums[...] if sums is not None else jnp.zeros((1, 2 * cases), F32)
-            for at, extra in enumerate(extra_rows):
-                if extra and at != paired:
-                    o.face[at][cases:] = jnp.zeros((extra, width), F32)
 
         ins = dict(came=came, basis_slots=start.basis_slots, lines=own.lines, inner_faces=own.inner_faces, inv=inv[4:])
         if coef is not None:
@@ -410,7 +421,7 @@
                 o.face[paired][cases:] = jnp.broadcast_to(recur(i, o, step, factors, both)[1], (8, 2 * cases))
 
             ins.update(rest_ins)
-            outs.update(face=last_kinds)
+            outs.update(face=longer(faces_kind))
             made = stage("last", last, ins, outs)
             vars(state).update(vars(made))
             came_image = exchange(made.face)
@@ -420,7 +431,7 @@
             at_slots, o.factors[...], o.sums[...] = corrected(i)
             put_faces(o.face, at_slots)
 
-        made = stage("apply_rest", apply_rest, rest_ins, dict(face=face_kinds, factors=((cases, own_rows), F32), sums=pair))
+        made = stage("apply_rest", apply_rest, rest_ins, dict(face=longer(faces_kind), factors=((cases, own_rows), F32), sums=pair))
         came_image = exchange(made.face)
 
         def update(i, o, step=step):

time: 131 us -> 125 us (0.954)
  local copies, waits for them, and re-layouts: 6.09 us -> 0.99 us
  waiting for transfers between devices: 28.4 us -> 26.3 us
  starting transfers between devices: 63.8 us -> 65.3 us
    unnamed x22 -> x18, local copies, waits for them, and re-layouts: 6.09 us -> 0.99 us
    ppermute x27, starting transfers between devices: 35.5 us -> 37 us  [exchange(): lax.ppermute(array, AXIS, chosen[i][0])]
    ppermute x27, waiting for transfers between devices: 12 us -> 10.5 us  [exchange(): lax.ppermute(array, AXIS, chosen[i][0])]
    pallas_call x32 -> x33, Pallas kernels: 31 us -> 31 us  [stage(): pl.pallas_call(kernel, name=name, out_shape=[jax.ShapeDtypeStruct(*kind)...]
  transfers between devices with their start and end apart: 57 -> 57, of which waited for: 25 -> 24; matrix products, arithmetic and copies ran while one was open for 0% -> 0% of each run, Pallas kernels for 19% -> 19%
where the time goes in v8:
time: 125 us
  starting transfers between devices  65.3 us (52%)
  Pallas kernels  31 us (25%)
  waiting for transfers between devices  26.3 us (21%)
    ppermute x27, starting transfers between devices, exchange(): lax.ppermute(array, AXIS, chosen[i][0])  37 us
    pallas_call x33, Pallas kernels, stage(): pl.pallas_call(kernel, name=name, out_shape=[jax.ShapeDtypeStruct(*kind)...  31 us
    ppermute x30, starting transfers between devices, gather(): lax.ppermute(block, AXIS, [(i, i ^ far) for i in range(total)])  28.3 us
    ppermute x30, waiting for transfers between devices, gather(): lax.ppermute(block, AXIS, [(i, i ^ far) for i in range(total)])  15.8 us
    ppermute x27, waiting for transfers between devices, exchange(): lax.ppermute(array, AXIS, chosen[i][0])  10.5 us
  transfers between devices with their start and end apart: 57, of which 24 were waited for; matrix products, arithmetic and copies ran while one was open for 0% of the time, Pallas kernels for 19%

profile of v8, /device:TPU:0, one launch (start us, length us, event | category | flops | bytes accessed | tf_op | source)
XLA Modules:
  0.0 124.8 jit_solution(2703126051451417740)
XLA Ops:
  2.6 4.1 %collective-permute-start.2 = (f32[152,128]{1,0:T(8,128)S(1)}, f32[152,128]{1,0:T(8,128)S(1)}, u32[]{:S(2)}, u32[]{:S(2)}) collective-permute-start(f32[152,128]{1,0:T(8,128)S(1)} %get-tuple-element.118), channel_id=1, source_target_pairs={{0,16},{1,17},{2,18},{3,19},{4,20},{5,21},{6,22},{7,23},{8,24},{9,... | collective-permute-start | bytes 233480 | tf_op jit(solution)/shard_map/ppermute | solution.py:175
  7.4 2.7 %prepare_inv.1 = (bf16[1024,1024]{1,0:T(8,128)(2,1)S(1)}, bf16[1024,1024]{1,0:T(8,128)(2,1)S(1)}, bf16[384,1024]{1,0:T(8,128)(2,1)S(1)}, bf16[384,1024]{1,0:T(8,...) custom-call(f32[1,1024,1024]{2,1,0:T(8,128)S(1)} %copy-done, ...), custom_call_target="tpu_custom_call" | custom-call | tf_op jit(solution)/shard_map/prepare_inv/pallas_call | solution.py:93
  11.1 6.3 %collective-permute-start.3 = (f32[73,128]{1,0:T(8,128)S(1)}, f32[73,128]{1,0:T(8,128)S(1)}, u32[]{:S(2)}, u32[]{:S(2)}) collective-permute-start(f32[73,128]{1,0:T(8,128)S(1)} %get-tuple-element.130.refs_0_), channel_id=1, source_target_pairs={{0,16},{1,17},{2,18},{3,19},{4,20},{5,21},{6,22},{7,23},{8,24},{9,... | collective-permute-start | bytes 112136 | tf_op jit(solution)/shard_map/ppermute | solution.py:175
  18.3 2.7 %prepare_stiff.1 = (bf16[1024,1024]{1,0:T(8,128)(2,1)S(1)}, bf16[1024,1024]{1,0:T(8,128)(2,1)S(1)}, bf16[384,1024]{1,0:T(8,128)(2,1)S(1)}, bf16[384,1024]{1,0:T(...) custom-call(f32[1,1024,1024]{2,1,0:T(8,128)S(1)} %copy-done.1, ...), custom_call_target="tpu_custom_call" | custom-call | tf_op jit(solution)/shard_map/prepare_stiff/pallas_call | solution.py:93
  21.0 1.8 %collective-permute-start.4 = (f32[18,128]{1,0:T(8,128)S(1)}, f32[18,128]{1,0:T(8,128)S(1)}, u32[]{:S(2)}, u32[]{:S(2)}) collective-permute-start(f32[18,128]{1,0:T(8,128)S(1)} %join.10.refs_0_), channel_id=1, source_target_pairs={{0,12},{1,13},{2,14},{3,15},{4,8},{5,9},{6,10},{7,11},{8,4},{9,5},... | collective-permute-start | bytes 27656 | tf_op jit(solution)/shard_map/ppermute | solution.py:184
  24.9 1.7 %reach.1 = (bf16[64,2048]{1,0:T(8,128)(2,1)S(1)}, bf16[64,2048]{1,0:T(8,128)(2,1)S(1)}, bf16[64,384]{1,0:T(8,128)(2,1)S(1)}, bf16[64,384]{1,0:T(8,128)(2,1)S(1)}, f32[128,288]{1,0:T(8,128)S(1)}) custom-call(f32[16,1024]{1,0:T(8,128)S(1)} %get-tuple-element.121.refs_2_.refs_0_.refs_14_.refs_16_.refs_22_, f32[16,512]{1,0:T(8,128)S(1)} %copy-done.3, ...), custom_call_target="tpu_custom_call" | custom-call | tf_op jit(solution)/shard_map/reach/pallas_call | solution.py:93
  27.3 1.5 %collective-permute-start.7 = (f32[72,128]{1,0:T(8,128)S(1)}, f32[72,128]{1,0:T(8,128)S(1)}, u32[]{:S(2)}, u32[]{:S(2)}) collective-permute-start(f32[72,128]{1,0:T(8,128)S(1)} %join.11.refs_0_), channel_id=1, source_target_pairs={{0,3},{1,2},{2,1},{3,0},{4,7},{5,6},{6,5},{7,4},{8,11},{9,10},{10,... | collective-permute-start | bytes 110600 | tf_op jit(solution)/shard_map/ppermute | solution.py:184
  30.1 2.0 %apply_own.4 = (f32[64,1024]{1,0:T(8,128)S(1)}, f32[64,384]{1,0:T(8,128)S(1)}, f32[64,1024]{1,0:T(8,128)S(1)}, f32[64,1024]{1,0:T(8,128)S(1)}) custom-call(f32[144,128]{1,0:T(8,128)S(1)} %collective-permute-done.refs_0_.refs_2_, f32[144,128]{1,0:T(8,128)S(1)} %collective-permute-done.1.refs_1_.refs_3_, ...), custom_call_target="tpu_custom_call" | custom-call | tf_op jit(solution)/shard_map/apply_own/pallas_call | solution.py:93
  33.3 1.8 %collective-permute-start.14 = (f32[72,128]{1,0:T(8,128)S(1)}, f32[72,128]{1,0:T(8,128)S(1)}, u32[]{:S(2)}, u32[]{:S(2)}) collective-permute-start(f32[72,128]{1,0:T(8,128)S(1)} %get-tuple-element.147), channel_id=1, source_target_pairs={{0,16},{1,17},{2,18},{3,19},{4,20},{5,21},{6,22},{7,23},{8,24},{9,... | collective-permute-start | bytes 110600 | tf_op jit(solution)/shard_map/ppermute | solution.py:175
  36.2 2.4 %update.3 = (f32[64,1024]{1,0:T(8,128)S(1)}, f32[64,1024]{1,0:T(8,128)S(1)}, f32[16,64]{1,0:T(8,128)S(1)}, f32[64,384]{1,0:T(8,128)S(1)}, f32[64,1024]{1,0:T(8,128)S(1)}, /*index=5*/f32[1,128]{1,0:T(1,128)S(1)}) custom-call(f32[64,128]{1,0:T(8,128)S(1)} %collective-permute-done.10.refs_7_.refs_0_, f32[128,128]{1,0:T(8,128)S(1)} %collective-permute-done.11.refs_8_.refs_1_, ...), custom_call_target="tpu_custom_call" | custom-call | tf_op jit(solution)/shard_map/update/pallas_call | solution.py:93
  38.9 5.7 %collective-permute-start.15 = (f32[73,128]{1,0:T(8,128)S(1)}, f32[73,128]{1,0:T(8,128)S(1)}, u32[]{:S(2)}, u32[]{:S(2)}) collective-permute-start(f32[73,128]{1,0:T(8,128)S(1)} %get-tuple-element.158.refs_0_), channel_id=1, source_target_pairs={{0,16},{1,17},{2,18},{3,19},{4,20},{5,21},{6,22},{7,23},{8,24},{9,... | collective-permute-start | bytes 112136 | tf_op jit(solution)/shard_map/ppermute | solution.py:175
  46.6 3.0 %collective-permute-start.16 = (f32[18,128]{1,0:T(8,128)S(1)}, f32[18,128]{1,0:T(8,128)S(1)}, u32[]{:S(2)}, u32[]{:S(2)}) collective-permute-start(f32[18,128]{1,0:T(8,128)S(1)} %join.12.refs_0_), channel_id=1, source_target_pairs={{0,12},{1,13},{2,14},{3,15},{4,8},{5,9},{6,10},{7,11},{8,4},{9,5},... | collective-permute-start | bytes 27656 | tf_op jit(solution)/shard_map/ppermute | solution.py:184
  51.3 2.0 %collective-permute-done.17.refs_2_ = f32[18,128]{1,0:T(8,128)S(1)} collective-permute-done((f32[18,128]{1,0:T(8,128)S(1)}, f32[18,128]{1,0:T(8,128)S(1)}, u32[]{:S(2)}, u32[]{:S(2)}) %collective-permute-start.17) | collective-permute-done | bytes 9248 | tf_op jit(solution)/shard_map/ppermute | solution.py:184
  54.1 1.8 %collective-permute-start.21 = (f32[72,128]{1,0:T(8,128)S(1)}, f32[72,128]{1,0:T(8,128)S(1)}, u32[]{:S(2)}, u32[]{:S(2)}) collective-permute-start(f32[72,128]{1,0:T(8,128)S(1)} %join.13.refs_0_), channel_id=1, source_target_pairs={{0,1},{1,0},{2,3},{3,2},{4,5},{5,4},{6,7},{7,6},{8,9},{9,8},{10,11... | collective-permute-start | bytes 110600 | tf_op jit(solution)/shard_map/ppermute | solution.py:184
  55.9 2.0 %apply_own.5 = (f32[64,1024]{1,0:T(8,128)S(1)}, f32[64,384]{1,0:T(8,128)S(1)}, f32[64,1024]{1,0:T(8,128)S(1)}, f32[64,1024]{1,0:T(8,128)S(1)}) custom-call(f32[64,128]{1,0:T(8,128)S(1)} %collective-permute-done.12.refs_0_, f32[64,128]{1,0:T(8,128)S(1)} %collective-permute-done.13.refs_1_, f32[72,128]{1,0:T(8,128)S(1)} %collective-permute-done.14.refs_2_, ...), custom_call_target="tpu_custom_call" | custom-call | tf_op jit(solution)/shard_map/apply_own/pallas_call | solution.py:93
  60.5 2.5 %update.4 = (f32[64,1024]{1,0:T(8,128)S(1)}, f32[64,1024]{1,0:T(8,128)S(1)}, f32[1,128]{1,0:T(1,128)S(1)}, f32[64,1024]{1,0:T(8,128)S(1)}, f32[64,1024]{1,0:T(8,...) custom-call(f32[64,128]{1,0:T(8,128)S(1)} %collective-permute-done.2, ...), custom_call_target="tpu_custom_call" | custom-call | tf_op jit(solution)/shard_map/update/pallas_call | solution.py:93
  64.9 4.4 %collective-permute-start.27 = (f32[73,128]{1,0:T(8,128)S(1)}, f32[73,128]{1,0:T(8,128)S(1)}, u32[]{:S(2)}, u32[]{:S(2)}) collective-permute-start(f32[73,128]{1,0:T(8,128)S(1)} %get-tuple-element.177.refs_0_), channel_id=1, source_target_pairs={{0,16},{1,17},{2,18},{3,19},{4,20},{5,21},{6,22},{7,23},{8,24},{9,... | collective-permute-start | bytes 112136 | tf_op jit(solution)/shard_map/ppermute | solution.py:175
  71.3 2.3 %collective-permute-start.28 = (f32[18,128]{1,0:T(8,128)S(1)}, f32[18,128]{1,0:T(8,128)S(1)}, u32[]{:S(2)}, u32[]{:S(2)}) collective-permute-start(f32[18,128]{1,0:T(8,128)S(1)} %join.14.refs_0_), channel_id=1, source_target_pairs={{0,12},{1,13},{2,14},{3,15},{4,8},{5,9},{6,10},{7,11},{8,4},{9,5},... | collective-permute-start | bytes 27656 | tf_op jit(solution)/shard_map/ppermute | solution.py:184
  73.6 1.5 %collective-permute-start.29 = (f32[18,128]{1,0:T(8,128)S(1)}, f32[18,128]{1,0:T(8,128)S(1)}, u32[]{:S(2)}, u32[]{:S(2)}) collective-permute-start(f32[18,128]{1,0:T(8,128)S(1)} %join.14.refs_0_), channel_id=1, source_target_pairs={{0,8},{1,9},{2,10},{3,11},{4,12},{5,13},{6,14},{7,15},{8,0},{9,1},... | collective-permute-start | bytes 27656 | tf_op jit(solution)/shard_map/ppermute | solution.py:184
  75.8 1.4 %collective-permute-done.29.refs_2_ = f32[18,128]{1,0:T(8,128)S(1)} collective-permute-done((f32[18,128]{1,0:T(8,128)S(1)}, f32[18,128]{1,0:T(8,128)S(1)}, u32[]{:S(2)}, u32[]{:S(2)}) %collective-permute-start.29) | collective-permute-done | bytes 9248 | tf_op jit(solution)/shard_map/ppermute | solution.py:184
  77.2 1.5 %collective-permute-done.30.refs_3_ = f32[18,128]{1,0:T(8,128)S(1)} collective-permute-done((f32[18,128]{1,0:T(8,128)S(1)}, f32[18,128]{1,0:T(8,128)S(1)}, u32[]{:S(2)}, u32[]{:S(2)}) %collective-permute-start.30) | collective-permute-done | bytes 9248 | tf_op jit(solution)/shard_map/ppermute | solution.py:184
  78.8 1.8 %collective-permute-start.33 = (f32[72,128]{1,0:T(8,128)S(1)}, f32[72,128]{1,0:T(8,128)S(1)}, u32[]{:S(2)}, u32[]{:S(2)}) collective-permute-start(f32[72,128]{1,0:T(8,128)S(1)} %join.15.refs_0_), channel_id=1, source_target_pairs={{0,1},{1,0},{2,3},{3,2},{4,5},{5,4},{6,7},{7,6},{8,9},{9,8},{10,11... | collective-permute-start | bytes 110600 | tf_op jit(solution)/shard_map/ppermute | solution.py:184
  80.6 2.2 %apply_own.6 = (f32[64,1024]{1,0:T(8,128)S(1)}, f32[64,384]{1,0:T(8,128)S(1)}, f32[64,1024]{1,0:T(8,128)S(1)}, f32[64,1024]{1,0:T(8,128)S(1)}, f32[64,1024]{1,0:T(8,128)S(1)}) custom-call(f32[64,128]{1,0:T(8,128)S(1)} %collective-permute-done.24.refs_0_, f32[64,128]{1,0:T(8,128)S(1)} %collective-permute-done.25.refs_1_, ...), custom_call_target="tpu_custom_call" | custom-call | tf_op jit(solution)/shard_map/apply_own/pallas_call | solution.py:93
  85.5 2.5 %update.5 = (f32[64,1024]{1,0:T(8,128)S(1)}, f32[64,1024]{1,0:T(8,128)S(1)}, f32[1,128]{1,0:T(1,128)S(1)}, f32[64,1024]{1,0:T(8,128)S(1)}, f32[64,1024]{1,0:T(8,...) custom-call(f32[64,128]{1,0:T(8,128)S(1)} %collective-permute-done.3, ...), custom_call_target="tpu_custom_call" | custom-call | tf_op jit(solution)/shard_map/update/pallas_call | solution.py:93
  89.5 4.7 %collective-permute-start.41 = (f32[73,128]{1,0:T(8,128)S(1)}, f32[73,128]{1,0:T(8,128)S(1)}, u32[]{:S(2)}, u32[]{:S(2)}) collective-permute-start(f32[73,128]{1,0:T(8,128)S(1)} %get-tuple-element.205.refs_0_), channel_id=1, source_target_pairs={{0,16},{1,17},{2,18},{3,19},{4,20},{5,21},{6,22},{7,23},{8,24},{9,... | collective-permute-start | bytes 112136 | tf_op jit(solution)/shard_map/ppermute | solution.py:175
  96.2 2.8 %collective-permute-start.42 = (f32[18,128]{1,0:T(8,128)S(1)}, f32[18,128]{1,0:T(8,128)S(1)}, u32[]{:S(2)}, u32[]{:S(2)}) collective-permute-start(f32[18,128]{1,0:T(8,128)S(1)} %join.16.refs_0_), channel_id=1, source_target_pairs={{0,12},{1,13},{2,14},{3,15},{4,8},{5,9},{6,10},{7,11},{8,4},{9,5},... | collective-permute-start | bytes 27656 | tf_op jit(solution)/shard_map/ppermute | solution.py:184
  100.8 1.9 %collective-permute-done.43.refs_2_ = f32[18,128]{1,0:T(8,128)S(1)} collective-permute-done((f32[18,128]{1,0:T(8,128)S(1)}, f32[18,128]{1,0:T(8,128)S(1)}, u32[]{:S(2)}, u32[]{:S(2)}) %collective-permute-start.43) | collective-permute-done | bytes 9248 | tf_op jit(solution)/shard_map/ppermute | solution.py:184
  103.8 1.6 %collective-permute-start.47 = (f32[72,128]{1,0:T(8,128)S(1)}, f32[72,128]{1,0:T(8,128)S(1)}, u32[]{:S(2)}, u32[]{:S(2)}) collective-permute-start(f32[72,128]{1,0:T(8,128)S(1)} %join.17.refs_20_), channel_id=1, source_target_pairs={{0,1},{1,0},{2,3},{3,2},{4,5},{5,4},{6,7},{7,6},{8,9},{9,8},{10,11... | collective-permute-start | bytes 110600 | tf_op jit(solution)/shard_map/ppermute | solution.py:184
  105.4 2.2 %apply_own.7 = (f32[64,1024]{1,0:T(8,128)S(1)}, f32[64,384]{1,0:T(8,128)S(1)}, f32[64,1024]{1,0:T(8,128)S(1)}, f32[64,1024]{1,0:T(8,128)S(1)}, f32[64,1024]{1,0:T(8,128)S(1)}) custom-call(f32[64,128]{1,0:T(8,128)S(1)} %collective-permute-done.36.refs_0_, f32[64,128]{1,0:T(8,128)S(1)} %collective-permute-done.37.refs_1_, ...), custom_call_target="tpu_custom_call" | custom-call | tf_op jit(solution)/shard_map/apply_own/pallas_call | solution.py:93
  107.7 1.5 %last.1 = (f32[64,1024]{1,0:T(8,128)S(1)}, f32[64,1024]{1,0:T(8,128)S(1)}, f32[1,128]{1,0:T(1,128)S(1)}, f32[64,1024]{1,0:T(8,128)S(1)}, f32[64,1024]{1,0:T(8,12...) custom-call(f32[64,128]{1,0:T(8,128)S(1)} %collective-permute-done.3, ...), custom_call_target="tpu_custom_call" | custom-call | tf_op jit(solution)/shard_map/last/pallas_call | solution.py:93
  110.8 4.1 %collective-permute-done.48.refs_1_.refs_6_ = f32[72,128]{1,0:T(8,128)S(1)} collective-permute-done((f32[72,128]{1,0:T(8,128)S(1)}, f32[72,128]{1,0:T(8,128)S(1)}, u32[]{:S(2)}, u32[]{:S(2)}) %collective-permute-start.48) | collective-permute-done | bytes 36896 | tf_op jit(solution)/shard_map/ppermute | solution.py:175
  116.0 2.4 %collective-permute-start.51 = (f32[2,128]{1,0:T(2,128)S(1)}, f32[2,128]{1,0:T(2,128)S(1)}, u32[]{:S(2)}, u32[]{:S(2)}) collective-permute-start(f32[2,128]{1,0:T(2,128)S(1)} %join.18.refs_0_), channel_id=1, source_target_pairs={{0,4},{1,5},{2,6},{3,7},{4,0},{5,1},{6,2},{7,3},{8,12},{9,13},{10,... | collective-permute-start | bytes 3080 | tf_op jit(solution)/shard_map/ppermute | solution.py:184
  (133 shorter events, 40.8 us)
Async XLA Ops:
  2.6 8.2 %collective-permute-start.2 = (f32[152,128]{1,0:T(8,128)S(1)}, f32[152,128]{1,0:T(8,128)S(1)}, u32[]{:S(2)}, u32[]{:S(2)}) collective-permute-start(f32[152,128]{1,0:T(8,128)S(1)} %get-tuple-element.118), channel_id=1, source_target_pairs={{0,16},{1,17},{2,18},{3,19},{4,20},{5,21},{6,22},{7,23},{8,24},{9,... | collective-permute-start | bytes 233480 | tf_op jit(solution)/shard_map/ppermute | solution.py:175
  6.7 4.1 %collective-permute-start = (f32[144,128]{1,0:T(8,128)S(1)}, f32[144,128]{1,0:T(8,128)S(1)}, u32[]{:S(2)}, u32[]{:S(2)}) collective-permute-start(f32[144,128]{1,0:T(8,128)S(1)} %get-tuple-element.116), channel_id=1, source_target_pairs={{0,1},{2,3},{4,5},{6,7},{8,9},{10,11},{12,13},{14,15},{16,17},{18,... | collective-permute-start | bytes 221192 | tf_op jit(solution)/shard_map/ppermute | solution.py:175
  6.7 4.1 %collective-permute-start.1 = (f32[144,128]{1,0:T(8,128)S(1)}, f32[144,128]{1,0:T(8,128)S(1)}, u32[]{:S(2)}, u32[]{:S(2)}) collective-permute-start(f32[144,128]{1,0:T(8,128)S(1)} %get-tuple-element.117), channel_id=1, source_target_pairs={{1,2},{3,4},{5,6},{7,8},{9,10},{11,12},{13,14},{15,16},{17,18},{19... | collective-permute-start | bytes 221192 | tf_op jit(solution)/shard_map/ppermute | solution.py:175
  11.1 9.9 %collective-permute-start.3 = (f32[73,128]{1,0:T(8,128)S(1)}, f32[73,128]{1,0:T(8,128)S(1)}, u32[]{:S(2)}, u32[]{:S(2)}) collective-permute-start(f32[73,128]{1,0:T(8,128)S(1)} %get-tuple-element.130.refs_0_), channel_id=1, source_target_pairs={{0,16},{1,17},{2,18},{3,19},{4,20},{5,21},{6,22},{7,23},{8,24},{9,... | collective-permute-start | bytes 112136 | tf_op jit(solution)/shard_map/ppermute | solution.py:175
  17.5 14.6 %collective-permute-start.11 = (f32[128,128]{1,0:T(8,128)S(1)}, f32[128,128]{1,0:T(8,128)S(1)}, u32[]{:S(2)}, u32[]{:S(2)}) collective-permute-start(f32[128,128]{1,0:T(8,128)S(1)} %get-tuple-element.140), channel_id=1, source_target_pairs={{1,2},{3,4},{5,6},{7,8},{9,10},{11,12},{13,14},{15,16},{17,18},{19... | collective-permute-start | bytes 196616 | tf_op jit(solution)/shard_map/ppermute | solution.py:175
  21.0 5.6 %collective-permute-start.4 = (f32[18,128]{1,0:T(8,128)S(1)}, f32[18,128]{1,0:T(8,128)S(1)}, u32[]{:S(2)}, u32[]{:S(2)}) collective-permute-start(f32[18,128]{1,0:T(8,128)S(1)} %join.10.refs_0_), channel_id=1, source_target_pairs={{0,12},{1,13},{2,14},{3,15},{4,8},{5,9},{6,10},{7,11},{8,4},{9,5},... | collective-permute-start | bytes 27656 | tf_op jit(solution)/shard_map/ppermute | solution.py:184
  27.3 4.8 %collective-permute-start.7 = (f32[72,128]{1,0:T(8,128)S(1)}, f32[72,128]{1,0:T(8,128)S(1)}, u32[]{:S(2)}, u32[]{:S(2)}) collective-permute-start(f32[72,128]{1,0:T(8,128)S(1)} %join.11.refs_0_), channel_id=1, source_target_pairs={{0,3},{1,2},{2,1},{3,0},{4,7},{5,6},{6,5},{7,4},{8,11},{9,10},{10,... | collective-permute-start | bytes 110600 | tf_op jit(solution)/shard_map/ppermute | solution.py:184
  28.8 4.0 %collective-permute-start.8 = (f32[72,128]{1,0:T(8,128)S(1)}, f32[72,128]{1,0:T(8,128)S(1)}, u32[]{:S(2)}, u32[]{:S(2)}) collective-permute-start(f32[72,128]{1,0:T(8,128)S(1)} %join.11.refs_0_), channel_id=1, source_target_pairs={{0,2},{1,3},{2,0},{3,1},{4,6},{5,7},{6,4},{7,5},{8,10},{9,11},{10,... | collective-permute-start | bytes 110600 | tf_op jit(solution)/shard_map/ppermute | solution.py:184
  33.3 5.3 %collective-permute-start.14 = (f32[72,128]{1,0:T(8,128)S(1)}, f32[72,128]{1,0:T(8,128)S(1)}, u32[]{:S(2)}, u32[]{:S(2)}) collective-permute-start(f32[72,128]{1,0:T(8,128)S(1)} %get-tuple-element.147), channel_id=1, source_target_pairs={{0,16},{1,17},{2,18},{3,19},{4,20},{5,21},{6,22},{7,23},{8,24},{9,... | collective-permute-start | bytes 110600 | tf_op jit(solution)/shard_map/ppermute | solution.py:175
  38.9 7.7 %collective-permute-start.15 = (f32[73,128]{1,0:T(8,128)S(1)}, f32[73,128]{1,0:T(8,128)S(1)}, u32[]{:S(2)}, u32[]{:S(2)}) collective-permute-start(f32[73,128]{1,0:T(8,128)S(1)} %get-tuple-element.158.refs_0_), channel_id=1, source_target_pairs={{0,16},{1,17},{2,18},{3,19},{4,20},{5,21},{6,22},{7,23},{8,24},{9,... | collective-permute-start | bytes 112136 | tf_op jit(solution)/shard_map/ppermute | solution.py:175
  44.6 13.3 %collective-permute-start.23 = (f32[128,128]{1,0:T(8,128)S(1)}, f32[128,128]{1,0:T(8,128)S(1)}, u32[]{:S(2)}, u32[]{:S(2)}) collective-permute-start(f32[128,128]{1,0:T(8,128)S(1)} %get-tuple-element.160), channel_id=1, source_target_pairs={{1,2},{3,4},{5,6},{7,8},{9,10},{11,12},{13,14},{15,16},{17,18},{19... | collective-permute-start | bytes 196616 | tf_op jit(solution)/shard_map/ppermute | solution.py:175
  46.6 4.7 %collective-permute-start.16 = (f32[18,128]{1,0:T(8,128)S(1)}, f32[18,128]{1,0:T(8,128)S(1)}, u32[]{:S(2)}, u32[]{:S(2)}) collective-permute-start(f32[18,128]{1,0:T(8,128)S(1)} %join.12.refs_0_), channel_id=1, source_target_pairs={{0,12},{1,13},{2,14},{3,15},{4,8},{5,9},{6,10},{7,11},{8,4},{9,5},... | collective-permute-start | bytes 27656 | tf_op jit(solution)/shard_map/ppermute | solution.py:184
  54.0 4.2 %collective-permute-start.20 = (f32[72,128]{1,0:T(8,128)S(1)}, f32[72,128]{1,0:T(8,128)S(1)}, u32[]{:S(2)}, u32[]{:S(2)}) collective-permute-start(f32[72,128]{1,0:T(8,128)S(1)} %join.13.refs_0_), channel_id=1, source_target_pairs={{0,2},{1,3},{2,0},{3,1},{4,6},{5,7},{6,4},{7,5},{8,10},{9,11},{10,... | collective-permute-start | bytes 110600 | tf_op jit(solution)/shard_map/ppermute | solution.py:184
  54.1 4.1 %collective-permute-start.21 = (f32[72,128]{1,0:T(8,128)S(1)}, f32[72,128]{1,0:T(8,128)S(1)}, u32[]{:S(2)}, u32[]{:S(2)}) collective-permute-start(f32[72,128]{1,0:T(8,128)S(1)} %join.13.refs_0_), channel_id=1, source_target_pairs={{0,1},{1,0},{2,3},{3,2},{4,5},{5,4},{6,7},{7,6},{8,9},{9,8},{10,11... | collective-permute-start | bytes 110600 | tf_op jit(solution)/shard_map/ppermute | solution.py:184
  58.8 5.7 %collective-permute-start.26 = (f32[72,128]{1,0:T(8,128)S(1)}, f32[72,128]{1,0:T(8,128)S(1)}, u32[]{:S(2)}, u32[]{:S(2)}) collective-permute-start(f32[72,128]{1,0:T(8,128)S(1)} %get-tuple-element.166), channel_id=1, source_target_pairs={{0,16},{1,17},{2,18},{3,19},{4,20},{5,21},{6,22},{7,23},{8,24},{9,... | collective-permute-start | bytes 110600 | tf_op jit(solution)/shard_map/ppermute | solution.py:175
  64.9 6.4 %collective-permute-start.27 = (f32[73,128]{1,0:T(8,128)S(1)}, f32[73,128]{1,0:T(8,128)S(1)}, u32[]{:S(2)}, u32[]{:S(2)}) collective-permute-start(f32[73,128]{1,0:T(8,128)S(1)} %get-tuple-element.177.refs_0_), channel_id=1, source_target_pairs={{0,16},{1,17},{2,18},{3,19},{4,20},{5,21},{6,22},{7,23},{8,24},{9,... | collective-permute-start | bytes 112136 | tf_op jit(solution)/shard_map/ppermute | solution.py:175
  69.3 13.5 %collective-permute-start.35 = (f32[128,128]{1,0:T(8,128)S(1)}, f32[128,128]{1,0:T(8,128)S(1)}, u32[]{:S(2)}, u32[]{:S(2)}) collective-permute-start(f32[128,128]{1,0:T(8,128)S(1)} %get-tuple-element.179), channel_id=1, source_target_pairs={{1,2},{3,4},{5,6},{7,8},{9,10},{11,12},{13,14},{15,16},{17,18},{19... | collective-permute-start | bytes 196616 | tf_op jit(solution)/shard_map/ppermute | solution.py:175
  71.3 4.6 %collective-permute-start.28 = (f32[18,128]{1,0:T(8,128)S(1)}, f32[18,128]{1,0:T(8,128)S(1)}, u32[]{:S(2)}, u32[]{:S(2)}) collective-permute-start(f32[18,128]{1,0:T(8,128)S(1)} %join.14.refs_0_), channel_id=1, source_target_pairs={{0,12},{1,13},{2,14},{3,15},{4,8},{5,9},{6,10},{7,11},{8,4},{9,5},... | collective-permute-start | bytes 27656 | tf_op jit(solution)/shard_map/ppermute | solution.py:184
  78.7 4.1 %collective-permute-start.31 = (f32[72,128]{1,0:T(8,128)S(1)}, f32[72,128]{1,0:T(8,128)S(1)}, u32[]{:S(2)}, u32[]{:S(2)}) collective-permute-start(f32[72,128]{1,0:T(8,128)S(1)} %join.15.refs_0_), channel_id=1, source_target_pairs={{0,3},{1,2},{2,1},{3,0},{4,7},{5,6},{6,5},{7,4},{8,11},{9,10},{10,... | collective-permute-start | bytes 110600 | tf_op jit(solution)/shard_map/ppermute | solution.py:184
  78.8 4.2 %collective-permute-start.32 = (f32[72,128]{1,0:T(8,128)S(1)}, f32[72,128]{1,0:T(8,128)S(1)}, u32[]{:S(2)}, u32[]{:S(2)}) collective-permute-start(f32[72,128]{1,0:T(8,128)S(1)} %join.15.refs_0_), channel_id=1, source_target_pairs={{0,2},{1,3},{2,0},{3,1},{4,6},{5,7},{6,4},{7,5},{8,10},{9,11},{10,... | collective-permute-start | bytes 110600 | tf_op jit(solution)/shard_map/ppermute | solution.py:184
  78.8 4.1 %collective-permute-start.33 = (f32[72,128]{1,0:T(8,128)S(1)}, f32[72,128]{1,0:T(8,128)S(1)}, u32[]{:S(2)}, u32[]{:S(2)}) collective-permute-start(f32[72,128]{1,0:T(8,128)S(1)} %join.15.refs_0_), channel_id=1, source_target_pairs={{0,1},{1,0},{2,3},{3,2},{4,5},{5,4},{6,7},{7,6},{8,9},{9,8},{10,11... | collective-permute-start | bytes 110600 | tf_op jit(solution)/shard_map/ppermute | solution.py:184
  83.5 5.5 %collective-permute-start.38 = (f32[72,128]{1,0:T(8,128)S(1)}, f32[72,128]{1,0:T(8,128)S(1)}, u32[]{:S(2)}, u32[]{:S(2)}) collective-permute-start(f32[72,128]{1,0:T(8,128)S(1)} %get-tuple-element.186), channel_id=1, source_target_pairs={{0,16},{1,17},{2,18},{3,19},{4,20},{5,21},{6,22},{7,23},{8,24},{9,... | collective-permute-start | bytes 110600 | tf_op jit(solution)/shard_map/ppermute | solution.py:175
  89.5 6.7 %collective-permute-start.41 = (f32[73,128]{1,0:T(8,128)S(1)}, f32[73,128]{1,0:T(8,128)S(1)}, u32[]{:S(2)}, u32[]{:S(2)}) collective-permute-start(f32[73,128]{1,0:T(8,128)S(1)} %get-tuple-element.205.refs_0_), channel_id=1, source_target_pairs={{0,16},{1,17},{2,18},{3,19},{4,20},{5,21},{6,22},{7,23},{8,24},{9,... | collective-permute-start | bytes 112136 | tf_op jit(solution)/shard_map/ppermute | solution.py:175
  94.2 13.4 %collective-permute-start.40 = (f32[128,128]{1,0:T(8,128)S(1)}, f32[128,128]{1,0:T(8,128)S(1)}, u32[]{:S(2)}, u32[]{:S(2)}) collective-permute-start(f32[128,128]{1,0:T(8,128)S(1)} %get-tuple-element.204), channel_id=1, source_target_pairs={{1,2},{3,4},{5,6},{7,8},{9,10},{11,12},{13,14},{15,16},{17,18},{19... | collective-permute-start | bytes 196616 | tf_op jit(solution)/shard_map/ppermute | solution.py:175
  96.2 4.6 %collective-permute-start.42 = (f32[18,128]{1,0:T(8,128)S(1)}, f32[18,128]{1,0:T(8,128)S(1)}, u32[]{:S(2)}, u32[]{:S(2)}) collective-permute-start(f32[18,128]{1,0:T(8,128)S(1)} %join.16.refs_0_), channel_id=1, source_target_pairs={{0,12},{1,13},{2,14},{3,15},{4,8},{5,9},{6,10},{7,11},{8,4},{9,5},... | collective-permute-start | bytes 27656 | tf_op jit(solution)/shard_map/ppermute | solution.py:184
  103.6 4.1 %collective-permute-start.45 = (f32[72,128]{1,0:T(8,128)S(1)}, f32[72,128]{1,0:T(8,128)S(1)}, u32[]{:S(2)}, u32[]{:S(2)}) collective-permute-start(f32[72,128]{1,0:T(8,128)S(1)} %join.17.refs_20_), channel_id=1, source_target_pairs={{0,3},{1,2},{2,1},{3,0},{4,7},{5,6},{6,5},{7,4},{8,11},{9,10},{10,... | collective-permute-start | bytes 110600 | tf_op jit(solution)/shard_map/ppermute | solution.py:184
  103.6 4.2 %collective-permute-start.46 = (f32[72,128]{1,0:T(8,128)S(1)}, f32[72,128]{1,0:T(8,128)S(1)}, u32[]{:S(2)}, u32[]{:S(2)}) collective-permute-start(f32[72,128]{1,0:T(8,128)S(1)} %join.17.refs_20_), channel_id=1, source_target_pairs={{0,2},{1,3},{2,0},{3,1},{4,6},{5,7},{6,4},{7,5},{8,10},{9,11},{10,... | collective-permute-start | bytes 110600 | tf_op jit(solution)/shard_map/ppermute | solution.py:184
  109.3 5.7 %collective-permute-start.48 = (f32[72,128]{1,0:T(8,128)S(1)}, f32[72,128]{1,0:T(8,128)S(1)}, u32[]{:S(2)}, u32[]{:S(2)}) collective-permute-start(f32[72,128]{1,0:T(8,128)S(1)} %get-tuple-element.220.refs_0_), channel_id=1, source_target_pairs={{0,16},{1,17},{2,18},{3,19},{4,20},{5,21},{6,22},{7,23},{8,24},{9,... | collective-permute-start | bytes 110600 | tf_op jit(solution)/shard_map/ppermute | solution.py:175
  110.1 11.7 %collective-permute-start.55 = (f32[64,128]{1,0:T(8,128)S(1)}, f32[64,128]{1,0:T(8,128)S(1)}, u32[]{:S(2)}, u32[]{:S(2)}) collective-permute-start(f32[64,128]{1,0:T(8,128)S(1)} %get-tuple-element.221), channel_id=1, source_target_pairs={{0,1},{2,3},{4,5},{6,7},{8,9},{10,11},{12,13},{14,15},{16,17},{18,... | collective-permute-start | bytes 98312 | tf_op jit(solution)/shard_map/ppermute | solution.py:175
  110.2 11.7 %collective-permute-start.56 = (f32[64,128]{1,0:T(8,128)S(1)}, f32[64,128]{1,0:T(8,128)S(1)}, u32[]{:S(2)}, u32[]{:S(2)}) collective-permute-start(f32[64,128]{1,0:T(8,128)S(1)} %get-tuple-element.222), channel_id=1, source_target_pairs={{1,2},{3,4},{5,6},{7,8},{9,10},{11,12},{13,14},{15,16},{17,18},{19... | collective-permute-start | bytes 98312 | tf_op jit(solution)/shard_map/ppermute | solution.py:175
  114.9 4.5 %collective-permute-start.49 = (f32[2,128]{1,0:T(2,128)S(1)}, f32[2,128]{1,0:T(2,128)S(1)}, u32[]{:S(2)}, u32[]{:S(2)}) collective-permute-start(f32[2,128]{1,0:T(2,128)S(1)} %join.18.refs_0_), channel_id=1, source_target_pairs={{0,12},{1,13},{2,14},{3,15},{4,8},{5,9},{6,10},{7,11},{8,4},{9,5},... | collective-permute-start | bytes 3080 | tf_op jit(solution)/shard_map/ppermute | solution.py:184
  116.0 4.0 %collective-permute-start.51 = (f32[2,128]{1,0:T(2,128)S(1)}, f32[2,128]{1,0:T(2,128)S(1)}, u32[]{:S(2)}, u32[]{:S(2)}) collective-permute-start(f32[2,128]{1,0:T(2,128)S(1)} %join.18.refs_0_), channel_id=1, source_target_pairs={{0,4},{1,5},{2,6},{3,7},{4,0},{5,1},{6,2},{7,3},{8,12},{9,13},{10,... | collective-permute-start | bytes 3080 | tf_op jit(solution)/shard_map/ppermute | solution.py:184
  (34 other events, 119.4 us)

commit v9 on v8

--- a/solution.py
+++ b/solution.py
@@ -31,18 +31,30 @@
     return high, (value - high.astype(F32)).astype(BF)
 
 
-def times(value, high, low, dims=NN):
+def in_three(value):
+    top, rest = split(value)
+    return top, rest, (value - top.astype(F32) - rest.astype(F32)).astype(BF)
+
+
+def times(value, high, low, dims=NN, lowest=None):
     rows = value.shape[0]
-    top, rest = split(value)
-    both = contract(jnp.concatenate([top, rest], axis=0), high, dims)
-    return both[:rows] + both[rows:] + contract(top, low, dims)
+    top, rest, last = in_three(value)
+    first = contract(jnp.concatenate([top, rest, last], axis=0), high, dims)
+    second = contract(jnp.concatenate([top, rest], axis=0), low, dims)
+    small = first[2 * rows:] + second[rows:]
+    if lowest is not None:
+        small += contract(top, lowest, dims)
+    return first[:rows] + (first[rows:2 * rows] + second[:rows] + small)
+
+
+def product(left, right, dims=NN):
+    high, low, lowest = in_three(right)
+    return times(left, high, low, dims, lowest)
 
 
 def pick(value, onehot, dims=NN):
     rows = value.shape[0]
-    top, rest = split(value)
-    last = (value - top.astype(F32) - rest.astype(F32)).astype(BF)
-    parts = contract(jnp.concatenate([top, rest, last], axis=0), onehot, dims)
+    parts = contract(jnp.concatenate(in_three(value), axis=0), onehot, dims)
     return parts[:rows] + (parts[rows:2 * rows] + parts[2 * rows:])
 
 
@@ -117,8 +129,8 @@
     rounds = [[CYCLE]]
     if len(bits) % 2:
         rounds.append([bits.pop(0)])
-    while bits:
-        far, near = bits.pop(0), bits.pop(0)
+    middle = len(bits) // 2
+    for far, near in zip(bits[:middle], bits[middle:]):
         rounds.append([near + far, far, near])
     places = [0]
     for distances in rounds:
@@ -180,7 +192,7 @@
             def join(i, o):
                 o.block[...] = jnp.concatenate([ref[start:start + lines] for ref in i.pieces], axis=0)
 
-            block = stage("join", join, dict(pieces=pieces, beside=list(beside[at:at + 1])), dict(block=((lines * len(pieces), 2 * cases), F32))).block
+            block = stage("join", join, dict(pieces=pieces, beside=beside[at] if at < len(beside) else []), dict(block=((lines * len(pieces), 2 * cases), F32))).block
             pieces = [block] + [lax.ppermute(block, AXIS, [(i, i ^ far) for i in range(total)]) for far in distances]
             start, lines = 0, block.shape[0]
         return pieces
@@ -256,12 +268,12 @@
 
     def solve_own(part, i, o):
         scaled = part * i.weight[...]
-        o.lines[...] = times(i.weighted[...], *split(part), NT)
+        o.lines[...] = product(i.weighted[...], part, NT)
         o.inner_faces[...] = times(scaled, i.inv[2][...], i.inv[3][...], NT)
         o.inner[...] = times(scaled, i.inv[0][...], i.inv[1][...])
 
     def loads_faces(i, o):
-        o.lines[...] = times(i.weighted[...], *split(i.load[0]), NT)
+        o.lines[...] = product(i.weighted[...], i.load[0], NT)
         o.inner_faces[...] = times(i.load[0] * i.weight[...], i.inv[0][...], i.inv[1][...], NT)
 
     def loads_inner(i, o):
@@ -306,7 +318,7 @@
             arrived = joined(i.came)
             if coef is not None:
                 arrived = to_column(i.coef[:, cases:]) * -arrived
-            lines = i.lines[...] + times(i.basis_slots[...], *split(arrived), NT)
+            lines = i.lines[...] + product(i.basis_slots[...], arrived, NT)
             put_faces(o.face, 0.5 * (i.inner_faces[...] + times(0.5 * arrived, i.inv[0][...], i.inv[1][...])))
             o.face[paired][cases:cases + half] = jnp.concatenate([lines[:half], lines[half:]], axis=1)
             o.face[paired][cases + half:] = i.sums[...] if sums is not None else jnp.zeros((1, 2 * cases), F32)
@@ -349,8 +361,8 @@
 
     def corrected(i):
         rows = jnp.concatenate([ref[...] for ref in i.everyone], axis=0)
-        product = times(i.rows[...], *split(rows))
-        factors = (product[:own_rows, :cases] + product[own_rows:, cases:]).T
+        halves = product(i.rows[...], rows)
+        factors = (halves[:own_rows, :cases] + halves[own_rows:, cases:]).T
         at_slots = i.image_faces[...] + times(joined(i.came), i.stiff_block[0][...], i.stiff_block[1][...])
         both = both_sums([ref[...] for ref in i.everyone], lines_a_block)
         return at_slots + times(factors, i.reach_faces[0][...], i.reach_faces[1][...]), factors, both
@@ -401,7 +413,7 @@
         sent, came_solve = to_solve(came_image, own, coef, sums)
         applied = to_apply(step, came_image, own, state, coef)
         vars(state).update(vars(applied))
-        everyone = gather(sent, came_solve[paired], lines_a_block, (stiff[4], reached.rows) if step == 0 else ())
+        everyone = gather(sent, came_solve[paired], lines_a_block, ([stiff[4]], [reached.rows, own.inner]) if step == 0 else ())
         rest_ins = dict(everyone=everyone, rows=reached.rows, reach_faces=reached.reach_faces, came=came_solve, stiff_block=stiff[4:],
                         image_faces=state.image_faces)
         ins = dict(came=came_solve, picker=picker, stiff=stiff[2:4], weight=weight, residual=state.residual, reach=reached.reach,
@@ -446,21 +458,24 @@
         if step > 0:
             coef = own.coef
 
+    def settle(i, o):
+        alpha_old = as_columns(i.coef[...])[1]
+        o.w[...] = i.w_part[...] - alpha_old * pick(joined(i.came), i.picker[...])
+
     def finish(i, o):
         gamma_old, alpha_old = as_columns(i.coef[...])
-        w = i.w_part[...] - alpha_old * pick(joined(i.came), i.picker[...])
         gamma, delta = as_columns(both_sums([ref[...] for ref in i.everyone], 1))
         beta = gamma / gamma_old
         alpha = gamma / (delta - beta * gamma / alpha_old)
         o.solution[0] = i.x[...] + alpha * (i.u[...] + beta * i.p[...])
-        o.remainder[0] = i.residual[...] - alpha * (w + beta * i.s[...])
+        o.remainder[0] = i.residual[...] - alpha * (i.w[...] + beta * i.s[...])
 
     whole = ((1, cases, ndof), F32)
     everyone = gather(state.face[paired], came_image[paired], 1)
+    w = stage("settle", settle, dict(came=came_image, picker=picker, coef=state.coef, w_part=state.w_part), dict(w=vec)).w
     done = stage(
         "finish", finish,
-        dict(everyone=everyone, came=came_image, picker=picker, coef=state.coef, w_part=state.w_part, x=state.x, u=state.u, p=state.p,
-             residual=state.residual, s=state.s),
+        dict(everyone=everyone, coef=state.coef, w=w, x=state.x, u=state.u, p=state.p, residual=state.residual, s=state.s),
         dict(solution=whole, remainder=whole))
     return done.solution, done.remainder
 

time: 125 us -> 126 us (level)
  waiting for transfers between devices: 26.3 us -> 21.1 us
  starting transfers between devices: 65.3 us -> 69.1 us
  Pallas kernels: 31 us -> 33.1 us
    ppermute x27, waiting for transfers between devices: 10.5 us -> 7.62 us  [exchange(): lax.ppermute(array, AXIS, chosen[i][0])]
    ppermute x27, starting transfers between devices: 37 us -> 39.3 us  [exchange(): lax.ppermute(array, AXIS, chosen[i][0])]
    ppermute x30, waiting for transfers between devices: 15.8 us -> 13.5 us  [gather(): lax.ppermute(block, AXIS, [(i, i ^ far) for i in range(total)])]
    pallas_call x33 -> x34, Pallas kernels: 31 us -> 33.1 us  [stage(): pl.pallas_call(kernel, name=name, out_shape=[jax.ShapeDtypeStruct(*kind)...]
    ppermute x30, starting transfers between devices: 28.3 us -> 29.7 us  [gather(): lax.ppermute(block, AXIS, [(i, i ^ far) for i in range(total)])]
  transfers between devices with their start and end apart: 57 -> 57, of which waited for: 24 -> 24; matrix products, arithmetic and copies ran while one was open for 0% -> 0% of each run, Pallas kernels for 19% -> 20%
where the time goes in v9:
time: 126 us; the launch traced here: 125 us
  starting transfers between devices  69.1 us (55%)
  Pallas kernels  33.1 us (26%)
  waiting for transfers between devices  21.1 us (17%)
    ppermute x27, starting transfers between devices, exchange(): lax.ppermute(array, AXIS, chosen[i][0])  39.3 us
    pallas_call x34, Pallas kernels, stage(): pl.pallas_call(kernel, name=name, out_shape=[jax.ShapeDtypeStruct(*kind)...  33.1 us
    ppermute x30, starting transfers between devices, gather(): lax.ppermute(block, AXIS, [(i, i ^ far) for i in range(total)])  29.7 us
    ppermute x30, waiting for transfers between devices, gather(): lax.ppermute(block, AXIS, [(i, i ^ far) for i in range(total)])  13.5 us
    ppermute x27, waiting for transfers between devices, exchange(): lax.ppermute(array, AXIS, chosen[i][0])  7.62 us
  transfers between devices with their start and end apart: 57, of which 24 were waited for; matrix products, arithmetic and copies ran while one was open for 0% of the time, Pallas kernels for 20%

profile of v9, /device:TPU:0, one launch (start us, length us, event | category | flops | bytes accessed | tf_op | source)
XLA Modules:
  0.0 125.5 jit_solution(18125601031884301373)
XLA Ops:
  2.6 4.1 %collective-permute-start.2 = (f32[152,128]{1,0:T(8,128)S(1)}, f32[152,128]{1,0:T(8,128)S(1)}, u32[]{:S(2)}, u32[]{:S(2)}) collective-permute-start(f32[152,128]{1,0:T(8,128)S(1)} %get-tuple-element.118), channel_id=1, source_target_pairs={{0,16},{1,17},{2,18},{3,19},{4,20},{5,21},{6,22},{7,23},{8,24},{9,... | collective-permute-start | bytes 233480 | tf_op jit(solution)/shard_map/ppermute | solution.py:187
  7.4 2.7 %prepare_inv.1 = (bf16[1024,1024]{1,0:T(8,128)(2,1)S(1)}, bf16[1024,1024]{1,0:T(8,128)(2,1)S(1)}, bf16[384,1024]{1,0:T(8,128)(2,1)S(1)}, bf16[384,1024]{1,0:T(8,...) custom-call(f32[1,1024,1024]{2,1,0:T(8,128)S(1)} %copy-done, ...), custom_call_target="tpu_custom_call" | custom-call | tf_op jit(solution)/shard_map/prepare_inv/pallas_call | solution.py:105
  11.3 6.3 %collective-permute-start.3 = (f32[73,128]{1,0:T(8,128)S(1)}, f32[73,128]{1,0:T(8,128)S(1)}, u32[]{:S(2)}, u32[]{:S(2)}) collective-permute-start(f32[73,128]{1,0:T(8,128)S(1)} %get-tuple-element.130.refs_0_), channel_id=1, source_target_pairs={{0,16},{1,17},{2,18},{3,19},{4,20},{5,21},{6,22},{7,23},{8,24},{9,... | collective-permute-start | bytes 112136 | tf_op jit(solution)/shard_map/ppermute | solution.py:187
  18.3 2.7 %prepare_stiff.1 = (bf16[1024,1024]{1,0:T(8,128)(2,1)S(1)}, bf16[1024,1024]{1,0:T(8,128)(2,1)S(1)}, bf16[384,1024]{1,0:T(8,128)(2,1)S(1)}, bf16[384,1024]{1,0:T(...) custom-call(f32[1,1024,1024]{2,1,0:T(8,128)S(1)} %copy-done.1, ...), custom_call_target="tpu_custom_call" | custom-call | tf_op jit(solution)/shard_map/prepare_stiff/pallas_call | solution.py:105
  21.6 1.9 %collective-permute-start.5 = (f32[18,128]{1,0:T(8,128)S(1)}, f32[18,128]{1,0:T(8,128)S(1)}, u32[]{:S(2)}, u32[]{:S(2)}) collective-permute-start(f32[18,128]{1,0:T(8,128)S(1)} %join.10.refs_0_), channel_id=1, source_target_pairs={{0,8},{1,9},{2,10},{3,11},{4,12},{5,13},{6,14},{7,15},{8,0},{9,1},... | collective-permute-start | bytes 27656 | tf_op jit(solution)/shard_map/ppermute | solution.py:196
  23.5 1.4 %collective-permute-start.6 = (f32[18,128]{1,0:T(8,128)S(1)}, f32[18,128]{1,0:T(8,128)S(1)}, u32[]{:S(2)}, u32[]{:S(2)}) collective-permute-start(f32[18,128]{1,0:T(8,128)S(1)} %join.10.refs_0_), channel_id=1, source_target_pairs={{0,2},{1,3},{2,0},{3,1},{4,6},{5,7},{6,4},{7,5},{8,10},{9,11},{10,... | collective-permute-start | bytes 27656 | tf_op jit(solution)/shard_map/ppermute | solution.py:196
  25.8 1.7 %reach.1 = (bf16[64,2048]{1,0:T(8,128)(2,1)S(1)}, bf16[64,2048]{1,0:T(8,128)(2,1)S(1)}, bf16[64,384]{1,0:T(8,128)(2,1)S(1)}, bf16[64,384]{1,0:T(8,128)(2,1)S(1)}, f32[128,288]{1,0:T(8,128)S(1)}) custom-call(f32[16,1024]{1,0:T(8,128)S(1)} %get-tuple-element.121.refs_2_.refs_0_.refs_14_.refs_16_.refs_22_, f32[16,512]{1,0:T(8,128)S(1)} %copy-done.3, ...), custom_call_target="tpu_custom_call" | custom-call | tf_op jit(solution)/shard_map/reach/pallas_call | solution.py:105
  29.5 2.0 %apply_own.4 = (f32[64,1024]{1,0:T(8,128)S(1)}, f32[64,384]{1,0:T(8,128)S(1)}, f32[64,1024]{1,0:T(8,128)S(1)}, f32[64,1024]{1,0:T(8,128)S(1)}) custom-call(f32[144,128]{1,0:T(8,128)S(1)} %collective-permute-done.refs_0_.refs_2_, f32[144,128]{1,0:T(8,128)S(1)} %collective-permute-done.1.refs_1_.refs_3_, ...), custom_call_target="tpu_custom_call" | custom-call | tf_op jit(solution)/shard_map/apply_own/pallas_call | solution.py:105
  33.6 2.0 %collective-permute-start.14 = (f32[72,128]{1,0:T(8,128)S(1)}, f32[72,128]{1,0:T(8,128)S(1)}, u32[]{:S(2)}, u32[]{:S(2)}) collective-permute-start(f32[72,128]{1,0:T(8,128)S(1)} %get-tuple-element.147), channel_id=1, source_target_pairs={{0,16},{1,17},{2,18},{3,19},{4,20},{5,21},{6,22},{7,23},{8,24},{9,... | collective-permute-start | bytes 110600 | tf_op jit(solution)/shard_map/ppermute | solution.py:187
  36.4 2.4 %update.3 = (f32[64,1024]{1,0:T(8,128)S(1)}, f32[64,1024]{1,0:T(8,128)S(1)}, f32[16,64]{1,0:T(8,128)S(1)}, f32[64,384]{1,0:T(8,128)S(1)}, f32[64,1024]{1,0:T(8,128)S(1)}, /*index=5*/f32[1,128]{1,0:T(1,128)S(1)}) custom-call(f32[64,128]{1,0:T(8,128)S(1)} %collective-permute-done.10.refs_7_.refs_0_, f32[128,128]{1,0:T(8,128)S(1)} %collective-permute-done.11.refs_8_.refs_1_, ...), custom_call_target="tpu_custom_call" | custom-call | tf_op jit(solution)/shard_map/update/pallas_call | solution.py:105
  39.3 4.7 %collective-permute-start.15 = (f32[73,128]{1,0:T(8,128)S(1)}, f32[73,128]{1,0:T(8,128)S(1)}, u32[]{:S(2)}, u32[]{:S(2)}) collective-permute-start(f32[73,128]{1,0:T(8,128)S(1)} %get-tuple-element.158.refs_0_), channel_id=1, source_target_pairs={{0,16},{1,17},{2,18},{3,19},{4,20},{5,21},{6,22},{7,23},{8,24},{9,... | collective-permute-start | bytes 112136 | tf_op jit(solution)/shard_map/ppermute | solution.py:187
  44.7 2.2 %collective-permute-done.15.refs_1_.refs_9_.refs_2_ = f32[73,128]{1,0:T(8,128)S(1)} collective-permute-done((f32[73,128]{1,0:T(8,128)S(1)}, f32[73,128]{1,0:T(8,128)S(1)}, u32[]{:S(2)}, u32[]{:S(2)}) %collective-permute-start.15) | collective-permute-done | bytes 37408 | tf_op jit(solution)/shard_map/ppermute | solution.py:187
  46.9 2.1 %collective-permute-start.16 = (f32[18,128]{1,0:T(8,128)S(1)}, f32[18,128]{1,0:T(8,128)S(1)}, u32[]{:S(2)}, u32[]{:S(2)}) collective-permute-start(f32[18,128]{1,0:T(8,128)S(1)} %join.12.refs_0_), channel_id=1, source_target_pairs={{0,10},{1,11},{2,8},{3,9},{4,14},{5,15},{6,12},{7,13},{8,2},{9,3},... | collective-permute-start | bytes 27656 | tf_op jit(solution)/shard_map/ppermute | solution.py:196
  49.6 1.4 %collective-permute-start.18 = (f32[18,128]{1,0:T(8,128)S(1)}, f32[18,128]{1,0:T(8,128)S(1)}, u32[]{:S(2)}, u32[]{:S(2)}) collective-permute-start(f32[18,128]{1,0:T(8,128)S(1)} %join.12.refs_0_), channel_id=1, source_target_pairs={{0,2},{1,3},{2,0},{3,1},{4,6},{5,7},{6,4},{7,5},{8,10},{9,11},{10,... | collective-permute-start | bytes 27656 | tf_op jit(solution)/shard_map/ppermute | solution.py:196
  55.1 2.0 %apply_own.5 = (f32[64,1024]{1,0:T(8,128)S(1)}, f32[64,384]{1,0:T(8,128)S(1)}, f32[64,1024]{1,0:T(8,128)S(1)}, f32[64,1024]{1,0:T(8,128)S(1)}) custom-call(f32[64,128]{1,0:T(8,128)S(1)} %collective-permute-done.12.refs_0_, f32[64,128]{1,0:T(8,128)S(1)} %collective-permute-done.13.refs_1_, f32[72,128]{1,0:T(8,128)S(1)} %collective-permute-done.14.refs_2_, ...), custom_call_target="tpu_custom_call" | custom-call | tf_op jit(solution)/shard_map/apply_own/pallas_call | solution.py:105
  58.1 2.2 %collective-permute-start.26 = (f32[72,128]{1,0:T(8,128)S(1)}, f32[72,128]{1,0:T(8,128)S(1)}, u32[]{:S(2)}, u32[]{:S(2)}) collective-permute-start(f32[72,128]{1,0:T(8,128)S(1)} %get-tuple-element.166), channel_id=1, source_target_pairs={{0,16},{1,17},{2,18},{3,19},{4,20},{5,21},{6,22},{7,23},{8,24},{9,... | collective-permute-start | bytes 110600 | tf_op jit(solution)/shard_map/ppermute | solution.py:187
  61.0 2.5 %update.4 = (f32[64,1024]{1,0:T(8,128)S(1)}, f32[64,1024]{1,0:T(8,128)S(1)}, f32[1,128]{1,0:T(1,128)S(1)}, f32[64,1024]{1,0:T(8,128)S(1)}, f32[64,1024]{1,0:T(8,...) custom-call(f32[64,128]{1,0:T(8,128)S(1)} %collective-permute-done.2, ...), custom_call_target="tpu_custom_call" | custom-call | tf_op jit(solution)/shard_map/update/pallas_call | solution.py:105
  64.0 4.9 %collective-permute-start.27 = (f32[73,128]{1,0:T(8,128)S(1)}, f32[73,128]{1,0:T(8,128)S(1)}, u32[]{:S(2)}, u32[]{:S(2)}) collective-permute-start(f32[73,128]{1,0:T(8,128)S(1)} %get-tuple-element.177.refs_0_), channel_id=1, source_target_pairs={{0,16},{1,17},{2,18},{3,19},{4,20},{5,21},{6,22},{7,23},{8,24},{9,... | collective-permute-start | bytes 112136 | tf_op jit(solution)/shard_map/ppermute | solution.py:187
  71.0 2.2 %collective-permute-start.28 = (f32[18,128]{1,0:T(8,128)S(1)}, f32[18,128]{1,0:T(8,128)S(1)}, u32[]{:S(2)}, u32[]{:S(2)}) collective-permute-start(f32[18,128]{1,0:T(8,128)S(1)} %join.14.refs_0_), channel_id=1, source_target_pairs={{0,10},{1,11},{2,8},{3,9},{4,14},{5,15},{6,12},{7,13},{8,2},{9,3},... | collective-permute-start | bytes 27656 | tf_op jit(solution)/shard_map/ppermute | solution.py:196
  79.8 2.2 %apply_own.6 = (f32[64,1024]{1,0:T(8,128)S(1)}, f32[64,384]{1,0:T(8,128)S(1)}, f32[64,1024]{1,0:T(8,128)S(1)}, f32[64,1024]{1,0:T(8,128)S(1)}, f32[64,1024]{1,0:T(8,128)S(1)}) custom-call(f32[64,128]{1,0:T(8,128)S(1)} %collective-permute-done.24.refs_0_, f32[64,128]{1,0:T(8,128)S(1)} %collective-permute-done.25.refs_1_, ...), custom_call_target="tpu_custom_call" | custom-call | tf_op jit(solution)/shard_map/apply_own/pallas_call | solution.py:105
  82.9 1.5 %collective-permute-start.38 = (f32[72,128]{1,0:T(8,128)S(1)}, f32[72,128]{1,0:T(8,128)S(1)}, u32[]{:S(2)}, u32[]{:S(2)}) collective-permute-start(f32[72,128]{1,0:T(8,128)S(1)} %get-tuple-element.186), channel_id=1, source_target_pairs={{0,16},{1,17},{2,18},{3,19},{4,20},{5,21},{6,22},{7,23},{8,24},{9,... | collective-permute-start | bytes 110600 | tf_op jit(solution)/shard_map/ppermute | solution.py:187
  85.4 2.6 %update.5 = (f32[64,1024]{1,0:T(8,128)S(1)}, f32[64,1024]{1,0:T(8,128)S(1)}, f32[1,128]{1,0:T(1,128)S(1)}, f32[64,1024]{1,0:T(8,128)S(1)}, f32[64,1024]{1,0:T(8,...) custom-call(f32[64,128]{1,0:T(8,128)S(1)} %collective-permute-done.3, ...), custom_call_target="tpu_custom_call" | custom-call | tf_op jit(solution)/shard_map/update/pallas_call | solution.py:105
  89.0 5.1 %collective-permute-start.41 = (f32[73,128]{1,0:T(8,128)S(1)}, f32[73,128]{1,0:T(8,128)S(1)}, u32[]{:S(2)}, u32[]{:S(2)}) collective-permute-start(f32[73,128]{1,0:T(8,128)S(1)} %get-tuple-element.205.refs_0_), channel_id=1, source_target_pairs={{0,16},{1,17},{2,18},{3,19},{4,20},{5,21},{6,22},{7,23},{8,24},{9,... | collective-permute-start | bytes 112136 | tf_op jit(solution)/shard_map/ppermute | solution.py:187
  96.1 2.4 %collective-permute-start.42 = (f32[18,128]{1,0:T(8,128)S(1)}, f32[18,128]{1,0:T(8,128)S(1)}, u32[]{:S(2)}, u32[]{:S(2)}) collective-permute-start(f32[18,128]{1,0:T(8,128)S(1)} %join.16.refs_0_), channel_id=1, source_target_pairs={{0,10},{1,11},{2,8},{3,9},{4,14},{5,15},{6,12},{7,13},{8,2},{9,3},... | collective-permute-start | bytes 27656 | tf_op jit(solution)/shard_map/ppermute | solution.py:196
  99.1 1.4 %collective-permute-start.44 = (f32[18,128]{1,0:T(8,128)S(1)}, f32[18,128]{1,0:T(8,128)S(1)}, u32[]{:S(2)}, u32[]{:S(2)}) collective-permute-start(f32[18,128]{1,0:T(8,128)S(1)} %join.16.refs_0_), channel_id=1, source_target_pairs={{0,2},{1,3},{2,0},{3,1},{4,6},{5,7},{6,4},{7,5},{8,10},{9,11},{10,... | collective-permute-start | bytes 27656 | tf_op jit(solution)/shard_map/ppermute | solution.py:196
  100.7 1.5 %collective-permute-done.43.refs_2_ = f32[18,128]{1,0:T(8,128)S(1)} collective-permute-done((f32[18,128]{1,0:T(8,128)S(1)}, f32[18,128]{1,0:T(8,128)S(1)}, u32[]{:S(2)}, u32[]{:S(2)}) %collective-permute-start.43) | collective-permute-done | bytes 9248 | tf_op jit(solution)/shard_map/ppermute | solution.py:196
  104.6 2.2 %apply_own.7 = (f32[64,1024]{1,0:T(8,128)S(1)}, f32[64,384]{1,0:T(8,128)S(1)}, f32[64,1024]{1,0:T(8,128)S(1)}, f32[64,1024]{1,0:T(8,128)S(1)}, f32[64,1024]{1,0:T(8,128)S(1)}) custom-call(f32[64,128]{1,0:T(8,128)S(1)} %collective-permute-done.36.refs_0_, f32[64,128]{1,0:T(8,128)S(1)} %collective-permute-done.37.refs_1_, ...), custom_call_target="tpu_custom_call" | custom-call | tf_op jit(solution)/shard_map/apply_own/pallas_call | solution.py:105
  107.0 2.1 %last.1 = (f32[64,1024]{1,0:T(8,128)S(1)}, f32[64,1024]{1,0:T(8,128)S(1)}, f32[1,128]{1,0:T(1,128)S(1)}, f32[64,1024]{1,0:T(8,128)S(1)}, f32[64,1024]{1,0:T(8,12...) custom-call(f32[64,128]{1,0:T(8,128)S(1)} %collective-permute-done.3, ...), custom_call_target="tpu_custom_call" | custom-call | tf_op jit(solution)/shard_map/last/pallas_call | solution.py:105
  109.1 2.1 %collective-permute-start.48 = (f32[72,128]{1,0:T(8,128)S(1)}, f32[72,128]{1,0:T(8,128)S(1)}, u32[]{:S(2)}, u32[]{:S(2)}) collective-permute-start(f32[72,128]{1,0:T(8,128)S(1)} %get-tuple-element.220.refs_0_), channel_id=1, source_target_pairs={{0,16},{1,17},{2,18},{3,19},{4,20},{5,21},{6,22},{7,23},{8,24},{9,... | collective-permute-start | bytes 110600 | tf_op jit(solution)/shard_map/ppermute | solution.py:187
  111.9 2.1 %collective-permute-done.48.refs_1_.refs_2_ = f32[72,128]{1,0:T(8,128)S(1)} collective-permute-done((f32[72,128]{1,0:T(8,128)S(1)}, f32[72,128]{1,0:T(8,128)S(1)}, u32[]{:S(2)}, u32[]{:S(2)}) %collective-permute-start.48) | collective-permute-done | bytes 36896 | tf_op jit(solution)/shard_map/ppermute | solution.py:187
  114.0 2.8 %collective-permute-start.49 = (f32[2,128]{1,0:T(2,128)S(1)}, f32[2,128]{1,0:T(2,128)S(1)}, u32[]{:S(2)}, u32[]{:S(2)}) collective-permute-start(f32[2,128]{1,0:T(2,128)S(1)} %join.18.refs_0_), channel_id=1, source_target_pairs={{0,10},{1,11},{2,8},{3,9},{4,14},{5,15},{6,12},{7,13},{8,2},{9,3},... | collective-permute-start | bytes 3080 | tf_op jit(solution)/shard_map/ppermute | solution.py:196
  118.5 1.9 %collective-permute-done.50.refs_2_ = f32[2,128]{1,0:T(2,128)S(1)} collective-permute-done((f32[2,128]{1,0:T(2,128)S(1)}, f32[2,128]{1,0:T(2,128)S(1)}, u32[]{:S(2)}, u32[]{:S(2)}) %collective-permute-start.50) | collective-permute-done | bytes 1056 | tf_op jit(solution)/shard_map/ppermute | solution.py:196
  (134 shorter events, 42.9 us)
Async XLA Ops:
  2.6 8.3 %collective-permute-start.2 = (f32[152,128]{1,0:T(8,128)S(1)}, f32[152,128]{1,0:T(8,128)S(1)}, u32[]{:S(2)}, u32[]{:S(2)}) collective-permute-start(f32[152,128]{1,0:T(8,128)S(1)} %get-tuple-element.118), channel_id=1, source_target_pairs={{0,16},{1,17},{2,18},{3,19},{4,20},{5,21},{6,22},{7,23},{8,24},{9,... | collective-permute-start | bytes 233480 | tf_op jit(solution)/shard_map/ppermute | solution.py:187
  6.7 4.2 %collective-permute-start = (f32[144,128]{1,0:T(8,128)S(1)}, f32[144,128]{1,0:T(8,128)S(1)}, u32[]{:S(2)}, u32[]{:S(2)}) collective-permute-start(f32[144,128]{1,0:T(8,128)S(1)} %get-tuple-element.116), channel_id=1, source_target_pairs={{0,1},{2,3},{4,5},{6,7},{8,9},{10,11},{12,13},{14,15},{16,17},{18,... | collective-permute-start | bytes 221192 | tf_op jit(solution)/shard_map/ppermute | solution.py:187
  6.7 4.2 %collective-permute-start.1 = (f32[144,128]{1,0:T(8,128)S(1)}, f32[144,128]{1,0:T(8,128)S(1)}, u32[]{:S(2)}, u32[]{:S(2)}) collective-permute-start(f32[144,128]{1,0:T(8,128)S(1)} %get-tuple-element.117), channel_id=1, source_target_pairs={{1,2},{3,4},{5,6},{7,8},{9,10},{11,12},{13,14},{15,16},{17,18},{19... | collective-permute-start | bytes 221192 | tf_op jit(solution)/shard_map/ppermute | solution.py:187
  11.3 9.7 %collective-permute-start.3 = (f32[73,128]{1,0:T(8,128)S(1)}, f32[73,128]{1,0:T(8,128)S(1)}, u32[]{:S(2)}, u32[]{:S(2)}) collective-permute-start(f32[73,128]{1,0:T(8,128)S(1)} %get-tuple-element.130.refs_0_), channel_id=1, source_target_pairs={{0,16},{1,17},{2,18},{3,19},{4,20},{5,21},{6,22},{7,23},{8,24},{9,... | collective-permute-start | bytes 112136 | tf_op jit(solution)/shard_map/ppermute | solution.py:187
  17.6 13.9 %collective-permute-start.11 = (f32[128,128]{1,0:T(8,128)S(1)}, f32[128,128]{1,0:T(8,128)S(1)}, u32[]{:S(2)}, u32[]{:S(2)}) collective-permute-start(f32[128,128]{1,0:T(8,128)S(1)} %get-tuple-element.142), channel_id=1, source_target_pairs={{1,2},{3,4},{5,6},{7,8},{9,10},{11,12},{13,14},{15,16},{17,18},{19... | collective-permute-start | bytes 196616 | tf_op jit(solution)/shard_map/ppermute | solution.py:187
  21.0 6.5 %collective-permute-start.4 = (f32[18,128]{1,0:T(8,128)S(1)}, f32[18,128]{1,0:T(8,128)S(1)}, u32[]{:S(2)}, u32[]{:S(2)}) collective-permute-start(f32[18,128]{1,0:T(8,128)S(1)} %join.10.refs_0_), channel_id=1, source_target_pairs={{0,10},{1,11},{2,8},{3,9},{4,14},{5,15},{6,12},{7,13},{8,2},{9,3},... | collective-permute-start | bytes 27656 | tf_op jit(solution)/shard_map/ppermute | solution.py:196
  21.6 5.9 %collective-permute-start.5 = (f32[18,128]{1,0:T(8,128)S(1)}, f32[18,128]{1,0:T(8,128)S(1)}, u32[]{:S(2)}, u32[]{:S(2)}) collective-permute-start(f32[18,128]{1,0:T(8,128)S(1)} %join.10.refs_0_), channel_id=1, source_target_pairs={{0,8},{1,9},{2,10},{3,11},{4,12},{5,13},{6,14},{7,15},{8,0},{9,1},... | collective-permute-start | bytes 27656 | tf_op jit(solution)/shard_map/ppermute | solution.py:196
  23.5 4.0 %collective-permute-start.6 = (f32[18,128]{1,0:T(8,128)S(1)}, f32[18,128]{1,0:T(8,128)S(1)}, u32[]{:S(2)}, u32[]{:S(2)}) collective-permute-start(f32[18,128]{1,0:T(8,128)S(1)} %join.10.refs_0_), channel_id=1, source_target_pairs={{0,2},{1,3},{2,0},{3,1},{4,6},{5,7},{6,4},{7,5},{8,10},{9,11},{10,... | collective-permute-start | bytes 27656 | tf_op jit(solution)/shard_map/ppermute | solution.py:196
  27.6 4.0 %collective-permute-start.7 = (f32[72,128]{1,0:T(8,128)S(1)}, f32[72,128]{1,0:T(8,128)S(1)}, u32[]{:S(2)}, u32[]{:S(2)}) collective-permute-start(f32[72,128]{1,0:T(8,128)S(1)} %join.11.refs_0_), channel_id=1, source_target_pairs={{0,5},{1,4},{2,7},{3,6},{4,1},{5,0},{6,3},{7,2},{8,13},{9,12},{10,... | collective-permute-start | bytes 110600 | tf_op jit(solution)/shard_map/ppermute | solution.py:196
  28.9 4.0 %collective-permute-start.8 = (f32[72,128]{1,0:T(8,128)S(1)}, f32[72,128]{1,0:T(8,128)S(1)}, u32[]{:S(2)}, u32[]{:S(2)}) collective-permute-start(f32[72,128]{1,0:T(8,128)S(1)} %join.11.refs_0_), channel_id=1, source_target_pairs={{0,4},{1,5},{2,6},{3,7},{4,0},{5,1},{6,2},{7,3},{8,12},{9,13},{10,... | collective-permute-start | bytes 110600 | tf_op jit(solution)/shard_map/ppermute | solution.py:196
  28.9 4.0 %collective-permute-start.9 = (f32[72,128]{1,0:T(8,128)S(1)}, f32[72,128]{1,0:T(8,128)S(1)}, u32[]{:S(2)}, u32[]{:S(2)}) collective-permute-start(f32[72,128]{1,0:T(8,128)S(1)} %join.11.refs_0_), channel_id=1, source_target_pairs={{0,1},{1,0},{2,3},{3,2},{4,5},{5,4},{6,7},{7,6},{8,9},{9,8},{10,11... | collective-permute-start | bytes 110600 | tf_op jit(solution)/shard_map/ppermute | solution.py:196
  33.6 5.4 %collective-permute-start.14 = (f32[72,128]{1,0:T(8,128)S(1)}, f32[72,128]{1,0:T(8,128)S(1)}, u32[]{:S(2)}, u32[]{:S(2)}) collective-permute-start(f32[72,128]{1,0:T(8,128)S(1)} %get-tuple-element.147), channel_id=1, source_target_pairs={{0,16},{1,17},{2,18},{3,19},{4,20},{5,21},{6,22},{7,23},{8,24},{9,... | collective-permute-start | bytes 110600 | tf_op jit(solution)/shard_map/ppermute | solution.py:187
  39.3 7.6 %collective-permute-start.15 = (f32[73,128]{1,0:T(8,128)S(1)}, f32[73,128]{1,0:T(8,128)S(1)}, u32[]{:S(2)}, u32[]{:S(2)}) collective-permute-start(f32[73,128]{1,0:T(8,128)S(1)} %get-tuple-element.158.refs_0_), channel_id=1, source_target_pairs={{0,16},{1,17},{2,18},{3,19},{4,20},{5,21},{6,22},{7,23},{8,24},{9,... | collective-permute-start | bytes 112136 | tf_op jit(solution)/shard_map/ppermute | solution.py:187
  44.1 13.1 %collective-permute-start.23 = (f32[128,128]{1,0:T(8,128)S(1)}, f32[128,128]{1,0:T(8,128)S(1)}, u32[]{:S(2)}, u32[]{:S(2)}) collective-permute-start(f32[128,128]{1,0:T(8,128)S(1)} %get-tuple-element.160), channel_id=1, source_target_pairs={{1,2},{3,4},{5,6},{7,8},{9,10},{11,12},{13,14},{15,16},{17,18},{19... | collective-permute-start | bytes 196616 | tf_op jit(solution)/shard_map/ppermute | solution.py:187
  46.9 4.6 %collective-permute-start.16 = (f32[18,128]{1,0:T(8,128)S(1)}, f32[18,128]{1,0:T(8,128)S(1)}, u32[]{:S(2)}, u32[]{:S(2)}) collective-permute-start(f32[18,128]{1,0:T(8,128)S(1)} %join.12.refs_0_), channel_id=1, source_target_pairs={{0,10},{1,11},{2,8},{3,9},{4,14},{5,15},{6,12},{7,13},{8,2},{9,3},... | collective-permute-start | bytes 27656 | tf_op jit(solution)/shard_map/ppermute | solution.py:196
  53.5 4.0 %collective-permute-start.20 = (f32[72,128]{1,0:T(8,128)S(1)}, f32[72,128]{1,0:T(8,128)S(1)}, u32[]{:S(2)}, u32[]{:S(2)}) collective-permute-start(f32[72,128]{1,0:T(8,128)S(1)} %join.13.refs_0_), channel_id=1, source_target_pairs={{0,4},{1,5},{2,6},{3,7},{4,0},{5,1},{6,2},{7,3},{8,12},{9,13},{10,... | collective-permute-start | bytes 110600 | tf_op jit(solution)/shard_map/ppermute | solution.py:196
  58.1 5.4 %collective-permute-start.26 = (f32[72,128]{1,0:T(8,128)S(1)}, f32[72,128]{1,0:T(8,128)S(1)}, u32[]{:S(2)}, u32[]{:S(2)}) collective-permute-start(f32[72,128]{1,0:T(8,128)S(1)} %get-tuple-element.166), channel_id=1, source_target_pairs={{0,16},{1,17},{2,18},{3,19},{4,20},{5,21},{6,22},{7,23},{8,24},{9,... | collective-permute-start | bytes 110600 | tf_op jit(solution)/shard_map/ppermute | solution.py:187
  64.0 6.9 %collective-permute-start.27 = (f32[73,128]{1,0:T(8,128)S(1)}, f32[73,128]{1,0:T(8,128)S(1)}, u32[]{:S(2)}, u32[]{:S(2)}) collective-permute-start(f32[73,128]{1,0:T(8,128)S(1)} %get-tuple-element.177.refs_0_), channel_id=1, source_target_pairs={{0,16},{1,17},{2,18},{3,19},{4,20},{5,21},{6,22},{7,23},{8,24},{9,... | collective-permute-start | bytes 112136 | tf_op jit(solution)/shard_map/ppermute | solution.py:187
  69.0 13.1 %collective-permute-start.35 = (f32[128,128]{1,0:T(8,128)S(1)}, f32[128,128]{1,0:T(8,128)S(1)}, u32[]{:S(2)}, u32[]{:S(2)}) collective-permute-start(f32[128,128]{1,0:T(8,128)S(1)} %get-tuple-element.179), channel_id=1, source_target_pairs={{1,2},{3,4},{5,6},{7,8},{9,10},{11,12},{13,14},{15,16},{17,18},{19... | collective-permute-start | bytes 196616 | tf_op jit(solution)/shard_map/ppermute | solution.py:187
  71.0 4.6 %collective-permute-start.28 = (f32[18,128]{1,0:T(8,128)S(1)}, f32[18,128]{1,0:T(8,128)S(1)}, u32[]{:S(2)}, u32[]{:S(2)}) collective-permute-start(f32[18,128]{1,0:T(8,128)S(1)} %join.14.refs_0_), channel_id=1, source_target_pairs={{0,10},{1,11},{2,8},{3,9},{4,14},{5,15},{6,12},{7,13},{8,2},{9,3},... | collective-permute-start | bytes 27656 | tf_op jit(solution)/shard_map/ppermute | solution.py:196
  77.9 4.1 %collective-permute-start.31 = (f32[72,128]{1,0:T(8,128)S(1)}, f32[72,128]{1,0:T(8,128)S(1)}, u32[]{:S(2)}, u32[]{:S(2)}) collective-permute-start(f32[72,128]{1,0:T(8,128)S(1)} %join.15.refs_0_), channel_id=1, source_target_pairs={{0,5},{1,4},{2,7},{3,6},{4,1},{5,0},{6,3},{7,2},{8,13},{9,12},{10,... | collective-permute-start | bytes 110600 | tf_op jit(solution)/shard_map/ppermute | solution.py:196
  78.2 4.0 %collective-permute-start.32 = (f32[72,128]{1,0:T(8,128)S(1)}, f32[72,128]{1,0:T(8,128)S(1)}, u32[]{:S(2)}, u32[]{:S(2)}) collective-permute-start(f32[72,128]{1,0:T(8,128)S(1)} %join.15.refs_0_), channel_id=1, source_target_pairs={{0,4},{1,5},{2,6},{3,7},{4,0},{5,1},{6,2},{7,3},{8,12},{9,13},{10,... | collective-permute-start | bytes 110600 | tf_op jit(solution)/shard_map/ppermute | solution.py:196
  82.9 5.7 %collective-permute-start.38 = (f32[72,128]{1,0:T(8,128)S(1)}, f32[72,128]{1,0:T(8,128)S(1)}, u32[]{:S(2)}, u32[]{:S(2)}) collective-permute-start(f32[72,128]{1,0:T(8,128)S(1)} %get-tuple-element.186), channel_id=1, source_target_pairs={{0,16},{1,17},{2,18},{3,19},{4,20},{5,21},{6,22},{7,23},{8,24},{9,... | collective-permute-start | bytes 110600 | tf_op jit(solution)/shard_map/ppermute | solution.py:187
  89.0 7.0 %collective-permute-start.41 = (f32[73,128]{1,0:T(8,128)S(1)}, f32[73,128]{1,0:T(8,128)S(1)}, u32[]{:S(2)}, u32[]{:S(2)}) collective-permute-start(f32[73,128]{1,0:T(8,128)S(1)} %get-tuple-element.205.refs_0_), channel_id=1, source_target_pairs={{0,16},{1,17},{2,18},{3,19},{4,20},{5,21},{6,22},{7,23},{8,24},{9,... | collective-permute-start | bytes 112136 | tf_op jit(solution)/shard_map/ppermute | solution.py:187
  94.1 12.8 %collective-permute-start.40 = (f32[128,128]{1,0:T(8,128)S(1)}, f32[128,128]{1,0:T(8,128)S(1)}, u32[]{:S(2)}, u32[]{:S(2)}) collective-permute-start(f32[128,128]{1,0:T(8,128)S(1)} %get-tuple-element.204), channel_id=1, source_target_pairs={{1,2},{3,4},{5,6},{7,8},{9,10},{11,12},{13,14},{15,16},{17,18},{19... | collective-permute-start | bytes 196616 | tf_op jit(solution)/shard_map/ppermute | solution.py:187
  96.1 4.6 %collective-permute-start.42 = (f32[18,128]{1,0:T(8,128)S(1)}, f32[18,128]{1,0:T(8,128)S(1)}, u32[]{:S(2)}, u32[]{:S(2)}) collective-permute-start(f32[18,128]{1,0:T(8,128)S(1)} %join.16.refs_0_), channel_id=1, source_target_pairs={{0,10},{1,11},{2,8},{3,9},{4,14},{5,15},{6,12},{7,13},{8,2},{9,3},... | collective-permute-start | bytes 27656 | tf_op jit(solution)/shard_map/ppermute | solution.py:196
  102.8 4.1 %collective-permute-start.45 = (f32[72,128]{1,0:T(8,128)S(1)}, f32[72,128]{1,0:T(8,128)S(1)}, u32[]{:S(2)}, u32[]{:S(2)}) collective-permute-start(f32[72,128]{1,0:T(8,128)S(1)} %join.17.refs_20_), channel_id=1, source_target_pairs={{0,5},{1,4},{2,7},{3,6},{4,1},{5,0},{6,3},{7,2},{8,13},{9,12},{10,... | collective-permute-start | bytes 110600 | tf_op jit(solution)/shard_map/ppermute | solution.py:196
  103.1 4.0 %collective-permute-start.46 = (f32[72,128]{1,0:T(8,128)S(1)}, f32[72,128]{1,0:T(8,128)S(1)}, u32[]{:S(2)}, u32[]{:S(2)}) collective-permute-start(f32[72,128]{1,0:T(8,128)S(1)} %join.17.refs_20_), channel_id=1, source_target_pairs={{0,4},{1,5},{2,6},{3,7},{4,0},{5,1},{6,2},{7,3},{8,12},{9,13},{10,... | collective-permute-start | bytes 110600 | tf_op jit(solution)/shard_map/ppermute | solution.py:196
  109.1 4.9 %collective-permute-start.48 = (f32[72,128]{1,0:T(8,128)S(1)}, f32[72,128]{1,0:T(8,128)S(1)}, u32[]{:S(2)}, u32[]{:S(2)}) collective-permute-start(f32[72,128]{1,0:T(8,128)S(1)} %get-tuple-element.220.refs_0_), channel_id=1, source_target_pairs={{0,16},{1,17},{2,18},{3,19},{4,20},{5,21},{6,22},{7,23},{8,24},{9,... | collective-permute-start | bytes 110600 | tf_op jit(solution)/shard_map/ppermute | solution.py:187
  111.2 11.3 %collective-permute-start.55 = (f32[64,128]{1,0:T(8,128)S(1)}, f32[64,128]{1,0:T(8,128)S(1)}, u32[]{:S(2)}, u32[]{:S(2)}) collective-permute-start(f32[64,128]{1,0:T(8,128)S(1)} %get-tuple-element.222), channel_id=1, source_target_pairs={{0,1},{2,3},{4,5},{6,7},{8,9},{10,11},{12,13},{14,15},{16,17},{18,... | collective-permute-start | bytes 98312 | tf_op jit(solution)/shard_map/ppermute | solution.py:187
  111.2 11.3 %collective-permute-start.56 = (f32[64,128]{1,0:T(8,128)S(1)}, f32[64,128]{1,0:T(8,128)S(1)}, u32[]{:S(2)}, u32[]{:S(2)}) collective-permute-start(f32[64,128]{1,0:T(8,128)S(1)} %get-tuple-element.223), channel_id=1, source_target_pairs={{1,2},{3,4},{5,6},{7,8},{9,10},{11,12},{13,14},{15,16},{17,18},{19... | collective-permute-start | bytes 98312 | tf_op jit(solution)/shard_map/ppermute | solution.py:187
  114.0 4.5 %collective-permute-start.49 = (f32[2,128]{1,0:T(2,128)S(1)}, f32[2,128]{1,0:T(2,128)S(1)}, u32[]{:S(2)}, u32[]{:S(2)}) collective-permute-start(f32[2,128]{1,0:T(2,128)S(1)} %join.18.refs_0_), channel_id=1, source_target_pairs={{0,10},{1,11},{2,8},{3,9},{4,14},{5,15},{6,12},{7,13},{8,2},{9,3},... | collective-permute-start | bytes 3080 | tf_op jit(solution)/shard_map/ppermute | solution.py:196
  (34 other events, 105.2 us)

commit v10 on v9

--- a/solution.py
+++ b/solution.py
@@ -18,7 +18,7 @@
 STAGE_BYTES = 12 * 1024 * 1024
 TILES = 8
 AXIS = "sub"
-LONGER = 64
+LONGER = 32
 ROOM_FOR_COPIES = pl.CostEstimate(flops=4 * 10**9, bytes_accessed=16 * 10**6, transcendentals=0)
 
 
@@ -343,10 +343,11 @@
                 o.w[...] = i.w_part[...] + pick(arrived, i.picker[...])
             inner = i.weight[...] * (i.inner[...] + times(0.5 * arrived, i.inv[0][...], i.inv[1][...]))
             o.v[...] = inner
-            o.image_faces[...] = times(inner, i.stiff[2][...], i.stiff[3][...], NT)
-            o.image[...] = times(inner, i.stiff[0][...], i.stiff[1][...])
-
-        ins = dict(came=came, picker=picker, weight=weight, inner=own.inner, inv=inv[2:4], stiff=stiff[:4])
+            image = times(inner, i.stiff[0][...], i.stiff[1][...])
+            o.image[...] = image
+            o.image_faces[...] = pick(image, i.unpicker[...])
+
+        ins = dict(came=came, picker=picker, unpicker=unpicker, weight=weight, inner=own.inner, inv=inv[2:4], stiff=stiff[:2])
         outs = dict(v=vec, image_faces=faces, image=vec)
         if step == 0:
             ins.update(load=loads)

time: 126 us -> 125 us (level)
  waiting for transfers between devices: 21.1 us -> 24.1 us
  starting transfers between devices: 69.1 us -> 66.9 us
  Pallas kernels: 33.1 us -> 31.8 us
    ppermute x30, waiting for transfers between devices: 13.5 us -> 15.2 us  [gather(): lax.ppermute(block, AXIS, [(i, i ^ far) for i in range(total)])]
    pallas_call x34, Pallas kernels: 33.1 us -> 31.8 us  [stage(): pl.pallas_call(kernel, name=name, out_shape=[jax.ShapeDtypeStruct(*kind)...]
    ppermute x27, waiting for transfers between devices: 7.62 us -> 8.92 us  [exchange(): lax.ppermute(array, AXIS, chosen[i][0])]
    ppermute x27, starting transfers between devices: 39.3 us -> 38.1 us  [exchange(): lax.ppermute(array, AXIS, chosen[i][0])]
  transfers between devices with their start and end apart: 57 -> 57, of which waited for: 24 -> 23; matrix products, arithmetic and copies ran while one was open for 0% -> 0% of each run, Pallas kernels for 20% -> 19%
where the time goes in v10:
time: 125 us
  starting transfers between devices  66.9 us (54%)
  Pallas kernels  31.8 us (25%)
  waiting for transfers between devices  24.1 us (19%)
    ppermute x27, starting transfers between devices, exchange(): lax.ppermute(array, AXIS, chosen[i][0])  38.1 us
    pallas_call x34, Pallas kernels, stage(): pl.pallas_call(kernel, name=name, out_shape=[jax.ShapeDtypeStruct(*kind)...  31.8 us
    ppermute x30, starting transfers between devices, gather(): lax.ppermute(block, AXIS, [(i, i ^ far) for i in range(total)])  28.9 us
    ppermute x30, waiting for transfers between devices, gather(): lax.ppermute(block, AXIS, [(i, i ^ far) for i in range(total)])  15.2 us
    ppermute x27, waiting for transfers between devices, exchange(): lax.ppermute(array, AXIS, chosen[i][0])  8.92 us
  transfers between devices with their start and end apart: 57, of which 23 were waited for; matrix products, arithmetic and copies ran while one was open for 0% of the time, Pallas kernels for 19%

profile of v10, /device:TPU:0, one launch (start us, length us, event | category | flops | bytes accessed | tf_op | source)
XLA Modules:
  0.0 125.0 jit_solution(2172673987931167869)
XLA Ops:
  2.6 4.1 %collective-permute-start.2 = (f32[152,128]{1,0:T(8,128)S(1)}, f32[152,128]{1,0:T(8,128)S(1)}, u32[]{:S(2)}, u32[]{:S(2)}) collective-permute-start(f32[152,128]{1,0:T(8,128)S(1)} %get-tuple-element.118), channel_id=1, source_target_pairs={{0,16},{1,17},{2,18},{3,19},{4,20},{5,21},{6,22},{7,23},{8,24},{9,... | collective-permute-start | bytes 233480 | tf_op jit(solution)/shard_map/ppermute | solution.py:187
  7.4 2.7 %prepare_inv.1 = (bf16[1024,1024]{1,0:T(8,128)(2,1)S(1)}, bf16[1024,1024]{1,0:T(8,128)(2,1)S(1)}, bf16[384,1024]{1,0:T(8,128)(2,1)S(1)}, bf16[384,1024]{1,0:T(8,...) custom-call(f32[1,1024,1024]{2,1,0:T(8,128)S(1)} %copy-done, ...), custom_call_target="tpu_custom_call" | custom-call | tf_op jit(solution)/shard_map/prepare_inv/pallas_call | solution.py:105
  11.3 6.3 %collective-permute-start.3 = (f32[73,128]{1,0:T(8,128)S(1)}, f32[73,128]{1,0:T(8,128)S(1)}, u32[]{:S(2)}, u32[]{:S(2)}) collective-permute-start(f32[73,128]{1,0:T(8,128)S(1)} %get-tuple-element.130.refs_0_), channel_id=1, source_target_pairs={{0,16},{1,17},{2,18},{3,19},{4,20},{5,21},{6,22},{7,23},{8,24},{9,... | collective-permute-start | bytes 112136 | tf_op jit(solution)/shard_map/ppermute | solution.py:187
  18.3 2.7 %prepare_stiff.1 = (bf16[1024,1024]{1,0:T(8,128)(2,1)S(1)}, bf16[1024,1024]{1,0:T(8,128)(2,1)S(1)}, bf16[384,1024]{1,0:T(8,128)(2,1)S(1)}, bf16[384,1024]{1,0:T(...) custom-call(f32[1,1024,1024]{2,1,0:T(8,128)S(1)} %copy-done.1, ...), custom_call_target="tpu_custom_call" | custom-call | tf_op jit(solution)/shard_map/prepare_stiff/pallas_call | solution.py:105
  21.6 1.9 %collective-permute-start.5 = (f32[18,128]{1,0:T(8,128)S(1)}, f32[18,128]{1,0:T(8,128)S(1)}, u32[]{:S(2)}, u32[]{:S(2)}) collective-permute-start(f32[18,128]{1,0:T(8,128)S(1)} %join.10.refs_0_), channel_id=1, source_target_pairs={{0,8},{1,9},{2,10},{3,11},{4,12},{5,13},{6,14},{7,15},{8,0},{9,1},... | collective-permute-start | bytes 27656 | tf_op jit(solution)/shard_map/ppermute | solution.py:196
  25.7 1.7 %reach.1 = (bf16[64,2048]{1,0:T(8,128)(2,1)S(1)}, bf16[64,2048]{1,0:T(8,128)(2,1)S(1)}, bf16[64,384]{1,0:T(8,128)(2,1)S(1)}, bf16[64,384]{1,0:T(8,128)(2,1)S(1)}, f32[128,288]{1,0:T(8,128)S(1)}) custom-call(f32[16,1024]{1,0:T(8,128)S(1)} %get-tuple-element.121.refs_2_.refs_0_.refs_14_.refs_16_.refs_22_, f32[16,512]{1,0:T(8,128)S(1)} %copy-done.3, ...), custom_call_target="tpu_custom_call" | custom-call | tf_op jit(solution)/shard_map/reach/pallas_call | solution.py:105
  29.5 1.7 %apply_own.4 = (f32[64,1024]{1,0:T(8,128)S(1)}, f32[64,384]{1,0:T(8,128)S(1)}, f32[64,1024]{1,0:T(8,128)S(1)}, f32[64,1024]{1,0:T(8,128)S(1)}) custom-call(f32[144,128]{1,0:T(8,128)S(1)} %collective-permute-done.refs_0_.refs_2_, f32[144,128]{1,0:T(8,128)S(1)} %collective-permute-done.1.refs_1_.refs_3_, ...), custom_call_target="tpu_custom_call" | custom-call | tf_op jit(solution)/shard_map/apply_own/pallas_call | solution.py:105
  31.2 1.7 %collective-permute-done.8.refs_2_ = f32[72,128]{1,0:T(8,128)S(1)} collective-permute-done((f32[72,128]{1,0:T(8,128)S(1)}, f32[72,128]{1,0:T(8,128)S(1)}, u32[]{:S(2)}, u32[]{:S(2)}) %collective-permute-start.8) | collective-permute-done | bytes 36896 | tf_op jit(solution)/shard_map/ppermute | solution.py:196
  33.5 2.0 %collective-permute-start.14 = (f32[72,128]{1,0:T(8,128)S(1)}, f32[72,128]{1,0:T(8,128)S(1)}, u32[]{:S(2)}, u32[]{:S(2)}) collective-permute-start(f32[72,128]{1,0:T(8,128)S(1)} %get-tuple-element.147), channel_id=1, source_target_pairs={{0,16},{1,17},{2,18},{3,19},{4,20},{5,21},{6,22},{7,23},{8,24},{9,... | collective-permute-start | bytes 110600 | tf_op jit(solution)/shard_map/ppermute | solution.py:187
  36.3 2.5 %update.3 = (f32[64,1024]{1,0:T(8,128)S(1)}, f32[64,1024]{1,0:T(8,128)S(1)}, f32[16,64]{1,0:T(8,128)S(1)}, f32[64,384]{1,0:T(8,128)S(1)}, f32[64,1024]{1,0:T(8,128)S(1)}, /*index=5*/f32[1,128]{1,0:T(1,128)S(1)}) custom-call(f32[64,128]{1,0:T(8,128)S(1)} %collective-permute-done.10.refs_7_.refs_0_, f32[96,128]{1,0:T(8,128)S(1)} %collective-permute-done.11.refs_8_.refs_1_, ...), custom_call_target="tpu_custom_call" | custom-call | tf_op jit(solution)/shard_map/update/pallas_call | solution.py:105
  39.2 4.8 %collective-permute-start.15 = (f32[73,128]{1,0:T(8,128)S(1)}, f32[73,128]{1,0:T(8,128)S(1)}, u32[]{:S(2)}, u32[]{:S(2)}) collective-permute-start(f32[73,128]{1,0:T(8,128)S(1)} %get-tuple-element.158.refs_0_), channel_id=1, source_target_pairs={{0,16},{1,17},{2,18},{3,19},{4,20},{5,21},{6,22},{7,23},{8,24},{9,... | collective-permute-start | bytes 112136 | tf_op jit(solution)/shard_map/ppermute | solution.py:187
  44.6 2.1 %collective-permute-done.15.refs_1_.refs_9_.refs_2_ = f32[73,128]{1,0:T(8,128)S(1)} collective-permute-done((f32[73,128]{1,0:T(8,128)S(1)}, f32[73,128]{1,0:T(8,128)S(1)}, u32[]{:S(2)}, u32[]{:S(2)}) %collective-permute-start.15) | collective-permute-done | bytes 37408 | tf_op jit(solution)/shard_map/ppermute | solution.py:187
  46.8 2.2 %collective-permute-start.16 = (f32[18,128]{1,0:T(8,128)S(1)}, f32[18,128]{1,0:T(8,128)S(1)}, u32[]{:S(2)}, u32[]{:S(2)}) collective-permute-start(f32[18,128]{1,0:T(8,128)S(1)} %join.12.refs_0_), channel_id=1, source_target_pairs={{0,10},{1,11},{2,8},{3,9},{4,14},{5,15},{6,12},{7,13},{8,2},{9,3},... | collective-permute-start | bytes 27656 | tf_op jit(solution)/shard_map/ppermute | solution.py:196
  55.1 1.7 %apply_own.5 = (f32[64,1024]{1,0:T(8,128)S(1)}, f32[64,384]{1,0:T(8,128)S(1)}, f32[64,1024]{1,0:T(8,128)S(1)}, f32[64,1024]{1,0:T(8,128)S(1)}) custom-call(f32[64,128]{1,0:T(8,128)S(1)} %collective-permute-done.12.refs_0_, f32[64,128]{1,0:T(8,128)S(1)} %collective-permute-done.13.refs_1_, f32[72,128]{1,0:T(8,128)S(1)} %collective-permute-done.14.refs_2_, ...), custom_call_target="tpu_custom_call" | custom-call | tf_op jit(solution)/shard_map/apply_own/pallas_call | solution.py:105
  58.1 2.2 %collective-permute-start.26 = (f32[72,128]{1,0:T(8,128)S(1)}, f32[72,128]{1,0:T(8,128)S(1)}, u32[]{:S(2)}, u32[]{:S(2)}) collective-permute-start(f32[72,128]{1,0:T(8,128)S(1)} %get-tuple-element.166), channel_id=1, source_target_pairs={{0,16},{1,17},{2,18},{3,19},{4,20},{5,21},{6,22},{7,23},{8,24},{9,... | collective-permute-start | bytes 110600 | tf_op jit(solution)/shard_map/ppermute | solution.py:187
  60.9 2.5 %update.4 = (f32[64,1024]{1,0:T(8,128)S(1)}, f32[64,1024]{1,0:T(8,128)S(1)}, f32[1,128]{1,0:T(1,128)S(1)}, f32[64,1024]{1,0:T(8,128)S(1)}, f32[64,1024]{1,0:T(8,...) custom-call(f32[64,128]{1,0:T(8,128)S(1)} %collective-permute-done.2, ...), custom_call_target="tpu_custom_call" | custom-call | tf_op jit(solution)/shard_map/update/pallas_call | solution.py:105
  64.0 4.7 %collective-permute-start.27 = (f32[73,128]{1,0:T(8,128)S(1)}, f32[73,128]{1,0:T(8,128)S(1)}, u32[]{:S(2)}, u32[]{:S(2)}) collective-permute-start(f32[73,128]{1,0:T(8,128)S(1)} %get-tuple-element.177.refs_0_), channel_id=1, source_target_pairs={{0,16},{1,17},{2,18},{3,19},{4,20},{5,21},{6,22},{7,23},{8,24},{9,... | collective-permute-start | bytes 112136 | tf_op jit(solution)/shard_map/ppermute | solution.py:187
  69.3 1.6 %collective-permute-done.27.refs_1_.refs_9_.refs_2_ = f32[73,128]{1,0:T(8,128)S(1)} collective-permute-done((f32[73,128]{1,0:T(8,128)S(1)}, f32[73,128]{1,0:T(8,128)S(1)}, u32[]{:S(2)}, u32[]{:S(2)}) %collective-permute-start.27) | collective-permute-done | bytes 37408 | tf_op jit(solution)/shard_map/ppermute | solution.py:187
  70.9 2.2 %collective-permute-start.28 = (f32[18,128]{1,0:T(8,128)S(1)}, f32[18,128]{1,0:T(8,128)S(1)}, u32[]{:S(2)}, u32[]{:S(2)}) collective-permute-start(f32[18,128]{1,0:T(8,128)S(1)} %join.14.refs_0_), channel_id=1, source_target_pairs={{0,10},{1,11},{2,8},{3,9},{4,14},{5,15},{6,12},{7,13},{8,2},{9,3},... | collective-permute-start | bytes 27656 | tf_op jit(solution)/shard_map/ppermute | solution.py:196
  73.1 1.9 %collective-permute-start.29 = (f32[18,128]{1,0:T(8,128)S(1)}, f32[18,128]{1,0:T(8,128)S(1)}, u32[]{:S(2)}, u32[]{:S(2)}) collective-permute-start(f32[18,128]{1,0:T(8,128)S(1)} %join.14.refs_0_), channel_id=1, source_target_pairs={{0,8},{1,9},{2,10},{3,11},{4,12},{5,13},{6,14},{7,15},{8,0},{9,1},... | collective-permute-start | bytes 27656 | tf_op jit(solution)/shard_map/ppermute | solution.py:196
  76.9 1.9 %collective-permute-done.30.refs_3_ = f32[18,128]{1,0:T(8,128)S(1)} collective-permute-done((f32[18,128]{1,0:T(8,128)S(1)}, f32[18,128]{1,0:T(8,128)S(1)}, u32[]{:S(2)}, u32[]{:S(2)}) %collective-permute-start.30) | collective-permute-done | bytes 9248 | tf_op jit(solution)/shard_map/ppermute | solution.py:196
  78.8 1.8 %collective-permute-start.33 = (f32[72,128]{1,0:T(8,128)S(1)}, f32[72,128]{1,0:T(8,128)S(1)}, u32[]{:S(2)}, u32[]{:S(2)}) collective-permute-start(f32[72,128]{1,0:T(8,128)S(1)} %join.15.refs_0_), channel_id=1, source_target_pairs={{0,1},{1,0},{2,3},{3,2},{4,5},{5,4},{6,7},{7,6},{8,9},{9,8},{10,11... | collective-permute-start | bytes 110600 | tf_op jit(solution)/shard_map/ppermute | solution.py:196
  80.6 1.9 %apply_own.6 = (f32[64,1024]{1,0:T(8,128)S(1)}, f32[64,384]{1,0:T(8,128)S(1)}, f32[64,1024]{1,0:T(8,128)S(1)}, f32[64,1024]{1,0:T(8,128)S(1)}, f32[64,1024]{1,0:T(8,128)S(1)}) custom-call(f32[64,128]{1,0:T(8,128)S(1)} %collective-permute-done.24.refs_0_, f32[64,128]{1,0:T(8,128)S(1)} %collective-permute-done.25.refs_1_, ...), custom_call_target="tpu_custom_call" | custom-call | tf_op jit(solution)/shard_map/apply_own/pallas_call | solution.py:105
  85.3 2.6 %update.5 = (f32[64,1024]{1,0:T(8,128)S(1)}, f32[64,1024]{1,0:T(8,128)S(1)}, f32[1,128]{1,0:T(1,128)S(1)}, f32[64,1024]{1,0:T(8,128)S(1)}, f32[64,1024]{1,0:T(8,...) custom-call(f32[64,128]{1,0:T(8,128)S(1)} %collective-permute-done.3, ...), custom_call_target="tpu_custom_call" | custom-call | tf_op jit(solution)/shard_map/update/pallas_call | solution.py:105
  89.1 5.0 %collective-permute-start.41 = (f32[73,128]{1,0:T(8,128)S(1)}, f32[73,128]{1,0:T(8,128)S(1)}, u32[]{:S(2)}, u32[]{:S(2)}) collective-permute-start(f32[73,128]{1,0:T(8,128)S(1)} %get-tuple-element.205.refs_0_), channel_id=1, source_target_pairs={{0,16},{1,17},{2,18},{3,19},{4,20},{5,21},{6,22},{7,23},{8,24},{9,... | collective-permute-start | bytes 112136 | tf_op jit(solution)/shard_map/ppermute | solution.py:187
  94.8 1.8 %collective-permute-done.41.refs_1_.refs_2_ = f32[73,128]{1,0:T(8,128)S(1)} collective-permute-done((f32[73,128]{1,0:T(8,128)S(1)}, f32[73,128]{1,0:T(8,128)S(1)}, u32[]{:S(2)}, u32[]{:S(2)}) %collective-permute-start.41) | collective-permute-done | bytes 37408 | tf_op jit(solution)/shard_map/ppermute | solution.py:187
  96.6 1.8 %collective-permute-start.42 = (f32[18,128]{1,0:T(8,128)S(1)}, f32[18,128]{1,0:T(8,128)S(1)}, u32[]{:S(2)}, u32[]{:S(2)}) collective-permute-start(f32[18,128]{1,0:T(8,128)S(1)} %join.16.refs_0_), channel_id=1, source_target_pairs={{0,10},{1,11},{2,8},{3,9},{4,14},{5,15},{6,12},{7,13},{8,2},{9,3},... | collective-permute-start | bytes 27656 | tf_op jit(solution)/shard_map/ppermute | solution.py:196
  104.4 1.9 %apply_own.7 = (f32[64,1024]{1,0:T(8,128)S(1)}, f32[64,384]{1,0:T(8,128)S(1)}, f32[64,1024]{1,0:T(8,128)S(1)}, f32[64,1024]{1,0:T(8,128)S(1)}, f32[64,1024]{1,0:T(8,128)S(1)}) custom-call(f32[64,128]{1,0:T(8,128)S(1)} %collective-permute-done.36.refs_0_, f32[64,128]{1,0:T(8,128)S(1)} %collective-permute-done.37.refs_1_, ...), custom_call_target="tpu_custom_call" | custom-call | tf_op jit(solution)/shard_map/apply_own/pallas_call | solution.py:105
  106.9 2.1 %last.1 = (f32[64,1024]{1,0:T(8,128)S(1)}, f32[64,1024]{1,0:T(8,128)S(1)}, f32[1,128]{1,0:T(1,128)S(1)}, f32[64,1024]{1,0:T(8,128)S(1)}, f32[64,1024]{1,0:T(8,12...) custom-call(f32[64,128]{1,0:T(8,128)S(1)} %collective-permute-done.3, ...), custom_call_target="tpu_custom_call" | custom-call | tf_op jit(solution)/shard_map/last/pallas_call | solution.py:105
  109.0 2.0 %collective-permute-start.48 = (f32[72,128]{1,0:T(8,128)S(1)}, f32[72,128]{1,0:T(8,128)S(1)}, u32[]{:S(2)}, u32[]{:S(2)}) collective-permute-start(f32[72,128]{1,0:T(8,128)S(1)} %get-tuple-element.220.refs_0_), channel_id=1, source_target_pairs={{0,16},{1,17},{2,18},{3,19},{4,20},{5,21},{6,22},{7,23},{8,24},{9,... | collective-permute-start | bytes 110600 | tf_op jit(solution)/shard_map/ppermute | solution.py:187
  111.6 2.6 %collective-permute-done.48.refs_1_.refs_2_ = f32[72,128]{1,0:T(8,128)S(1)} collective-permute-done((f32[72,128]{1,0:T(8,128)S(1)}, f32[72,128]{1,0:T(8,128)S(1)}, u32[]{:S(2)}, u32[]{:S(2)}) %collective-permute-start.48) | collective-permute-done | bytes 36896 | tf_op jit(solution)/shard_map/ppermute | solution.py:187
  114.2 2.3 %collective-permute-start.49 = (f32[2,128]{1,0:T(2,128)S(1)}, f32[2,128]{1,0:T(2,128)S(1)}, u32[]{:S(2)}, u32[]{:S(2)}) collective-permute-start(f32[2,128]{1,0:T(2,128)S(1)} %join.18.refs_0_), channel_id=1, source_target_pairs={{0,10},{1,11},{2,8},{3,9},{4,14},{5,15},{6,12},{7,13},{8,2},{9,3},... | collective-permute-start | bytes 3080 | tf_op jit(solution)/shard_map/ppermute | solution.py:196
  (134 shorter events, 43.0 us)
Async XLA Ops:
  2.6 8.3 %collective-permute-start.2 = (f32[152,128]{1,0:T(8,128)S(1)}, f32[152,128]{1,0:T(8,128)S(1)}, u32[]{:S(2)}, u32[]{:S(2)}) collective-permute-start(f32[152,128]{1,0:T(8,128)S(1)} %get-tuple-element.118), channel_id=1, source_target_pairs={{0,16},{1,17},{2,18},{3,19},{4,20},{5,21},{6,22},{7,23},{8,24},{9,... | collective-permute-start | bytes 233480 | tf_op jit(solution)/shard_map/ppermute | solution.py:187
  6.7 4.2 %collective-permute-start = (f32[144,128]{1,0:T(8,128)S(1)}, f32[144,128]{1,0:T(8,128)S(1)}, u32[]{:S(2)}, u32[]{:S(2)}) collective-permute-start(f32[144,128]{1,0:T(8,128)S(1)} %get-tuple-element.116), channel_id=1, source_target_pairs={{0,1},{2,3},{4,5},{6,7},{8,9},{10,11},{12,13},{14,15},{16,17},{18,... | collective-permute-start | bytes 221192 | tf_op jit(solution)/shard_map/ppermute | solution.py:187
  6.7 4.2 %collective-permute-start.1 = (f32[144,128]{1,0:T(8,128)S(1)}, f32[144,128]{1,0:T(8,128)S(1)}, u32[]{:S(2)}, u32[]{:S(2)}) collective-permute-start(f32[144,128]{1,0:T(8,128)S(1)} %get-tuple-element.117), channel_id=1, source_target_pairs={{1,2},{3,4},{5,6},{7,8},{9,10},{11,12},{13,14},{15,16},{17,18},{19... | collective-permute-start | bytes 221192 | tf_op jit(solution)/shard_map/ppermute | solution.py:187
  11.3 9.7 %collective-permute-start.3 = (f32[73,128]{1,0:T(8,128)S(1)}, f32[73,128]{1,0:T(8,128)S(1)}, u32[]{:S(2)}, u32[]{:S(2)}) collective-permute-start(f32[73,128]{1,0:T(8,128)S(1)} %get-tuple-element.130.refs_0_), channel_id=1, source_target_pairs={{0,16},{1,17},{2,18},{3,19},{4,20},{5,21},{6,22},{7,23},{8,24},{9,... | collective-permute-start | bytes 112136 | tf_op jit(solution)/shard_map/ppermute | solution.py:187
  17.6 13.6 %collective-permute-start.11 = (f32[96,128]{1,0:T(8,128)S(1)}, f32[96,128]{1,0:T(8,128)S(1)}, u32[]{:S(2)}, u32[]{:S(2)}) collective-permute-start(f32[96,128]{1,0:T(8,128)S(1)} %get-tuple-element.142), channel_id=1, source_target_pairs={{1,2},{3,4},{5,6},{7,8},{9,10},{11,12},{13,14},{15,16},{17,18},{19... | collective-permute-start | bytes 147464 | tf_op jit(solution)/shard_map/ppermute | solution.py:187
  21.0 6.5 %collective-permute-start.4 = (f32[18,128]{1,0:T(8,128)S(1)}, f32[18,128]{1,0:T(8,128)S(1)}, u32[]{:S(2)}, u32[]{:S(2)}) collective-permute-start(f32[18,128]{1,0:T(8,128)S(1)} %join.10.refs_0_), channel_id=1, source_target_pairs={{0,10},{1,11},{2,8},{3,9},{4,14},{5,15},{6,12},{7,13},{8,2},{9,3},... | collective-permute-start | bytes 27656 | tf_op jit(solution)/shard_map/ppermute | solution.py:196
  21.6 5.9 %collective-permute-start.5 = (f32[18,128]{1,0:T(8,128)S(1)}, f32[18,128]{1,0:T(8,128)S(1)}, u32[]{:S(2)}, u32[]{:S(2)}) collective-permute-start(f32[18,128]{1,0:T(8,128)S(1)} %join.10.refs_0_), channel_id=1, source_target_pairs={{0,8},{1,9},{2,10},{3,11},{4,12},{5,13},{6,14},{7,15},{8,0},{9,1},... | collective-permute-start | bytes 27656 | tf_op jit(solution)/shard_map/ppermute | solution.py:196
  23.5 4.0 %collective-permute-start.6 = (f32[18,128]{1,0:T(8,128)S(1)}, f32[18,128]{1,0:T(8,128)S(1)}, u32[]{:S(2)}, u32[]{:S(2)}) collective-permute-start(f32[18,128]{1,0:T(8,128)S(1)} %join.10.refs_0_), channel_id=1, source_target_pairs={{0,2},{1,3},{2,0},{3,1},{4,6},{5,7},{6,4},{7,5},{8,10},{9,11},{10,... | collective-permute-start | bytes 27656 | tf_op jit(solution)/shard_map/ppermute | solution.py:196
  28.9 4.0 %collective-permute-start.8 = (f32[72,128]{1,0:T(8,128)S(1)}, f32[72,128]{1,0:T(8,128)S(1)}, u32[]{:S(2)}, u32[]{:S(2)}) collective-permute-start(f32[72,128]{1,0:T(8,128)S(1)} %join.11.refs_0_), channel_id=1, source_target_pairs={{0,4},{1,5},{2,6},{3,7},{4,0},{5,1},{6,2},{7,3},{8,12},{9,13},{10,... | collective-permute-start | bytes 110600 | tf_op jit(solution)/shard_map/ppermute | solution.py:196
  28.9 4.0 %collective-permute-start.9 = (f32[72,128]{1,0:T(8,128)S(1)}, f32[72,128]{1,0:T(8,128)S(1)}, u32[]{:S(2)}, u32[]{:S(2)}) collective-permute-start(f32[72,128]{1,0:T(8,128)S(1)} %join.11.refs_0_), channel_id=1, source_target_pairs={{0,1},{1,0},{2,3},{3,2},{4,5},{5,4},{6,7},{7,6},{8,9},{9,8},{10,11... | collective-permute-start | bytes 110600 | tf_op jit(solution)/shard_map/ppermute | solution.py:196
  33.5 5.3 %collective-permute-start.14 = (f32[72,128]{1,0:T(8,128)S(1)}, f32[72,128]{1,0:T(8,128)S(1)}, u32[]{:S(2)}, u32[]{:S(2)}) collective-permute-start(f32[72,128]{1,0:T(8,128)S(1)} %get-tuple-element.147), channel_id=1, source_target_pairs={{0,16},{1,17},{2,18},{3,19},{4,20},{5,21},{6,22},{7,23},{8,24},{9,... | collective-permute-start | bytes 110600 | tf_op jit(solution)/shard_map/ppermute | solution.py:187
  39.2 7.6 %collective-permute-start.15 = (f32[73,128]{1,0:T(8,128)S(1)}, f32[73,128]{1,0:T(8,128)S(1)}, u32[]{:S(2)}, u32[]{:S(2)}) collective-permute-start(f32[73,128]{1,0:T(8,128)S(1)} %get-tuple-element.158.refs_0_), channel_id=1, source_target_pairs={{0,16},{1,17},{2,18},{3,19},{4,20},{5,21},{6,22},{7,23},{8,24},{9,... | collective-permute-start | bytes 112136 | tf_op jit(solution)/shard_map/ppermute | solution.py:187
  44.0 12.9 %collective-permute-start.23 = (f32[96,128]{1,0:T(8,128)S(1)}, f32[96,128]{1,0:T(8,128)S(1)}, u32[]{:S(2)}, u32[]{:S(2)}) collective-permute-start(f32[96,128]{1,0:T(8,128)S(1)} %get-tuple-element.160), channel_id=1, source_target_pairs={{1,2},{3,4},{5,6},{7,8},{9,10},{11,12},{13,14},{15,16},{17,18},{19... | collective-permute-start | bytes 147464 | tf_op jit(solution)/shard_map/ppermute | solution.py:187
  46.8 4.6 %collective-permute-start.16 = (f32[18,128]{1,0:T(8,128)S(1)}, f32[18,128]{1,0:T(8,128)S(1)}, u32[]{:S(2)}, u32[]{:S(2)}) collective-permute-start(f32[18,128]{1,0:T(8,128)S(1)} %join.12.refs_0_), channel_id=1, source_target_pairs={{0,10},{1,11},{2,8},{3,9},{4,14},{5,15},{6,12},{7,13},{8,2},{9,3},... | collective-permute-start | bytes 27656 | tf_op jit(solution)/shard_map/ppermute | solution.py:196
  53.4 4.0 %collective-permute-start.20 = (f32[72,128]{1,0:T(8,128)S(1)}, f32[72,128]{1,0:T(8,128)S(1)}, u32[]{:S(2)}, u32[]{:S(2)}) collective-permute-start(f32[72,128]{1,0:T(8,128)S(1)} %join.13.refs_0_), channel_id=1, source_target_pairs={{0,4},{1,5},{2,6},{3,7},{4,0},{5,1},{6,2},{7,3},{8,12},{9,13},{10,... | collective-permute-start | bytes 110600 | tf_op jit(solution)/shard_map/ppermute | solution.py:196
  58.1 5.4 %collective-permute-start.26 = (f32[72,128]{1,0:T(8,128)S(1)}, f32[72,128]{1,0:T(8,128)S(1)}, u32[]{:S(2)}, u32[]{:S(2)}) collective-permute-start(f32[72,128]{1,0:T(8,128)S(1)} %get-tuple-element.166), channel_id=1, source_target_pairs={{0,16},{1,17},{2,18},{3,19},{4,20},{5,21},{6,22},{7,23},{8,24},{9,... | collective-permute-start | bytes 110600 | tf_op jit(solution)/shard_map/ppermute | solution.py:187
  64.0 6.9 %collective-permute-start.27 = (f32[73,128]{1,0:T(8,128)S(1)}, f32[73,128]{1,0:T(8,128)S(1)}, u32[]{:S(2)}, u32[]{:S(2)}) collective-permute-start(f32[73,128]{1,0:T(8,128)S(1)} %get-tuple-element.177.refs_0_), channel_id=1, source_target_pairs={{0,16},{1,17},{2,18},{3,19},{4,20},{5,21},{6,22},{7,23},{8,24},{9,... | collective-permute-start | bytes 112136 | tf_op jit(solution)/shard_map/ppermute | solution.py:187
  68.7 13.9 %collective-permute-start.35 = (f32[96,128]{1,0:T(8,128)S(1)}, f32[96,128]{1,0:T(8,128)S(1)}, u32[]{:S(2)}, u32[]{:S(2)}) collective-permute-start(f32[96,128]{1,0:T(8,128)S(1)} %get-tuple-element.179), channel_id=1, source_target_pairs={{1,2},{3,4},{5,6},{7,8},{9,10},{11,12},{13,14},{15,16},{17,18},{19... | collective-permute-start | bytes 147464 | tf_op jit(solution)/shard_map/ppermute | solution.py:187
  70.9 4.6 %collective-permute-start.28 = (f32[18,128]{1,0:T(8,128)S(1)}, f32[18,128]{1,0:T(8,128)S(1)}, u32[]{:S(2)}, u32[]{:S(2)}) collective-permute-start(f32[18,128]{1,0:T(8,128)S(1)} %join.14.refs_0_), channel_id=1, source_target_pairs={{0,10},{1,11},{2,8},{3,9},{4,14},{5,15},{6,12},{7,13},{8,2},{9,3},... | collective-permute-start | bytes 27656 | tf_op jit(solution)/shard_map/ppermute | solution.py:196
  78.8 3.8 %collective-permute-start.31 = (f32[72,128]{1,0:T(8,128)S(1)}, f32[72,128]{1,0:T(8,128)S(1)}, u32[]{:S(2)}, u32[]{:S(2)}) collective-permute-start(f32[72,128]{1,0:T(8,128)S(1)} %join.15.refs_0_), channel_id=1, source_target_pairs={{0,5},{1,4},{2,7},{3,6},{4,1},{5,0},{6,3},{7,2},{8,13},{9,12},{10,... | collective-permute-start | bytes 110600 | tf_op jit(solution)/shard_map/ppermute | solution.py:196
  78.8 4.2 %collective-permute-start.32 = (f32[72,128]{1,0:T(8,128)S(1)}, f32[72,128]{1,0:T(8,128)S(1)}, u32[]{:S(2)}, u32[]{:S(2)}) collective-permute-start(f32[72,128]{1,0:T(8,128)S(1)} %join.15.refs_0_), channel_id=1, source_target_pairs={{0,4},{1,5},{2,6},{3,7},{4,0},{5,1},{6,2},{7,3},{8,12},{9,13},{10,... | collective-permute-start | bytes 110600 | tf_op jit(solution)/shard_map/ppermute | solution.py:196
  78.8 4.1 %collective-permute-start.33 = (f32[72,128]{1,0:T(8,128)S(1)}, f32[72,128]{1,0:T(8,128)S(1)}, u32[]{:S(2)}, u32[]{:S(2)}) collective-permute-start(f32[72,128]{1,0:T(8,128)S(1)} %join.15.refs_0_), channel_id=1, source_target_pairs={{0,1},{1,0},{2,3},{3,2},{4,5},{5,4},{6,7},{7,6},{8,9},{9,8},{10,11... | collective-permute-start | bytes 110600 | tf_op jit(solution)/shard_map/ppermute | solution.py:196
  83.6 5.0 %collective-permute-start.38 = (f32[72,128]{1,0:T(8,128)S(1)}, f32[72,128]{1,0:T(8,128)S(1)}, u32[]{:S(2)}, u32[]{:S(2)}) collective-permute-start(f32[72,128]{1,0:T(8,128)S(1)} %get-tuple-element.186), channel_id=1, source_target_pairs={{0,16},{1,17},{2,18},{3,19},{4,20},{5,21},{6,22},{7,23},{8,24},{9,... | collective-permute-start | bytes 110600 | tf_op jit(solution)/shard_map/ppermute | solution.py:187
  89.1 7.5 %collective-permute-start.41 = (f32[73,128]{1,0:T(8,128)S(1)}, f32[73,128]{1,0:T(8,128)S(1)}, u32[]{:S(2)}, u32[]{:S(2)}) collective-permute-start(f32[73,128]{1,0:T(8,128)S(1)} %get-tuple-element.205.refs_0_), channel_id=1, source_target_pairs={{0,16},{1,17},{2,18},{3,19},{4,20},{5,21},{6,22},{7,23},{8,24},{9,... | collective-permute-start | bytes 112136 | tf_op jit(solution)/shard_map/ppermute | solution.py:187
  94.2 12.1 %collective-permute-start.40 = (f32[96,128]{1,0:T(8,128)S(1)}, f32[96,128]{1,0:T(8,128)S(1)}, u32[]{:S(2)}, u32[]{:S(2)}) collective-permute-start(f32[96,128]{1,0:T(8,128)S(1)} %get-tuple-element.204), channel_id=1, source_target_pairs={{1,2},{3,4},{5,6},{7,8},{9,10},{11,12},{13,14},{15,16},{17,18},{19... | collective-permute-start | bytes 147464 | tf_op jit(solution)/shard_map/ppermute | solution.py:187
  96.6 4.6 %collective-permute-start.42 = (f32[18,128]{1,0:T(8,128)S(1)}, f32[18,128]{1,0:T(8,128)S(1)}, u32[]{:S(2)}, u32[]{:S(2)}) collective-permute-start(f32[18,128]{1,0:T(8,128)S(1)} %join.16.refs_0_), channel_id=1, source_target_pairs={{0,10},{1,11},{2,8},{3,9},{4,14},{5,15},{6,12},{7,13},{8,2},{9,3},... | collective-permute-start | bytes 27656 | tf_op jit(solution)/shard_map/ppermute | solution.py:196
  102.5 3.8 %collective-permute-start.45 = (f32[72,128]{1,0:T(8,128)S(1)}, f32[72,128]{1,0:T(8,128)S(1)}, u32[]{:S(2)}, u32[]{:S(2)}) collective-permute-start(f32[72,128]{1,0:T(8,128)S(1)} %join.17.refs_20_), channel_id=1, source_target_pairs={{0,5},{1,4},{2,7},{3,6},{4,1},{5,0},{6,3},{7,2},{8,13},{9,12},{10,... | collective-permute-start | bytes 110600 | tf_op jit(solution)/shard_map/ppermute | solution.py:196
  102.9 4.0 %collective-permute-start.46 = (f32[72,128]{1,0:T(8,128)S(1)}, f32[72,128]{1,0:T(8,128)S(1)}, u32[]{:S(2)}, u32[]{:S(2)}) collective-permute-start(f32[72,128]{1,0:T(8,128)S(1)} %join.17.refs_20_), channel_id=1, source_target_pairs={{0,4},{1,5},{2,6},{3,7},{4,0},{5,1},{6,2},{7,3},{8,12},{9,13},{10,... | collective-permute-start | bytes 110600 | tf_op jit(solution)/shard_map/ppermute | solution.py:196
  109.0 5.3 %collective-permute-start.48 = (f32[72,128]{1,0:T(8,128)S(1)}, f32[72,128]{1,0:T(8,128)S(1)}, u32[]{:S(2)}, u32[]{:S(2)}) collective-permute-start(f32[72,128]{1,0:T(8,128)S(1)} %get-tuple-element.220.refs_0_), channel_id=1, source_target_pairs={{0,16},{1,17},{2,18},{3,19},{4,20},{5,21},{6,22},{7,23},{8,24},{9,... | collective-permute-start | bytes 110600 | tf_op jit(solution)/shard_map/ppermute | solution.py:187
  111.0 11.2 %collective-permute-start.55 = (f32[64,128]{1,0:T(8,128)S(1)}, f32[64,128]{1,0:T(8,128)S(1)}, u32[]{:S(2)}, u32[]{:S(2)}) collective-permute-start(f32[64,128]{1,0:T(8,128)S(1)} %get-tuple-element.222), channel_id=1, source_target_pairs={{0,1},{2,3},{4,5},{6,7},{8,9},{10,11},{12,13},{14,15},{16,17},{18,... | collective-permute-start | bytes 98312 | tf_op jit(solution)/shard_map/ppermute | solution.py:187
  111.0 11.2 %collective-permute-start.56 = (f32[64,128]{1,0:T(8,128)S(1)}, f32[64,128]{1,0:T(8,128)S(1)}, u32[]{:S(2)}, u32[]{:S(2)}) collective-permute-start(f32[64,128]{1,0:T(8,128)S(1)} %get-tuple-element.223), channel_id=1, source_target_pairs={{1,2},{3,4},{5,6},{7,8},{9,10},{11,12},{13,14},{15,16},{17,18},{19... | collective-permute-start | bytes 98312 | tf_op jit(solution)/shard_map/ppermute | solution.py:187
  114.2 4.5 %collective-permute-start.49 = (f32[2,128]{1,0:T(2,128)S(1)}, f32[2,128]{1,0:T(2,128)S(1)}, u32[]{:S(2)}, u32[]{:S(2)}) collective-permute-start(f32[2,128]{1,0:T(2,128)S(1)} %join.18.refs_0_), channel_id=1, source_target_pairs={{0,10},{1,11},{2,8},{3,9},{4,14},{5,15},{6,12},{7,13},{8,2},{9,3},... | collective-permute-start | bytes 3080 | tf_op jit(solution)/shard_map/ppermute | solution.py:196
  (34 other events, 102.9 us)

commit v11 on v10

--- a/solution.py
+++ b/solution.py
@@ -391,16 +391,18 @@
                 alpha = gamma / (delta - beta * gamma / alpha_old)
                 q = inner + beta * i.q[...]
                 s = w + beta * i.s[...]
-                p = i.u[...] + beta * i.p[...]
-                x = i.x[...] + alpha * p
+                if step + 1 < ITERS:
+                    p = i.u[...] + beta * i.p[...]
+                    x = i.x[...] + alpha * p
                 before = w - (alpha * beta) * i.z[...]
             residual = i.residual[...] - alpha * s
             u = i.u[...] - alpha * q
             part = before - alpha * image
             delta = dot(weight * before - alpha * image, u)
             o.coef[...] = jnp.concatenate([both[:, :cases], to_row(alpha)], axis=1)
-            o.s[...], o.p[...], o.x[...], o.residual[...] = s, p, x, residual
+            o.s[...], o.residual[...] = s, residual
             if step + 1 < ITERS:
+                o.p[...], o.x[...] = p, x
                 o.q[...] = q
                 o.z_part[...] = image if step == 1 else image + beta * i.z[...]
         o.u[...] = u
@@ -422,11 +424,13 @@
         outs = dict(u=vec, w_part=vec)
         if step > 0:
             ins.update(w=state.w, u=state.u)
-            outs.update(coef=pair, s=vec, p=vec, x=vec, residual=vec)
+            outs.update(coef=pair, s=vec, residual=vec)
             if not final:
-                outs.update(q=vec, z_part=vec)
+                outs.update(p=vec, x=vec, q=vec, z_part=vec)
         if step > 1:
-            ins.update(coef=coef, q=state.q, s=state.s, p=state.p, x=state.x, z=state.z)
+            ins.update(coef=coef, q=state.q, s=state.s, z=state.z)
+            if not final:
+                ins.update(p=state.p, x=state.x)
         if final:
             def last(i, o):
                 at_slots, factors, both = corrected(i)
@@ -435,6 +439,7 @@
 
             ins.update(rest_ins)
             outs.update(face=longer(faces_kind))
+            earlier = dict(u=state.u, p=state.p, x=state.x, coef_old=coef)
             made = stage("last", last, ins, outs)
             vars(state).update(vars(made))
             came_image = exchange(made.face)
@@ -460,7 +465,10 @@
             coef = own.coef
 
     def settle(i, o):
-        alpha_old = as_columns(i.coef[...])[1]
+        gamma, alpha_old = as_columns(i.coef[...])
+        p = i.u[...] + gamma / as_columns(i.coef_old[...])[0] * i.p[...]
+        o.p[...] = p
+        o.x[...] = i.x[...] + alpha_old * p
         o.w[...] = i.w_part[...] - alpha_old * pick(joined(i.came), i.picker[...])
 
     def finish(i, o):
@@ -473,10 +481,11 @@
 
     whole = ((1, cases, ndof), F32)
     everyone = gather(state.face[paired], came_image[paired], 1)
-    w = stage("settle", settle, dict(came=came_image, picker=picker, coef=state.coef, w_part=state.w_part), dict(w=vec)).w
+    ins = dict(came=came_image, picker=picker, coef=state.coef, w_part=state.w_part)
+    settled = stage("settle", settle, ins | earlier, dict(w=vec, p=vec, x=vec))
     done = stage(
         "finish", finish,
-        dict(everyone=everyone, coef=state.coef, w=w, x=state.x, u=state.u, p=state.p, residual=state.residual, s=state.s),
+        dict(everyone=everyone, coef=state.coef, w=settled.w, x=settled.x, u=state.u, p=settled.p, residual=state.residual, s=state.s),
         dict(solution=whole, remainder=whole))
     return done.solution, done.remainder
 

time: 125 us -> 125 us (level)
  no operation moved by 1% of the time
where the time goes in v11:
time: 125 us
  starting transfers between devices  66.8 us (53%)
  Pallas kernels  31.8 us (25%)
  waiting for transfers between devices  24.2 us (19%)
    ppermute x27, starting transfers between devices, exchange(): lax.ppermute(array, AXIS, chosen[i][0])  38 us
    pallas_call x34, Pallas kernels, stage(): pl.pallas_call(kernel, name=name, out_shape=[jax.ShapeDtypeStruct(*kind)...  31.8 us
    ppermute x30, starting transfers between devices, gather(): lax.ppermute(block, AXIS, [(i, i ^ far) for i in range(total)])  28.8 us
    ppermute x30, waiting for transfers between devices, gather(): lax.ppermute(block, AXIS, [(i, i ^ far) for i in range(total)])  15.2 us
    ppermute x27, waiting for transfers between devices, exchange(): lax.ppermute(array, AXIS, chosen[i][0])  8.97 us
  transfers between devices with their start and end apart: 57, of which 23 were waited for; matrix products, arithmetic and copies ran while one was open for 0% of the time, Pallas kernels for 19%

profile of v11, /device:TPU:0, one launch (start us, length us, event | category | flops | bytes accessed | tf_op | source)
XLA Modules:
  0.0 125.0 jit_solution(14677630307576237739)
XLA Ops:
  2.6 4.1 %collective-permute-start.2 = (f32[152,128]{1,0:T(8,128)S(1)}, f32[152,128]{1,0:T(8,128)S(1)}, u32[]{:S(2)}, u32[]{:S(2)}) collective-permute-start(f32[152,128]{1,0:T(8,128)S(1)} %get-tuple-element.119), channel_id=1, source_target_pairs={{0,16},{1,17},{2,18},{3,19},{4,20},{5,21},{6,22},{7,23},{8,24},{9,... | collective-permute-start | bytes 233480 | tf_op jit(solution)/shard_map/ppermute | solution.py:187
  7.4 2.7 %prepare_inv.1 = (bf16[1024,1024]{1,0:T(8,128)(2,1)S(1)}, bf16[1024,1024]{1,0:T(8,128)(2,1)S(1)}, bf16[384,1024]{1,0:T(8,128)(2,1)S(1)}, bf16[384,1024]{1,0:T(8,...) custom-call(f32[1,1024,1024]{2,1,0:T(8,128)S(1)} %copy-done, ...), custom_call_target="tpu_custom_call" | custom-call | tf_op jit(solution)/shard_map/prepare_inv/pallas_call | solution.py:105
  11.3 6.3 %collective-permute-start.3 = (f32[73,128]{1,0:T(8,128)S(1)}, f32[73,128]{1,0:T(8,128)S(1)}, u32[]{:S(2)}, u32[]{:S(2)}) collective-permute-start(f32[73,128]{1,0:T(8,128)S(1)} %get-tuple-element.131.refs_0_), channel_id=1, source_target_pairs={{0,16},{1,17},{2,18},{3,19},{4,20},{5,21},{6,22},{7,23},{8,24},{9,... | collective-permute-start | bytes 112136 | tf_op jit(solution)/shard_map/ppermute | solution.py:187
  18.3 2.7 %prepare_stiff.1 = (bf16[1024,1024]{1,0:T(8,128)(2,1)S(1)}, bf16[1024,1024]{1,0:T(8,128)(2,1)S(1)}, bf16[384,1024]{1,0:T(8,128)(2,1)S(1)}, bf16[384,1024]{1,0:T(...) custom-call(f32[1,1024,1024]{2,1,0:T(8,128)S(1)} %copy-done.1, ...), custom_call_target="tpu_custom_call" | custom-call | tf_op jit(solution)/shard_map/prepare_stiff/pallas_call | solution.py:105
  21.6 1.9 %collective-permute-start.5 = (f32[18,128]{1,0:T(8,128)S(1)}, f32[18,128]{1,0:T(8,128)S(1)}, u32[]{:S(2)}, u32[]{:S(2)}) collective-permute-start(f32[18,128]{1,0:T(8,128)S(1)} %join.10.refs_0_), channel_id=1, source_target_pairs={{0,8},{1,9},{2,10},{3,11},{4,12},{5,13},{6,14},{7,15},{8,0},{9,1},... | collective-permute-start | bytes 27656 | tf_op jit(solution)/shard_map/ppermute | solution.py:196
  25.7 1.7 %reach.1 = (bf16[64,2048]{1,0:T(8,128)(2,1)S(1)}, bf16[64,2048]{1,0:T(8,128)(2,1)S(1)}, bf16[64,384]{1,0:T(8,128)(2,1)S(1)}, bf16[64,384]{1,0:T(8,128)(2,1)S(1)}, f32[128,288]{1,0:T(8,128)S(1)}) custom-call(f32[16,1024]{1,0:T(8,128)S(1)} %get-tuple-element.122.refs_2_.refs_0_.refs_14_.refs_16_.refs_22_, f32[16,512]{1,0:T(8,128)S(1)} %copy-done.3, ...), custom_call_target="tpu_custom_call" | custom-call | tf_op jit(solution)/shard_map/reach/pallas_call | solution.py:105
  29.5 1.7 %apply_own.4 = (f32[64,1024]{1,0:T(8,128)S(1)}, f32[64,384]{1,0:T(8,128)S(1)}, f32[64,1024]{1,0:T(8,128)S(1)}, f32[64,1024]{1,0:T(8,128)S(1)}) custom-call(f32[144,128]{1,0:T(8,128)S(1)} %collective-permute-done.refs_0_.refs_2_, f32[144,128]{1,0:T(8,128)S(1)} %collective-permute-done.1.refs_1_.refs_3_, ...), custom_call_target="tpu_custom_call" | custom-call | tf_op jit(solution)/shard_map/apply_own/pallas_call | solution.py:105
  31.2 1.7 %collective-permute-done.8.refs_2_ = f32[72,128]{1,0:T(8,128)S(1)} collective-permute-done((f32[72,128]{1,0:T(8,128)S(1)}, f32[72,128]{1,0:T(8,128)S(1)}, u32[]{:S(2)}, u32[]{:S(2)}) %collective-permute-start.8) | collective-permute-done | bytes 36896 | tf_op jit(solution)/shard_map/ppermute | solution.py:196
  33.5 2.0 %collective-permute-start.14 = (f32[72,128]{1,0:T(8,128)S(1)}, f32[72,128]{1,0:T(8,128)S(1)}, u32[]{:S(2)}, u32[]{:S(2)}) collective-permute-start(f32[72,128]{1,0:T(8,128)S(1)} %get-tuple-element.148), channel_id=1, source_target_pairs={{0,16},{1,17},{2,18},{3,19},{4,20},{5,21},{6,22},{7,23},{8,24},{9,... | collective-permute-start | bytes 110600 | tf_op jit(solution)/shard_map/ppermute | solution.py:187
  36.3 2.4 %update.3 = (f32[64,1024]{1,0:T(8,128)S(1)}, f32[64,1024]{1,0:T(8,128)S(1)}, f32[16,64]{1,0:T(8,128)S(1)}, f32[64,384]{1,0:T(8,128)S(1)}, f32[64,1024]{1,0:T(8,128)S(1)}, /*index=5*/f32[1,128]{1,0:T(1,128)S(1)}) custom-call(f32[64,128]{1,0:T(8,128)S(1)} %collective-permute-done.10.refs_7_.refs_0_, f32[96,128]{1,0:T(8,128)S(1)} %collective-permute-done.11.refs_8_.refs_1_, ...), custom_call_target="tpu_custom_call" | custom-call | tf_op jit(solution)/shard_map/update/pallas_call | solution.py:105
  39.2 4.8 %collective-permute-start.15 = (f32[73,128]{1,0:T(8,128)S(1)}, f32[73,128]{1,0:T(8,128)S(1)}, u32[]{:S(2)}, u32[]{:S(2)}) collective-permute-start(f32[73,128]{1,0:T(8,128)S(1)} %get-tuple-element.159.refs_0_), channel_id=1, source_target_pairs={{0,16},{1,17},{2,18},{3,19},{4,20},{5,21},{6,22},{7,23},{8,24},{9,... | collective-permute-start | bytes 112136 | tf_op jit(solution)/shard_map/ppermute | solution.py:187
  44.6 2.2 %collective-permute-done.15.refs_1_.refs_9_.refs_2_ = f32[73,128]{1,0:T(8,128)S(1)} collective-permute-done((f32[73,128]{1,0:T(8,128)S(1)}, f32[73,128]{1,0:T(8,128)S(1)}, u32[]{:S(2)}, u32[]{:S(2)}) %collective-permute-start.15) | collective-permute-done | bytes 37408 | tf_op jit(solution)/shard_map/ppermute | solution.py:187
  46.8 2.2 %collective-permute-start.16 = (f32[18,128]{1,0:T(8,128)S(1)}, f32[18,128]{1,0:T(8,128)S(1)}, u32[]{:S(2)}, u32[]{:S(2)}) collective-permute-start(f32[18,128]{1,0:T(8,128)S(1)} %join.12.refs_0_), channel_id=1, source_target_pairs={{0,10},{1,11},{2,8},{3,9},{4,14},{5,15},{6,12},{7,13},{8,2},{9,3},... | collective-permute-start | bytes 27656 | tf_op jit(solution)/shard_map/ppermute | solution.py:196
  55.1 1.7 %apply_own.5 = (f32[64,1024]{1,0:T(8,128)S(1)}, f32[64,384]{1,0:T(8,128)S(1)}, f32[64,1024]{1,0:T(8,128)S(1)}, f32[64,1024]{1,0:T(8,128)S(1)}) custom-call(f32[64,128]{1,0:T(8,128)S(1)} %collective-permute-done.12.refs_0_, f32[64,128]{1,0:T(8,128)S(1)} %collective-permute-done.13.refs_1_, f32[72,128]{1,0:T(8,128)S(1)} %collective-permute-done.14.refs_2_, ...), custom_call_target="tpu_custom_call" | custom-call | tf_op jit(solution)/shard_map/apply_own/pallas_call | solution.py:105
  58.1 2.2 %collective-permute-start.26 = (f32[72,128]{1,0:T(8,128)S(1)}, f32[72,128]{1,0:T(8,128)S(1)}, u32[]{:S(2)}, u32[]{:S(2)}) collective-permute-start(f32[72,128]{1,0:T(8,128)S(1)} %get-tuple-element.167), channel_id=1, source_target_pairs={{0,16},{1,17},{2,18},{3,19},{4,20},{5,21},{6,22},{7,23},{8,24},{9,... | collective-permute-start | bytes 110600 | tf_op jit(solution)/shard_map/ppermute | solution.py:187
  60.9 2.5 %update.4 = (f32[64,1024]{1,0:T(8,128)S(1)}, f32[64,1024]{1,0:T(8,128)S(1)}, f32[1,128]{1,0:T(1,128)S(1)}, f32[64,1024]{1,0:T(8,128)S(1)}, f32[64,1024]{1,0:T(8,...) custom-call(f32[64,128]{1,0:T(8,128)S(1)} %collective-permute-done.2, ...), custom_call_target="tpu_custom_call" | custom-call | tf_op jit(solution)/shard_map/update/pallas_call | solution.py:105
  64.0 4.6 %collective-permute-start.27 = (f32[73,128]{1,0:T(8,128)S(1)}, f32[73,128]{1,0:T(8,128)S(1)}, u32[]{:S(2)}, u32[]{:S(2)}) collective-permute-start(f32[73,128]{1,0:T(8,128)S(1)} %get-tuple-element.178.refs_0_), channel_id=1, source_target_pairs={{0,16},{1,17},{2,18},{3,19},{4,20},{5,21},{6,22},{7,23},{8,24},{9,... | collective-permute-start | bytes 112136 | tf_op jit(solution)/shard_map/ppermute | solution.py:187
  69.3 1.6 %collective-permute-done.27.refs_1_.refs_9_.refs_2_ = f32[73,128]{1,0:T(8,128)S(1)} collective-permute-done((f32[73,128]{1,0:T(8,128)S(1)}, f32[73,128]{1,0:T(8,128)S(1)}, u32[]{:S(2)}, u32[]{:S(2)}) %collective-permute-start.27) | collective-permute-done | bytes 37408 | tf_op jit(solution)/shard_map/ppermute | solution.py:187
  70.9 2.2 %collective-permute-start.28 = (f32[18,128]{1,0:T(8,128)S(1)}, f32[18,128]{1,0:T(8,128)S(1)}, u32[]{:S(2)}, u32[]{:S(2)}) collective-permute-start(f32[18,128]{1,0:T(8,128)S(1)} %join.14.refs_0_), channel_id=1, source_target_pairs={{0,10},{1,11},{2,8},{3,9},{4,14},{5,15},{6,12},{7,13},{8,2},{9,3},... | collective-permute-start | bytes 27656 | tf_op jit(solution)/shard_map/ppermute | solution.py:196
  73.1 1.9 %collective-permute-start.29 = (f32[18,128]{1,0:T(8,128)S(1)}, f32[18,128]{1,0:T(8,128)S(1)}, u32[]{:S(2)}, u32[]{:S(2)}) collective-permute-start(f32[18,128]{1,0:T(8,128)S(1)} %join.14.refs_0_), channel_id=1, source_target_pairs={{0,8},{1,9},{2,10},{3,11},{4,12},{5,13},{6,14},{7,15},{8,0},{9,1},... | collective-permute-start | bytes 27656 | tf_op jit(solution)/shard_map/ppermute | solution.py:196
  76.9 1.9 %collective-permute-done.30.refs_3_ = f32[18,128]{1,0:T(8,128)S(1)} collective-permute-done((f32[18,128]{1,0:T(8,128)S(1)}, f32[18,128]{1,0:T(8,128)S(1)}, u32[]{:S(2)}, u32[]{:S(2)}) %collective-permute-start.30) | collective-permute-done | bytes 9248 | tf_op jit(solution)/shard_map/ppermute | solution.py:196
  78.8 1.8 %collective-permute-start.33 = (f32[72,128]{1,0:T(8,128)S(1)}, f32[72,128]{1,0:T(8,128)S(1)}, u32[]{:S(2)}, u32[]{:S(2)}) collective-permute-start(f32[72,128]{1,0:T(8,128)S(1)} %join.15.refs_0_), channel_id=1, source_target_pairs={{0,1},{1,0},{2,3},{3,2},{4,5},{5,4},{6,7},{7,6},{8,9},{9,8},{10,11... | collective-permute-start | bytes 110600 | tf_op jit(solution)/shard_map/ppermute | solution.py:196
  80.6 1.9 %apply_own.6 = (f32[64,1024]{1,0:T(8,128)S(1)}, f32[64,384]{1,0:T(8,128)S(1)}, f32[64,1024]{1,0:T(8,128)S(1)}, f32[64,1024]{1,0:T(8,128)S(1)}, f32[64,1024]{1,0:T(8,128)S(1)}) custom-call(f32[64,128]{1,0:T(8,128)S(1)} %collective-permute-done.24.refs_0_, f32[64,128]{1,0:T(8,128)S(1)} %collective-permute-done.25.refs_1_, ...), custom_call_target="tpu_custom_call" | custom-call | tf_op jit(solution)/shard_map/apply_own/pallas_call | solution.py:105
  85.2 2.6 %update.5 = (f32[64,1024]{1,0:T(8,128)S(1)}, f32[64,1024]{1,0:T(8,128)S(1)}, f32[1,128]{1,0:T(1,128)S(1)}, f32[64,1024]{1,0:T(8,128)S(1)}, f32[64,1024]{1,0:T(8,...) custom-call(f32[64,128]{1,0:T(8,128)S(1)} %collective-permute-done.3, ...), custom_call_target="tpu_custom_call" | custom-call | tf_op jit(solution)/shard_map/update/pallas_call | solution.py:105
  89.1 5.1 %collective-permute-start.41 = (f32[73,128]{1,0:T(8,128)S(1)}, f32[73,128]{1,0:T(8,128)S(1)}, u32[]{:S(2)}, u32[]{:S(2)}) collective-permute-start(f32[73,128]{1,0:T(8,128)S(1)} %get-tuple-element.206.refs_0_), channel_id=1, source_target_pairs={{0,16},{1,17},{2,18},{3,19},{4,20},{5,21},{6,22},{7,23},{8,24},{9,... | collective-permute-start | bytes 112136 | tf_op jit(solution)/shard_map/ppermute | solution.py:187
  94.8 1.8 %collective-permute-done.41.refs_1_.refs_2_ = f32[73,128]{1,0:T(8,128)S(1)} collective-permute-done((f32[73,128]{1,0:T(8,128)S(1)}, f32[73,128]{1,0:T(8,128)S(1)}, u32[]{:S(2)}, u32[]{:S(2)}) %collective-permute-start.41) | collective-permute-done | bytes 37408 | tf_op jit(solution)/shard_map/ppermute | solution.py:187
  96.6 1.8 %collective-permute-start.42 = (f32[18,128]{1,0:T(8,128)S(1)}, f32[18,128]{1,0:T(8,128)S(1)}, u32[]{:S(2)}, u32[]{:S(2)}) collective-permute-start(f32[18,128]{1,0:T(8,128)S(1)} %join.16.refs_0_), channel_id=1, source_target_pairs={{0,10},{1,11},{2,8},{3,9},{4,14},{5,15},{6,12},{7,13},{8,2},{9,3},... | collective-permute-start | bytes 27656 | tf_op jit(solution)/shard_map/ppermute | solution.py:196
  104.4 1.9 %apply_own.7 = (f32[64,1024]{1,0:T(8,128)S(1)}, f32[64,384]{1,0:T(8,128)S(1)}, f32[64,1024]{1,0:T(8,128)S(1)}, f32[64,1024]{1,0:T(8,128)S(1)}, f32[64,1024]{1,0:T(8,128)S(1)}) custom-call(f32[64,128]{1,0:T(8,128)S(1)} %collective-permute-done.36.refs_0_, f32[64,128]{1,0:T(8,128)S(1)} %collective-permute-done.37.refs_1_, ...), custom_call_target="tpu_custom_call" | custom-call | tf_op jit(solution)/shard_map/apply_own/pallas_call | solution.py:105
  106.9 2.1 %last.1 = (f32[64,1024]{1,0:T(8,128)S(1)}, f32[64,1024]{1,0:T(8,128)S(1)}, f32[1,128]{1,0:T(1,128)S(1)}, f32[64,1024]{1,0:T(8,128)S(1)}, f32[64,1024]{1,0:T(8,12...) custom-call(f32[64,128]{1,0:T(8,128)S(1)} %collective-permute-done.39.refs_0_, ...), custom_call_target="tpu_custom_call" | custom-call | tf_op jit(solution)/shard_map/last/pallas_call | solution.py:105
  108.9 2.0 %collective-permute-start.48 = (f32[72,128]{1,0:T(8,128)S(1)}, f32[72,128]{1,0:T(8,128)S(1)}, u32[]{:S(2)}, u32[]{:S(2)}) collective-permute-start(f32[72,128]{1,0:T(8,128)S(1)} %get-tuple-element.219.refs_0_), channel_id=1, source_target_pairs={{0,16},{1,17},{2,18},{3,19},{4,20},{5,21},{6,22},{7,23},{8,24},{9,... | collective-permute-start | bytes 110600 | tf_op jit(solution)/shard_map/ppermute | solution.py:187
  111.6 2.6 %collective-permute-done.48.refs_1_.refs_2_ = f32[72,128]{1,0:T(8,128)S(1)} collective-permute-done((f32[72,128]{1,0:T(8,128)S(1)}, f32[72,128]{1,0:T(8,128)S(1)}, u32[]{:S(2)}, u32[]{:S(2)}) %collective-permute-start.48) | collective-permute-done | bytes 36896 | tf_op jit(solution)/shard_map/ppermute | solution.py:187
  114.2 2.3 %collective-permute-start.49 = (f32[2,128]{1,0:T(2,128)S(1)}, f32[2,128]{1,0:T(2,128)S(1)}, u32[]{:S(2)}, u32[]{:S(2)}) collective-permute-start(f32[2,128]{1,0:T(2,128)S(1)} %join.18.refs_0_), channel_id=1, source_target_pairs={{0,10},{1,11},{2,8},{3,9},{4,14},{5,15},{6,12},{7,13},{8,2},{9,3},... | collective-permute-start | bytes 3080 | tf_op jit(solution)/shard_map/ppermute | solution.py:196
  (134 shorter events, 43.0 us)
Async XLA Ops:
  2.6 8.3 %collective-permute-start.2 = (f32[152,128]{1,0:T(8,128)S(1)}, f32[152,128]{1,0:T(8,128)S(1)}, u32[]{:S(2)}, u32[]{:S(2)}) collective-permute-start(f32[152,128]{1,0:T(8,128)S(1)} %get-tuple-element.119), channel_id=1, source_target_pairs={{0,16},{1,17},{2,18},{3,19},{4,20},{5,21},{6,22},{7,23},{8,24},{9,... | collective-permute-start | bytes 233480 | tf_op jit(solution)/shard_map/ppermute | solution.py:187
  6.7 4.2 %collective-permute-start = (f32[144,128]{1,0:T(8,128)S(1)}, f32[144,128]{1,0:T(8,128)S(1)}, u32[]{:S(2)}, u32[]{:S(2)}) collective-permute-start(f32[144,128]{1,0:T(8,128)S(1)} %get-tuple-element.117), channel_id=1, source_target_pairs={{0,1},{2,3},{4,5},{6,7},{8,9},{10,11},{12,13},{14,15},{16,17},{18,... | collective-permute-start | bytes 221192 | tf_op jit(solution)/shard_map/ppermute | solution.py:187
  6.7 4.2 %collective-permute-start.1 = (f32[144,128]{1,0:T(8,128)S(1)}, f32[144,128]{1,0:T(8,128)S(1)}, u32[]{:S(2)}, u32[]{:S(2)}) collective-permute-start(f32[144,128]{1,0:T(8,128)S(1)} %get-tuple-element.118), channel_id=1, source_target_pairs={{1,2},{3,4},{5,6},{7,8},{9,10},{11,12},{13,14},{15,16},{17,18},{19... | collective-permute-start | bytes 221192 | tf_op jit(solution)/shard_map/ppermute | solution.py:187
  11.3 9.7 %collective-permute-start.3 = (f32[73,128]{1,0:T(8,128)S(1)}, f32[73,128]{1,0:T(8,128)S(1)}, u32[]{:S(2)}, u32[]{:S(2)}) collective-permute-start(f32[73,128]{1,0:T(8,128)S(1)} %get-tuple-element.131.refs_0_), channel_id=1, source_target_pairs={{0,16},{1,17},{2,18},{3,19},{4,20},{5,21},{6,22},{7,23},{8,24},{9,... | collective-permute-start | bytes 112136 | tf_op jit(solution)/shard_map/ppermute | solution.py:187
  17.6 13.6 %collective-permute-start.11 = (f32[96,128]{1,0:T(8,128)S(1)}, f32[96,128]{1,0:T(8,128)S(1)}, u32[]{:S(2)}, u32[]{:S(2)}) collective-permute-start(f32[96,128]{1,0:T(8,128)S(1)} %get-tuple-element.143), channel_id=1, source_target_pairs={{1,2},{3,4},{5,6},{7,8},{9,10},{11,12},{13,14},{15,16},{17,18},{19... | collective-permute-start | bytes 147464 | tf_op jit(solution)/shard_map/ppermute | solution.py:187
  21.0 6.5 %collective-permute-start.4 = (f32[18,128]{1,0:T(8,128)S(1)}, f32[18,128]{1,0:T(8,128)S(1)}, u32[]{:S(2)}, u32[]{:S(2)}) collective-permute-start(f32[18,128]{1,0:T(8,128)S(1)} %join.10.refs_0_), channel_id=1, source_target_pairs={{0,10},{1,11},{2,8},{3,9},{4,14},{5,15},{6,12},{7,13},{8,2},{9,3},... | collective-permute-start | bytes 27656 | tf_op jit(solution)/shard_map/ppermute | solution.py:196
  21.6 5.9 %collective-permute-start.5 = (f32[18,128]{1,0:T(8,128)S(1)}, f32[18,128]{1,0:T(8,128)S(1)}, u32[]{:S(2)}, u32[]{:S(2)}) collective-permute-start(f32[18,128]{1,0:T(8,128)S(1)} %join.10.refs_0_), channel_id=1, source_target_pairs={{0,8},{1,9},{2,10},{3,11},{4,12},{5,13},{6,14},{7,15},{8,0},{9,1},... | collective-permute-start | bytes 27656 | tf_op jit(solution)/shard_map/ppermute | solution.py:196
  23.5 4.0 %collective-permute-start.6 = (f32[18,128]{1,0:T(8,128)S(1)}, f32[18,128]{1,0:T(8,128)S(1)}, u32[]{:S(2)}, u32[]{:S(2)}) collective-permute-start(f32[18,128]{1,0:T(8,128)S(1)} %join.10.refs_0_), channel_id=1, source_target_pairs={{0,2},{1,3},{2,0},{3,1},{4,6},{5,7},{6,4},{7,5},{8,10},{9,11},{10,... | collective-permute-start | bytes 27656 | tf_op jit(solution)/shard_map/ppermute | solution.py:196
  28.9 4.0 %collective-permute-start.8 = (f32[72,128]{1,0:T(8,128)S(1)}, f32[72,128]{1,0:T(8,128)S(1)}, u32[]{:S(2)}, u32[]{:S(2)}) collective-permute-start(f32[72,128]{1,0:T(8,128)S(1)} %join.11.refs_0_), channel_id=1, source_target_pairs={{0,4},{1,5},{2,6},{3,7},{4,0},{5,1},{6,2},{7,3},{8,12},{9,13},{10,... | collective-permute-start | bytes 110600 | tf_op jit(solution)/shard_map/ppermute | solution.py:196
  28.9 4.0 %collective-permute-start.9 = (f32[72,128]{1,0:T(8,128)S(1)}, f32[72,128]{1,0:T(8,128)S(1)}, u32[]{:S(2)}, u32[]{:S(2)}) collective-permute-start(f32[72,128]{1,0:T(8,128)S(1)} %join.11.refs_0_), channel_id=1, source_target_pairs={{0,1},{1,0},{2,3},{3,2},{4,5},{5,4},{6,7},{7,6},{8,9},{9,8},{10,11... | collective-permute-start | bytes 110600 | tf_op jit(solution)/shard_map/ppermute | solution.py:196
  33.5 5.3 %collective-permute-start.14 = (f32[72,128]{1,0:T(8,128)S(1)}, f32[72,128]{1,0:T(8,128)S(1)}, u32[]{:S(2)}, u32[]{:S(2)}) collective-permute-start(f32[72,128]{1,0:T(8,128)S(1)} %get-tuple-element.148), channel_id=1, source_target_pairs={{0,16},{1,17},{2,18},{3,19},{4,20},{5,21},{6,22},{7,23},{8,24},{9,... | collective-permute-start | bytes 110600 | tf_op jit(solution)/shard_map/ppermute | solution.py:187
  39.2 7.6 %collective-permute-start.15 = (f32[73,128]{1,0:T(8,128)S(1)}, f32[73,128]{1,0:T(8,128)S(1)}, u32[]{:S(2)}, u32[]{:S(2)}) collective-permute-start(f32[73,128]{1,0:T(8,128)S(1)} %get-tuple-element.159.refs_0_), channel_id=1, source_target_pairs={{0,16},{1,17},{2,18},{3,19},{4,20},{5,21},{6,22},{7,23},{8,24},{9,... | collective-permute-start | bytes 112136 | tf_op jit(solution)/shard_map/ppermute | solution.py:187
  44.0 12.8 %collective-permute-start.23 = (f32[96,128]{1,0:T(8,128)S(1)}, f32[96,128]{1,0:T(8,128)S(1)}, u32[]{:S(2)}, u32[]{:S(2)}) collective-permute-start(f32[96,128]{1,0:T(8,128)S(1)} %get-tuple-element.161), channel_id=1, source_target_pairs={{1,2},{3,4},{5,6},{7,8},{9,10},{11,12},{13,14},{15,16},{17,18},{19... | collective-permute-start | bytes 147464 | tf_op jit(solution)/shard_map/ppermute | solution.py:187
  46.8 4.6 %collective-permute-start.16 = (f32[18,128]{1,0:T(8,128)S(1)}, f32[18,128]{1,0:T(8,128)S(1)}, u32[]{:S(2)}, u32[]{:S(2)}) collective-permute-start(f32[18,128]{1,0:T(8,128)S(1)} %join.12.refs_0_), channel_id=1, source_target_pairs={{0,10},{1,11},{2,8},{3,9},{4,14},{5,15},{6,12},{7,13},{8,2},{9,3},... | collective-permute-start | bytes 27656 | tf_op jit(solution)/shard_map/ppermute | solution.py:196
  53.4 4.0 %collective-permute-start.20 = (f32[72,128]{1,0:T(8,128)S(1)}, f32[72,128]{1,0:T(8,128)S(1)}, u32[]{:S(2)}, u32[]{:S(2)}) collective-permute-start(f32[72,128]{1,0:T(8,128)S(1)} %join.13.refs_0_), channel_id=1, source_target_pairs={{0,4},{1,5},{2,6},{3,7},{4,0},{5,1},{6,2},{7,3},{8,12},{9,13},{10,... | collective-permute-start | bytes 110600 | tf_op jit(solution)/shard_map/ppermute | solution.py:196
  58.1 5.4 %collective-permute-start.26 = (f32[72,128]{1,0:T(8,128)S(1)}, f32[72,128]{1,0:T(8,128)S(1)}, u32[]{:S(2)}, u32[]{:S(2)}) collective-permute-start(f32[72,128]{1,0:T(8,128)S(1)} %get-tuple-element.167), channel_id=1, source_target_pairs={{0,16},{1,17},{2,18},{3,19},{4,20},{5,21},{6,22},{7,23},{8,24},{9,... | collective-permute-start | bytes 110600 | tf_op jit(solution)/shard_map/ppermute | solution.py:187
  64.0 6.9 %collective-permute-start.27 = (f32[73,128]{1,0:T(8,128)S(1)}, f32[73,128]{1,0:T(8,128)S(1)}, u32[]{:S(2)}, u32[]{:S(2)}) collective-permute-start(f32[73,128]{1,0:T(8,128)S(1)} %get-tuple-element.178.refs_0_), channel_id=1, source_target_pairs={{0,16},{1,17},{2,18},{3,19},{4,20},{5,21},{6,22},{7,23},{8,24},{9,... | collective-permute-start | bytes 112136 | tf_op jit(solution)/shard_map/ppermute | solution.py:187
  68.6 13.9 %collective-permute-start.35 = (f32[96,128]{1,0:T(8,128)S(1)}, f32[96,128]{1,0:T(8,128)S(1)}, u32[]{:S(2)}, u32[]{:S(2)}) collective-permute-start(f32[96,128]{1,0:T(8,128)S(1)} %get-tuple-element.180), channel_id=1, source_target_pairs={{1,2},{3,4},{5,6},{7,8},{9,10},{11,12},{13,14},{15,16},{17,18},{19... | collective-permute-start | bytes 147464 | tf_op jit(solution)/shard_map/ppermute | solution.py:187
  70.9 4.6 %collective-permute-start.28 = (f32[18,128]{1,0:T(8,128)S(1)}, f32[18,128]{1,0:T(8,128)S(1)}, u32[]{:S(2)}, u32[]{:S(2)}) collective-permute-start(f32[18,128]{1,0:T(8,128)S(1)} %join.14.refs_0_), channel_id=1, source_target_pairs={{0,10},{1,11},{2,8},{3,9},{4,14},{5,15},{6,12},{7,13},{8,2},{9,3},... | collective-permute-start | bytes 27656 | tf_op jit(solution)/shard_map/ppermute | solution.py:196
  78.8 3.8 %collective-permute-start.31 = (f32[72,128]{1,0:T(8,128)S(1)}, f32[72,128]{1,0:T(8,128)S(1)}, u32[]{:S(2)}, u32[]{:S(2)}) collective-permute-start(f32[72,128]{1,0:T(8,128)S(1)} %join.15.refs_0_), channel_id=1, source_target_pairs={{0,5},{1,4},{2,7},{3,6},{4,1},{5,0},{6,3},{7,2},{8,13},{9,12},{10,... | collective-permute-start | bytes 110600 | tf_op jit(solution)/shard_map/ppermute | solution.py:196
  78.8 4.2 %collective-permute-start.32 = (f32[72,128]{1,0:T(8,128)S(1)}, f32[72,128]{1,0:T(8,128)S(1)}, u32[]{:S(2)}, u32[]{:S(2)}) collective-permute-start(f32[72,128]{1,0:T(8,128)S(1)} %join.15.refs_0_), channel_id=1, source_target_pairs={{0,4},{1,5},{2,6},{3,7},{4,0},{5,1},{6,2},{7,3},{8,12},{9,13},{10,... | collective-permute-start | bytes 110600 | tf_op jit(solution)/shard_map/ppermute | solution.py:196
  78.8 4.1 %collective-permute-start.33 = (f32[72,128]{1,0:T(8,128)S(1)}, f32[72,128]{1,0:T(8,128)S(1)}, u32[]{:S(2)}, u32[]{:S(2)}) collective-permute-start(f32[72,128]{1,0:T(8,128)S(1)} %join.15.refs_0_), channel_id=1, source_target_pairs={{0,1},{1,0},{2,3},{3,2},{4,5},{5,4},{6,7},{7,6},{8,9},{9,8},{10,11... | collective-permute-start | bytes 110600 | tf_op jit(solution)/shard_map/ppermute | solution.py:196
  83.6 5.0 %collective-permute-start.38 = (f32[72,128]{1,0:T(8,128)S(1)}, f32[72,128]{1,0:T(8,128)S(1)}, u32[]{:S(2)}, u32[]{:S(2)}) collective-permute-start(f32[72,128]{1,0:T(8,128)S(1)} %get-tuple-element.187), channel_id=1, source_target_pairs={{0,16},{1,17},{2,18},{3,19},{4,20},{5,21},{6,22},{7,23},{8,24},{9,... | collective-permute-start | bytes 110600 | tf_op jit(solution)/shard_map/ppermute | solution.py:187
  89.1 7.5 %collective-permute-start.41 = (f32[73,128]{1,0:T(8,128)S(1)}, f32[73,128]{1,0:T(8,128)S(1)}, u32[]{:S(2)}, u32[]{:S(2)}) collective-permute-start(f32[73,128]{1,0:T(8,128)S(1)} %get-tuple-element.206.refs_0_), channel_id=1, source_target_pairs={{0,16},{1,17},{2,18},{3,19},{4,20},{5,21},{6,22},{7,23},{8,24},{9,... | collective-permute-start | bytes 112136 | tf_op jit(solution)/shard_map/ppermute | solution.py:187
  94.2 12.1 %collective-permute-start.40 = (f32[96,128]{1,0:T(8,128)S(1)}, f32[96,128]{1,0:T(8,128)S(1)}, u32[]{:S(2)}, u32[]{:S(2)}) collective-permute-start(f32[96,128]{1,0:T(8,128)S(1)} %get-tuple-element.205), channel_id=1, source_target_pairs={{1,2},{3,4},{5,6},{7,8},{9,10},{11,12},{13,14},{15,16},{17,18},{19... | collective-permute-start | bytes 147464 | tf_op jit(solution)/shard_map/ppermute | solution.py:187
  96.6 4.7 %collective-permute-start.42 = (f32[18,128]{1,0:T(8,128)S(1)}, f32[18,128]{1,0:T(8,128)S(1)}, u32[]{:S(2)}, u32[]{:S(2)}) collective-permute-start(f32[18,128]{1,0:T(8,128)S(1)} %join.16.refs_0_), channel_id=1, source_target_pairs={{0,10},{1,11},{2,8},{3,9},{4,14},{5,15},{6,12},{7,13},{8,2},{9,3},... | collective-permute-start | bytes 27656 | tf_op jit(solution)/shard_map/ppermute | solution.py:196
  102.5 3.8 %collective-permute-start.45 = (f32[72,128]{1,0:T(8,128)S(1)}, f32[72,128]{1,0:T(8,128)S(1)}, u32[]{:S(2)}, u32[]{:S(2)}) collective-permute-start(f32[72,128]{1,0:T(8,128)S(1)} %join.17.refs_18_), channel_id=1, source_target_pairs={{0,5},{1,4},{2,7},{3,6},{4,1},{5,0},{6,3},{7,2},{8,13},{9,12},{10,... | collective-permute-start | bytes 110600 | tf_op jit(solution)/shard_map/ppermute | solution.py:196
  102.9 4.0 %collective-permute-start.46 = (f32[72,128]{1,0:T(8,128)S(1)}, f32[72,128]{1,0:T(8,128)S(1)}, u32[]{:S(2)}, u32[]{:S(2)}) collective-permute-start(f32[72,128]{1,0:T(8,128)S(1)} %join.17.refs_18_), channel_id=1, source_target_pairs={{0,4},{1,5},{2,6},{3,7},{4,0},{5,1},{6,2},{7,3},{8,12},{9,13},{10,... | collective-permute-start | bytes 110600 | tf_op jit(solution)/shard_map/ppermute | solution.py:196
  108.9 5.3 %collective-permute-start.48 = (f32[72,128]{1,0:T(8,128)S(1)}, f32[72,128]{1,0:T(8,128)S(1)}, u32[]{:S(2)}, u32[]{:S(2)}) collective-permute-start(f32[72,128]{1,0:T(8,128)S(1)} %get-tuple-element.219.refs_0_), channel_id=1, source_target_pairs={{0,16},{1,17},{2,18},{3,19},{4,20},{5,21},{6,22},{7,23},{8,24},{9,... | collective-permute-start | bytes 110600 | tf_op jit(solution)/shard_map/ppermute | solution.py:187
  110.9 11.2 %collective-permute-start.55 = (f32[64,128]{1,0:T(8,128)S(1)}, f32[64,128]{1,0:T(8,128)S(1)}, u32[]{:S(2)}, u32[]{:S(2)}) collective-permute-start(f32[64,128]{1,0:T(8,128)S(1)} %get-tuple-element.221), channel_id=1, source_target_pairs={{0,1},{2,3},{4,5},{6,7},{8,9},{10,11},{12,13},{14,15},{16,17},{18,... | collective-permute-start | bytes 98312 | tf_op jit(solution)/shard_map/ppermute | solution.py:187
  110.9 11.2 %collective-permute-start.56 = (f32[64,128]{1,0:T(8,128)S(1)}, f32[64,128]{1,0:T(8,128)S(1)}, u32[]{:S(2)}, u32[]{:S(2)}) collective-permute-start(f32[64,128]{1,0:T(8,128)S(1)} %get-tuple-element.222), channel_id=1, source_target_pairs={{1,2},{3,4},{5,6},{7,8},{9,10},{11,12},{13,14},{15,16},{17,18},{19... | collective-permute-start | bytes 98312 | tf_op jit(solution)/shard_map/ppermute | solution.py:187
  114.2 4.5 %collective-permute-start.49 = (f32[2,128]{1,0:T(2,128)S(1)}, f32[2,128]{1,0:T(2,128)S(1)}, u32[]{:S(2)}, u32[]{:S(2)}) collective-permute-start(f32[2,128]{1,0:T(2,128)S(1)} %join.18.refs_0_), channel_id=1, source_target_pairs={{0,10},{1,11},{2,8},{3,9},{4,14},{5,15},{6,12},{7,13},{8,2},{9,3},... | collective-permute-start | bytes 3080 | tf_op jit(solution)/shard_map/ppermute | solution.py:196
  (34 other events, 102.9 us)
